TPU v7x, 256 devices: a whole 4x4x8 slice. The times are simulated.
256 devices in a mesh: ctx: 32 (over x, z_lo, core), tp: 8 (over z_hi, y).
Axes of the slice: x: 4, y: 4, z: 8 (z_hi: 2, z_lo: 4; z = z_hi * 4 + z_lo), core: 2. Of those that a mesh axis runs over, the one named last changes fastest.
Arguments:
- queries: bfloat16 [4096, 4096], P('ctx', 'tp'), may hold values from -256 to 256
- keys: bfloat16 [4096, 1024], P('ctx', 'tp'), may hold values from -4 to 4
- values: bfloat16 [4096, 1024], P('ctx', 'tp'), may hold values from -6 to 6
- stretch_of: int32 [64], replicated, may hold values from 0 to 63, as said below
- out_weight: bfloat16 [4096, 8192], P('tp'), may hold values from -0.09375 to 0.09375
- grad_heads: bfloat16 [4096, 4096], P('ctx', 'tp'), may hold values from -6 to 6
Outputs:
- mixed: bfloat16 [4096, 8192], P(('ctx', 'tp'))
- q_grad: bfloat16 [4096, 4096], P('ctx', 'tp')
- k_grad: bfloat16 [4096, 1024], P('ctx', 'tp')
- v_grad: bfloat16 [4096, 1024], P('ctx', 'tp')
Inputs may be any that keep to these rules, and one draw needn't show every extreme that they name: `stretch_of`: a permutation of the 64 stretch numbers; the two slots of index i of ctx, slots 2 * i and 2 * i + 1, hold stretches j and 63 - j in either order.
All inputs are finite; a program needn't handle non-finite values.
Results may differ from a plain program's by a relative error of at most 0.039.
Values may be sent and summed in bfloat16 or wider, within the bound.
No kernel may reach another device: no remote copies, remote signals or barrier semaphores. Data moves between devices by JAX's collectives and lax.ppermute only.
A program may use at most 64 MiB of HBM per device.

v0:
```python
import jax
import jax.numpy as jnp
from jax import lax
from jax.sharding import PartitionSpec as P

HD = 128
QPG = 4


NEG = -1e30


def group_rows(block):
    rows = block.shape[0]
    return block.reshape(rows, QPG, HD).transpose(1, 0, 2).reshape(QPG * rows, HD)


def ungroup(stacked, rows):
    return stacked.reshape(QPG, rows, HD).transpose(1, 0, 2).reshape(rows, QPG * HD)


def masked_scores(q_rows, k_block, q_pos, k_pos):
    scores = lax.dot_general(
        q_rows, k_block, (((1,), (1,)), ((), ())), preferred_element_type=jnp.float32
    ) * HD ** (-0.5)
    return jnp.where(k_pos[None, :] <= q_pos[:, None], scores, NEG)


def forward_block(q_part, p_part, k_group, v_group, trips, span):
    count = q_part.shape[0]
    key_count = k_group.shape[0]
    offsets = jnp.arange(span, dtype=jnp.int32)

    def score_step(index, buffer):
        start = index * span
        k_block = lax.dynamic_slice_in_dim(k_group, start, span, 0)
        scores = masked_scores(q_part, k_block, p_part, start + offsets)
        return lax.dynamic_update_slice_in_dim(buffer, scores, start, 1)

    buffer = lax.fori_loop(0, trips, score_step, jnp.full((count, key_count), NEG, jnp.float32))
    top = jnp.max(buffer, axis=1)
    lse = top + jnp.log(jnp.sum(jnp.exp(buffer - top[:, None]), axis=1))

    def value_step(index, accum):
        start = index * span
        v_block = lax.dynamic_slice_in_dim(v_group, start, span, 0)
        scores = lax.dynamic_slice_in_dim(buffer, start, span, 1)
        weights = jnp.exp(scores - lse[:, None]).astype(jnp.bfloat16)
        return accum + jnp.dot(weights, v_block, preferred_element_type=jnp.float32)

    accum = lax.fori_loop(0, trips, value_step, jnp.zeros((count, HD), jnp.float32))
    return (accum.astype(jnp.bfloat16), lse)


def forward_rows(q_rows, q_pos, k_group, v_group, trips, span):
    o_part, lse_part = forward_block(q_rows, q_pos, k_group, v_group, trips, span)
    return (o_part, lse_part)


def backward_rows(item, k_group, v_group, span, grads):
    q_rows, q_pos, do_rows, lse, delta, trips, top_id = item
    count = q_rows.shape[0]
    offsets = jnp.arange(span, dtype=jnp.int32)

    def grad_step(index, carry):
        start = index * span
        k_block = lax.dynamic_slice_in_dim(k_group, start, span, 0)
        v_block = lax.dynamic_slice_in_dim(v_group, start, span, 0)
        scores = masked_scores(q_rows, k_block, q_pos, start + offsets)
        probs = jnp.exp(scores - lse[:, None])
        dprobs = lax.dot_general(
            do_rows, v_block, (((1,), (1,)), ((), ())), preferred_element_type=jnp.float32
        )
        dscores = (probs * (dprobs - delta[:, None])).astype(jnp.bfloat16)
        q_accum = carry[0] + jnp.dot(dscores, k_block, preferred_element_type=jnp.float32)
        weights = probs.astype(jnp.bfloat16)
        k_piece = lax.dot_general(
            dscores, q_rows, (((0,), (0,)), ((), ())), preferred_element_type=jnp.float32
        ) * HD ** (-0.5)
        v_piece = lax.dot_general(
            weights, do_rows, (((0,), (0,)), ((), ())), preferred_element_type=jnp.float32
        )
        k_sum = lax.dynamic_update_slice_in_dim(
            carry[1], lax.dynamic_slice_in_dim(carry[1], start, span, 0) + k_piece, start, 0
        )
        v_sum = lax.dynamic_update_slice_in_dim(
            carry[2], lax.dynamic_slice_in_dim(carry[2], start, span, 0) + v_piece, start, 0
        )
        return (q_accum, k_sum, v_sum)

    start_carry = (jnp.zeros((count, HD), jnp.float32),)
    start_carry = (start_carry[0], grads[0], grads[1])
    return lax.fori_loop(0, trips, grad_step, start_carry)


def on_device(queries, keys, values, stretch_of, out_weight, grad_heads):
    tokens = queries.shape[0]
    stretch = tokens // 2
    groups = keys.shape[1] // HD
    width = groups * HD
    span = 4 * stretch
    slots = 2 * lax.axis_size("ctx")
    total = slots * stretch
    mine = lax.axis_index("ctx")
    gathered_k, gathered_v = (
        lax.all_gather(keys, "ctx", axis=0, tiled=True),
        lax.all_gather(values, "ctx", axis=0, tiled=True),
    )
    slot_ids = jnp.arange(slots, dtype=jnp.int32)
    inverse = jnp.sum(
        jnp.where(stretch_of[None, :] == slot_ids[:, None], slot_ids[None, :], 0), axis=1
    )
    keys_sorted = jnp.take(gathered_k.reshape(slots, stretch, width), inverse, axis=0).reshape(
        total, width
    )
    values_sorted = jnp.take(gathered_v.reshape(slots, stretch, width), inverse, axis=0).reshape(
        total, width
    )
    local_ids = [jnp.take(stretch_of, 2 * mine + part) for part in range(2)]
    offsets = jnp.tile(jnp.arange(stretch, dtype=jnp.int32), QPG)
    items = []
    outs_group = []
    for part in range(2):
        q_rows = group_rows(queries[part * stretch : (part + 1) * stretch])
        q_pos = local_ids[part] * stretch + offsets
        trips = (local_ids[part] * stretch + stretch - 1) // span + 1
        o_rows, lse = forward_rows(q_rows, q_pos, keys_sorted, values_sorted, trips, span)
        do_rows = group_rows(grad_heads[part * stretch : (part + 1) * stretch])
        delta = jnp.sum(do_rows.astype(jnp.float32) * o_rows.astype(jnp.float32), axis=1)
        items.append((q_rows, q_pos, do_rows, lse, delta, trips, local_ids[part]))
        outs_group.append(ungroup(o_rows, stretch))
    attn_groups = jnp.concatenate(outs_group, axis=0)
    mixed = lax.psum_scatter(
        jnp.dot(attn_groups, out_weight, preferred_element_type=jnp.float32).astype(jnp.bfloat16),
        "tp",
        scatter_dimension=0,
        tiled=True,
    )
    grads = (jnp.zeros((total, HD), jnp.float32), jnp.zeros((total, HD), jnp.float32))
    parts_out = []
    for item in items:
        q_accum, k_sum, v_sum = backward_rows(item, keys_sorted, values_sorted, span, grads)
        grads = (k_sum, v_sum)
        parts_out.append(ungroup((q_accum * HD ** (-0.5)).astype(jnp.bfloat16), stretch))
    q_groups = jnp.concatenate(parts_out, axis=0)
    k_list = [grads[0]]
    v_list = [grads[1]]
    sorted_term = jnp.concatenate(k_list + v_list, axis=1)
    term = jnp.take(sorted_term.reshape(slots, stretch, 2 * width), stretch_of, axis=0).reshape(
        total, 2 * width
    )
    reduced = lax.psum_scatter(term, "ctx", scatter_dimension=0, tiled=True)
    k_grad = reduced[:, :width].astype(jnp.bfloat16)
    v_grad = reduced[:, width:].astype(jnp.bfloat16)
    return (mixed, q_groups, k_grad, v_grad)


def solution(mesh):
    placed = (P("ctx", "tp"), P("ctx", "tp"), P("ctx", "tp"), P(), P("tp", None), P("ctx", "tp"))
    return jax.shard_map(
        on_device,
        mesh=mesh,
        in_specs=placed,
        out_specs=(P(("ctx", "tp"), None), P("ctx", "tp"), P("ctx", "tp"), P("ctx", "tp")),
        check_vma=False,
    )
```

profile of v0, /device:TPU:1, one launch (start us, length us, event | category | flops | bytes accessed | tf_op | source)
XLA Modules:
  0.0 564.5 jit_solution(16604799683749099138)
XLA Ops:
  15.5 57.5 %all-gather.5.cloned.1.call-done = bf16[4096,128]{1,0:T(8,128)(2,1)} async-done(((bf16[128,128]{1,0:T(8,128)(2,1)}), bf16[4096,128]{1,0:T(8,128)(2,1)}) %all-gather.5.cloned.1.call-update) | async-done | bytes 1048592 | tf_op jit(solution)/shard_map/all_gather | solution.py:107
  73.0 2.0 gather_fusion.2
  74.9 57.7 %all-gather.3.cloned.1.call-done = bf16[4096,128]{1,0:T(8,128)(2,1)} async-done(((bf16[128,128]{1,0:T(8,128)(2,1)}), bf16[4096,128]{1,0:T(8,128)(2,1)}) %all-gather.3.cloned.1.call-update) | async-done | bytes 1048592 | tf_op jit(solution)/shard_map/all_gather | solution.py:106
  132.6 2.9 gather_fusion.1
  135.5 2.5 broadcast_select_fusion
  138.0 2.2 broadcast.85.clone
  140.2 5.4 while.77
  145.6 2.7 reduce_max.19
  148.4 2.8 exponential_reduce_fusion
  151.2 4.2 while.75
  155.4 2.2 broadcast.85.clone.1
  157.6 25.6 %while.76 = (s32[]{:T(128)}, f32[256,4096]{0,1:T(8,128)}, s32[]{:T(128)}, bf16[4096,128]{1,0:T(8,128)(2,1)}, bf16[256,128]{1,0:T(8,128)(2,1)S(1)}, /*index=5*/s3...) while((s32[]{:T(128)}, f32[256,4096]{0,1:T(8,128)}, s32[]{:T(128)}, ...), condition=%wide.region_2.4_spmd.clone, body=%wide.region_1.3_spmd.clone.sunk | while | flops 16974340 | bytes 400547 | solution.py:40
  165.0 1.8 fusion.127
  166.8 1.7 fusion.127
  172.3 1.8 fusion.127
  174.2 1.7 fusion.127
  177.8 1.8 fusion.127
  183.2 2.7 reduce_max.18
  186.0 2.8 exponential_reduce_fusion.1
  188.8 19.4 %while.74 = (s32[]{:T(128)}, f32[256,128]{1,0:T(8,128)S(1)}, s32[]{:T(128)}, f32[256,4096]{0,1:T(8,128)}, f32[256]{0:T(256)S(1)}, /*index=5*/bf16[4096,128]{1,0:...) while((s32[]{:T(128)}, f32[256,128]{1,0:T(8,128)S(1)}, s32[]{:T(128)}, f32[256,4096]{0,1:T(8,128)}, ...), condition=%wide.region_6.8_spmd, body=%wide.region_5.7_spmd.sunk | while | flops 16941060 | bytes 1639587 | solution.py:51
  210.8 72.7 %while.78 = (s32[]{:T(128)}, f32[256,128]{1,0:T(8,128)S(1)}, f32[4096,128]{1,0:T(8,128)S(1)}, f32[4096,128]{1,0:T(8,128)}, s32[]{:T(128)}, /*index=5*/bf16[4096,...) while((s32[]{:T(128)}, f32[256,128]{1,0:T(8,128)S(1)}, ...), condition=%wide.region_16.18_spmd.clone, body=%wide.region_15.17_spmd.clone.sunk | while | flops 84541952 | bytes 2433255 | solution.py:93
  229.8 1.7 fusion.144
  266.1 1.8 fusion.144
  271.3 1.7 fusion.144
  276.5 1.7 fusion.144
  283.6 15.6 %while.79 = (s32[]{:T(128)}, f32[256,128]{1,0:T(8,128)S(1)}, f32[4096,128]{1,0:T(8,128)S(1)}, f32[4096,128]{1,0:T(8,128)}, s32[]{:T(128)}, /*index=5*/bf16[4096,...) while((s32[]{:T(128)}, f32[256,128]{1,0:T(8,128)S(1)}, ...), condition=%wide.region_19.21_spmd.clone, body=%wide.region_18.20_spmd.clone.sunk | while | flops 84541952 | bytes 2433255 | solution.py:93
  299.2 3.8 pad_maximum_fusion
  303.0 5.0 gather_fusion
  307.9 3.9 bitcast_select_fusion
  312.0 6.0 %convolution_convert_fusion = bf16[128,8192]{1,0:T(8,128)(2,1)} fusion(bf16[512,8192]{1,0:T(8,128)(2,1)} %param.24, bf16[64,512]{1,0:T(8,128)(2,1)S(1)} %bitcast.179, bf16[64,512]{1,0:T(8,128)(2,1)S(1)} %bitcast.180), kind=kOutput, calls=%fused_computation.87 | convolution fusion | flops 1075052544 | bytes 10616832 | tf_op jit(solution)/shard_map/dot_general | solution.py:134
  318.9 139.3 %reduce-scatter.5.cloned.1.call-done = f32[128,256]{1,0:T(8,128)} async-done(((f32[4096,256]{1,0:T(8,128)}), f32[128,256]{1,0:T(8,128)}) %reduce-scatter.5.cloned.1.call-update) | async-done | bytes 131088 | tf_op jit(solution)/shard_map/reduce_scatter | solution.py:152
  459.7 98.2 %reduce-scatter.3.cloned.1.call-done = bf16[16,8192]{1,0:T(8,128)(2,1)} async-done(((bf16[128,8192]{1,0:T(8,128)(2,1)}), bf16[16,8192]{1,0:T(8,128)(2,1)}) %reduce-scatter.3.cloned.1.call-update) | async-done | bytes 262160 | tf_op jit(solution)/shard_map/reduce_scatter | solution.py:133
  (293 shorter events, 138.0 us)
Async XLA Ops:
  7.2 65.8 %all-gather.5.cloned.1.call-start = ((), (), s32[]{:S(2)}) async-start(), calls=%async_computation.3 | async-start | bytes 1081344 | tf_op jit(solution)/shard_map/all_gather | solution.py:107
  7.9 124.7 %all-gather.3.cloned.1.call-start = ((), (), s32[]{:S(2)}) async-start(), calls=%async_computation.2 | async-start | bytes 1081344 | tf_op jit(solution)/shard_map/all_gather | solution.py:106
  8.6 449.5 %reduce-scatter.5.cloned.1.call-start = ((), (), s32[]{:S(2)}) async-start(), calls=%async_computation.5 | async-start | bytes 4325376 | tf_op jit(solution)/shard_map/reduce_scatter | solution.py:152
  208.2 1.0 copy-start
  311.8 246.1 %reduce-scatter.3.cloned.1.call-start = ((), (), s32[]{:S(2)}) async-start(), calls=%async_computation.4 | async-start | bytes 2359296 | tf_op jit(solution)/shard_map/reduce_scatter | solution.py:133
Sparse Core Ops, SparseCore 0:
  9.9 63.0 all-gather.4
  74.8 57.7 all-gather.2
  311.9 146.1 reduce-scatter.4
  462.7 95.2 reduce-scatter.2
where the time goes:
time: 570 us; the launch traced here: 564 us
  waiting for transfers between devices  354 us (62%)
  matrix products  126 us (22%)
  local copies, waits for them, and re-layouts  42.5 us (7%)
  other arithmetic  25.5 us (4%)
  between operations  15.3 us (3%)
    reduce_scatter x1, waiting for transfers between devices, on_device(): reduced = lax.psum_scatter(term, 'ctx', scatter_dimension=0, tiled=True)  139 us
    reduce_scatter x1, waiting for transfers between devices, on_device(): lax.psum_scatter(jnp.dot(attn_groups, out_weight, preferred_element_type=...  98.2 us
    all_gather x1, waiting for transfers between devices, on_device(): lax.all_gather(keys, 'ctx', axis=0, tiled=True)  57.7 us
    all_gather x1, waiting for transfers between devices, on_device(): lax.all_gather(values, 'ctx', axis=0, tiled=True)  57.5 us
    dot_general x34, matrix products, masked_scores(): lax.dot_general(q_rows, k_block, (((1,), (1,)), ((), ())), preferred_elem...  47.3 us
    dot_general x17, matrix products, grad_step(): lax.dot_general(weights, do_rows, (((0,), (0,)), ((), ())), preferred_ele...  29.5 us
    dynamic_slice x34, local copies, waits for them, and re-layouts, value_step(): scores = lax.dynamic_slice_in_dim(buffer, start, span, 1)  18.7 us
    dot_general x17, matrix products, grad_step(): jnp.dot(dscores, k_block, preferred_element_type=jnp.float32)  18.3 us
  transfers between devices with their start and end apart: 4, of which 4 were waited for; matrix products, arithmetic and copies ran while one was open for 3% of the time, Pallas kernels for 0%

commit v1 on v0

v1 whole, which is shorter than its diff:
```python
import functools
import jax
import jax.numpy as jnp
from jax import lax
from jax.experimental import pallas as pl
from jax.experimental.pallas import tpu as pltpu

HD = 128
QPG = 4
NEG = -1e30
SCALE = HD ** (-0.5)
NT = (((1,), (1,)), ((), ()))
NN = (((1,), (0,)), ((), ()))
TN = (((0,), (0,)), ((), ()))


def dot(a, b, dims):
    return lax.dot_general(a, b, dims, preferred_element_type=jnp.float32)


def fwd_kernel(stretch, span, ids_ref, own_ref, q_ref, kv_ref, do_ref,
               attn_ref, p_ref, ks_ref, vs_ref, qs_ref, ds_ref, delta_ref,
               s_buf, top_ref, sum_ref, acc_ref, diff_ref):
    slots = ids_ref.shape[0]
    steps = p_ref.shape[0]
    cols = QPG * stretch
    for slot in range(slots):
        start = pl.multiple_of(ids_ref[slot] * stretch, stretch)
        ks_ref[pl.ds(start, stretch), :] = kv_ref[slot * stretch:(slot + 1) * stretch, :HD]
        vs_ref[pl.ds(start, stretch), :] = kv_ref[slot * stretch:(slot + 1) * stretch, HD:]
    for part in range(2):
        for head in range(QPG):
            rows = slice(part * stretch, (part + 1) * stretch)
            to = slice(head * stretch, (head + 1) * stretch)
            qs_ref[part, to, :] = q_ref[rows, head * HD:(head + 1) * HD]
            ds_ref[part, to, :] = do_ref[rows, head * HD:(head + 1) * HD]
    k_at = lax.broadcasted_iota(jnp.int32, (span, cols), 0)
    q_at = lax.broadcasted_iota(jnp.int32, (span, cols), 1) % stretch
    diff_ref[...] = k_at - q_at
    top_ref[...] = jnp.full_like(top_ref, NEG)
    sum_ref[...] = jnp.zeros_like(sum_ref)
    acc_ref[...] = jnp.zeros_like(acc_ref)
    first = (own_ref[0] * stretch + stretch - 1) // span + 1

    def place(step):
        part = jnp.where(step >= first, 1, 0)
        chunk = step - part * first
        return part, chunk

    def score_step(step, carry):
        part, chunk = place(step)
        start = pl.multiple_of(chunk * span, span)
        scores = dot(ks_ref[pl.ds(start, span), :], qs_ref[part], NT) * SCALE
        limit = own_ref[part] * stretch - start
        scores = jnp.where(diff_ref[...] <= limit, scores, NEG)
        s_buf[step] = scores
        top_ref[part] = jnp.maximum(top_ref[part], jnp.max(scores.reshape(span // 8, 8, cols), axis=0))
        return carry

    lax.fori_loop(0, steps, score_step, 0, unroll=UNROLL)
    for part in range(2):
        top_ref[part] = jnp.broadcast_to(jnp.max(top_ref[part], axis=0, keepdims=True), (8, cols))

    def sum_step(step, carry):
        part, chunk = place(step)
        shifted = jnp.exp(s_buf[step].reshape(span // 8, 8, cols) - top_ref[part][None])
        s_buf[step] = shifted.reshape(span, cols)
        sum_ref[part] += jnp.sum(shifted, axis=0)
        return carry

    lax.fori_loop(0, steps, sum_step, 0, unroll=UNROLL)
    for part in range(2):
        total = jnp.sum(sum_ref[part], axis=0, keepdims=True)
        sum_ref[part] = jnp.broadcast_to(1.0 / total, (8, cols))

    def value_step(step, carry):
        part, chunk = place(step)
        start = pl.multiple_of(chunk * span, span)
        weights = (s_buf[step].reshape(span // 8, 8, cols) * sum_ref[part][None]).reshape(span, cols)
        weights = weights.astype(jnp.bfloat16)
        p_ref[step] = weights
        acc_ref[part] += dot(vs_ref[pl.ds(start, span), :], weights, TN)
        return carry

    lax.fori_loop(0, steps, value_step, 0, unroll=UNROLL)
    for part in range(2):
        out = acc_ref[part].T.astype(jnp.bfloat16)
        prod = ds_ref[part].astype(jnp.float32) * out.astype(jnp.float32)
        delta_ref[part] = jnp.broadcast_to(jnp.sum(prod.T, axis=0, keepdims=True), (8, cols))
        for head in range(QPG):
            attn_ref[part * stretch:(part + 1) * stretch, head * HD:(head + 1) * HD] = (
                out[head * stretch:(head + 1) * stretch])


def bwd_kernel(stretch, span, ids_ref, own_ref, p_ref, ks_ref, vs_ref, qs_ref, ds_ref, delta_ref,
               dq_ref, dkv_ref, acc_ref, dk_ref, dv_ref):
    slots = ids_ref.shape[0]
    steps = p_ref.shape[0]
    cols = QPG * stretch
    acc_ref[...] = jnp.zeros_like(acc_ref)
    dk_ref[...] = jnp.zeros_like(dk_ref)
    dv_ref[...] = jnp.zeros_like(dv_ref)
    first = (own_ref[0] * stretch + stretch - 1) // span + 1

    def grad_step(step, carry):
        part = jnp.where(step >= first, 1, 0)
        start = pl.multiple_of((step - part * first) * span, span)
        here = pl.ds(start, span)
        weights = p_ref[step]
        grad_probs = dot(vs_ref[here, :], ds_ref[part], NT)
        moved = (grad_probs.reshape(span // 8, 8, cols) - delta_ref[part][None]).reshape(span, cols)
        grad_scores = (weights.astype(jnp.float32) * moved).astype(jnp.bfloat16)
        dv_ref[here, :] += dot(weights, ds_ref[part], NN)
        dk_ref[here, :] += dot(grad_scores, qs_ref[part], NN)
        acc_ref[part] += dot(ks_ref[here, :], grad_scores, TN)
        return carry

    lax.fori_loop(0, steps, grad_step, 0, unroll=UNROLL)
    for part in range(2):
        out = (acc_ref[part].T * SCALE).astype(jnp.bfloat16)
        for head in range(QPG):
            dq_ref[part * stretch:(part + 1) * stretch, head * HD:(head + 1) * HD] = (
                out[head * stretch:(head + 1) * stretch])
    for slot in range(slots):
        start = pl.multiple_of(ids_ref[slot] * stretch, stretch)
        to = slice(slot * stretch, (slot + 1) * stretch)
        dkv_ref[to, :HD] = (dk_ref[pl.ds(start, stretch), :] * SCALE).astype(jnp.bfloat16)
        dkv_ref[to, HD:] = dv_ref[pl.ds(start, stretch), :].astype(jnp.bfloat16)


UNROLL = 1
MIB = 1024 * 1024


def forward(ids, own, queries, kv, grad_heads):
    tokens = queries.shape[0]
    stretch = tokens // 2
    total = kv.shape[0]
    span = 4 * stretch
    cols = QPG * stretch
    steps = total // span + 1
    smem = pl.BlockSpec(memory_space=pltpu.SMEM)
    vmem = pl.BlockSpec(memory_space=pltpu.VMEM)
    b16, f32 = jnp.bfloat16, jnp.float32
    shape = jax.ShapeDtypeStruct
    return pl.pallas_call(
        functools.partial(fwd_kernel, stretch, span),
        out_shape=(
            shape((tokens, QPG * HD), b16),
            shape((steps, span, cols), b16),
            shape((total, HD), b16),
            shape((total, HD), b16),
            shape((2, cols, HD), b16),
            shape((2, cols, HD), b16),
            shape((2, 8, cols), f32),
        ),
        in_specs=[smem, smem, vmem, vmem, vmem],
        out_specs=[vmem] * 7,
        scratch_shapes=[
            pltpu.VMEM((steps, span, cols), f32),
            pltpu.VMEM((2, 8, cols), f32),
            pltpu.VMEM((2, 8, cols), f32),
            pltpu.VMEM((2, HD, cols), f32),
            pltpu.VMEM((span, cols), jnp.int32),
        ],
        compiler_params=pltpu.CompilerParams(vmem_limit_bytes=32 * MIB),
        name="attention_forward",
    )(ids, own, queries, kv, grad_heads)


def backward(ids, own, saved):
    probs, ks, vs, qs, ds, delta = saved
    total = ks.shape[0]
    steps, span, cols = probs.shape
    stretch = cols // QPG
    smem = pl.BlockSpec(memory_space=pltpu.SMEM)
    vmem = pl.BlockSpec(memory_space=pltpu.VMEM)
    b16, f32 = jnp.bfloat16, jnp.float32
    shape = jax.ShapeDtypeStruct
    return pl.pallas_call(
        functools.partial(bwd_kernel, stretch, span),
        out_shape=(shape((2 * stretch, QPG * HD), b16), shape((total, 2 * HD), b16)),
        in_specs=[smem, smem] + [vmem] * 6,
        out_specs=[vmem] * 2,
        scratch_shapes=[
            pltpu.VMEM((2, HD, cols), f32),
            pltpu.VMEM((total, HD), f32),
            pltpu.VMEM((total, HD), f32),
        ],
        compiler_params=pltpu.CompilerParams(vmem_limit_bytes=32 * MIB),
        name="attention_backward",
    )(ids, own, probs, ks, vs, qs, ds, delta)


def on_device(queries, keys, values, stretch_of, out_weight, grad_heads):
    own = lax.dynamic_slice_in_dim(stretch_of, 2 * lax.axis_index("ctx"), 2, 0)
    kv = lax.all_gather(jnp.concatenate([keys, values], axis=1), "ctx", axis=0, tiled=True)
    attn, *saved = forward(stretch_of, own, queries, kv, grad_heads)
    mixed = lax.psum_scatter(
        jnp.dot(attn, out_weight, preferred_element_type=jnp.float32).astype(jnp.bfloat16),
        "tp", scatter_dimension=0, tiled=True)
    q_grad, term = backward(stretch_of, own, saved)
    reduced = lax.psum_scatter(term, "ctx", scatter_dimension=0, tiled=True)
    return mixed, q_grad, reduced[:, :HD], reduced[:, HD:]


def solution(mesh):
    from jax.sharding import PartitionSpec as P
    placed = (P("ctx", "tp"), P("ctx", "tp"), P("ctx", "tp"), P(), P("tp", None), P("ctx", "tp"))
    return jax.shard_map(
        on_device,
        mesh=mesh,
        in_specs=placed,
        out_specs=(P(("ctx", "tp"), None), P("ctx", "tp"), P("ctx", "tp"), P("ctx", "tp")),
        check_vma=False,
    )
```

time: 570 us -> 346 us (0.61)
  matrix products: 126 us -> 5.99 us
  waiting for transfers between devices: 354 us -> 299 us
  local copies, waits for them, and re-layouts: 42.5 us -> 6.19 us
  other arithmetic: 25.5 us -> 1.41 us
  Pallas kernels: 0 us -> 17.9 us
    dot_general x120 -> x1, matrix products: 126 us -> 5.99 us  [on_device(): jnp.dot(attn, out_weight, preferred_element_type=jnp.float32)]
    all_gather x2 -> x1, waiting for transfers between devices: 115 us -> 65.4 us  [on_device(): lax.all_gather(jnp.concatenate([keys, values], axis=1), 'ctx', axis=0, ti...]
    dynamic_slice x34 -> x1, local copies, waits for them, and re-layouts: 18.7 us -> 0.73 us  [on_device(): own = lax.dynamic_slice_in_dim(stretch_of, 2 * lax.axis_index('ctx'), 2, 0)]
    pallas_call x0 -> x2, Pallas kernels: none -> 17.9 us  [the longest x1 9.02 us: backward(): pl.pallas_call(functools.partial(bwd_kernel, stretch, span), out_shape=(s...]
    gather x3 -> x0, local copies, waits for them, and re-layouts: 9.83 us -> none  [the longest x1 4.96 us: on_device(): jnp.take(sorted_term.reshape(slots, stretch, 2 * width), stretch_of, axis=0)]
    another operation x9 -> x0, local copies, waits for them, and re-layouts: 7.36 us -> none
    select_n x4 -> x0, other arithmetic: 7 us -> none  [the longest x2 4.53 us: on_device(): jnp.take(sorted_term.reshape(slots, stretch, 2 * width), stretch_of, axis=0)]
    reduce_sum x5 -> x0, other arithmetic: 6.64 us -> none  [the longest x2 5.63 us: forward_block(): lse = top + jnp.log(jnp.sum(jnp.exp(buffer - top[:, None]), axis=1))]
  transfers between devices with their start and end apart: 4 -> 3, of which waited for: 4 -> 3; matrix products, arithmetic and copies ran while one was open for 3% -> 2% of each run, Pallas kernels for 0% -> 0%
where the time goes in v1:
time: 346 us; the launch traced here: 345 us
  waiting for transfers between devices  299 us (86%)
  Pallas kernels  17.9 us (5%)
  between operations  13.8 us (4%)
  local copies, waits for them, and re-layouts  6.19 us (2%)
  matrix products  5.99 us (2%)
    reduce_scatter x1, waiting for transfers between devices, on_device(): reduced = lax.psum_scatter(term, 'ctx', scatter_dimension=0, tiled=True)  135 us
    reduce_scatter x1, waiting for transfers between devices, on_device(): lax.psum_scatter(jnp.dot(attn, out_weight, preferred_element_type=jnp.flo...  99.4 us
    all_gather x1, waiting for transfers between devices, on_device(): lax.all_gather(jnp.concatenate([keys, values], axis=1), 'ctx', axis=0, ti...  65.4 us
    pallas_call x1, Pallas kernels, backward(): pl.pallas_call(functools.partial(bwd_kernel, stretch, span), out_shape=(s...  9.02 us
    pallas_call x1, Pallas kernels, forward(): pl.pallas_call(functools.partial(fwd_kernel, stretch, span), out_shape=(s...  8.87 us
  transfers between devices with their start and end apart: 3, of which 3 were waited for; matrix products, arithmetic and copies ran while one was open for 2% of the time, Pallas kernels for 0%

profile of v1, /device:TPU:1, one launch (start us, length us, event | category | flops | bytes accessed | tf_op | source)
XLA Modules:
  0.0 344.8 jit_solution(2606311655619844829)
XLA Ops:
  7.2 0.0 all-gather.2.cloned.1.call-start
  7.2 1.4 pad_maximum_fusion
  8.6 0.0 all-gather.2.cloned.1.call-update
  8.6 0.0 reduce-scatter.5.cloned.1.call-start
  8.7 0.7 dynamic_slice.3.own_ref
  9.4 65.4 %all-gather.2.cloned.1.call-done.kv_ref = bf16[4096,256]{1,0:T(8,128)(2,1)} async-done(((bf16[128,256]{1,0:T(8,128)(2,1)}), bf16[4096,256]{1,0:T(8,128)(2,1)}) %all-gather.2.cloned.1.call-update) | async-done | bytes 2097168 | tf_op jit(solution)/shard_map/all_gather | solution.py:197
  74.8 0.0 copy-start
  74.8 1.6 copy-done
  76.4 0.0 copy-start.1
  76.4 0.9 copy-done.1
  77.3 0.0 copy-start.2
  77.3 0.9 copy-done.2
  78.2 0.0 copy-start.3
  78.2 0.7 copy-done.3
  78.9 8.9 %attention_forward.1 = (bf16[128,512]{1,0:T(8,128)(2,1)S(1)}, bf16[17,256,256]{2,1,0:T(8,128)(2,1)S(1)}, bf16[4096,128]{1,0:T(8,128)(2,1)S(1)}, bf16[4096,128]{1...) custom-call(s32[64]{0:T(128)S(1)} %copy-done.3, ...), custom_call_target="tpu_custom_call" | custom-call | tf_op jit(solution)/shard_map/attention_forward/pallas_call | solution.py:146
  87.8 9.0 %attention_backward.1 = (bf16[128,512]{1,0:T(8,128)(2,1)}, bf16[4096,256]{1,0:T(8,128)(2,1)}) custom-call(s32[64]{0:T(128)S(1)} %copy-done.3, s32[2]{0:T(128)S(1)} %dynamic_slice.3.own_ref, bf16[17,256,256]{2,1,0:T(8,128)(2,1)S(1)} %get-tuple-element.14.p_ref, bf16[4096,128]{1,0:T(8,128)(2,1)S(1)} %get-tuple-element.15.ks_ref, ...), custom_call_target="tpu_custom_call" | custom-call | tf_op jit(solution)/shard_map/attention_backward/pallas_call | solution.py:180
  96.8 0.0 reduce-scatter.5.cloned.1.call-update
  96.8 0.0 reduce-scatter.3.cloned.1.call-start
  96.9 6.0 %convolution_convert_fusion = bf16[128,8192]{1,0:T(8,128)(2,1)} fusion(bf16[128,512]{1,0:T(8,128)(2,1)S(1)} %get-tuple-element.13, bf16[512,8192]{1,0:T(8,128)(2,1)} %param.10), kind=kOutput, calls=%fused_computation | convolution fusion | flops 1074790400 | bytes 10616832 | tf_op jit(solution)/shard_map/dot_general | solution.py:200
  102.9 0.0 reduce-scatter.3.cloned.1.call-update
  102.9 134.6 %reduce-scatter.5.cloned.1.call-done = bf16[128,256]{1,0:T(8,128)(2,1)} async-done(((bf16[4096,256]{1,0:T(8,128)(2,1)}), bf16[128,256]{1,0:T(8,128)(2,1)}) %reduce-scatter.5.cloned.1.call-update) | async-done | bytes 65552 | tf_op jit(solution)/shard_map/reduce_scatter | solution.py:203
  237.5 1.4 fusion
  238.9 99.4 %reduce-scatter.3.cloned.1.call-done = bf16[16,8192]{1,0:T(8,128)(2,1)} async-done(((bf16[128,8192]{1,0:T(8,128)(2,1)}), bf16[16,8192]{1,0:T(8,128)(2,1)}) %reduce-scatter.3.cloned.1.call-update) | async-done | bytes 262160 | tf_op jit(solution)/shard_map/reduce_scatter | solution.py:199
Async XLA Ops:
  7.2 67.7 %all-gather.2.cloned.1.call-start = ((), (), s32[]{:S(2)}) async-start(), calls=%async_computation.2 | async-start | bytes 2162688 | tf_op jit(solution)/shard_map/all_gather | solution.py:197
  8.6 228.8 %reduce-scatter.5.cloned.1.call-start = ((), (), s32[]{:S(2)}) async-start(), calls=%async_computation.4 | async-start | bytes 2162688 | tf_op jit(solution)/shard_map/reduce_scatter | solution.py:203
  74.8 1.6 copy-start
  76.4 0.9 copy-start.1
  77.3 0.9 copy-start.2
  78.2 0.7 copy-start.3
  96.8 241.5 %reduce-scatter.3.cloned.1.call-start = ((), (), s32[]{:S(2)}) async-start(), calls=%async_computation.3 | async-start | bytes 2359296 | tf_op jit(solution)/shard_map/reduce_scatter | solution.py:199
Sparse Core Ops, SparseCore 0:
  10.4 64.3 all-gather.1
  96.9 140.5 reduce-scatter.4
  242.7 95.5 reduce-scatter.2

commit v2 on v1

v2 whole, which is shorter than its diff:
```python
import functools
import jax
import jax.numpy as jnp
from jax import lax
from jax.experimental import pallas as pl
from jax.experimental.pallas import tpu as pltpu
from jax.sharding import Mesh, PartitionSpec as P

HD = 128
QPG = 4
NEG = -1e30
SCALE = HD ** (-0.5)
NT = (((1,), (1,)), ((), ()))
NN = (((1,), (0,)), ((), ()))
TN = (((0,), (0,)), ((), ()))
MIB = 1024 * 1024
NX, NZ, NC, NH, NY = 4, 4, 2, 2, 4
CTX = ("x", "zl", "core")
TP = ("zh", "y")
MIX_SPAN = 1024
UNROLL_F = 1
UNROLL_B = 1


def dot(a, b, dims):
    return lax.dot_general(a, b, dims, preferred_element_type=jnp.float32)


def slot_of(x, zl, core, half):
    return ((x * NZ + zl) * NC + core) * 2 + half


def own_slot():
    return slot_of(lax.axis_index("x"), lax.axis_index("zl"), lax.axis_index("core"), 0)


def fwd_kernel(stretch, span, ids_ref, q_hbm, kv_hbm, do_hbm, w_hbm,
               mix0, mix1, mix2, mix3, p_ref, kv_ref, qs_ref, ds_ref, delta_ref,
               q_ref, do_ref, w_ref, s_buf, top_ref, sum_ref, acc_ref, diff_ref, attn_ref, turned_ref,
               mixed_ref, kv_sem, q_sem, do_sem, w_sem, out_sem):
    steps = p_ref.shape[0]
    cols = QPG * stretch
    copies = [pltpu.make_async_copy(q_hbm, q_ref, q_sem), pltpu.make_async_copy(do_hbm, do_ref, do_sem)]
    for copy in copies:
        copy.start()
    zl = lax.axis_index("zl")
    place_of = 0
    for core in range(NC):
        for x in range(NX):
            for step in range(NZ):
                first_slot = slot_of(x, jnp.bitwise_xor(zl, step), core, 0)
                for half in range(2):
                    start = pl.multiple_of(ids_ref[first_slot + half] * stretch, stretch)
                    pltpu.make_async_copy(
                        kv_hbm.at[pl.ds(place_of * stretch, stretch), :],
                        kv_ref.at[pl.ds(start, stretch), :], kv_sem).start()
                    place_of += 1
    weight_copy = pltpu.make_async_copy(w_hbm, w_ref, w_sem)
    weight_copy.start()
    k_at = lax.broadcasted_iota(jnp.int32, (span, cols), 0)
    q_at = lax.broadcasted_iota(jnp.int32, (span, cols), 1) % stretch
    diff_ref[...] = k_at - q_at
    top_ref[...] = jnp.full_like(top_ref, NEG)
    sum_ref[...] = jnp.zeros_like(sum_ref)
    acc_ref[...] = jnp.zeros_like(acc_ref)
    for copy in copies:
        copy.wait()
    for part in range(2):
        for head in range(QPG):
            rows = slice(part * stretch, (part + 1) * stretch)
            to = slice(head * stretch, (head + 1) * stretch)
            qs_ref[part, to, :] = q_ref[rows, head * HD:(head + 1) * HD]
            ds_ref[part, to, :] = do_ref[rows, head * HD:(head + 1) * HD]
    mine = own_slot()
    own = [ids_ref[mine], ids_ref[mine + 1]]
    first = (own[0] * stretch + stretch - 1) // span + 1
    pltpu.make_async_copy(kv_hbm, kv_ref, kv_sem).wait()

    def place(step):
        late = step >= first
        part = jnp.where(late, 1, 0)
        chunk = step - part * first
        return part, pl.multiple_of(chunk * span, span), jnp.where(late, own[1], own[0]) * stretch

    def score_step(step, carry):
        part, start, at = place(step)
        scores = dot(kv_ref[pl.ds(start, span), :HD], qs_ref[part], NT) * SCALE
        scores = jnp.where(diff_ref[...] <= at - start, scores, NEG)
        s_buf[step] = scores
        top_ref[part] = jnp.maximum(top_ref[part], jnp.max(scores.reshape(span // 8, 8, cols), axis=0))
        return carry

    lax.fori_loop(0, steps, score_step, 0, unroll=UNROLL_F)
    for part in range(2):
        top_ref[part] = jnp.broadcast_to(jnp.max(top_ref[part], axis=0, keepdims=True), (8, cols))

    def sum_step(step, carry):
        part, start, at = place(step)
        shifted = jnp.exp(s_buf[step].reshape(span // 8, 8, cols) - top_ref[part][None])
        s_buf[step] = shifted.reshape(span, cols)
        sum_ref[part] += jnp.sum(shifted, axis=0)
        return carry

    lax.fori_loop(0, steps, sum_step, 0, unroll=UNROLL_F)
    for part in range(2):
        total = jnp.sum(sum_ref[part], axis=0, keepdims=True)
        sum_ref[part] = jnp.broadcast_to(1.0 / total, (8, cols))

    def value_step(step, carry):
        part, start, at = place(step)
        weights = (s_buf[step].reshape(span // 8, 8, cols) * sum_ref[part][None]).reshape(span, cols)
        weights = weights.astype(jnp.bfloat16)
        p_ref[step] = weights
        acc_ref[part] += dot(kv_ref[pl.ds(start, span), HD:], weights, TN)
        return carry

    lax.fori_loop(0, steps, value_step, 0, unroll=UNROLL_F)
    for part in range(2):
        out = acc_ref[part].T.astype(jnp.bfloat16)
        prod = ds_ref[part].astype(jnp.float32) * out.astype(jnp.float32)
        delta_ref[part] = jnp.broadcast_to(jnp.sum(prod.T, axis=0, keepdims=True), (8, cols))
        for head in range(QPG):
            attn_ref[part * stretch:(part + 1) * stretch, head * HD:(head + 1) * HD] = (
                out[head * stretch:(head + 1) * stretch])
    rows = attn_ref.shape[0] // (NH * NY)
    zh, y = lax.axis_index("zh"), lax.axis_index("y")
    for y_step in range(NY):
        for h_step in range(NH):
            block = jnp.bitwise_xor(zh, h_step) * NY + lax.rem(y + y_step, NY)
            to = (y_step * NH + h_step) * rows
            turned_ref[to:to + rows, :] = attn_ref[pl.ds(pl.multiple_of(block * rows, rows), rows), :]
    weight_copy.wait()
    mixes = (mix0, mix1, mix2, mix3)
    piece = NH * rows
    spans = w_ref.shape[1] // MIX_SPAN
    outs = []
    for index in range(spans):
        at = slice(index * MIX_SPAN, (index + 1) * MIX_SPAN)
        mixed_ref[:, at] = dot(turned_ref[...], w_ref[:, at], NN).astype(jnp.bfloat16)
        for number, mix in enumerate(mixes):
            copy = pltpu.make_async_copy(
                mixed_ref.at[number * piece:(number + 1) * piece, at], mix.at[:, at], out_sem.at[index, number])
            copy.start()
            outs.append(copy)
    for copy in outs:
        copy.wait()


def bwd_kernel(stretch, span, ids_ref, p_ref, kv_ref, qs_ref, ds_ref, delta_ref,
               dq_ref, keep_ref, give_ref, acc_ref, dk_ref, dv_ref):
    steps = p_ref.shape[0]
    cols = QPG * stretch
    acc_ref[...] = jnp.zeros_like(acc_ref)
    dk_ref[...] = jnp.zeros_like(dk_ref)
    dv_ref[...] = jnp.zeros_like(dv_ref)
    mine = own_slot()
    first = (ids_ref[mine] * stretch + stretch - 1) // span + 1

    def grad_step(step, carry):
        part = jnp.where(step >= first, 1, 0)
        start = pl.multiple_of((step - part * first) * span, span)
        here = pl.ds(start, span)
        weights = p_ref[step]
        grad_probs = dot(kv_ref[here, HD:], ds_ref[part], NT)
        moved = (grad_probs.reshape(span // 8, 8, cols) - delta_ref[part][None]).reshape(span, cols)
        grad_scores = (weights.astype(jnp.float32) * moved).astype(jnp.bfloat16)
        dv_ref[here, :] += dot(weights, ds_ref[part], NN)
        dk_ref[here, :] += dot(grad_scores, qs_ref[part], NN)
        acc_ref[part] += dot(kv_ref[here, :HD], grad_scores, TN)
        return carry

    lax.fori_loop(0, steps, grad_step, 0, unroll=UNROLL_B)
    x, zl, core = (lax.axis_index(name) for name in CTX)
    for c_step, out in ((1, give_ref), (0, keep_ref)):
        to = 0
        for x_step in range(NX):
            for z_step in range(NZ):
                slot = slot_of(lax.rem(x + x_step, NX), jnp.bitwise_xor(zl, z_step),
                               jnp.bitwise_xor(core, c_step), 0)
                for half in range(2):
                    start = pl.multiple_of(ids_ref[slot + half] * stretch, stretch)
                    here = pl.ds(start, stretch)
                    out[to:to + stretch, :HD] = (dk_ref[here, :] * SCALE).astype(jnp.bfloat16)
                    out[to:to + stretch, HD:] = dv_ref[here, :].astype(jnp.bfloat16)
                    to += stretch
    for part in range(2):
        out = (acc_ref[part].T * SCALE).astype(jnp.bfloat16)
        for head in range(QPG):
            dq_ref[part * stretch:(part + 1) * stretch, head * HD:(head + 1) * HD] = (
                out[head * stretch:(head + 1) * stretch])


def forward(ids, queries, kv, grad_heads, out_weight):
    tokens = queries.shape[0]
    stretch = tokens // 2
    total = kv.shape[0]
    span = 4 * stretch
    cols = QPG * stretch
    steps = total // span + 1
    depth, width = out_weight.shape
    smem = pl.BlockSpec(memory_space=pltpu.SMEM)
    vmem = pl.BlockSpec(memory_space=pltpu.VMEM)
    hbm = pl.BlockSpec(memory_space=pltpu.HBM)
    b16, f32 = jnp.bfloat16, jnp.float32
    shape = jax.ShapeDtypeStruct
    return pl.pallas_call(
        functools.partial(fwd_kernel, stretch, span),
        out_shape=(shape((tokens // NY, width), b16),) * NY + (
            shape((steps, span, cols), b16),
            shape((total, 2 * HD), b16),
            shape((2, cols, HD), b16),
            shape((2, cols, HD), b16),
            shape((2, 8, cols), f32),
        ),
        in_specs=[smem, hbm, hbm, hbm, hbm],
        out_specs=[hbm] * NY + [vmem] * 5,
        scratch_shapes=[
            pltpu.VMEM((tokens, QPG * HD), b16),
            pltpu.VMEM((tokens, QPG * HD), b16),
            pltpu.VMEM((depth, width), b16),
            pltpu.VMEM((steps, span, cols), f32),
            pltpu.VMEM((2, 8, cols), f32),
            pltpu.VMEM((2, 8, cols), f32),
            pltpu.VMEM((2, HD, cols), f32),
            pltpu.VMEM((span, cols), jnp.int32),
            pltpu.VMEM((tokens, QPG * HD), b16),
            pltpu.VMEM((tokens, QPG * HD), b16),
            pltpu.VMEM((tokens, width), b16),
            pltpu.SemaphoreType.DMA,
            pltpu.SemaphoreType.DMA,
            pltpu.SemaphoreType.DMA,
            pltpu.SemaphoreType.DMA,
            pltpu.SemaphoreType.DMA((width // MIX_SPAN, NY)),
        ],
        compiler_params=pltpu.CompilerParams(vmem_limit_bytes=40 * MIB),
        cost_estimate=pl.CostEstimate(flops=4 * 10**9, bytes_accessed=12 * 10**6, transcendentals=10**6),
        name="attention_forward",
    )(ids, queries, kv, grad_heads, out_weight)


def backward(ids, saved):
    probs, kv, qs, ds, delta = saved
    total = kv.shape[0]
    steps, span, cols = probs.shape
    stretch = cols // QPG
    smem = pl.BlockSpec(memory_space=pltpu.SMEM)
    vmem = pl.BlockSpec(memory_space=pltpu.VMEM)
    b16, f32 = jnp.bfloat16, jnp.float32
    shape = jax.ShapeDtypeStruct
    return pl.pallas_call(
        functools.partial(bwd_kernel, stretch, span),
        out_shape=(shape((2 * stretch, QPG * HD), b16), shape((total // 2, 2 * HD), b16),
                   shape((total // 2, 2 * HD), b16)),
        in_specs=[smem] + [vmem] * 5,
        out_specs=[vmem] * 3,
        scratch_shapes=[
            pltpu.VMEM((2, HD, cols), f32),
            pltpu.VMEM((total, HD), f32),
            pltpu.VMEM((total, HD), f32),
        ],
        compiler_params=pltpu.CompilerParams(vmem_limit_bytes=32 * MIB),
        cost_estimate=pl.CostEstimate(flops=4 * 10**9, bytes_accessed=12 * 10**6, transcendentals=0),
        name="attention_backward",
    )(ids, probs, kv, qs, ds, delta)


def ahead(block, axis, step):
    count = lax.axis_size(axis)
    return lax.ppermute(block, axis, [(i, (i + step) % count) for i in range(count)])


def across(block, axis, step):
    count = lax.axis_size(axis)
    return lax.ppermute(block, axis, [(i, i ^ step) for i in range(count)])


def total_of(parts):
    total = parts[0].astype(jnp.float32)
    for part in parts[1:]:
        total = total + part.astype(jnp.float32)
    return total.astype(jnp.bfloat16)


def on_device(queries, keys, values, stretch_of, out_weight, grad_heads):
    kv = jnp.concatenate([keys, values], axis=1)
    kv = jnp.concatenate([kv] + [across(kv, "zl", step) for step in range(1, NZ)], axis=0)
    kv = lax.all_gather(kv, "x", axis=0, tiled=True)
    kv = lax.all_gather(kv, "core", axis=0, tiled=True)
    *mixes, probs, kv, qs, ds, delta = forward(stretch_of, queries, kv, grad_heads, out_weight)
    mixed = total_of([mixes[0]] + [ahead(mixes[step], "y", step) for step in range(1, NY)])
    rows = mixed.shape[0] // NH
    mixed = total_of([mixed[:rows], across(mixed[rows:], "zh", 1)])
    q_grad, keep, give = backward(stretch_of, (probs, kv, qs, ds, delta))
    term = total_of([keep, across(give, "core", 1)])
    part = term.shape[0] // NX
    term = total_of([term[:part]] + [
        ahead(term[step * part:(step + 1) * part], "x", step) for step in range(1, NX)])
    part = term.shape[0] // NZ
    term = total_of([term[:part]] + [
        across(term[step * part:(step + 1) * part], "zl", step) for step in range(1, NZ)])
    return mixed, q_grad, term[:, :HD], term[:, HD:]


def solution(mesh):
    fine = Mesh(mesh.devices.reshape(NX, NZ, NC, NH, NY), CTX + TP)
    return jax.shard_map(
        on_device,
        mesh=fine,
        in_specs=(P(CTX, TP), P(CTX, TP), P(CTX, TP), P(), P(TP, None), P(CTX, TP)),
        out_specs=(P(CTX + TP, None), P(CTX, TP), P(CTX, TP), P(CTX, TP)),
        check_vma=False,
    )
```

time: 346 us -> 154 us (0.45)
  waiting for transfers between devices: 299 us -> 83.8 us
  starting transfers between devices: 0.12 us -> 23.9 us
  matrix products: 5.99 us -> 0 us
  Pallas kernels: 17.9 us -> 23.8 us
    reduce_scatter x2 -> x0, waiting for transfers between devices: 234 us -> none  [the longest x1 135 us: on_device(): reduced = lax.psum_scatter(term, 'ctx', scatter_dimension=0, tiled=True)]
    ppermute x0 -> x14, waiting for transfers between devices: none -> 36 us  [the longest x8 19.7 us: across(): return lax.ppermute(block, axis, [(i, i ^ step) for i in range(count)])]
    ppermute x0 -> x14, starting transfers between devices: none -> 23.8 us  [the longest x8 14.1 us: across(): return lax.ppermute(block, axis, [(i, i ^ step) for i in range(count)])]
    all_gather x1 -> x2, waiting for transfers between devices: 65.4 us -> 47.8 us  [the longest x1 28.1 us: on_device(): kv = lax.all_gather(kv, 'x', axis=0, tiled=True)]
    pallas_call x1, Pallas kernels: 8.87 us -> 15.6 us  [forward(): pl.pallas_call(functools.partial(fwd_kernel, stretch, span), out_shape=(s...]
    dot_general x1 -> x0, matrix products: 5.99 us -> none  [on_device(): jnp.dot(attn, out_weight, preferred_element_type=jnp.float32)]
  transfers between devices with their start and end apart: 3 -> 16, of which waited for: 3 -> 10; matrix products, arithmetic and copies ran while one was open for 2% -> 1% of each run, Pallas kernels for 0% -> 0%
where the time goes in v2:
time: 154 us
  waiting for transfers between devices  83.8 us (54%)
  starting transfers between devices  23.9 us (16%)
  Pallas kernels  23.8 us (15%)
  between operations  14.1 us (9%)
  local copies, waits for them, and re-layouts  6.31 us (4%)
  other arithmetic  2.2 us (1%)
    all_gather x1, waiting for transfers between devices, on_device(): kv = lax.all_gather(kv, 'x', axis=0, tiled=True)  28.1 us
    all_gather x1, waiting for transfers between devices, on_device(): kv = lax.all_gather(kv, 'core', axis=0, tiled=True)  19.7 us
    ppermute x8, waiting for transfers between devices, across(): return lax.ppermute(block, axis, [(i, i ^ step) for i in range(count)])  19.7 us
    ppermute x6, waiting for transfers between devices, ahead(): lax.ppermute(block, axis, [(i, (i + step) % count) for i in range(count)])  16.3 us
    pallas_call x1, Pallas kernels, forward(): pl.pallas_call(functools.partial(fwd_kernel, stretch, span), out_shape=(s...  15.6 us
    ppermute x8, starting transfers between devices, across(): return lax.ppermute(block, axis, [(i, i ^ step) for i in range(count)])  14.1 us
    ppermute x6, starting transfers between devices, ahead(): lax.ppermute(block, axis, [(i, (i + step) % count) for i in range(count)])  9.7 us
    pallas_call x1, Pallas kernels, backward(): pl.pallas_call(functools.partial(bwd_kernel, stretch, span), out_shape=(s...  8.26 us
  transfers between devices with their start and end apart: 16, of which 10 were waited for; matrix products, arithmetic and copies ran while one was open for 1% of the time, Pallas kernels for 0%

profile of v2, /device:TPU:1, one launch (start us, length us, event | category | flops | bytes accessed | tf_op | source)
XLA Modules:
  0.0 154.2 jit_solution(4464928115889669662)
XLA Ops:
  7.2 0.8 constant_dynamic-update-slice_fusion.1
  8.0 0.8 constant_dynamic-update-slice_fusion
  8.7 5.3 %collective-permute-start.2 = (bf16[128,256]{1,0:T(8,128)(2,1)S(1)}, bf16[128,256]{1,0:T(8,128)(2,1)S(1)}, u32[]{:S(2)}, u32[]{:S(2)}) collective-permute-start(bf16[128,256]{1,0:T(8,128)(2,1)S(1)} %constant_dynamic-update-slice_fusion), channel_id=1, source_target_pairs={{0,48},{16,32},{32,16},{48,0},{1,49},{17,33},{33,17},{49,1},{2,50}... | collective-permute-start | bytes 196616 | tf_op jit(solution)/shard_map/ppermute | solution.py:274
  14.4 1.4 collective-permute-done.2
  15.8 3.4 %collective-permute-done.1 = bf16[128,256]{1,0:T(8,128)(2,1)S(1)} collective-permute-done((bf16[128,256]{1,0:T(8,128)(2,1)S(1)}, bf16[128,256]{1,0:T(8,128)(2,1)S(1)}, u32[]{:S(2)}, u32[]{:S(2)}) %collective-permute-start.1) | collective-permute-done | bytes 65568 | tf_op jit(solution)/shard_map/ppermute | solution.py:274
  19.2 0.7 pad_maximum_fusion
  20.0 28.1 %all-gather.3.cloned.1.call-done = bf16[2048,256]{1,0:T(8,128)(2,1)} async-done(((bf16[512,256]{1,0:T(8,128)(2,1)}), bf16[2048,256]{1,0:T(8,128)(2,1)}) %all-gather.3.cloned.1.call-update) | async-done | bytes 1048592 | tf_op jit(solution)/shard_map/all_gather | solution.py:287
  48.1 19.7 %all-gather.5.cloned.1.call-done.kv_hbm = bf16[4096,256]{1,0:T(8,128)(2,1)} async-done(((bf16[2048,256]{1,0:T(8,128)(2,1)}), bf16[4096,256]{1,0:T(8,128)(2,1)}) %all-gather.5.cloned.1.call-update) | async-done | bytes 2097168 | tf_op jit(solution)/shard_map/all_gather | solution.py:288
  67.8 1.6 %copy-done = bf16[4096,256]{1,0:T(8,128)(2,1)S(1)} copy-done((bf16[4096,256]{1,0:T(8,128)(2,1)S(1)}, bf16[4096,256]{1,0:T(8,128)(2,1)}, u32[]{:S(2)}) %copy-start) | copy-done | bytes 2097176
  69.4 0.9 copy-done.1
  70.3 0.9 copy-done.2
  71.2 0.7 copy-done.3
  71.8 15.6 %attention_forward.1 = (bf16[32,8192]{1,0:T(8,128)(2,1)S(1)}, bf16[32,8192]{1,0:T(8,128)(2,1)S(1)}, bf16[32,8192]{1,0:T(8,128)(2,1)S(1)}, bf16[32,8192]{1,0:T(8,...) custom-call(s32[64]{0:T(128)S(1)} %copy-done.3, ...), custom_call_target="tpu_custom_call" | custom-call | flops 4000000000 | bytes 12000000 | tf_op jit(solution)/shard_map/attention_forward/pallas_call | solution.py:206
  87.4 8.3 %attention_backward.1 = (bf16[128,512]{1,0:T(8,128)(2,1)}, bf16[2048,256]{1,0:T(8,128)(2,1)S(1)}, bf16[2048,256]{1,0:T(8,128)(2,1)S(1)}) custom-call(s32[64]{0:T(128)S(1)} %copy-done.3, bf16[17,256,256]{2,1,0:T(8,128)(2,1)S(1)} %get-tuple-element.20.p_ref, bf16[4096,256]{1,0:T(8,128)(2,1)S(1)} %get-tuple-element.21.kv_ref, ...), custom_call_target="tpu_custom_call" | custom-call | flops 4000000000 | bytes 12000000 | tf_op jit(solution)/shard_map/attention_backward/pallas_call | solution.py:250
  95.9 0.9 collective-permute-start.3
  96.8 2.5 %collective-permute-start.4 = (bf16[32,8192]{1,0:T(8,128)(2,1)S(1)}, bf16[32,8192]{1,0:T(8,128)(2,1)S(1)}, u32[]{:S(2)}, u32[]{:S(2)}) collective-permute-start(bf16[32,8192]{1,0:T(8,128)(2,1)S(1)} %get-tuple-element.18), channel_id=1, source_target_pairs={{0,2},{1,3},{2,0},{3,1},{4,6},{5,7},{6,4},{7,5},{8,10},{9,11},{10,... | collective-permute-start | bytes 1572872 | tf_op jit(solution)/shard_map/ppermute | solution.py:269
  99.3 1.2 collective-permute-start.5
  100.8 1.3 collective-permute-start.8
  102.1 1.5 collective-permute-start.10
  103.6 6.8 %collective-permute-done.3 = bf16[32,8192]{1,0:T(8,128)(2,1)S(1)} collective-permute-done((bf16[32,8192]{1,0:T(8,128)(2,1)S(1)}, bf16[32,8192]{1,0:T(8,128)(2,1)S(1)}, u32[]{:S(2)}, u32[]{:S(2)}) %collective-permute-start.3) | collective-permute-done | bytes 524320 | tf_op jit(solution)/shard_map/ppermute | solution.py:269
  110.4 2.4 %collective-permute-start.9 = (bf16[512,256]{1,0:T(8,128)(2,1)S(1)}, bf16[512,256]{1,0:T(8,128)(2,1)S(1)}, u32[]{:S(2)}, u32[]{:S(2)}) collective-permute-start(bf16[512,256]{1,0:T(8,128)(2,1)S(1)} %get-tuple-element.30), channel_id=1, source_target_pairs={{0,128},{64,192},{128,0},{192,64},{1,129},{65,193},{129,1},{193,65... | collective-permute-start | bytes 786440 | tf_op jit(solution)/shard_map/ppermute | solution.py:269
  112.8 9.5 %collective-permute-done.4 = bf16[32,8192]{1,0:T(8,128)(2,1)S(1)} collective-permute-done((bf16[32,8192]{1,0:T(8,128)(2,1)S(1)}, bf16[32,8192]{1,0:T(8,128)(2,1)S(1)}, u32[]{:S(2)}, u32[]{:S(2)}) %collective-permute-start.4) | collective-permute-done | bytes 524320 | tf_op jit(solution)/shard_map/ppermute | solution.py:269
  122.6 5.5 %collective-permute-start.6 = (bf16[16,8192]{1,0:T(8,128)(2,1)S(1)}, bf16[16,8192]{1,0:T(8,128)(2,1)S(1)}, u32[]{:S(2)}, u32[]{:S(2)}) collective-permute-start(bf16[16,8192]{1,0:T(8,128)(2,1)S(1)} %slice.49), channel_id=1, source_target_pairs={{0,4},{4,0},{1,5},{5,1},{2,6},{6,2},{3,7},{7,3},{8,12},{12,8},{9,1... | collective-permute-start | bytes 786440 | tf_op jit(solution)/shard_map/ppermute | solution.py:274
  128.3 0.5 collective-permute-start.11
  128.8 1.3 collective-permute-start.13
  130.0 1.0 collective-permute-start.12
  131.0 4.1 %collective-permute-done.6 = bf16[16,8192]{1,0:T(8,128)(2,1)S(1)} collective-permute-done((bf16[16,8192]{1,0:T(8,128)(2,1)S(1)}, bf16[16,8192]{1,0:T(8,128)(2,1)S(1)}, u32[]{:S(2)}, u32[]{:S(2)}) %collective-permute-start.6) | collective-permute-done | bytes 262176 | tf_op jit(solution)/shard_map/ppermute | solution.py:274
  135.1 0.8 add_convert_fusion.3
  135.9 4.8 %collective-permute-done.11 = bf16[128,256]{1,0:T(8,128)(2,1)S(1)} collective-permute-done((bf16[128,256]{1,0:T(8,128)(2,1)S(1)}, bf16[128,256]{1,0:T(8,128)(2,1)S(1)}, u32[]{:S(2)}, u32[]{:S(2)}) %collective-permute-start.11) | collective-permute-done | bytes 65568 | tf_op jit(solution)/shard_map/ppermute | solution.py:274
  140.7 2.8 %collective-permute-done.13 = bf16[128,256]{1,0:T(8,128)(2,1)S(1)} collective-permute-done((bf16[128,256]{1,0:T(8,128)(2,1)S(1)}, bf16[128,256]{1,0:T(8,128)(2,1)S(1)}, u32[]{:S(2)}, u32[]{:S(2)}) %collective-permute-start.13) | collective-permute-done | bytes 65568 | tf_op jit(solution)/shard_map/ppermute | solution.py:274
  143.5 3.2 %collective-permute-done.12 = bf16[128,256]{1,0:T(8,128)(2,1)S(1)} collective-permute-done((bf16[128,256]{1,0:T(8,128)(2,1)S(1)}, bf16[128,256]{1,0:T(8,128)(2,1)S(1)}, u32[]{:S(2)}, u32[]{:S(2)}) %collective-permute-start.12) | collective-permute-done | bytes 65568 | tf_op jit(solution)/shard_map/ppermute | solution.py:274
  146.7 0.6 fusion.2
  (24 shorter events, 1.5 us)
Async XLA Ops:
  7.2 40.9 %all-gather.3.cloned.1.call-start = ((), (), s32[]{:S(2)}) async-start(), calls=%async_computation | async-start | bytes 1310720 | tf_op jit(solution)/shard_map/all_gather | solution.py:287
  8.7 7.0 %collective-permute-start.2 = (bf16[128,256]{1,0:T(8,128)(2,1)S(1)}, bf16[128,256]{1,0:T(8,128)(2,1)S(1)}, u32[]{:S(2)}, u32[]{:S(2)}) collective-permute-start(bf16[128,256]{1,0:T(8,128)(2,1)S(1)} %constant_dynamic-update-slice_fusion), channel_id=1, source_target_pairs={{0,48},{16,32},{32,16},{48,0},{1,49},{17,33},{33,17},{49,1},{2,50}... | collective-permute-start | bytes 196616 | tf_op jit(solution)/shard_map/ppermute | solution.py:274
  14.0 5.2 %collective-permute-start.1 = (bf16[128,256]{1,0:T(8,128)(2,1)S(1)}, bf16[128,256]{1,0:T(8,128)(2,1)S(1)}, u32[]{:S(2)}, u32[]{:S(2)}) collective-permute-start(bf16[128,256]{1,0:T(8,128)(2,1)S(1)} %constant_dynamic-update-slice_fusion), channel_id=1, source_target_pairs={{0,32},{16,48},{32,0},{48,16},{1,33},{17,49},{33,1},{49,17},{2,34}... | collective-permute-start | bytes 196616 | tf_op jit(solution)/shard_map/ppermute | solution.py:274
  14.0 5.2 %collective-permute-start = (bf16[128,256]{1,0:T(8,128)(2,1)S(1)}, bf16[128,256]{1,0:T(8,128)(2,1)S(1)}, u32[]{:S(2)}, u32[]{:S(2)}) collective-permute-start(bf16[128,256]{1,0:T(8,128)(2,1)S(1)} %constant_dynamic-update-slice_fusion), channel_id=1, source_target_pairs={{0,16},{16,0},{32,48},{48,32},{1,17},{17,1},{33,49},{49,33},{2,18}... | collective-permute-start | bytes 196616 | tf_op jit(solution)/shard_map/ppermute | solution.py:274
  19.9 47.8 %all-gather.5.cloned.1.call-start = ((), (), s32[]{:S(2)}) async-start(), calls=%async_computation.1 | async-start | bytes 3145728 | tf_op jit(solution)/shard_map/all_gather | solution.py:288
  67.8 1.6 %copy-start = (bf16[4096,256]{1,0:T(8,128)(2,1)S(1)}, bf16[4096,256]{1,0:T(8,128)(2,1)}, u32[]{:S(2)}) copy-start(bf16[4096,256]{1,0:T(8,128)(2,1)} %all-gather.5.cloned.1.call-done.kv_hbm) | copy-start | bytes 6291460
  69.4 0.9 copy-start.1
  70.3 0.9 copy-start.2
  71.2 0.7 copy-start.3
  95.7 4.8 %collective-permute-start.7 = (bf16[2048,256]{1,0:T(8,128)(2,1)S(1)}, bf16[2048,256]{1,0:T(8,128)(2,1)S(1)}, u32[]{:S(2)}, u32[]{:S(2)}) collective-permute-start(bf16[2048,256]{1,0:T(8,128)(2,1)S(1)} %get-tuple-element.27), channel_id=1, source_target_pairs={{0,8},{8,0},{1,9},{9,1},{2,10},{10,2},{3,11},{11,3},{4,12},{12,4},... | collective-permute-start | bytes 3145736 | tf_op jit(solution)/shard_map/ppermute | solution.py:274
  95.9 14.4 %collective-permute-start.3 = (bf16[32,8192]{1,0:T(8,128)(2,1)S(1)}, bf16[32,8192]{1,0:T(8,128)(2,1)S(1)}, u32[]{:S(2)}, u32[]{:S(2)}) collective-permute-start(bf16[32,8192]{1,0:T(8,128)(2,1)S(1)} %get-tuple-element.17), channel_id=1, source_target_pairs={{0,1},{1,2},{2,3},{3,0},{4,5},{5,6},{6,7},{7,4},{8,9},{9,10},{10,1... | collective-permute-start | bytes 1572872 | tf_op jit(solution)/shard_map/ppermute | solution.py:269
  96.8 25.4 %collective-permute-start.4 = (bf16[32,8192]{1,0:T(8,128)(2,1)S(1)}, bf16[32,8192]{1,0:T(8,128)(2,1)S(1)}, u32[]{:S(2)}, u32[]{:S(2)}) collective-permute-start(bf16[32,8192]{1,0:T(8,128)(2,1)S(1)} %get-tuple-element.18), channel_id=1, source_target_pairs={{0,2},{1,3},{2,0},{3,1},{4,6},{5,7},{6,4},{7,5},{8,10},{9,11},{10,... | collective-permute-start | bytes 1572872 | tf_op jit(solution)/shard_map/ppermute | solution.py:269
  99.3 23.0 %collective-permute-start.5 = (bf16[32,8192]{1,0:T(8,128)(2,1)S(1)}, bf16[32,8192]{1,0:T(8,128)(2,1)S(1)}, u32[]{:S(2)}, u32[]{:S(2)}) collective-permute-start(bf16[32,8192]{1,0:T(8,128)(2,1)S(1)} %get-tuple-element.19), channel_id=1, source_target_pairs={{0,3},{1,0},{2,1},{3,2},{4,7},{5,4},{6,5},{7,6},{8,11},{9,8},{10,9... | collective-permute-start | bytes 1572872 | tf_op jit(solution)/shard_map/ppermute | solution.py:269
  100.8 27.3 %collective-permute-start.8 = (bf16[512,256]{1,0:T(8,128)(2,1)S(1)}, bf16[512,256]{1,0:T(8,128)(2,1)S(1)}, u32[]{:S(2)}, u32[]{:S(2)}) collective-permute-start(bf16[512,256]{1,0:T(8,128)(2,1)S(1)} %get-tuple-element.28), channel_id=1, source_target_pairs={{0,64},{64,128},{128,192},{192,0},{1,65},{65,129},{129,193},{193,1... | collective-permute-start | bytes 786440 | tf_op jit(solution)/shard_map/ppermute | solution.py:269
  102.1 26.0 %collective-permute-start.10 = (bf16[512,256]{1,0:T(8,128)(2,1)S(1)}, bf16[512,256]{1,0:T(8,128)(2,1)S(1)}, u32[]{:S(2)}, u32[]{:S(2)}) collective-permute-start(bf16[512,256]{1,0:T(8,128)(2,1)S(1)} %get-tuple-element.29), channel_id=1, source_target_pairs={{0,192},{64,0},{128,64},{192,128},{1,193},{65,1},{129,65},{193,129... | collective-permute-start | bytes 786440 | tf_op jit(solution)/shard_map/ppermute | solution.py:269
  110.4 17.8 %collective-permute-start.9 = (bf16[512,256]{1,0:T(8,128)(2,1)S(1)}, bf16[512,256]{1,0:T(8,128)(2,1)S(1)}, u32[]{:S(2)}, u32[]{:S(2)}) collective-permute-start(bf16[512,256]{1,0:T(8,128)(2,1)S(1)} %get-tuple-element.30), channel_id=1, source_target_pairs={{0,128},{64,192},{128,0},{192,64},{1,129},{65,193},{129,1},{193,65... | collective-permute-start | bytes 786440 | tf_op jit(solution)/shard_map/ppermute | solution.py:269
  122.6 12.6 %collective-permute-start.6 = (bf16[16,8192]{1,0:T(8,128)(2,1)S(1)}, bf16[16,8192]{1,0:T(8,128)(2,1)S(1)}, u32[]{:S(2)}, u32[]{:S(2)}) collective-permute-start(bf16[16,8192]{1,0:T(8,128)(2,1)S(1)} %slice.49), channel_id=1, source_target_pairs={{0,4},{4,0},{1,5},{5,1},{2,6},{6,2},{3,7},{7,3},{8,12},{12,8},{9,1... | collective-permute-start | bytes 786440 | tf_op jit(solution)/shard_map/ppermute | solution.py:274
  128.3 12.4 %collective-permute-start.11 = (bf16[128,256]{1,0:T(8,128)(2,1)S(1)}, bf16[128,256]{1,0:T(8,128)(2,1)S(1)}, u32[]{:S(2)}, u32[]{:S(2)}) collective-permute-start(bf16[128,256]{1,0:T(8,128)(2,1)S(1)} %get-tuple-element.31), channel_id=1, source_target_pairs={{0,16},{16,0},{32,48},{48,32},{1,17},{17,1},{33,49},{49,33},{2,18}... | collective-permute-start | bytes 196616 | tf_op jit(solution)/shard_map/ppermute | solution.py:274
  128.8 14.8 %collective-permute-start.13 = (bf16[128,256]{1,0:T(8,128)(2,1)S(1)}, bf16[128,256]{1,0:T(8,128)(2,1)S(1)}, u32[]{:S(2)}, u32[]{:S(2)}) collective-permute-start(bf16[128,256]{1,0:T(8,128)(2,1)S(1)} %get-tuple-element.32), channel_id=1, source_target_pairs={{0,48},{16,32},{32,16},{48,0},{1,49},{17,33},{33,17},{49,1},{2,50}... | collective-permute-start | bytes 196616 | tf_op jit(solution)/shard_map/ppermute | solution.py:274
  130.0 16.7 %collective-permute-start.12 = (bf16[128,256]{1,0:T(8,128)(2,1)S(1)}, bf16[128,256]{1,0:T(8,128)(2,1)S(1)}, u32[]{:S(2)}, u32[]{:S(2)}) collective-permute-start(bf16[128,256]{1,0:T(8,128)(2,1)S(1)} %get-tuple-element.33), channel_id=1, source_target_pairs={{0,32},{16,48},{32,0},{48,16},{1,33},{17,49},{33,1},{49,17},{2,34}... | collective-permute-start | bytes 196616 | tf_op jit(solution)/shard_map/ppermute | solution.py:274
Sparse Core Ops, SparseCore 0:
  20.1 27.9 all-gather.2
  49.8 17.8 all-gather.4

commit v3 on v2

v3 whole, which is shorter than its diff:
```python
import functools
import jax
import jax.numpy as jnp
from jax import lax
from jax.experimental import pallas as pl
from jax.experimental.pallas import tpu as pltpu
from jax.sharding import Mesh, PartitionSpec as P

HD = 128
QPG = 4
NEG = -1e30
SCALE = HD ** (-0.5)
NT = (((1,), (1,)), ((), ()))
NN = (((1,), (0,)), ((), ()))
TN = (((0,), (0,)), ((), ()))
MIB = 1024 * 1024
NX, NZ, NC, NH, NY = 4, 4, 2, 2, 4
CTX = ("x", "zl", "core")
TP = ("zh", "y")
MIX_SPAN = 1024
UNROLL_S = 17
UNROLL_V = 17
UNROLL_B = 17
SMEM = pl.BlockSpec(memory_space=pltpu.SMEM)
VMEM = pl.BlockSpec(memory_space=pltpu.VMEM)
HBM = pl.BlockSpec(memory_space=pltpu.HBM)


def dot(a, b, dims):
    return lax.dot_general(a, b, dims, preferred_element_type=jnp.float32)


def slot_of(x, zl, core, half):
    return ((x * NZ + zl) * NC + core) * 2 + half


def place_of(c_step, x_step, z_step):
    x, zl, core = (lax.axis_index(name) for name in CTX)
    return slot_of(lax.rem(x + x_step, NX), jnp.bitwise_xor(zl, z_step), jnp.bitwise_xor(core, c_step), 0)


def pair_kernel(k_hbm, v_hbm, kv_ref, sem):
    copies = [pltpu.make_async_copy(k_hbm, kv_ref.at[:, :HD], sem.at[0]),
              pltpu.make_async_copy(v_hbm, kv_ref.at[:, HD:], sem.at[1])]
    for copy in copies:
        copy.start()
    for copy in copies:
        copy.wait()


def heads_kernel(ids_ref, q_hbm, do_hbm, same_ref, qs_ref, ds_ref, sem):
    stretch = q_hbm.shape[0] // 2
    for slot in range(ids_ref.shape[0]):
        same_ref[slot] = ids_ref[slot]
    copies = []
    for which, (source, target) in enumerate(((q_hbm, qs_ref), (do_hbm, ds_ref))):
        for part in range(2):
            for head in range(QPG):
                copies.append(pltpu.make_async_copy(
                    source.at[part * stretch:(part + 1) * stretch, head * HD:(head + 1) * HD],
                    target.at[part, head * stretch:(head + 1) * stretch, :],
                    sem.at[which, part, head]))
    for copy in copies:
        copy.start()
    for copy in copies:
        copy.wait()


def fwd_kernel(stretch, span, ids_ref, qs_ref, ds_ref, *rest):
    pieces, rest = rest[:NC * NX], rest[NC * NX:]
    w_hbm, rest = rest[0], rest[1:]
    mixes, rest = rest[:NY], rest[NY:]
    (p_ref, kv_ref, delta_ref, inv_ref,
     w_ref, s_buf, top_ref, sum_ref, acc_ref, diff_ref, attn_ref, turned_ref, w_sem) = rest
    steps = p_ref.shape[0]
    cols = QPG * stretch
    weight_copy = pltpu.make_async_copy(w_hbm, w_ref, w_sem)
    weight_copy.start()
    for c_step in range(NC):
        for x_step in range(NX):
            piece = pieces[c_step * NX + x_step]
            for z_step in range(NZ):
                slot = place_of(c_step, x_step, z_step)
                for half in range(2):
                    start = pl.multiple_of(ids_ref[slot + half] * stretch, stretch)
                    at = (z_step * 2 + half) * stretch
                    kv_ref[pl.ds(start, stretch), :] = piece[at:at + stretch, :]
    k_at = lax.broadcasted_iota(jnp.int32, (span, cols), 0)
    q_at = lax.broadcasted_iota(jnp.int32, (span, cols), 1) % stretch
    diff_ref[...] = k_at - q_at
    top_ref[...] = jnp.full_like(top_ref, NEG)
    sum_ref[...] = jnp.zeros_like(sum_ref)
    acc_ref[...] = jnp.zeros_like(acc_ref)
    mine = place_of(0, 0, 0)
    own = [ids_ref[mine], ids_ref[mine + 1]]
    first = (own[0] * stretch + stretch - 1) // span + 1

    def place(step):
        late = step >= first
        part = jnp.where(late, 1, 0)
        chunk = step - part * first
        return part, pl.multiple_of(chunk * span, span), jnp.where(late, own[1], own[0]) * stretch

    def score_step(step, carry):
        part, start, at = place(step)
        scores = dot(kv_ref[pl.ds(start, span), :HD], qs_ref[part], NT)
        scores = jnp.where(diff_ref[...] <= at - start, scores, NEG)
        s_buf[step] = scores
        top_ref[part] = jnp.maximum(top_ref[part], jnp.max(scores.reshape(span // 8, 8, cols), axis=0))
        return carry

    lax.fori_loop(0, steps, score_step, 0, unroll=UNROLL_S)
    for part in range(2):
        top_ref[part] = jnp.broadcast_to(jnp.max(top_ref[part], axis=0, keepdims=True), (8, cols))

    def value_step(step, carry):
        part, start, at = place(step)
        shifted = jnp.exp((s_buf[step].reshape(span // 8, 8, cols) - top_ref[part][None]) * SCALE)
        sum_ref[part] += jnp.sum(shifted, axis=0)
        weights = shifted.reshape(span, cols).astype(jnp.bfloat16)
        p_ref[step] = weights
        acc_ref[part] += dot(kv_ref[pl.ds(start, span), HD:], weights, TN)
        return carry

    lax.fori_loop(0, steps, value_step, 0, unroll=UNROLL_V)
    for part in range(2):
        inverse = 1.0 / jnp.sum(sum_ref[part], axis=0, keepdims=True)
        inv_ref[part] = jnp.broadcast_to(inverse, (8, cols))
        out = (acc_ref[part] * inverse).T.astype(jnp.bfloat16)
        prod = ds_ref[part].astype(jnp.float32) * out.astype(jnp.float32)
        delta_ref[part] = jnp.broadcast_to(jnp.sum(prod.T, axis=0, keepdims=True), (8, cols))
        for head in range(QPG):
            attn_ref[part * stretch:(part + 1) * stretch, head * HD:(head + 1) * HD] = (
                out[head * stretch:(head + 1) * stretch])
    rows = attn_ref.shape[0] // (NH * NY)
    zh, y = lax.axis_index("zh"), lax.axis_index("y")
    for y_step in range(NY):
        for h_step in range(NH):
            block = jnp.bitwise_xor(zh, h_step) * NY + lax.rem(y + y_step, NY)
            to = (y_step * NH + h_step) * rows
            turned_ref[to:to + rows, :] = attn_ref[pl.ds(pl.multiple_of(block * rows, rows), rows), :]
    weight_copy.wait()
    piece = NH * rows

    for index in range(w_ref.shape[1] // MIX_SPAN):
        at = slice(index * MIX_SPAN, (index + 1) * MIX_SPAN)
        mixed = dot(turned_ref[...], w_ref[:, at], NN).astype(jnp.bfloat16)
        for number, mix in enumerate(mixes):
            mix[:, at] = mixed[number * piece:(number + 1) * piece]


def bwd_kernel(stretch, span, ids_ref, p_ref, kv_ref, qs_ref, ds_ref, delta_ref, inv_ref,
               dq_ref, keep_ref, give_ref, acc_ref, dk_ref, dv_ref, dn_ref):
    steps = p_ref.shape[0]
    cols = QPG * stretch
    acc_ref[...] = jnp.zeros_like(acc_ref)
    dk_ref[...] = jnp.zeros_like(dk_ref)
    dv_ref[...] = jnp.zeros_like(dv_ref)
    for part in range(2):
        column = jnp.broadcast_to(inv_ref[part][:1], (HD, cols)).T
        dn_ref[part] = (ds_ref[part].astype(jnp.float32) * column).astype(jnp.bfloat16)
    first = (ids_ref[place_of(0, 0, 0)] * stretch + stretch - 1) // span + 1

    def grad_step(step, carry):
        part = jnp.where(step >= first, 1, 0)
        start = pl.multiple_of((step - part * first) * span, span)
        here = pl.ds(start, span)
        weights = p_ref[step]
        grad_probs = dot(kv_ref[here, HD:], ds_ref[part], NT)
        moved = (grad_probs.reshape(span // 8, 8, cols) - delta_ref[part][None]) * inv_ref[part][None]
        grad_scores = (weights.astype(jnp.float32) * moved.reshape(span, cols)).astype(jnp.bfloat16)
        dv_ref[here, :] += dot(weights, dn_ref[part], NN)
        dk_ref[here, :] += dot(grad_scores, qs_ref[part], NN)
        acc_ref[part] += dot(kv_ref[here, :HD], grad_scores, TN)
        return carry

    lax.fori_loop(0, steps, grad_step, 0, unroll=UNROLL_B)
    for c_step, out in ((1, give_ref), (0, keep_ref)):
        to = 0
        for x_step in range(NX):
            for z_step in range(NZ):
                slot = place_of(c_step, x_step, z_step)
                for half in range(2):
                    here = pl.ds(pl.multiple_of(ids_ref[slot + half] * stretch, stretch), stretch)
                    out[to:to + stretch, :HD] = (dk_ref[here, :] * SCALE).astype(jnp.bfloat16)
                    out[to:to + stretch, HD:] = dv_ref[here, :].astype(jnp.bfloat16)
                    to += stretch
    for part in range(2):
        out = (acc_ref[part].T * SCALE).astype(jnp.bfloat16)
        for head in range(QPG):
            dq_ref[part * stretch:(part + 1) * stretch, head * HD:(head + 1) * HD] = (
                out[head * stretch:(head + 1) * stretch])


def pair(keys, values):
    return pl.pallas_call(
        pair_kernel,
        out_shape=jax.ShapeDtypeStruct((keys.shape[0], 2 * HD), jnp.bfloat16),
        in_specs=[HBM] * 2,
        out_specs=VMEM,
        scratch_shapes=[pltpu.SemaphoreType.DMA((2,))],
        compiler_params=pltpu.CompilerParams(vmem_limit_bytes=60 * MIB),
        name="pair",
    )(keys, values)


def by_heads(ids, queries, grad_heads):
    shape = jax.ShapeDtypeStruct((2, QPG * queries.shape[0] // 2, HD), jnp.bfloat16)
    return pl.pallas_call(
        heads_kernel,
        out_shape=(jax.ShapeDtypeStruct(ids.shape, ids.dtype), shape, shape),
        in_specs=[SMEM] + [HBM] * 2,
        out_specs=[SMEM] + [VMEM] * 2,
        scratch_shapes=[pltpu.SemaphoreType.DMA((2, 2, QPG))],
        compiler_params=pltpu.CompilerParams(vmem_limit_bytes=4 * MIB),
        name="by_heads",
    )(ids, queries, grad_heads)


def forward(ids, qs, ds, pieces, out_weight):
    cols = qs.shape[1]
    stretch = cols // QPG
    tokens = 2 * stretch
    total = sum(piece.shape[0] for piece in pieces)
    span = 4 * stretch
    steps = total // span + 1
    depth, width = out_weight.shape
    b16, f32 = jnp.bfloat16, jnp.float32
    shape = jax.ShapeDtypeStruct
    return pl.pallas_call(
        functools.partial(fwd_kernel, stretch, span),
        out_shape=(shape((tokens // NY, width), b16),) * NY + (
            shape((steps, span, cols), b16),
            shape((total, 2 * HD), b16),
            shape((2, 8, cols), f32),
            shape((2, 8, cols), f32),
        ),
        in_specs=[SMEM] + [VMEM] * (2 + len(pieces)) + [HBM],
        out_specs=[VMEM] * (NY + 4),
        scratch_shapes=[
            pltpu.VMEM((depth, width), b16),
            pltpu.VMEM((steps, span, cols), f32),
            pltpu.VMEM((2, 8, cols), f32),
            pltpu.VMEM((2, 8, cols), f32),
            pltpu.VMEM((2, HD, cols), f32),
            pltpu.VMEM((span, cols), jnp.int32),
            pltpu.VMEM((tokens, QPG * HD), b16),
            pltpu.VMEM((tokens, QPG * HD), b16),
            pltpu.SemaphoreType.DMA,
        ],
        compiler_params=pltpu.CompilerParams(vmem_limit_bytes=40 * MIB),
        cost_estimate=pl.CostEstimate(flops=4 * 10**9, bytes_accessed=12 * 10**6, transcendentals=10**6),
        name="attention_forward",
    )(ids, qs, ds, *pieces, out_weight)


def backward(ids, probs, kv, qs, ds, delta, inverse):
    total = kv.shape[0]
    steps, span, cols = probs.shape
    stretch = cols // QPG
    b16, f32 = jnp.bfloat16, jnp.float32
    shape = jax.ShapeDtypeStruct
    return pl.pallas_call(
        functools.partial(bwd_kernel, stretch, span),
        out_shape=(shape((2 * stretch, QPG * HD), b16), shape((total // 2, 2 * HD), b16),
                   shape((total // 2, 2 * HD), b16)),
        in_specs=[SMEM] + [VMEM] * 6,
        out_specs=[VMEM] * 3,
        scratch_shapes=[
            pltpu.VMEM((2, HD, cols), f32),
            pltpu.VMEM((total, HD), f32),
            pltpu.VMEM((total, HD), f32),
            pltpu.VMEM((2, cols, HD), b16),
        ],
        compiler_params=pltpu.CompilerParams(vmem_limit_bytes=32 * MIB),
        cost_estimate=pl.CostEstimate(flops=5 * 10**10, bytes_accessed=12 * 10**6, transcendentals=0),
        name="attention_backward",
    )(ids, probs, kv, qs, ds, delta, inverse)


def ahead(block, axis, step):
    count = lax.axis_size(axis)
    return lax.ppermute(block, axis, [(i, (i + step) % count) for i in range(count)])


def behind(block, axis, step):
    count = lax.axis_size(axis)
    return lax.ppermute(block, axis, [((i + step) % count, i) for i in range(count)])


def across(block, axis, step):
    count = lax.axis_size(axis)
    return lax.ppermute(block, axis, [(i, i ^ step) for i in range(count)])


def total_of(parts):
    total = parts[0].astype(jnp.float32)
    for part in parts[1:]:
        total = total + part.astype(jnp.float32)
    return total.astype(jnp.bfloat16)


def on_device(queries, keys, values, stretch_of, out_weight, grad_heads):
    kv = pair(keys, values)
    stretch_of, qs, ds = by_heads(stretch_of, queries, grad_heads)
    kv = jnp.concatenate([kv] + [across(kv, "zl", step) for step in range(1, NZ)], axis=0)
    pieces = [kv] + [behind(kv, "x", step) for step in range(1, NX)]
    pieces = pieces + [across(piece, "core", 1) for piece in pieces]
    *mixes, probs, kv, delta, inverse = forward(stretch_of, qs, ds, pieces, out_weight)
    mixed = total_of([mixes[0]] + [ahead(mixes[step], "y", step) for step in range(1, NY)])
    rows = mixed.shape[0] // NH
    mixed = total_of([mixed[:rows], across(mixed[rows:], "zh", 1)])
    q_grad, keep, give = backward(stretch_of, probs, kv, qs, ds, delta, inverse)
    term = total_of([keep, across(give, "core", 1)])
    part = term.shape[0] // NX
    term = total_of([term[:part]] + [
        ahead(term[step * part:(step + 1) * part], "x", step) for step in range(1, NX)])
    part = term.shape[0] // NZ
    term = total_of([term[:part]] + [
        across(term[step * part:(step + 1) * part], "zl", step) for step in range(1, NZ)])
    return mixed, q_grad, term[:, :HD], term[:, HD:]


def solution(mesh):
    fine = Mesh(mesh.devices.reshape(NX, NZ, NC, NH, NY), CTX + TP)
    return jax.shard_map(
        on_device,
        mesh=fine,
        in_specs=(P(CTX, TP), P(CTX, TP), P(CTX, TP), P(), P(TP, None), P(CTX, TP)),
        out_specs=(P(CTX + TP, None), P(CTX, TP), P(CTX, TP), P(CTX, TP)),
        check_vma=False,
    )
```

time: 154 us -> 101 us (0.66)
  waiting for transfers between devices: 83.8 us -> 39 us
  starting transfers between devices: 23.9 us -> 38.5 us
  between operations: 14.1 us -> 0.76 us
  Pallas kernels: 23.8 us -> 17.3 us
  local copies, waits for them, and re-layouts: 6.31 us -> 3.18 us
    all_gather x2 -> x0, waiting for transfers between devices: 47.8 us -> none  [the longest x1 28.1 us: on_device(): kv = lax.all_gather(kv, 'x', axis=0, tiled=True)]
    ppermute x8 -> x12, starting transfers between devices: 14.1 us -> 24.7 us  [across(): return lax.ppermute(block, axis, [(i, i ^ step) for i in range(count)])]
    pallas_call x1, Pallas kernels: 15.6 us -> 8.43 us  [forward(): pl.pallas_call(functools.partial(fwd_kernel, stretch, span), out_shape=(s...]
    ppermute x0 -> x3, starting transfers between devices: none -> 4.57 us  [behind(): lax.ppermute(block, axis, [((i + step) % count, i) for i in range(count)])]
    pallas_call x0 -> x2, Pallas kernels: none -> 2.81 us  [the longest x1 1.42 us: pair(): pl.pallas_call(pair_kernel, out_shape=jax.ShapeDtypeStruct((keys.shape[0]...]
    ppermute x0 -> x3, waiting for transfers between devices: none -> 2.54 us  [behind(): lax.ppermute(block, axis, [((i + step) % count, i) for i in range(count)])]
    unnamed x9 -> x6, local copies, waits for them, and re-layouts: 4.82 us -> 2.46 us
    pallas_call x1, Pallas kernels: 8.26 us -> 6.1 us  [backward(): pl.pallas_call(functools.partial(bwd_kernel, stretch, span), out_shape=(s...]
  transfers between devices with their start and end apart: 16 -> 21, of which waited for: 10 -> 9; matrix products, arithmetic and copies ran while one was open for 1% -> 2% of each run, Pallas kernels for 0% -> 1%
where the time goes in v3:
time: 101 us
  waiting for transfers between devices  39 us (39%)
  starting transfers between devices  38.5 us (38%)
  Pallas kernels  17.3 us (17%)
  local copies, waits for them, and re-layouts  3.18 us (3%)
  other arithmetic  2.34 us (2%)
    ppermute x12, starting transfers between devices, across(): return lax.ppermute(block, axis, [(i, i ^ step) for i in range(count)])  24.7 us
    ppermute x12, waiting for transfers between devices, across(): return lax.ppermute(block, axis, [(i, i ^ step) for i in range(count)])  18.8 us
    ppermute x6, waiting for transfers between devices, ahead(): lax.ppermute(block, axis, [(i, (i + step) % count) for i in range(count)])  17.7 us
    ppermute x6, starting transfers between devices, ahead(): lax.ppermute(block, axis, [(i, (i + step) % count) for i in range(count)])  9.26 us
    pallas_call x1, Pallas kernels, forward(): pl.pallas_call(functools.partial(fwd_kernel, stretch, span), out_shape=(s...  8.43 us
    pallas_call x1, Pallas kernels, backward(): pl.pallas_call(functools.partial(bwd_kernel, stretch, span), out_shape=(s...  6.1 us
    ppermute x3, starting transfers between devices, behind(): lax.ppermute(block, axis, [((i + step) % count, i) for i in range(count)])  4.57 us
    ppermute x3, waiting for transfers between devices, behind(): lax.ppermute(block, axis, [((i + step) % count, i) for i in range(count)])  2.54 us
  transfers between devices with their start and end apart: 21, of which 9 were waited for; matrix products, arithmetic and copies ran while one was open for 2% of the time, Pallas kernels for 1%

profile of v3, /device:TPU:1, one launch (start us, length us, event | category | flops | bytes accessed | tf_op | source)
XLA Modules:
  0.0 101.1 jit_solution(2265576079590507296)
XLA Ops:
  0.6 1.4 %pair.1 = bf16[128,256]{1,0:T(8,128)(2,1)} custom-call(bf16[128,128]{1,0:T(8,128)(2,1)} %k_hbm.1, bf16[128,128]{1,0:T(8,128)(2,1)} %v_hbm.1), custom_call_target="tpu_custom_call" | custom-call | tf_op jit(solution)/shard_map/pair/pallas_call | solution.py:196
  2.1 5.3 %collective-permute-start.2 = (bf16[128,256]{1,0:T(8,128)(2,1)}, bf16[128,256]{1,0:T(8,128)(2,1)S(1)}, u32[]{:S(2)}, u32[]{:S(2)}) collective-permute-start(bf16[128,256]{1,0:T(8,128)(2,1)} %pair.1), channel_id=1, source_target_pairs={{0,48},{16,32},{32,16},{48,0},{1,49},{17,33},{33,17},{49,1},{2,50}... | collective-permute-start | bytes 196616 | tf_op jit(solution)/shard_map/ppermute | solution.py:293
  7.7 1.6 %collective-permute-done.2 = bf16[128,256]{1,0:T(8,128)(2,1)S(1)} collective-permute-done((bf16[128,256]{1,0:T(8,128)(2,1)}, bf16[128,256]{1,0:T(8,128)(2,1)S(1)}, u32[]{:S(2)}, u32[]{:S(2)}) %collective-permute-start.2) | collective-permute-done | bytes 65568 | tf_op jit(solution)/shard_map/ppermute | solution.py:293
  9.3 3.4 %collective-permute-done.1 = bf16[128,256]{1,0:T(8,128)(2,1)S(1)} collective-permute-done((bf16[128,256]{1,0:T(8,128)(2,1)}, bf16[128,256]{1,0:T(8,128)(2,1)S(1)}, u32[]{:S(2)}, u32[]{:S(2)}) %collective-permute-start.1) | collective-permute-done | bytes 65568 | tf_op jit(solution)/shard_map/ppermute | solution.py:293
  12.7 0.9 pad_maximum_fusion.rest_0_
  13.6 1.0 collective-permute-start.5
  14.6 2.5 %collective-permute-start.4 = (bf16[512,256]{1,0:T(8,128)(2,1)S(1)}, bf16[512,256]{1,0:T(8,128)(2,1)S(1)}, u32[]{:S(2)}, u32[]{:S(2)}) collective-permute-start(bf16[512,256]{1,0:T(8,128)(2,1)S(1)} %pad_maximum_fusion.rest_0_), channel_id=1, source_target_pairs={{128,0},{192,64},{0,128},{64,192},{129,1},{193,65},{1,129},{65,193... | collective-permute-start | bytes 786440 | tf_op jit(solution)/shard_map/ppermute | solution.py:288
  17.0 1.2 %collective-permute-start.3 = (bf16[512,256]{1,0:T(8,128)(2,1)S(1)}, bf16[512,256]{1,0:T(8,128)(2,1)S(1)}, u32[]{:S(2)}, u32[]{:S(2)}) collective-permute-start(bf16[512,256]{1,0:T(8,128)(2,1)S(1)} %pad_maximum_fusion.rest_0_), channel_id=1, source_target_pairs={{64,0},{128,64},{192,128},{0,192},{65,1},{129,65},{193,129},{1,193... | collective-permute-start | bytes 786440 | tf_op jit(solution)/shard_map/ppermute | solution.py:288
  18.2 2.6 %collective-permute-start.6 = (bf16[512,256]{1,0:T(8,128)(2,1)S(1)}, bf16[512,256]{1,0:T(8,128)(2,1)S(1)}, u32[]{:S(2)}, u32[]{:S(2)}) collective-permute-start(bf16[512,256]{1,0:T(8,128)(2,1)S(1)} %pad_maximum_fusion.rest_0_), channel_id=1, source_target_pairs={{0,8},{8,0},{1,9},{9,1},{2,10},{10,2},{3,11},{11,3},{4,12},{12,4},... | collective-permute-start | bytes 786440 | tf_op jit(solution)/shard_map/ppermute | solution.py:293
  21.3 3.9 %collective-permute-start.9 = (bf16[512,256]{1,0:T(8,128)(2,1)S(1)}, bf16[512,256]{1,0:T(8,128)(2,1)S(1)}, u32[]{:S(2)}, u32[]{:S(2)}) collective-permute-start(bf16[512,256]{1,0:T(8,128)(2,1)S(1)} %collective-permute-done.5.rest_3_), channel_id=1, source_target_pairs={{0,8},{8,0},{1,9},{9,1},{2,10},{10,2},{3,11},{11,3},{4,12},{12,4},... | collective-permute-start | bytes 786440 | tf_op jit(solution)/shard_map/ppermute | solution.py:293
  25.2 2.0 %collective-permute-done.4.rest_2_ = bf16[512,256]{1,0:T(8,128)(2,1)S(1)} collective-permute-done((bf16[512,256]{1,0:T(8,128)(2,1)S(1)}, bf16[512,256]{1,0:T(8,128)(2,1)S(1)}, u32[]{:S(2)}, u32[]{:S(2)}) %collective-permute-start.4) | collective-permute-done | bytes 262176 | tf_op jit(solution)/shard_map/ppermute | solution.py:288
  27.2 2.7 %collective-permute-start.8 = (bf16[512,256]{1,0:T(8,128)(2,1)S(1)}, bf16[512,256]{1,0:T(8,128)(2,1)S(1)}, u32[]{:S(2)}, u32[]{:S(2)}) collective-permute-start(bf16[512,256]{1,0:T(8,128)(2,1)S(1)} %collective-permute-done.4.rest_2_), channel_id=1, source_target_pairs={{0,8},{8,0},{1,9},{9,1},{2,10},{10,2},{3,11},{11,3},{4,12},{12,4},... | collective-permute-start | bytes 786440 | tf_op jit(solution)/shard_map/ppermute | solution.py:293
  29.9 0.9 copy-done
  30.8 0.9 copy-done.1
  32.4 1.4 %by_heads.1 = (s32[64]{0:T(128)S(1)}, bf16[2,256,128]{2,1,0:T(8,128)(2,1)S(1)}, bf16[2,256,128]{2,1,0:T(8,128)(2,1)S(1)}) custom-call(s32[64]{0:T(128)S(1)} %copy-done.2, bf16[128,512]{1,0:T(8,128)(2,1)S(1)} %copy-done, bf16[128,512]{1,0:T(8,128)(2,1)S(1)} %copy-done.1), custom_call_target="tpu_custom_call" | custom-call | tf_op jit(solution)/shard_map/by_heads/pallas_call | solution.py:209
  33.8 8.4 %attention_forward.1 = (bf16[32,8192]{1,0:T(8,128)(2,1)S(1)}, bf16[32,8192]{1,0:T(8,128)(2,1)S(1)}, bf16[32,8192]{1,0:T(8,128)(2,1)S(1)}, bf16[32,8192]{1,0:T(8,...) custom-call(s32[64]{0:T(128)S(1)} %get-tuple-element.18.ids_ref, ...), custom_call_target="tpu_custom_call" | custom-call | flops 4000000000 | bytes 12000000 | tf_op jit(solution)/shard_map/attention_forward/pallas_call | solution.py:230
  42.2 6.1 %attention_backward.1 = (bf16[128,512]{1,0:T(8,128)(2,1)}, bf16[2048,256]{1,0:T(8,128)(2,1)S(1)}, bf16[2048,256]{1,0:T(8,128)(2,1)S(1)}) custom-call(s32[64]{0:T(128)S(1)} %get-tuple-element.18.ids_ref, bf16[17,256,256]{2,1,0:T(8,128)(2,1)S(1)} %get-tuple-element.25.p_ref, bf16[4096,256]{1,0:T(8,128)(2,1)S(1)} %get-tuple-element.26.kv_ref, ...), custom_call_target="tpu_custom_call" | custom-call | flops 49999998976 | bytes 12000000 | tf_op jit(solution)/shard_map/attention_backward/pallas_call | solution.py:263
  48.8 1.3 %collective-permute-start.10 = (bf16[32,8192]{1,0:T(8,128)(2,1)S(1)}, bf16[32,8192]{1,0:T(8,128)(2,1)S(1)}, u32[]{:S(2)}, u32[]{:S(2)}) collective-permute-start(bf16[32,8192]{1,0:T(8,128)(2,1)S(1)} %get-tuple-element.22), channel_id=1, source_target_pairs={{0,1},{1,2},{2,3},{3,0},{4,5},{5,6},{6,7},{7,4},{8,9},{9,10},{10,1... | collective-permute-start | bytes 1572872 | tf_op jit(solution)/shard_map/ppermute | solution.py:283
  50.1 2.6 %collective-permute-start.11 = (bf16[32,8192]{1,0:T(8,128)(2,1)S(1)}, bf16[32,8192]{1,0:T(8,128)(2,1)S(1)}, u32[]{:S(2)}, u32[]{:S(2)}) collective-permute-start(bf16[32,8192]{1,0:T(8,128)(2,1)S(1)} %get-tuple-element.23), channel_id=1, source_target_pairs={{0,2},{1,3},{2,0},{3,1},{4,6},{5,7},{6,4},{7,5},{8,10},{9,11},{10,... | collective-permute-start | bytes 1572872 | tf_op jit(solution)/shard_map/ppermute | solution.py:283
  52.7 1.1 %collective-permute-start.12 = (bf16[32,8192]{1,0:T(8,128)(2,1)S(1)}, bf16[32,8192]{1,0:T(8,128)(2,1)S(1)}, u32[]{:S(2)}, u32[]{:S(2)}) collective-permute-start(bf16[32,8192]{1,0:T(8,128)(2,1)S(1)} %get-tuple-element.24), channel_id=1, source_target_pairs={{0,3},{1,0},{2,1},{3,2},{4,7},{5,4},{6,5},{7,6},{8,11},{9,8},{10,9... | collective-permute-start | bytes 1572872 | tf_op jit(solution)/shard_map/ppermute | solution.py:283
  54.2 0.8 collective-permute-start.15
  55.0 2.1 %collective-permute-start.17 = (bf16[512,256]{1,0:T(8,128)(2,1)S(1)}, bf16[512,256]{1,0:T(8,128)(2,1)S(1)}, u32[]{:S(2)}, u32[]{:S(2)}) collective-permute-start(bf16[512,256]{1,0:T(8,128)(2,1)S(1)} %get-tuple-element.33), channel_id=1, source_target_pairs={{0,192},{64,0},{128,64},{192,128},{1,193},{65,1},{129,65},{193,129... | collective-permute-start | bytes 786440 | tf_op jit(solution)/shard_map/ppermute | solution.py:283
  57.1 6.6 %collective-permute-done.10 = bf16[32,8192]{1,0:T(8,128)(2,1)S(1)} collective-permute-done((bf16[32,8192]{1,0:T(8,128)(2,1)S(1)}, bf16[32,8192]{1,0:T(8,128)(2,1)S(1)}, u32[]{:S(2)}, u32[]{:S(2)}) %collective-permute-start.10) | collective-permute-done | bytes 524320 | tf_op jit(solution)/shard_map/ppermute | solution.py:283
  63.7 1.3 %collective-permute-start.16 = (bf16[512,256]{1,0:T(8,128)(2,1)S(1)}, bf16[512,256]{1,0:T(8,128)(2,1)S(1)}, u32[]{:S(2)}, u32[]{:S(2)}) collective-permute-start(bf16[512,256]{1,0:T(8,128)(2,1)S(1)} %get-tuple-element.34), channel_id=1, source_target_pairs={{0,128},{64,192},{128,0},{192,64},{1,129},{65,193},{129,1},{193,65... | collective-permute-start | bytes 786440 | tf_op jit(solution)/shard_map/ppermute | solution.py:283
  65.0 11.1 %collective-permute-done.11 = bf16[32,8192]{1,0:T(8,128)(2,1)S(1)} collective-permute-done((bf16[32,8192]{1,0:T(8,128)(2,1)S(1)}, bf16[32,8192]{1,0:T(8,128)(2,1)S(1)}, u32[]{:S(2)}, u32[]{:S(2)}) %collective-permute-start.11) | collective-permute-done | bytes 524320 | tf_op jit(solution)/shard_map/ppermute | solution.py:283
  76.4 6.6 %collective-permute-start.13 = (bf16[16,8192]{1,0:T(8,128)(2,1)S(1)}, bf16[16,8192]{1,0:T(8,128)(2,1)S(1)}, u32[]{:S(2)}, u32[]{:S(2)}) collective-permute-start(bf16[16,8192]{1,0:T(8,128)(2,1)S(1)} %slice.49), channel_id=1, source_target_pairs={{0,4},{4,0},{1,5},{5,1},{2,6},{6,2},{3,7},{7,3},{8,12},{12,8},{9,1... | collective-permute-start | bytes 786440 | tf_op jit(solution)/shard_map/ppermute | solution.py:293
  83.3 1.7 %collective-permute-start.20 = (bf16[128,256]{1,0:T(8,128)(2,1)S(1)}, bf16[128,256]{1,0:T(8,128)(2,1)S(1)}, u32[]{:S(2)}, u32[]{:S(2)}) collective-permute-start(bf16[128,256]{1,0:T(8,128)(2,1)S(1)} %get-tuple-element.36), channel_id=1, source_target_pairs={{0,48},{16,32},{32,16},{48,0},{1,49},{17,33},{33,17},{49,1},{2,50}... | collective-permute-start | bytes 196616 | tf_op jit(solution)/shard_map/ppermute | solution.py:293
  85.0 0.9 collective-permute-start.19
  85.9 7.6 %collective-permute-done.13 = bf16[16,8192]{1,0:T(8,128)(2,1)S(1)} collective-permute-done((bf16[16,8192]{1,0:T(8,128)(2,1)S(1)}, bf16[16,8192]{1,0:T(8,128)(2,1)S(1)}, u32[]{:S(2)}, u32[]{:S(2)}) %collective-permute-start.13) | collective-permute-done | bytes 262176 | tf_op jit(solution)/shard_map/ppermute | solution.py:293
  93.5 0.8 add_convert_fusion.3
  94.2 2.0 %collective-permute-done.20 = bf16[128,256]{1,0:T(8,128)(2,1)S(1)} collective-permute-done((bf16[128,256]{1,0:T(8,128)(2,1)S(1)}, bf16[128,256]{1,0:T(8,128)(2,1)S(1)}, u32[]{:S(2)}, u32[]{:S(2)}) %collective-permute-start.20) | collective-permute-done | bytes 65568 | tf_op jit(solution)/shard_map/ppermute | solution.py:293
  96.2 4.2 %collective-permute-done.19 = bf16[128,256]{1,0:T(8,128)(2,1)S(1)} collective-permute-done((bf16[128,256]{1,0:T(8,128)(2,1)S(1)}, bf16[128,256]{1,0:T(8,128)(2,1)S(1)}, u32[]{:S(2)}, u32[]{:S(2)}) %collective-permute-start.19) | collective-permute-done | bytes 65568 | tf_op jit(solution)/shard_map/ppermute | solution.py:293
  (30 shorter events, 3.6 us)
Async XLA Ops:
  2.1 7.2 %collective-permute-start.2 = (bf16[128,256]{1,0:T(8,128)(2,1)}, bf16[128,256]{1,0:T(8,128)(2,1)S(1)}, u32[]{:S(2)}, u32[]{:S(2)}) collective-permute-start(bf16[128,256]{1,0:T(8,128)(2,1)} %pair.1), channel_id=1, source_target_pairs={{0,48},{16,32},{32,16},{48,0},{1,49},{17,33},{33,17},{49,1},{2,50}... | collective-permute-start | bytes 196616 | tf_op jit(solution)/shard_map/ppermute | solution.py:293
  7.3 5.4 %collective-permute-start.1 = (bf16[128,256]{1,0:T(8,128)(2,1)}, bf16[128,256]{1,0:T(8,128)(2,1)S(1)}, u32[]{:S(2)}, u32[]{:S(2)}) collective-permute-start(bf16[128,256]{1,0:T(8,128)(2,1)} %pair.1), channel_id=1, source_target_pairs={{0,32},{16,48},{32,0},{48,16},{1,33},{17,49},{33,1},{49,17},{2,34}... | collective-permute-start | bytes 196616 | tf_op jit(solution)/shard_map/ppermute | solution.py:293
  7.3 5.4 %collective-permute-start = (bf16[128,256]{1,0:T(8,128)(2,1)}, bf16[128,256]{1,0:T(8,128)(2,1)S(1)}, u32[]{:S(2)}, u32[]{:S(2)}) collective-permute-start(bf16[128,256]{1,0:T(8,128)(2,1)} %pair.1), channel_id=1, source_target_pairs={{0,16},{16,0},{32,48},{48,32},{1,17},{17,1},{33,49},{49,33},{2,18}... | collective-permute-start | bytes 196616 | tf_op jit(solution)/shard_map/ppermute | solution.py:293
  13.6 7.7 %collective-permute-start.5 = (bf16[512,256]{1,0:T(8,128)(2,1)S(1)}, bf16[512,256]{1,0:T(8,128)(2,1)S(1)}, u32[]{:S(2)}, u32[]{:S(2)}) collective-permute-start(bf16[512,256]{1,0:T(8,128)(2,1)S(1)} %pad_maximum_fusion.rest_0_), channel_id=1, source_target_pairs={{192,0},{0,64},{64,128},{128,192},{193,1},{1,65},{65,129},{129,193... | collective-permute-start | bytes 786440 | tf_op jit(solution)/shard_map/ppermute | solution.py:288
  14.6 12.7 %collective-permute-start.4 = (bf16[512,256]{1,0:T(8,128)(2,1)S(1)}, bf16[512,256]{1,0:T(8,128)(2,1)S(1)}, u32[]{:S(2)}, u32[]{:S(2)}) collective-permute-start(bf16[512,256]{1,0:T(8,128)(2,1)S(1)} %pad_maximum_fusion.rest_0_), channel_id=1, source_target_pairs={{128,0},{192,64},{0,128},{64,192},{129,1},{193,65},{1,129},{65,193... | collective-permute-start | bytes 786440 | tf_op jit(solution)/shard_map/ppermute | solution.py:288
  17.0 12.9 %collective-permute-start.3 = (bf16[512,256]{1,0:T(8,128)(2,1)S(1)}, bf16[512,256]{1,0:T(8,128)(2,1)S(1)}, u32[]{:S(2)}, u32[]{:S(2)}) collective-permute-start(bf16[512,256]{1,0:T(8,128)(2,1)S(1)} %pad_maximum_fusion.rest_0_), channel_id=1, source_target_pairs={{64,0},{128,64},{192,128},{0,192},{65,1},{129,65},{193,129},{1,193... | collective-permute-start | bytes 786440 | tf_op jit(solution)/shard_map/ppermute | solution.py:288
  18.2 15.6 %collective-permute-start.6 = (bf16[512,256]{1,0:T(8,128)(2,1)S(1)}, bf16[512,256]{1,0:T(8,128)(2,1)S(1)}, u32[]{:S(2)}, u32[]{:S(2)}) collective-permute-start(bf16[512,256]{1,0:T(8,128)(2,1)S(1)} %pad_maximum_fusion.rest_0_), channel_id=1, source_target_pairs={{0,8},{8,0},{1,9},{9,1},{2,10},{10,2},{3,11},{11,3},{4,12},{12,4},... | collective-permute-start | bytes 786440 | tf_op jit(solution)/shard_map/ppermute | solution.py:293
  21.3 12.5 %collective-permute-start.9 = (bf16[512,256]{1,0:T(8,128)(2,1)S(1)}, bf16[512,256]{1,0:T(8,128)(2,1)S(1)}, u32[]{:S(2)}, u32[]{:S(2)}) collective-permute-start(bf16[512,256]{1,0:T(8,128)(2,1)S(1)} %collective-permute-done.5.rest_3_), channel_id=1, source_target_pairs={{0,8},{8,0},{1,9},{9,1},{2,10},{10,2},{3,11},{11,3},{4,12},{12,4},... | collective-permute-start | bytes 786440 | tf_op jit(solution)/shard_map/ppermute | solution.py:293
  27.2 6.6 %collective-permute-start.8 = (bf16[512,256]{1,0:T(8,128)(2,1)S(1)}, bf16[512,256]{1,0:T(8,128)(2,1)S(1)}, u32[]{:S(2)}, u32[]{:S(2)}) collective-permute-start(bf16[512,256]{1,0:T(8,128)(2,1)S(1)} %collective-permute-done.4.rest_2_), channel_id=1, source_target_pairs={{0,8},{8,0},{1,9},{9,1},{2,10},{10,2},{3,11},{11,3},{4,12},{12,4},... | collective-permute-start | bytes 786440 | tf_op jit(solution)/shard_map/ppermute | solution.py:293
  29.9 3.9 %collective-permute-start.7 = (bf16[512,256]{1,0:T(8,128)(2,1)S(1)}, bf16[512,256]{1,0:T(8,128)(2,1)S(1)}, u32[]{:S(2)}, u32[]{:S(2)}) collective-permute-start(bf16[512,256]{1,0:T(8,128)(2,1)S(1)} %collective-permute-done.3.rest_1_), channel_id=1, source_target_pairs={{0,8},{8,0},{1,9},{9,1},{2,10},{10,2},{3,11},{11,3},{4,12},{12,4},... | collective-permute-start | bytes 786440 | tf_op jit(solution)/shard_map/ppermute | solution.py:293
  29.9 0.9 copy-start
  30.8 0.9 copy-start.1
  31.7 0.7 copy-start.2
  48.3 5.5 %collective-permute-start.14 = (bf16[2048,256]{1,0:T(8,128)(2,1)S(1)}, bf16[2048,256]{1,0:T(8,128)(2,1)S(1)}, u32[]{:S(2)}, u32[]{:S(2)}) collective-permute-start(bf16[2048,256]{1,0:T(8,128)(2,1)S(1)} %get-tuple-element.31), channel_id=1, source_target_pairs={{0,8},{8,0},{1,9},{9,1},{2,10},{10,2},{3,11},{11,3},{4,12},{12,4},... | collective-permute-start | bytes 3145736 | tf_op jit(solution)/shard_map/ppermute | solution.py:293
  48.8 14.9 %collective-permute-start.10 = (bf16[32,8192]{1,0:T(8,128)(2,1)S(1)}, bf16[32,8192]{1,0:T(8,128)(2,1)S(1)}, u32[]{:S(2)}, u32[]{:S(2)}) collective-permute-start(bf16[32,8192]{1,0:T(8,128)(2,1)S(1)} %get-tuple-element.22), channel_id=1, source_target_pairs={{0,1},{1,2},{2,3},{3,0},{4,5},{5,6},{6,7},{7,4},{8,9},{9,10},{10,1... | collective-permute-start | bytes 1572872 | tf_op jit(solution)/shard_map/ppermute | solution.py:283
  50.1 25.9 %collective-permute-start.11 = (bf16[32,8192]{1,0:T(8,128)(2,1)S(1)}, bf16[32,8192]{1,0:T(8,128)(2,1)S(1)}, u32[]{:S(2)}, u32[]{:S(2)}) collective-permute-start(bf16[32,8192]{1,0:T(8,128)(2,1)S(1)} %get-tuple-element.23), channel_id=1, source_target_pairs={{0,2},{1,3},{2,0},{3,1},{4,6},{5,7},{6,4},{7,5},{8,10},{9,11},{10,... | collective-permute-start | bytes 1572872 | tf_op jit(solution)/shard_map/ppermute | solution.py:283
  52.7 23.3 %collective-permute-start.12 = (bf16[32,8192]{1,0:T(8,128)(2,1)S(1)}, bf16[32,8192]{1,0:T(8,128)(2,1)S(1)}, u32[]{:S(2)}, u32[]{:S(2)}) collective-permute-start(bf16[32,8192]{1,0:T(8,128)(2,1)S(1)} %get-tuple-element.24), channel_id=1, source_target_pairs={{0,3},{1,0},{2,1},{3,2},{4,7},{5,4},{6,5},{7,6},{8,11},{9,8},{10,9... | collective-permute-start | bytes 1572872 | tf_op jit(solution)/shard_map/ppermute | solution.py:283
  54.2 28.8 %collective-permute-start.15 = (bf16[512,256]{1,0:T(8,128)(2,1)S(1)}, bf16[512,256]{1,0:T(8,128)(2,1)S(1)}, u32[]{:S(2)}, u32[]{:S(2)}) collective-permute-start(bf16[512,256]{1,0:T(8,128)(2,1)S(1)} %get-tuple-element.32), channel_id=1, source_target_pairs={{0,64},{64,128},{128,192},{192,0},{1,65},{65,129},{129,193},{193,1... | collective-permute-start | bytes 786440 | tf_op jit(solution)/shard_map/ppermute | solution.py:283
  55.0 28.0 %collective-permute-start.17 = (bf16[512,256]{1,0:T(8,128)(2,1)S(1)}, bf16[512,256]{1,0:T(8,128)(2,1)S(1)}, u32[]{:S(2)}, u32[]{:S(2)}) collective-permute-start(bf16[512,256]{1,0:T(8,128)(2,1)S(1)} %get-tuple-element.33), channel_id=1, source_target_pairs={{0,192},{64,0},{128,64},{192,128},{1,193},{65,1},{129,65},{193,129... | collective-permute-start | bytes 786440 | tf_op jit(solution)/shard_map/ppermute | solution.py:283
  63.7 19.3 %collective-permute-start.16 = (bf16[512,256]{1,0:T(8,128)(2,1)S(1)}, bf16[512,256]{1,0:T(8,128)(2,1)S(1)}, u32[]{:S(2)}, u32[]{:S(2)}) collective-permute-start(bf16[512,256]{1,0:T(8,128)(2,1)S(1)} %get-tuple-element.34), channel_id=1, source_target_pairs={{0,128},{64,192},{128,0},{192,64},{1,129},{65,193},{129,1},{193,65... | collective-permute-start | bytes 786440 | tf_op jit(solution)/shard_map/ppermute | solution.py:283
  76.4 17.1 %collective-permute-start.13 = (bf16[16,8192]{1,0:T(8,128)(2,1)S(1)}, bf16[16,8192]{1,0:T(8,128)(2,1)S(1)}, u32[]{:S(2)}, u32[]{:S(2)}) collective-permute-start(bf16[16,8192]{1,0:T(8,128)(2,1)S(1)} %slice.49), channel_id=1, source_target_pairs={{0,4},{4,0},{1,5},{5,1},{2,6},{6,2},{3,7},{7,3},{8,12},{12,8},{9,1... | collective-permute-start | bytes 786440 | tf_op jit(solution)/shard_map/ppermute | solution.py:293
  83.1 11.1 %collective-permute-start.18 = (bf16[128,256]{1,0:T(8,128)(2,1)S(1)}, bf16[128,256]{1,0:T(8,128)(2,1)S(1)}, u32[]{:S(2)}, u32[]{:S(2)}) collective-permute-start(bf16[128,256]{1,0:T(8,128)(2,1)S(1)} %get-tuple-element.35), channel_id=1, source_target_pairs={{0,16},{16,0},{32,48},{48,32},{1,17},{17,1},{33,49},{49,33},{2,18}... | collective-permute-start | bytes 196616 | tf_op jit(solution)/shard_map/ppermute | solution.py:293
  83.3 12.9 %collective-permute-start.20 = (bf16[128,256]{1,0:T(8,128)(2,1)S(1)}, bf16[128,256]{1,0:T(8,128)(2,1)S(1)}, u32[]{:S(2)}, u32[]{:S(2)}) collective-permute-start(bf16[128,256]{1,0:T(8,128)(2,1)S(1)} %get-tuple-element.36), channel_id=1, source_target_pairs={{0,48},{16,32},{32,16},{48,0},{1,49},{17,33},{33,17},{49,1},{2,50}... | collective-permute-start | bytes 196616 | tf_op jit(solution)/shard_map/ppermute | solution.py:293
  85.0 15.5 %collective-permute-start.19 = (bf16[128,256]{1,0:T(8,128)(2,1)S(1)}, bf16[128,256]{1,0:T(8,128)(2,1)S(1)}, u32[]{:S(2)}, u32[]{:S(2)}) collective-permute-start(bf16[128,256]{1,0:T(8,128)(2,1)S(1)} %get-tuple-element.37), channel_id=1, source_target_pairs={{0,32},{16,48},{32,0},{48,16},{1,33},{17,49},{33,1},{49,17},{2,34}... | collective-permute-start | bytes 196616 | tf_op jit(solution)/shard_map/ppermute | solution.py:293

commit v4 on v3

v4 whole, which is shorter than its diff:
```python
import functools
import jax
import jax.numpy as jnp
from jax import lax
from jax.experimental import pallas as pl
from jax.experimental.pallas import tpu as pltpu
from jax.sharding import Mesh, PartitionSpec as P

HD = 128
QPG = 4
NEG = -1e30
SCALE = HD ** (-0.5)
NT = (((1,), (1,)), ((), ()))
NN = (((1,), (0,)), ((), ()))
TN = (((0,), (0,)), ((), ()))
MIB = 1024 * 1024
NX, NZ, NC, NH, NY = 4, 4, 2, 2, 4
CTX = ("x", "zl", "core")
TP = ("zh", "y")
MIX_SPAN = 1024
CHUNK = 4
BWD_FLOPS = 2 * 10**10
SMEM = pl.BlockSpec(memory_space=pltpu.SMEM)
VMEM = pl.BlockSpec(memory_space=pltpu.VMEM)
HBM = pl.BlockSpec(memory_space=pltpu.HBM)
ANY = pl.BlockSpec(memory_space=pl.ANY)


def dot(a, b, dims):
    return lax.dot_general(a, b, dims, preferred_element_type=jnp.float32)


def slot_of(x, zl, core, half):
    return ((x * NZ + zl) * NC + core) * 2 + half


def place_of(c_step, x_step, z_step):
    x, zl, core = (lax.axis_index(name) for name in CTX)
    return slot_of(lax.rem(x + x_step, NX), jnp.bitwise_xor(zl, z_step), jnp.bitwise_xor(core, c_step), 0)


def pair_kernel(k_hbm, v_hbm, kv_ref, sem):
    copies = [pltpu.make_async_copy(k_hbm, kv_ref.at[:, :HD], sem.at[0]),
              pltpu.make_async_copy(v_hbm, kv_ref.at[:, HD:], sem.at[1])]
    for copy in copies:
        copy.start()
    for copy in copies:
        copy.wait()


def heads_kernel(q_hbm, do_hbm, kv_ref, qs_ref, ds_ref, same_ref, sem):
    stretch = q_hbm.shape[0] // 2
    copies = []
    for which, (source, target) in enumerate(((q_hbm, qs_ref), (do_hbm, ds_ref))):
        for part in range(2):
            for head in range(QPG):
                copies.append(pltpu.make_async_copy(
                    source.at[part * stretch:(part + 1) * stretch, head * HD:(head + 1) * HD],
                    target.at[part, head * stretch:(head + 1) * stretch, :],
                    sem.at[which, part, head]))
    for copy in copies:
        copy.start()
    same_ref[...] = kv_ref[...]
    for copy in copies:
        copy.wait()


def plan_kernel(ids_ref, plan_ref, slot_ref):
    slots = ids_ref.shape[0]
    core = lax.axis_index("core")
    mine = place_of(0, 0, 0)
    own = [ids_ref[mine], ids_ref[mine + 1]]
    for slot in range(slots):
        slot_ref[ids_ref[slot]] = jnp.int32(slot)
    near, far, *seen = (jnp.int32(0),) * 6
    for value in range(slots):
        slot = slot_ref[value]
        away = jnp.bitwise_xor(lax.rem(slot // 2, NC), core)
        at = jnp.where(away == 0, near, slots // 2 + far)
        plan_ref[slot] = at
        plan_ref[slots + at] = jnp.int32(value)
        near, far = near + (1 - away), far + away
        seen = [before + jnp.where((own[part] >= value) & (away == side), 1, 0)
                for before, (side, part) in zip(seen, ((0, 0), (0, 1), (1, 0), (1, 1)))]
    for index in range(4):
        plan_ref[2 * slots + index] = (seen[index] + CHUNK - 1) // CHUNK
    for part in range(2):
        plan_ref[2 * slots + 4 + part] = own[part]


class Plan:
    def __init__(self, ref, slots, stretch):
        self.ref, self.slots, self.stretch = ref, slots, stretch
        self.span = CHUNK * stretch

    def row(self, slot):
        return pl.multiple_of(self.ref[slot] * self.stretch, self.stretch)

    def step(self, side, index):
        first = self.ref[2 * self.slots + 2 * side]
        count = first + self.ref[2 * self.slots + 2 * side + 1]
        late = index >= first
        part = jnp.where(late, 1, 0)
        last = self.slots // 2 // CHUNK - 1
        chunk = jnp.minimum(index - part * first, last)
        row = pl.multiple_of(chunk * self.span, self.span)
        return part, row, chunk, index < count

    def limits(self, side, part, chunk, valid):
        own = self.ref[2 * self.slots + 4 + part]
        at = self.slots + side * (self.slots // 2) + chunk * CHUNK
        return [jnp.where(valid, (own - self.ref[at + group]) * self.stretch, -2 * self.stretch)
                for group in range(CHUNK)]


def fwd_kernel(stretch, plan_ref, qs_ref, ds_ref, *rest):
    pieces, rest = rest[:NC * NX], rest[NC * NX:]
    (w_hbm, own_ref, front_ref, back_ref, far_a, far_b, p_ref, kv_ref, delta_ref, inv_ref,
     w_ref, s_buf, top_ref, sum_ref, acc_ref, diff_ref, attn_ref, turned_ref, w_sem) = rest
    steps, span, cols = p_ref.shape
    total = kv_ref.shape[0]
    plan = Plan(plan_ref, total // stretch, stretch)
    weight_copies = []
    for index in range(w_ref.shape[1] // MIX_SPAN):
        at = slice(index * MIX_SPAN, (index + 1) * MIX_SPAN)
        weight_copies.append(pltpu.make_async_copy(w_hbm.at[:, at], w_ref.at[:, at], w_sem.at[index]))
    for copy in weight_copies:
        copy.start()
    for c_step in range(NC):
        for x_step in range(NX):
            piece = pieces[c_step * NX + x_step]
            for z_step in range(NZ):
                slot = place_of(c_step, x_step, z_step)
                for half in range(2):
                    at = (z_step * 2 + half) * stretch
                    kv_ref[pl.ds(plan.row(slot + half), stretch), :] = piece[at:at + stretch, :]
    k_at = lax.broadcasted_iota(jnp.int32, (stretch, cols), 0)
    q_at = lax.broadcasted_iota(jnp.int32, (stretch, cols), 1) % stretch
    diff_ref[...] = k_at - q_at
    top_ref[...] = jnp.full_like(top_ref, NEG)
    sum_ref[...] = jnp.zeros_like(sum_ref)
    acc_ref[...] = jnp.zeros_like(acc_ref)

    for step in range(steps):
        side, index = divmod(step, steps // 2)
        part, row, chunk, valid = plan.step(side, index)
        scores = dot(kv_ref[pl.ds(side * (total // 2) + row, span), :HD], qs_ref[part], NT)
        limits = plan.limits(side, part, chunk, valid)
        top = top_ref[part]
        for group, limit in enumerate(limits):
            rows = slice(group * stretch, (group + 1) * stretch)
            block = jnp.where(diff_ref[...] <= limit, scores[rows], NEG)
            s_buf[step, rows] = block
            top = jnp.maximum(top, jnp.max(block.reshape(stretch // 8, 8, cols), axis=0))
        top_ref[part] = top
    for part in range(2):
        top_ref[part] = jnp.broadcast_to(jnp.max(top_ref[part], axis=0, keepdims=True), (8, cols))

    for step in range(steps):
        side, index = divmod(step, steps // 2)
        part, row, chunk, valid = plan.step(side, index)
        shifted = jnp.exp((s_buf[step].reshape(span // 8, 8, cols) - top_ref[part][None]) * SCALE)
        sum_ref[part] += jnp.sum(shifted, axis=0)
        weights = shifted.reshape(span, cols).astype(jnp.bfloat16)
        p_ref[step] = weights
        acc_ref[part] += dot(kv_ref[pl.ds(side * (total // 2) + row, span), HD:], weights, TN)

    for part in range(2):
        inverse = 1.0 / jnp.sum(sum_ref[part], axis=0, keepdims=True)
        inv_ref[part] = jnp.broadcast_to(inverse, (8, cols))
        out = (acc_ref[part] * inverse).T.astype(jnp.bfloat16)
        prod = ds_ref[part].astype(jnp.float32) * out.astype(jnp.float32)
        delta_ref[part] = jnp.broadcast_to(jnp.sum(prod.T, axis=0, keepdims=True), (8, cols))
        for head in range(QPG):
            attn_ref[part * stretch:(part + 1) * stretch, head * HD:(head + 1) * HD] = (
                out[head * stretch:(head + 1) * stretch])
    rows = attn_ref.shape[0] // (NH * NY)
    zh, y = lax.axis_index("zh"), lax.axis_index("y")
    for y_step in range(NY):
        for h_step in range(NH):
            block = jnp.bitwise_xor(zh, h_step) * NY + lax.rem(y + y_step, NY)
            to = (y_step * NH + h_step) * rows
            turned_ref[to:to + rows, :] = attn_ref[pl.ds(pl.multiple_of(block * rows, rows), rows), :]
    piece = NH * rows
    for index in range(w_ref.shape[1] // MIX_SPAN):
        at = slice(index * MIX_SPAN, (index + 1) * MIX_SPAN)
        weight_copies[index].wait()
        mixed = dot(turned_ref[...], w_ref[:, at], NN).astype(jnp.bfloat16)
        own_ref[:, at] = mixed[:piece]
        front_ref[:, at] = mixed[piece:2 * piece]
        back_ref[:, at] = mixed[3 * piece:]
        half = w_ref.shape[1] // 2
        if at.start < half:
            far_a[:, at] = mixed[2 * piece:3 * piece]
        else:
            far_b[:, at.start - half:at.stop - half] = mixed[2 * piece:3 * piece]


def bwd_kernel(stretch, side, plan_ref, p_ref, kv_ref, qs_ref, ds_ref, delta_ref, inv_ref, *rest):
    steps, span, cols = p_ref.shape
    total = kv_ref.shape[0]
    plan = Plan(plan_ref, total // stretch, stretch)
    if side == 0:
        acc_in, token_ref, dq_ref, out_ref, acc_ref, dk_ref, dv_ref, dn_ref = rest
        acc_ref[...] = acc_in[...]
    else:
        acc_ref, out_ref, dk_ref, dv_ref, dn_ref = rest
        acc_ref[...] = jnp.zeros_like(acc_ref)
    dk_ref[...] = jnp.zeros_like(dk_ref)
    dv_ref[...] = jnp.zeros_like(dv_ref)
    for part in range(2):
        column = jnp.broadcast_to(inv_ref[part][:1], (HD, cols)).T
        dn_ref[part] = (ds_ref[part].astype(jnp.float32) * column).astype(jnp.bfloat16)

    for index in range(steps // 2):
        part, row, chunk, valid = plan.step(side, index)
        here = pl.ds(row, span)
        there = pl.ds(side * (total // 2) + row, span)
        weights = p_ref[side * (steps // 2) + index]
        grad_probs = dot(kv_ref[there, HD:], ds_ref[part], NT)
        moved = (grad_probs.reshape(span // 8, 8, cols) - delta_ref[part][None]) * inv_ref[part][None]
        grad_scores = (weights.astype(jnp.float32) * moved.reshape(span, cols)).astype(jnp.bfloat16)
        dv_ref[here, :] += dot(weights, dn_ref[part], NN)
        dk_ref[here, :] += dot(grad_scores, qs_ref[part], NN)
        acc_ref[part] += dot(kv_ref[there, :HD], grad_scores, TN)

    to = 0
    for x_step in range(NX):
        for z_step in range(NZ):
            slot = place_of(side, x_step, z_step)
            for half in range(2):
                here = pl.ds(plan.row(slot + half) - side * (total // 2), stretch)
                out_ref[to:to + stretch, :HD] = (dk_ref[here, :] * SCALE).astype(jnp.bfloat16)
                out_ref[to:to + stretch, HD:] = dv_ref[here, :].astype(jnp.bfloat16)
                to += stretch
    if side == 0:
        for part in range(2):
            out = (acc_ref[part].T * SCALE).astype(jnp.bfloat16)
            for head in range(QPG):
                dq_ref[part * stretch:(part + 1) * stretch, head * HD:(head + 1) * HD] = (
                    out[head * stretch:(head + 1) * stretch])


def pair(keys, values):
    return pl.pallas_call(
        pair_kernel,
        out_shape=jax.ShapeDtypeStruct((keys.shape[0], 2 * HD), jnp.bfloat16),
        in_specs=[HBM] * 2,
        out_specs=VMEM,
        scratch_shapes=[pltpu.SemaphoreType.DMA((2,))],
        compiler_params=pltpu.CompilerParams(vmem_limit_bytes=60 * MIB),
        name="pair",
    )(keys, values)


def by_heads(queries, grad_heads, kv):
    shape = jax.ShapeDtypeStruct((2, QPG * queries.shape[0] // 2, HD), jnp.bfloat16)
    return pl.pallas_call(
        heads_kernel,
        out_shape=(shape, shape, jax.ShapeDtypeStruct(kv.shape, kv.dtype)),
        in_specs=[HBM] * 2 + [VMEM],
        out_specs=[VMEM] * 3,
        scratch_shapes=[pltpu.SemaphoreType.DMA((2, 2, QPG))],
        compiler_params=pltpu.CompilerParams(vmem_limit_bytes=4 * MIB),
        name="by_heads",
    )(queries, grad_heads, kv)


def plan_of(ids):
    slots = ids.shape[0]
    return pl.pallas_call(
        plan_kernel,
        out_shape=jax.ShapeDtypeStruct((2 * slots + 8,), jnp.int32),
        in_specs=[SMEM],
        out_specs=SMEM,
        scratch_shapes=[pltpu.SMEM((slots,), jnp.int32)],
        compiler_params=pltpu.CompilerParams(vmem_limit_bytes=4 * MIB),
        name="plan",
    )(ids)


def relay_kernel(front_in, back_in, front_add, back_add, front_ref, back_ref):
    half = front_add.shape[1]
    for index in range(2):
        at = slice(index * half // 2, (index + 1) * half // 2)
        front_ref[:, at] = (front_in[:, at].astype(jnp.float32) + front_add[:, at].astype(jnp.float32)
                            ).astype(jnp.bfloat16)
        to = slice(half + index * half // 2, half + (index + 1) * half // 2)
        back_ref[:, to] = (back_in[:, to].astype(jnp.float32) + back_add[:, at].astype(jnp.float32)
                           ).astype(jnp.bfloat16)


def relay(front, back, front_add, back_add):
    shape = jax.ShapeDtypeStruct(front.shape, front.dtype)
    return pl.pallas_call(
        relay_kernel,
        out_shape=(shape, shape),
        in_specs=[VMEM] * 4,
        out_specs=[VMEM] * 2,
        input_output_aliases={0: 0, 1: 1},
        compiler_params=pltpu.CompilerParams(vmem_limit_bytes=8 * MIB),
        name="relay",
    )(front, back, front_add, back_add)


def stack_kernel(token_ref, *refs):
    *parts, out_ref = refs
    rows = parts[0].shape[0]
    for index, part in enumerate(parts):
        out_ref[index * rows:(index + 1) * rows, :] = part[...]


def stack(token, *parts):
    rows, width = parts[0].shape
    return pl.pallas_call(
        stack_kernel,
        out_shape=jax.ShapeDtypeStruct((len(parts) * rows, width), parts[0].dtype),
        in_specs=[ANY] + [VMEM] * len(parts),
        out_specs=VMEM,
        compiler_params=pltpu.CompilerParams(vmem_limit_bytes=4 * MIB),
        name="stack",
    )(token, *parts)


def forward(plan, qs, ds, pieces, out_weight):
    cols = qs.shape[1]
    stretch = cols // QPG
    tokens = 2 * stretch
    total = sum(piece.shape[0] for piece in pieces)
    span = CHUNK * stretch
    steps = total // span + 2
    depth, width = out_weight.shape
    b16, f32 = jnp.bfloat16, jnp.float32
    shape = jax.ShapeDtypeStruct
    return pl.pallas_call(
        functools.partial(fwd_kernel, stretch),
        out_shape=(shape((tokens // NY, width), b16),) * 3 + (shape((tokens // NY, width // 2), b16),) * 2 + (
            shape((steps, span, cols), b16),
            shape((total, 2 * HD), b16),
            shape((2, 8, cols), f32),
            shape((2, 8, cols), f32),
        ),
        in_specs=[SMEM] + [VMEM] * (2 + len(pieces)) + [HBM],
        out_specs=[VMEM] * 9,
        scratch_shapes=[
            pltpu.VMEM((depth, width), b16),
            pltpu.VMEM((steps, span, cols), f32),
            pltpu.VMEM((2, 8, cols), f32),
            pltpu.VMEM((2, 8, cols), f32),
            pltpu.VMEM((2, HD, cols), f32),
            pltpu.VMEM((stretch, cols), jnp.int32),
            pltpu.VMEM((tokens, QPG * HD), b16),
            pltpu.VMEM((tokens, QPG * HD), b16),
            pltpu.SemaphoreType.DMA((width // MIX_SPAN,)),
        ],
        compiler_params=pltpu.CompilerParams(vmem_limit_bytes=40 * MIB),
        cost_estimate=pl.CostEstimate(flops=4 * 10**9, bytes_accessed=12 * 10**6, transcendentals=10**6),
        name="attention_forward",
    )(plan, qs, ds, *pieces, out_weight)


def backward(side, plan, probs, kv, qs, ds, delta, inverse, *partial):
    total = kv.shape[0]
    steps, span, cols = probs.shape
    stretch = cols // QPG
    b16, f32 = jnp.bfloat16, jnp.float32
    shape = jax.ShapeDtypeStruct
    terms = shape((total // 2, 2 * HD), b16)
    sums = (2, HD, cols)
    scratch = [
        pltpu.VMEM((total // 2, HD), f32),
        pltpu.VMEM((total // 2, HD), f32),
        pltpu.VMEM((2, cols, HD), b16),
    ]
    return pl.pallas_call(
        functools.partial(bwd_kernel, stretch, side),
        out_shape=(shape(sums, f32) if side else shape((2 * stretch, QPG * HD), b16), terms),
        in_specs=[SMEM] + [VMEM] * 6 + [VMEM, ANY][:len(partial)],
        out_specs=[VMEM] * 2,
        scratch_shapes=scratch if side else [pltpu.VMEM(sums, f32)] + scratch,
        compiler_params=pltpu.CompilerParams(vmem_limit_bytes=32 * MIB),
        cost_estimate=pl.CostEstimate(flops=BWD_FLOPS, bytes_accessed=8 * 10**6, transcendentals=0),
        name="attention_backward_%d" % side,
    )(plan, probs, kv, qs, ds, delta, inverse, *partial)


def ahead(block, axis, step):
    count = lax.axis_size(axis)
    return lax.ppermute(block, axis, [(i, (i + step) % count) for i in range(count)])


def behind(block, axis, step):
    count = lax.axis_size(axis)
    return lax.ppermute(block, axis, [((i + step) % count, i) for i in range(count)])


def across(block, axis, step):
    count = lax.axis_size(axis)
    return lax.ppermute(block, axis, [(i, i ^ step) for i in range(count)])


def total_of(parts):
    total = parts[0].astype(jnp.float32)
    for part in parts[1:]:
        total = total + part.astype(jnp.float32)
    return total.astype(jnp.bfloat16)


def on_device(queries, keys, values, stretch_of, out_weight, grad_heads):
    kv = pair(keys, values)
    qs, ds, same = by_heads(queries, grad_heads, kv)
    plan = plan_of(stretch_of)
    kv = stack(qs, same, *[across(kv, "zl", step) for step in range(1, NZ)])
    pieces = [kv] + [behind(kv, "x", step) for step in range(1, NX)]
    pieces = pieces + [across(piece, "core", 1) for piece in pieces]
    own, front, back, far_a, far_b, probs, kv, delta, inverse = forward(plan, qs, ds, pieces, out_weight)
    saved = (plan, probs, kv, qs, ds, delta, inverse)
    far_a, far_b = ahead(far_a, "y", 1), ahead(far_b, "y", NY - 1)
    partial, give = backward(1, *saved)
    front, back = relay(front, back, far_a, far_b)
    mixed = total_of([own, ahead(front, "y", 1), ahead(back, "y", NY - 1)])
    rows = mixed.shape[0] // NH
    mixed = total_of([mixed[:rows], across(mixed[rows:], "zh", 1)])
    q_grad, keep = backward(0, *saved, partial, front)
    term = total_of([keep, across(give, "core", 1)])
    part = term.shape[0] // NX
    term = total_of([term[:part]] + [
        ahead(term[step * part:(step + 1) * part], "x", step) for step in range(1, NX)])
    part = term.shape[0] // NZ
    term = total_of([term[:part]] + [
        across(term[step * part:(step + 1) * part], "zl", step) for step in range(1, NZ)])
    return mixed, q_grad, term[:, :HD], term[:, HD:]


def solution(mesh):
    fine = Mesh(mesh.devices.reshape(NX, NZ, NC, NH, NY), CTX + TP)
    return jax.shard_map(
        on_device,
        mesh=fine,
        in_specs=(P(CTX, TP), P(CTX, TP), P(CTX, TP), P(), P(TP, None), P(CTX, TP)),
        out_specs=(P(CTX + TP, None), P(CTX, TP), P(CTX, TP), P(CTX, TP)),
        check_vma=False,
    )
```

time: 101 us -> 89.8 us (0.89)
  waiting for transfers between devices: 39 us -> 24.5 us
  Pallas kernels: 17.3 us -> 18.8 us
  starting transfers between devices: 38.5 us -> 39.9 us
    ppermute x6 -> x7, waiting for transfers between devices: 17.7 us -> 6.05 us  [ahead(): lax.ppermute(block, axis, [(i, (i + step) % count) for i in range(count)])]
    ppermute x12, waiting for transfers between devices: 18.8 us -> 15.9 us  [across(): return lax.ppermute(block, axis, [(i, i ^ step) for i in range(count)])]
    pallas_call x3 -> x7, Pallas kernels: 15.9 us -> 17.4 us  [the longest x1 7.75 us: forward(): pl.pallas_call(functools.partial(fwd_kernel, stretch), out_shape=(shape((...]
    ppermute x6 -> x7, starting transfers between devices: 9.26 us -> 10.2 us  [ahead(): lax.ppermute(block, axis, [(i, (i + step) % count) for i in range(count)])]
    unnamed x6 -> x8, local copies, waits for them, and re-layouts: 2.46 us -> 3.33 us
  transfers between devices with their start and end apart: 21 -> 22, of which waited for: 9 -> 10; matrix products, arithmetic and copies ran while one was open for 2% -> 2% of each run, Pallas kernels for 1% -> 11%
where the time goes in v4:
time: 89.8 us; the launch traced here: 89.4 us
  starting transfers between devices  39.9 us (44%)
  waiting for transfers between devices  24.5 us (27%)
  Pallas kernels  18.8 us (21%)
  local copies, waits for them, and re-layouts  4.05 us (5%)
  other arithmetic  1.4 us (2%)
    ppermute x12, starting transfers between devices, across(): return lax.ppermute(block, axis, [(i, i ^ step) for i in range(count)])  25.1 us
    ppermute x12, waiting for transfers between devices, across(): return lax.ppermute(block, axis, [(i, i ^ step) for i in range(count)])  15.9 us
    ppermute x7, starting transfers between devices, ahead(): lax.ppermute(block, axis, [(i, (i + step) % count) for i in range(count)])  10.2 us
    pallas_call x1, Pallas kernels, forward(): pl.pallas_call(functools.partial(fwd_kernel, stretch), out_shape=(shape((...  7.75 us
    pallas_call x2, Pallas kernels, backward(): pl.pallas_call(functools.partial(bwd_kernel, stretch, side), out_shape=(s...  6.85 us
    ppermute x7, waiting for transfers between devices, ahead(): lax.ppermute(block, axis, [(i, (i + step) % count) for i in range(count)])  6.05 us
    ppermute x3, starting transfers between devices, behind(): lax.ppermute(block, axis, [((i + step) % count, i) for i in range(count)])  4.57 us
    unnamed x8, local copies, waits for them, and re-layouts  3.33 us
  transfers between devices with their start and end apart: 22, of which 10 were waited for; matrix products, arithmetic and copies ran while one was open for 2% of the time, Pallas kernels for 11%

profile of v4, /device:TPU:1, one launch (start us, length us, event | category | flops | bytes accessed | tf_op | source)
XLA Modules:
  0.0 89.4 jit_solution(385085001719508005)
XLA Ops:
  0.6 1.4 %pair.1.kv_ref = bf16[128,256]{1,0:T(8,128)(2,1)} custom-call(bf16[128,128]{1,0:T(8,128)(2,1)} %k_hbm.1, bf16[128,128]{1,0:T(8,128)(2,1)} %v_hbm.1), custom_call_target="tpu_custom_call" | custom-call | tf_op jit(solution)/shard_map/pair/pallas_call | solution.py:245
  2.1 5.3 %collective-permute-start.2 = (bf16[128,256]{1,0:T(8,128)(2,1)}, bf16[128,256]{1,0:T(8,128)(2,1)S(1)}, u32[]{:S(2)}, u32[]{:S(2)}) collective-permute-start(bf16[128,256]{1,0:T(8,128)(2,1)} %pair.1.kv_ref), channel_id=1, source_target_pairs={{0,48},{16,32},{32,16},{48,0},{1,49},{17,33},{33,17},{49,1},{2,50}... | collective-permute-start | bytes 196616 | tf_op jit(solution)/shard_map/ppermute | solution.py:399
  8.6 0.9 %copy-done.1 = bf16[128,512]{1,0:T(8,128)(2,1)S(1)} copy-done((bf16[128,512]{1,0:T(8,128)(2,1)S(1)}, bf16[128,512]{1,0:T(8,128)(2,1)}, u32[]{:S(2)}) %copy-start.1) | copy-done | bytes 131096
  9.5 0.9 %copy-done.2 = bf16[128,512]{1,0:T(8,128)(2,1)S(1)} copy-done((bf16[128,512]{1,0:T(8,128)(2,1)S(1)}, bf16[128,512]{1,0:T(8,128)(2,1)}, u32[]{:S(2)}) %copy-start.2) | copy-done | bytes 131096
  10.6 2.1 %collective-permute-done.1.refs_2_ = bf16[128,256]{1,0:T(8,128)(2,1)S(1)} collective-permute-done((bf16[128,256]{1,0:T(8,128)(2,1)}, bf16[128,256]{1,0:T(8,128)(2,1)S(1)}, u32[]{:S(2)}, u32[]{:S(2)}) %collective-permute-start.1) | collective-permute-done | bytes 65568 | tf_op jit(solution)/shard_map/ppermute | solution.py:399
  12.8 1.0 %collective-permute-start.5 = (bf16[512,256]{1,0:T(8,128)(2,1)S(1)}, bf16[512,256]{1,0:T(8,128)(2,1)S(1)}, u32[]{:S(2)}, u32[]{:S(2)}) collective-permute-start(bf16[512,256]{1,0:T(8,128)(2,1)S(1)} %stack.1.rest_0_), channel_id=1, source_target_pairs={{192,0},{0,64},{64,128},{128,192},{193,1},{1,65},{65,129},{129,193... | collective-permute-start | bytes 786440 | tf_op jit(solution)/shard_map/ppermute | solution.py:394
  13.7 2.5 %collective-permute-start.4 = (bf16[512,256]{1,0:T(8,128)(2,1)S(1)}, bf16[512,256]{1,0:T(8,128)(2,1)S(1)}, u32[]{:S(2)}, u32[]{:S(2)}) collective-permute-start(bf16[512,256]{1,0:T(8,128)(2,1)S(1)} %stack.1.rest_0_), channel_id=1, source_target_pairs={{128,0},{192,64},{0,128},{64,192},{129,1},{193,65},{1,129},{65,193... | collective-permute-start | bytes 786440 | tf_op jit(solution)/shard_map/ppermute | solution.py:394
  16.2 1.2 %collective-permute-start.3 = (bf16[512,256]{1,0:T(8,128)(2,1)S(1)}, bf16[512,256]{1,0:T(8,128)(2,1)S(1)}, u32[]{:S(2)}, u32[]{:S(2)}) collective-permute-start(bf16[512,256]{1,0:T(8,128)(2,1)S(1)} %stack.1.rest_0_), channel_id=1, source_target_pairs={{64,0},{128,64},{192,128},{0,192},{65,1},{129,65},{193,129},{1,193... | collective-permute-start | bytes 786440 | tf_op jit(solution)/shard_map/ppermute | solution.py:394
  17.3 2.6 %collective-permute-start.6 = (bf16[512,256]{1,0:T(8,128)(2,1)S(1)}, bf16[512,256]{1,0:T(8,128)(2,1)S(1)}, u32[]{:S(2)}, u32[]{:S(2)}) collective-permute-start(bf16[512,256]{1,0:T(8,128)(2,1)S(1)} %stack.1.rest_0_), channel_id=1, source_target_pairs={{0,8},{8,0},{1,9},{9,1},{2,10},{10,2},{3,11},{11,3},{4,12},{12,4},... | collective-permute-start | bytes 786440 | tf_op jit(solution)/shard_map/ppermute | solution.py:399
  20.4 3.9 %collective-permute-start.9 = (bf16[512,256]{1,0:T(8,128)(2,1)S(1)}, bf16[512,256]{1,0:T(8,128)(2,1)S(1)}, u32[]{:S(2)}, u32[]{:S(2)}) collective-permute-start(bf16[512,256]{1,0:T(8,128)(2,1)S(1)} %collective-permute-done.5.rest_3_), channel_id=1, source_target_pairs={{0,8},{8,0},{1,9},{9,1},{2,10},{10,2},{3,11},{11,3},{4,12},{12,4},... | collective-permute-start | bytes 786440 | tf_op jit(solution)/shard_map/ppermute | solution.py:399
  24.4 2.0 %collective-permute-done.4.rest_2_ = bf16[512,256]{1,0:T(8,128)(2,1)S(1)} collective-permute-done((bf16[512,256]{1,0:T(8,128)(2,1)S(1)}, bf16[512,256]{1,0:T(8,128)(2,1)S(1)}, u32[]{:S(2)}, u32[]{:S(2)}) %collective-permute-start.4) | collective-permute-done | bytes 262176 | tf_op jit(solution)/shard_map/ppermute | solution.py:394
  26.4 2.7 %collective-permute-start.8 = (bf16[512,256]{1,0:T(8,128)(2,1)S(1)}, bf16[512,256]{1,0:T(8,128)(2,1)S(1)}, u32[]{:S(2)}, u32[]{:S(2)}) collective-permute-start(bf16[512,256]{1,0:T(8,128)(2,1)S(1)} %collective-permute-done.4.rest_2_), channel_id=1, source_target_pairs={{0,8},{8,0},{1,9},{9,1},{2,10},{10,2},{3,11},{11,3},{4,12},{12,4},... | collective-permute-start | bytes 786440 | tf_op jit(solution)/shard_map/ppermute | solution.py:399
  29.7 2.2 %plan.1.plan_ref = s32[136]{0:T(256)S(1)} custom-call(s32[64]{0:T(128)S(1)} %copy-done.3), custom_call_target="tpu_custom_call" | custom-call | tf_op jit(solution)/shard_map/plan/pallas_call | solution.py:271
  31.9 7.7 %attention_forward.1 = (bf16[32,8192]{1,0:T(8,128)(2,1)S(1)}, bf16[32,8192]{1,0:T(8,128)(2,1)S(1)}, bf16[32,8192]{1,0:T(8,128)(2,1)S(1)}, bf16[32,4096]{1,0:T(8,...) custom-call(s32[136]{0:T(256)S(1)} %plan.1.plan_ref, ...), custom_call_target="tpu_custom_call" | custom-call | flops 4000000000 | bytes 12000000 | tf_op jit(solution)/shard_map/attention_forward/pallas_call | solution.py:335
  39.7 1.5 %collective-permute-start.10 = (bf16[32,4096]{1,0:T(8,128)(2,1)S(1)}, bf16[32,4096]{1,0:T(8,128)(2,1)S(1)}, u32[]{:S(2)}, u32[]{:S(2)}) collective-permute-start(bf16[32,4096]{1,0:T(8,128)(2,1)S(1)} %get-tuple-element.28), channel_id=1, source_target_pairs={{0,1},{1,2},{2,3},{3,0},{4,5},{5,6},{6,7},{7,4},{8,9},{9,10},{10,1... | collective-permute-start | bytes 786440 | tf_op jit(solution)/shard_map/ppermute | solution.py:389
  41.2 1.5 %collective-permute-start.11 = (bf16[32,4096]{1,0:T(8,128)(2,1)S(1)}, bf16[32,4096]{1,0:T(8,128)(2,1)S(1)}, u32[]{:S(2)}, u32[]{:S(2)}) collective-permute-start(bf16[32,4096]{1,0:T(8,128)(2,1)S(1)} %get-tuple-element.29), channel_id=1, source_target_pairs={{0,3},{1,0},{2,1},{3,2},{4,7},{5,4},{6,5},{7,6},{8,11},{9,8},{10,9... | collective-permute-start | bytes 786440 | tf_op jit(solution)/shard_map/ppermute | solution.py:389
  42.8 3.0 %attention_backward_1.1 = (f32[2,128,256]{2,1,0:T(8,128)S(1)}, bf16[2048,256]{1,0:T(8,128)(2,1)S(1)}) custom-call(s32[136]{0:T(256)S(1)} %plan.1.plan_ref, bf16[18,256,256]{2,1,0:T(8,128)(2,1)S(1)} %get-tuple-element.32.p_ref, bf16[4096,256]{1,0:T(8,128)(2,1)S(1)} %get-tuple-element.33.kv_ref, bf16[2,256,128]{2,1,0:T(8,128)(2,1)S(1)} %get-tuple-element.22.token_ref.qs_ref, ...), custom_call_target="tpu_custom_call" | custom-call | flops 20000000000 | bytes 8000000 | tf_op jit(solution)/shard_map/attention_backward_1/pallas_call | solution.py:375
  45.8 1.0 %collective-permute-start.15 = (bf16[2048,256]{1,0:T(8,128)(2,1)S(1)}, bf16[2048,256]{1,0:T(8,128)(2,1)S(1)}, u32[]{:S(2)}, u32[]{:S(2)}) collective-permute-start(bf16[2048,256]{1,0:T(8,128)(2,1)S(1)} %get-tuple-element.39), channel_id=1, source_target_pairs={{0,8},{8,0},{1,9},{9,1},{2,10},{10,2},{3,11},{11,3},{4,12},{12,4},... | collective-permute-start | bytes 3145736 | tf_op jit(solution)/shard_map/ppermute | solution.py:399
  46.8 1.8 %collective-permute-done.10.front_add = bf16[32,4096]{1,0:T(8,128)(2,1)S(1)} collective-permute-done((bf16[32,4096]{1,0:T(8,128)(2,1)S(1)}, bf16[32,4096]{1,0:T(8,128)(2,1)S(1)}, u32[]{:S(2)}, u32[]{:S(2)}) %collective-permute-start.10) | collective-permute-done | bytes 262176 | tf_op jit(solution)/shard_map/ppermute | solution.py:389
  49.0 2.6 %collective-permute-start.13 = (bf16[32,8192]{1,0:T(8,128)(2,1)S(1)}, bf16[32,8192]{1,0:T(8,128)(2,1)S(1)}, u32[]{:S(2)}, u32[]{:S(2)}) collective-permute-start(bf16[32,8192]{1,0:T(8,128)(2,1)S(1)} %get-tuple-element.31), channel_id=1, source_target_pairs={{0,3},{1,0},{2,1},{3,2},{4,7},{5,4},{6,5},{7,6},{8,11},{9,8},{10,9... | collective-permute-start | bytes 1572872 | tf_op jit(solution)/shard_map/ppermute | solution.py:389
  51.6 3.8 %attention_backward_0.1 = (bf16[128,512]{1,0:T(8,128)(2,1)}, bf16[2048,256]{1,0:T(8,128)(2,1)S(1)}) custom-call(s32[136]{0:T(256)S(1)} %plan.1.plan_ref, bf16[18,256,256]{2,1,0:T(8,128)(2,1)S(1)} %get-tuple-element.32.p_ref, bf16[4096,256]{1,0:T(8,128)(2,1)S(1)} %get-tuple-element.33.kv_ref, bf16[2,256,128]{2,1,0:T(8,128)(2,1)S(1)} %get-tuple-element.22.token_ref.qs_ref, ...), custom_call_target="tpu_custom_call" | custom-call | flops 20000000000 | bytes 8000000 | tf_op jit(solution)/shard_map/attention_backward_0/pallas_call | solution.py:375
  55.8 1.7 %collective-permute-start.16 = (bf16[512,256]{1,0:T(8,128)(2,1)S(1)}, bf16[512,256]{1,0:T(8,128)(2,1)S(1)}, u32[]{:S(2)}, u32[]{:S(2)}) collective-permute-start(bf16[512,256]{1,0:T(8,128)(2,1)S(1)} %get-tuple-element.40), channel_id=1, source_target_pairs={{0,64},{64,128},{128,192},{192,0},{1,65},{65,129},{129,193},{193,1... | collective-permute-start | bytes 786440 | tf_op jit(solution)/shard_map/ppermute | solution.py:389
  57.5 1.0 %collective-permute-start.18 = (bf16[512,256]{1,0:T(8,128)(2,1)S(1)}, bf16[512,256]{1,0:T(8,128)(2,1)S(1)}, u32[]{:S(2)}, u32[]{:S(2)}) collective-permute-start(bf16[512,256]{1,0:T(8,128)(2,1)S(1)} %get-tuple-element.41), channel_id=1, source_target_pairs={{0,192},{64,0},{128,64},{192,128},{1,193},{65,1},{129,65},{193,129... | collective-permute-start | bytes 786440 | tf_op jit(solution)/shard_map/ppermute | solution.py:389
  58.5 1.7 %collective-permute-start.17 = (bf16[512,256]{1,0:T(8,128)(2,1)S(1)}, bf16[512,256]{1,0:T(8,128)(2,1)S(1)}, u32[]{:S(2)}, u32[]{:S(2)}) collective-permute-start(bf16[512,256]{1,0:T(8,128)(2,1)S(1)} %get-tuple-element.42), channel_id=1, source_target_pairs={{0,128},{64,192},{128,0},{192,64},{1,129},{65,193},{129,1},{193,65... | collective-permute-start | bytes 786440 | tf_op jit(solution)/shard_map/ppermute | solution.py:389
  60.3 1.1 %collective-permute-done.13 = bf16[32,8192]{1,0:T(8,128)(2,1)S(1)} collective-permute-done((bf16[32,8192]{1,0:T(8,128)(2,1)S(1)}, bf16[32,8192]{1,0:T(8,128)(2,1)S(1)}, u32[]{:S(2)}, u32[]{:S(2)}) %collective-permute-start.13) | collective-permute-done | bytes 524320 | tf_op jit(solution)/shard_map/ppermute | solution.py:389
  61.3 3.1 %collective-permute-done.12 = bf16[32,8192]{1,0:T(8,128)(2,1)S(1)} collective-permute-done((bf16[32,8192]{1,0:T(8,128)(2,1)S(1)}, bf16[32,8192]{1,0:T(8,128)(2,1)S(1)}, u32[]{:S(2)}, u32[]{:S(2)}) %collective-permute-start.12) | collective-permute-done | bytes 524320 | tf_op jit(solution)/shard_map/ppermute | solution.py:389
  64.7 6.6 %collective-permute-start.14 = (bf16[16,8192]{1,0:T(8,128)(2,1)S(1)}, bf16[16,8192]{1,0:T(8,128)(2,1)S(1)}, u32[]{:S(2)}, u32[]{:S(2)}) collective-permute-start(bf16[16,8192]{1,0:T(8,128)(2,1)S(1)} %slice.49), channel_id=1, source_target_pairs={{0,4},{4,0},{1,5},{5,1},{2,6},{6,2},{3,7},{7,3},{8,12},{12,8},{9,1... | collective-permute-start | bytes 786440 | tf_op jit(solution)/shard_map/ppermute | solution.py:399
  71.5 1.8 %collective-permute-start.21 = (bf16[128,256]{1,0:T(8,128)(2,1)S(1)}, bf16[128,256]{1,0:T(8,128)(2,1)S(1)}, u32[]{:S(2)}, u32[]{:S(2)}) collective-permute-start(bf16[128,256]{1,0:T(8,128)(2,1)S(1)} %get-tuple-element.44), channel_id=1, source_target_pairs={{0,48},{16,32},{32,16},{48,0},{1,49},{17,33},{33,17},{49,1},{2,50}... | collective-permute-start | bytes 196616 | tf_op jit(solution)/shard_map/ppermute | solution.py:399
  73.3 0.9 collective-permute-start.20
  74.2 4.3 %collective-permute-done.14 = bf16[16,8192]{1,0:T(8,128)(2,1)S(1)} collective-permute-done((bf16[16,8192]{1,0:T(8,128)(2,1)S(1)}, bf16[16,8192]{1,0:T(8,128)(2,1)S(1)}, u32[]{:S(2)}, u32[]{:S(2)}) %collective-permute-start.14) | collective-permute-done | bytes 262176 | tf_op jit(solution)/shard_map/ppermute | solution.py:399
  79.3 4.3 %collective-permute-done.21 = bf16[128,256]{1,0:T(8,128)(2,1)S(1)} collective-permute-done((bf16[128,256]{1,0:T(8,128)(2,1)S(1)}, bf16[128,256]{1,0:T(8,128)(2,1)S(1)}, u32[]{:S(2)}, u32[]{:S(2)}) %collective-permute-start.21) | collective-permute-done | bytes 65568 | tf_op jit(solution)/shard_map/ppermute | solution.py:399
  83.7 5.1 %collective-permute-done.20 = bf16[128,256]{1,0:T(8,128)(2,1)S(1)} collective-permute-done((bf16[128,256]{1,0:T(8,128)(2,1)S(1)}, bf16[128,256]{1,0:T(8,128)(2,1)S(1)}, u32[]{:S(2)}, u32[]{:S(2)}) %collective-permute-start.20) | collective-permute-done | bytes 65568 | tf_op jit(solution)/shard_map/ppermute | solution.py:399
  (37 shorter events, 5.4 us)
Async XLA Ops:
  2.1 8.6 %collective-permute-start.2 = (bf16[128,256]{1,0:T(8,128)(2,1)}, bf16[128,256]{1,0:T(8,128)(2,1)S(1)}, u32[]{:S(2)}, u32[]{:S(2)}) collective-permute-start(bf16[128,256]{1,0:T(8,128)(2,1)} %pair.1.kv_ref), channel_id=1, source_target_pairs={{0,48},{16,32},{32,16},{48,0},{1,49},{17,33},{33,17},{49,1},{2,50}... | collective-permute-start | bytes 196616 | tf_op jit(solution)/shard_map/ppermute | solution.py:399
  7.3 5.4 %collective-permute-start.1 = (bf16[128,256]{1,0:T(8,128)(2,1)}, bf16[128,256]{1,0:T(8,128)(2,1)S(1)}, u32[]{:S(2)}, u32[]{:S(2)}) collective-permute-start(bf16[128,256]{1,0:T(8,128)(2,1)} %pair.1.kv_ref), channel_id=1, source_target_pairs={{0,32},{16,48},{32,0},{48,16},{1,33},{17,49},{33,1},{49,17},{2,34}... | collective-permute-start | bytes 196616 | tf_op jit(solution)/shard_map/ppermute | solution.py:399
  7.3 5.4 %collective-permute-start = (bf16[128,256]{1,0:T(8,128)(2,1)}, bf16[128,256]{1,0:T(8,128)(2,1)S(1)}, u32[]{:S(2)}, u32[]{:S(2)}) collective-permute-start(bf16[128,256]{1,0:T(8,128)(2,1)} %pair.1.kv_ref), channel_id=1, source_target_pairs={{0,16},{16,0},{32,48},{48,32},{1,17},{17,1},{33,49},{49,33},{2,18}... | collective-permute-start | bytes 196616 | tf_op jit(solution)/shard_map/ppermute | solution.py:399
  7.7 0.9 copy-start
  8.6 0.9 %copy-start.1 = (bf16[128,512]{1,0:T(8,128)(2,1)S(1)}, bf16[128,512]{1,0:T(8,128)(2,1)}, u32[]{:S(2)}) copy-start(bf16[128,512]{1,0:T(8,128)(2,1)} %q_hbm.1) | copy-start | bytes 393220
  9.5 0.9 %copy-start.2 = (bf16[128,512]{1,0:T(8,128)(2,1)S(1)}, bf16[128,512]{1,0:T(8,128)(2,1)}, u32[]{:S(2)}) copy-start(bf16[128,512]{1,0:T(8,128)(2,1)} %do_hbm.1) | copy-start | bytes 393220
  12.8 7.7 %collective-permute-start.5 = (bf16[512,256]{1,0:T(8,128)(2,1)S(1)}, bf16[512,256]{1,0:T(8,128)(2,1)S(1)}, u32[]{:S(2)}, u32[]{:S(2)}) collective-permute-start(bf16[512,256]{1,0:T(8,128)(2,1)S(1)} %stack.1.rest_0_), channel_id=1, source_target_pairs={{192,0},{0,64},{64,128},{128,192},{193,1},{1,65},{65,129},{129,193... | collective-permute-start | bytes 786440 | tf_op jit(solution)/shard_map/ppermute | solution.py:394
  13.7 12.7 %collective-permute-start.4 = (bf16[512,256]{1,0:T(8,128)(2,1)S(1)}, bf16[512,256]{1,0:T(8,128)(2,1)S(1)}, u32[]{:S(2)}, u32[]{:S(2)}) collective-permute-start(bf16[512,256]{1,0:T(8,128)(2,1)S(1)} %stack.1.rest_0_), channel_id=1, source_target_pairs={{128,0},{192,64},{0,128},{64,192},{129,1},{193,65},{1,129},{65,193... | collective-permute-start | bytes 786440 | tf_op jit(solution)/shard_map/ppermute | solution.py:394
  16.2 12.9 %collective-permute-start.3 = (bf16[512,256]{1,0:T(8,128)(2,1)S(1)}, bf16[512,256]{1,0:T(8,128)(2,1)S(1)}, u32[]{:S(2)}, u32[]{:S(2)}) collective-permute-start(bf16[512,256]{1,0:T(8,128)(2,1)S(1)} %stack.1.rest_0_), channel_id=1, source_target_pairs={{64,0},{128,64},{192,128},{0,192},{65,1},{129,65},{193,129},{1,193... | collective-permute-start | bytes 786440 | tf_op jit(solution)/shard_map/ppermute | solution.py:394
  17.3 14.6 %collective-permute-start.6 = (bf16[512,256]{1,0:T(8,128)(2,1)S(1)}, bf16[512,256]{1,0:T(8,128)(2,1)S(1)}, u32[]{:S(2)}, u32[]{:S(2)}) collective-permute-start(bf16[512,256]{1,0:T(8,128)(2,1)S(1)} %stack.1.rest_0_), channel_id=1, source_target_pairs={{0,8},{8,0},{1,9},{9,1},{2,10},{10,2},{3,11},{11,3},{4,12},{12,4},... | collective-permute-start | bytes 786440 | tf_op jit(solution)/shard_map/ppermute | solution.py:399
  20.4 11.5 %collective-permute-start.9 = (bf16[512,256]{1,0:T(8,128)(2,1)S(1)}, bf16[512,256]{1,0:T(8,128)(2,1)S(1)}, u32[]{:S(2)}, u32[]{:S(2)}) collective-permute-start(bf16[512,256]{1,0:T(8,128)(2,1)S(1)} %collective-permute-done.5.rest_3_), channel_id=1, source_target_pairs={{0,8},{8,0},{1,9},{9,1},{2,10},{10,2},{3,11},{11,3},{4,12},{12,4},... | collective-permute-start | bytes 786440 | tf_op jit(solution)/shard_map/ppermute | solution.py:399
  26.4 5.5 %collective-permute-start.8 = (bf16[512,256]{1,0:T(8,128)(2,1)S(1)}, bf16[512,256]{1,0:T(8,128)(2,1)S(1)}, u32[]{:S(2)}, u32[]{:S(2)}) collective-permute-start(bf16[512,256]{1,0:T(8,128)(2,1)S(1)} %collective-permute-done.4.rest_2_), channel_id=1, source_target_pairs={{0,8},{8,0},{1,9},{9,1},{2,10},{10,2},{3,11},{11,3},{4,12},{12,4},... | collective-permute-start | bytes 786440 | tf_op jit(solution)/shard_map/ppermute | solution.py:399
  29.0 2.9 %collective-permute-start.7 = (bf16[512,256]{1,0:T(8,128)(2,1)S(1)}, bf16[512,256]{1,0:T(8,128)(2,1)S(1)}, u32[]{:S(2)}, u32[]{:S(2)}) collective-permute-start(bf16[512,256]{1,0:T(8,128)(2,1)S(1)} %collective-permute-done.3.rest_1_), channel_id=1, source_target_pairs={{0,8},{8,0},{1,9},{9,1},{2,10},{10,2},{3,11},{11,3},{4,12},{12,4},... | collective-permute-start | bytes 786440 | tf_op jit(solution)/shard_map/ppermute | solution.py:399
  29.1 0.7 copy-start.3
  39.7 9.0 %collective-permute-start.10 = (bf16[32,4096]{1,0:T(8,128)(2,1)S(1)}, bf16[32,4096]{1,0:T(8,128)(2,1)S(1)}, u32[]{:S(2)}, u32[]{:S(2)}) collective-permute-start(bf16[32,4096]{1,0:T(8,128)(2,1)S(1)} %get-tuple-element.28), channel_id=1, source_target_pairs={{0,1},{1,2},{2,3},{3,0},{4,5},{5,6},{6,7},{7,4},{8,9},{9,10},{10,1... | collective-permute-start | bytes 786440 | tf_op jit(solution)/shard_map/ppermute | solution.py:389
  41.2 7.4 %collective-permute-start.11 = (bf16[32,4096]{1,0:T(8,128)(2,1)S(1)}, bf16[32,4096]{1,0:T(8,128)(2,1)S(1)}, u32[]{:S(2)}, u32[]{:S(2)}) collective-permute-start(bf16[32,4096]{1,0:T(8,128)(2,1)S(1)} %get-tuple-element.29), channel_id=1, source_target_pairs={{0,3},{1,0},{2,1},{3,2},{4,7},{5,4},{6,5},{7,6},{8,11},{9,8},{10,9... | collective-permute-start | bytes 786440 | tf_op jit(solution)/shard_map/ppermute | solution.py:389
  45.8 9.6 %collective-permute-start.15 = (bf16[2048,256]{1,0:T(8,128)(2,1)S(1)}, bf16[2048,256]{1,0:T(8,128)(2,1)S(1)}, u32[]{:S(2)}, u32[]{:S(2)}) collective-permute-start(bf16[2048,256]{1,0:T(8,128)(2,1)S(1)} %get-tuple-element.39), channel_id=1, source_target_pairs={{0,8},{8,0},{1,9},{9,1},{2,10},{10,2},{3,11},{11,3},{4,12},{12,4},... | collective-permute-start | bytes 3145736 | tf_op jit(solution)/shard_map/ppermute | solution.py:399
  49.0 12.3 %collective-permute-start.13 = (bf16[32,8192]{1,0:T(8,128)(2,1)S(1)}, bf16[32,8192]{1,0:T(8,128)(2,1)S(1)}, u32[]{:S(2)}, u32[]{:S(2)}) collective-permute-start(bf16[32,8192]{1,0:T(8,128)(2,1)S(1)} %get-tuple-element.31), channel_id=1, source_target_pairs={{0,3},{1,0},{2,1},{3,2},{4,7},{5,4},{6,5},{7,6},{8,11},{9,8},{10,9... | collective-permute-start | bytes 1572872 | tf_op jit(solution)/shard_map/ppermute | solution.py:389
  51.6 12.8 %collective-permute-start.12 = (bf16[32,8192]{1,0:T(8,128)(2,1)S(1)}, bf16[32,8192]{1,0:T(8,128)(2,1)S(1)}, u32[]{:S(2)}, u32[]{:S(2)}) collective-permute-start(bf16[32,8192]{1,0:T(8,128)(2,1)S(1)} %get-tuple-element.30.rest_1_), channel_id=1, source_target_pairs={{0,1},{1,2},{2,3},{3,0},{4,5},{5,6},{6,7},{7,4},{8,9},{9,10},{10,1... | collective-permute-start | bytes 1572872 | tf_op jit(solution)/shard_map/ppermute | solution.py:389
  55.8 15.5 %collective-permute-start.16 = (bf16[512,256]{1,0:T(8,128)(2,1)S(1)}, bf16[512,256]{1,0:T(8,128)(2,1)S(1)}, u32[]{:S(2)}, u32[]{:S(2)}) collective-permute-start(bf16[512,256]{1,0:T(8,128)(2,1)S(1)} %get-tuple-element.40), channel_id=1, source_target_pairs={{0,64},{64,128},{128,192},{192,0},{1,65},{65,129},{129,193},{193,1... | collective-permute-start | bytes 786440 | tf_op jit(solution)/shard_map/ppermute | solution.py:389
  57.5 13.8 %collective-permute-start.18 = (bf16[512,256]{1,0:T(8,128)(2,1)S(1)}, bf16[512,256]{1,0:T(8,128)(2,1)S(1)}, u32[]{:S(2)}, u32[]{:S(2)}) collective-permute-start(bf16[512,256]{1,0:T(8,128)(2,1)S(1)} %get-tuple-element.41), channel_id=1, source_target_pairs={{0,192},{64,0},{128,64},{192,128},{1,193},{65,1},{129,65},{193,129... | collective-permute-start | bytes 786440 | tf_op jit(solution)/shard_map/ppermute | solution.py:389
  58.5 12.7 %collective-permute-start.17 = (bf16[512,256]{1,0:T(8,128)(2,1)S(1)}, bf16[512,256]{1,0:T(8,128)(2,1)S(1)}, u32[]{:S(2)}, u32[]{:S(2)}) collective-permute-start(bf16[512,256]{1,0:T(8,128)(2,1)S(1)} %get-tuple-element.42), channel_id=1, source_target_pairs={{0,128},{64,192},{128,0},{192,64},{1,129},{65,193},{129,1},{193,65... | collective-permute-start | bytes 786440 | tf_op jit(solution)/shard_map/ppermute | solution.py:389
  64.7 13.8 %collective-permute-start.14 = (bf16[16,8192]{1,0:T(8,128)(2,1)S(1)}, bf16[16,8192]{1,0:T(8,128)(2,1)S(1)}, u32[]{:S(2)}, u32[]{:S(2)}) collective-permute-start(bf16[16,8192]{1,0:T(8,128)(2,1)S(1)} %slice.49), channel_id=1, source_target_pairs={{0,4},{4,0},{1,5},{5,1},{2,6},{6,2},{3,7},{7,3},{8,12},{12,8},{9,1... | collective-permute-start | bytes 786440 | tf_op jit(solution)/shard_map/ppermute | solution.py:399
  71.4 7.9 %collective-permute-start.19 = (bf16[128,256]{1,0:T(8,128)(2,1)S(1)}, bf16[128,256]{1,0:T(8,128)(2,1)S(1)}, u32[]{:S(2)}, u32[]{:S(2)}) collective-permute-start(bf16[128,256]{1,0:T(8,128)(2,1)S(1)} %get-tuple-element.43), channel_id=1, source_target_pairs={{0,16},{16,0},{32,48},{48,32},{1,17},{17,1},{33,49},{49,33},{2,18}... | collective-permute-start | bytes 196616 | tf_op jit(solution)/shard_map/ppermute | solution.py:399
  71.5 12.1 %collective-permute-start.21 = (bf16[128,256]{1,0:T(8,128)(2,1)S(1)}, bf16[128,256]{1,0:T(8,128)(2,1)S(1)}, u32[]{:S(2)}, u32[]{:S(2)}) collective-permute-start(bf16[128,256]{1,0:T(8,128)(2,1)S(1)} %get-tuple-element.44), channel_id=1, source_target_pairs={{0,48},{16,32},{32,16},{48,0},{1,49},{17,33},{33,17},{49,1},{2,50}... | collective-permute-start | bytes 196616 | tf_op jit(solution)/shard_map/ppermute | solution.py:399
  73.3 15.4 %collective-permute-start.20 = (bf16[128,256]{1,0:T(8,128)(2,1)S(1)}, bf16[128,256]{1,0:T(8,128)(2,1)S(1)}, u32[]{:S(2)}, u32[]{:S(2)}) collective-permute-start(bf16[128,256]{1,0:T(8,128)(2,1)S(1)} %get-tuple-element.45), channel_id=1, source_target_pairs={{0,32},{16,48},{32,0},{48,16},{1,33},{17,49},{33,1},{49,17},{2,34}... | collective-permute-start | bytes 196616 | tf_op jit(solution)/shard_map/ppermute | solution.py:399

commit v5 on v4

--- a/solution.py
+++ b/solution.py
@@ -19,6 +19,7 @@
 TP = ("zh", "y")
 MIX_SPAN = 1024
 CHUNK = 4
+FWD_MIB = 32
 BWD_FLOPS = 2 * 10**10
 SMEM = pl.BlockSpec(memory_space=pltpu.SMEM)
 VMEM = pl.BlockSpec(memory_space=pltpu.VMEM)
@@ -65,7 +66,8 @@
         copy.wait()
 
 
-def plan_kernel(ids_ref, plan_ref, slot_ref):
+def stage_kernel(ids_ref, piece_ref, plan_ref, same_ref, slot_ref):
+    same_ref[...] = piece_ref[...]
     slots = ids_ref.shape[0]
     core = lax.axis_index("core")
     mine = place_of(0, 0, 0)
@@ -113,27 +115,16 @@
                 for group in range(CHUNK)]
 
 
-def fwd_kernel(stretch, plan_ref, qs_ref, ds_ref, *rest):
-    pieces, rest = rest[:NC * NX], rest[NC * NX:]
-    (w_hbm, own_ref, front_ref, back_ref, far_a, far_b, p_ref, kv_ref, delta_ref, inv_ref,
-     w_ref, s_buf, top_ref, sum_ref, acc_ref, diff_ref, attn_ref, turned_ref, w_sem) = rest
+def attend(stretch, side, plan_ref, qs_ref, pieces, p_ref, kv_ref, top_ref, sum_ref, acc_ref, s_buf, diff_ref):
     steps, span, cols = p_ref.shape
-    total = kv_ref.shape[0]
-    plan = Plan(plan_ref, total // stretch, stretch)
-    weight_copies = []
-    for index in range(w_ref.shape[1] // MIX_SPAN):
-        at = slice(index * MIX_SPAN, (index + 1) * MIX_SPAN)
-        weight_copies.append(pltpu.make_async_copy(w_hbm.at[:, at], w_ref.at[:, at], w_sem.at[index]))
-    for copy in weight_copies:
-        copy.start()
-    for c_step in range(NC):
-        for x_step in range(NX):
-            piece = pieces[c_step * NX + x_step]
-            for z_step in range(NZ):
-                slot = place_of(c_step, x_step, z_step)
-                for half in range(2):
-                    at = (z_step * 2 + half) * stretch
-                    kv_ref[pl.ds(plan.row(slot + half), stretch), :] = piece[at:at + stretch, :]
+    rows = kv_ref.shape[0]
+    plan = Plan(plan_ref, 2 * rows // stretch, stretch)
+    for x_step in range(NX):
+        for z_step in range(NZ):
+            slot = place_of(side, x_step, z_step)
+            for half in range(2):
+                at = (z_step * 2 + half) * stretch
+                kv_ref[pl.ds(plan.row(slot + half) - side * rows, stretch), :] = pieces[x_step][at:at + stretch, :]
     k_at = lax.broadcasted_iota(jnp.int32, (stretch, cols), 0)
     q_at = lax.broadcasted_iota(jnp.int32, (stretch, cols), 1) % stretch
     diff_ref[...] = k_at - q_at
@@ -141,34 +132,49 @@
     sum_ref[...] = jnp.zeros_like(sum_ref)
     acc_ref[...] = jnp.zeros_like(acc_ref)
 
-    for step in range(steps):
-        side, index = divmod(step, steps // 2)
+    for index in range(steps):
         part, row, chunk, valid = plan.step(side, index)
-        scores = dot(kv_ref[pl.ds(side * (total // 2) + row, span), :HD], qs_ref[part], NT)
-        limits = plan.limits(side, part, chunk, valid)
+        scores = dot(kv_ref[pl.ds(row, span), :HD], qs_ref[part], NT)
         top = top_ref[part]
-        for group, limit in enumerate(limits):
-            rows = slice(group * stretch, (group + 1) * stretch)
-            block = jnp.where(diff_ref[...] <= limit, scores[rows], NEG)
-            s_buf[step, rows] = block
+        for group, limit in enumerate(plan.limits(side, part, chunk, valid)):
+            at = slice(group * stretch, (group + 1) * stretch)
+            block = jnp.where(diff_ref[...] <= limit, scores[at], NEG)
+            s_buf[index, at] = block
             top = jnp.maximum(top, jnp.max(block.reshape(stretch // 8, 8, cols), axis=0))
         top_ref[part] = top
     for part in range(2):
         top_ref[part] = jnp.broadcast_to(jnp.max(top_ref[part], axis=0, keepdims=True), (8, cols))
 
-    for step in range(steps):
-        side, index = divmod(step, steps // 2)
+    for index in range(steps):
         part, row, chunk, valid = plan.step(side, index)
-        shifted = jnp.exp((s_buf[step].reshape(span // 8, 8, cols) - top_ref[part][None]) * SCALE)
+        shifted = jnp.exp((s_buf[index].reshape(span // 8, 8, cols) - top_ref[part][None]) * SCALE)
         sum_ref[part] += jnp.sum(shifted, axis=0)
         weights = shifted.reshape(span, cols).astype(jnp.bfloat16)
-        p_ref[step] = weights
-        acc_ref[part] += dot(kv_ref[pl.ds(side * (total // 2) + row, span), HD:], weights, TN)
-
+        p_ref[index] = weights
+        acc_ref[part] += dot(kv_ref[pl.ds(row, span), HD:], weights, TN)
+
+
+def near_kernel(stretch, plan_ref, qs_ref, *rest):
+    attend(stretch, 0, plan_ref, qs_ref, rest[:NX], *rest[NX:])
+
+
+def far_kernel(stretch, plan_ref, qs_ref, *rest):
+    pieces, rest = rest[:NX], rest[NX:]
+    (ds_ref, w_ref, near_top, near_sum, near_acc,
+     own_ref, front_ref, back_ref, far_a, far_b, p_ref, kv_ref, delta_ref, near_inv, far_inv,
+     top_ref, sum_ref, acc_ref, s_buf, diff_ref, attn_ref, turned_ref) = rest
+    attend(stretch, 1, plan_ref, qs_ref, pieces, p_ref, kv_ref, top_ref, sum_ref, acc_ref, s_buf, diff_ref)
+    cols = qs_ref.shape[1]
     for part in range(2):
-        inverse = 1.0 / jnp.sum(sum_ref[part], axis=0, keepdims=True)
-        inv_ref[part] = jnp.broadcast_to(inverse, (8, cols))
-        out = (acc_ref[part] * inverse).T.astype(jnp.bfloat16)
+        top = jnp.maximum(near_top[part][:1], top_ref[part][:1])
+        near = jnp.exp((near_top[part][:1] - top) * SCALE)
+        far = jnp.exp((top_ref[part][:1] - top) * SCALE)
+        total = (jnp.sum(near_sum[part], axis=0, keepdims=True) * near
+                 + jnp.sum(sum_ref[part], axis=0, keepdims=True) * far)
+        near, far = near / total, far / total
+        near_inv[part] = jnp.broadcast_to(near, (8, cols))
+        far_inv[part] = jnp.broadcast_to(far, (8, cols))
+        out = (near_acc[part] * near + acc_ref[part] * far).T.astype(jnp.bfloat16)
         prod = ds_ref[part].astype(jnp.float32) * out.astype(jnp.float32)
         delta_ref[part] = jnp.broadcast_to(jnp.sum(prod.T, axis=0, keepdims=True), (8, cols))
         for head in range(QPG):
@@ -182,14 +188,13 @@
             to = (y_step * NH + h_step) * rows
             turned_ref[to:to + rows, :] = attn_ref[pl.ds(pl.multiple_of(block * rows, rows), rows), :]
     piece = NH * rows
+    half = w_ref.shape[1] // 2
     for index in range(w_ref.shape[1] // MIX_SPAN):
         at = slice(index * MIX_SPAN, (index + 1) * MIX_SPAN)
-        weight_copies[index].wait()
         mixed = dot(turned_ref[...], w_ref[:, at], NN).astype(jnp.bfloat16)
         own_ref[:, at] = mixed[:piece]
         front_ref[:, at] = mixed[piece:2 * piece]
         back_ref[:, at] = mixed[3 * piece:]
-        half = w_ref.shape[1] // 2
         if at.start < half:
             far_a[:, at] = mixed[2 * piece:3 * piece]
         else:
@@ -198,10 +203,10 @@
 
 def bwd_kernel(stretch, side, plan_ref, p_ref, kv_ref, qs_ref, ds_ref, delta_ref, inv_ref, *rest):
     steps, span, cols = p_ref.shape
-    total = kv_ref.shape[0]
+    total = 2 * kv_ref.shape[0]
     plan = Plan(plan_ref, total // stretch, stretch)
     if side == 0:
-        acc_in, token_ref, dq_ref, out_ref, acc_ref, dk_ref, dv_ref, dn_ref = rest
+        acc_in, dq_ref, out_ref, acc_ref, dk_ref, dv_ref, dn_ref = rest
         acc_ref[...] = acc_in[...]
     else:
         acc_ref, out_ref, dk_ref, dv_ref, dn_ref = rest
@@ -212,17 +217,16 @@
         column = jnp.broadcast_to(inv_ref[part][:1], (HD, cols)).T
         dn_ref[part] = (ds_ref[part].astype(jnp.float32) * column).astype(jnp.bfloat16)
 
-    for index in range(steps // 2):
+    for index in range(steps):
         part, row, chunk, valid = plan.step(side, index)
         here = pl.ds(row, span)
-        there = pl.ds(side * (total // 2) + row, span)
-        weights = p_ref[side * (steps // 2) + index]
-        grad_probs = dot(kv_ref[there, HD:], ds_ref[part], NT)
+        weights = p_ref[index]
+        grad_probs = dot(kv_ref[here, HD:], ds_ref[part], NT)
         moved = (grad_probs.reshape(span // 8, 8, cols) - delta_ref[part][None]) * inv_ref[part][None]
         grad_scores = (weights.astype(jnp.float32) * moved.reshape(span, cols)).astype(jnp.bfloat16)
         dv_ref[here, :] += dot(weights, dn_ref[part], NN)
         dk_ref[here, :] += dot(grad_scores, qs_ref[part], NN)
-        acc_ref[part] += dot(kv_ref[there, :HD], grad_scores, TN)
+        acc_ref[part] += dot(kv_ref[here, :HD], grad_scores, TN)
 
     to = 0
     for x_step in range(NX):
@@ -266,17 +270,18 @@
     )(queries, grad_heads, kv)
 
 
-def plan_of(ids):
+def stage(ids, piece):
     slots = ids.shape[0]
-    return pl.pallas_call(
-        plan_kernel,
-        out_shape=jax.ShapeDtypeStruct((2 * slots + 8,), jnp.int32),
-        in_specs=[SMEM],
-        out_specs=SMEM,
+    shape = jax.ShapeDtypeStruct
+    return pl.pallas_call(
+        stage_kernel,
+        out_shape=(shape((2 * slots + 8,), jnp.int32), shape(piece.shape, piece.dtype)),
+        in_specs=[SMEM, VMEM],
+        out_specs=[SMEM, VMEM],
         scratch_shapes=[pltpu.SMEM((slots,), jnp.int32)],
         compiler_params=pltpu.CompilerParams(vmem_limit_bytes=4 * MIB),
-        name="plan",
-    )(ids)
+        name="stage",
+    )(ids, piece)
 
 
 def relay_kernel(front_in, back_in, front_add, back_add, front_ref, back_ref):
@@ -322,45 +327,40 @@
     )(token, *parts)
 
 
-def forward(plan, qs, ds, pieces, out_weight):
+def forward(side, plan, qs, pieces, *more):
     cols = qs.shape[1]
     stretch = cols // QPG
     tokens = 2 * stretch
     total = sum(piece.shape[0] for piece in pieces)
     span = CHUNK * stretch
-    steps = total // span + 2
-    depth, width = out_weight.shape
+    steps = total // span + 1
     b16, f32 = jnp.bfloat16, jnp.float32
     shape = jax.ShapeDtypeStruct
-    return pl.pallas_call(
-        functools.partial(fwd_kernel, stretch),
-        out_shape=(shape((tokens // NY, width), b16),) * 3 + (shape((tokens // NY, width // 2), b16),) * 2 + (
-            shape((steps, span, cols), b16),
-            shape((total, 2 * HD), b16),
-            shape((2, 8, cols), f32),
-            shape((2, 8, cols), f32),
-        ),
-        in_specs=[SMEM] + [VMEM] * (2 + len(pieces)) + [HBM],
-        out_specs=[VMEM] * 9,
-        scratch_shapes=[
-            pltpu.VMEM((depth, width), b16),
-            pltpu.VMEM((steps, span, cols), f32),
-            pltpu.VMEM((2, 8, cols), f32),
-            pltpu.VMEM((2, 8, cols), f32),
-            pltpu.VMEM((2, HD, cols), f32),
-            pltpu.VMEM((stretch, cols), jnp.int32),
-            pltpu.VMEM((tokens, QPG * HD), b16),
-            pltpu.VMEM((tokens, QPG * HD), b16),
-            pltpu.SemaphoreType.DMA((width // MIX_SPAN,)),
-        ],
-        compiler_params=pltpu.CompilerParams(vmem_limit_bytes=40 * MIB),
-        cost_estimate=pl.CostEstimate(flops=4 * 10**9, bytes_accessed=12 * 10**6, transcendentals=10**6),
-        name="attention_forward",
-    )(plan, qs, ds, *pieces, out_weight)
+    weights, keys = shape((steps, span, cols), b16), shape((total, 2 * HD), b16)
+    row, sums = (2, 8, cols), (2, HD, cols)
+    scratch = [pltpu.VMEM((steps, span, cols), f32), pltpu.VMEM((stretch, cols), jnp.int32)]
+    if side:
+        width = more[1].shape[1]
+        outs = (shape((tokens // NY, width), b16),) * 3 + (shape((tokens // NY, width // 2), b16),) * 2 + (
+            weights, keys, shape(row, f32), shape(row, f32), shape(row, f32))
+        scratch = [pltpu.VMEM(row, f32), pltpu.VMEM(row, f32), pltpu.VMEM(sums, f32)] + scratch + [
+            pltpu.VMEM((tokens, QPG * HD), b16), pltpu.VMEM((tokens, QPG * HD), b16)]
+    else:
+        outs = (weights, keys, shape(row, f32), shape(row, f32), shape(sums, f32))
+    return pl.pallas_call(
+        functools.partial(far_kernel if side else near_kernel, stretch),
+        out_shape=outs,
+        in_specs=[SMEM] + [VMEM] * (1 + len(pieces) + len(more)),
+        out_specs=[VMEM] * len(outs),
+        scratch_shapes=scratch,
+        compiler_params=pltpu.CompilerParams(vmem_limit_bytes=FWD_MIB * MIB),
+        cost_estimate=pl.CostEstimate(flops=3 * 10**9, bytes_accessed=8 * 10**6, transcendentals=10**6),
+        name="attention_forward_%d" % side,
+    )(plan, qs, *pieces, *more)
 
 
 def backward(side, plan, probs, kv, qs, ds, delta, inverse, *partial):
-    total = kv.shape[0]
+    total = 2 * kv.shape[0]
     steps, span, cols = probs.shape
     stretch = cols // QPG
     b16, f32 = jnp.bfloat16, jnp.float32
@@ -375,7 +375,7 @@
     return pl.pallas_call(
         functools.partial(bwd_kernel, stretch, side),
         out_shape=(shape(sums, f32) if side else shape((2 * stretch, QPG * HD), b16), terms),
-        in_specs=[SMEM] + [VMEM] * 6 + [VMEM, ANY][:len(partial)],
+        in_specs=[SMEM] + [VMEM] * (6 + len(partial)),
         out_specs=[VMEM] * 2,
         scratch_shapes=scratch if side else [pltpu.VMEM(sums, f32)] + scratch,
         compiler_params=pltpu.CompilerParams(vmem_limit_bytes=32 * MIB),
@@ -409,19 +409,20 @@
 def on_device(queries, keys, values, stretch_of, out_weight, grad_heads):
     kv = pair(keys, values)
     qs, ds, same = by_heads(queries, grad_heads, kv)
-    plan = plan_of(stretch_of)
     kv = stack(qs, same, *[across(kv, "zl", step) for step in range(1, NZ)])
-    pieces = [kv] + [behind(kv, "x", step) for step in range(1, NX)]
-    pieces = pieces + [across(piece, "core", 1) for piece in pieces]
-    own, front, back, far_a, far_b, probs, kv, delta, inverse = forward(plan, qs, ds, pieces, out_weight)
-    saved = (plan, probs, kv, qs, ds, delta, inverse)
+    plan, same = stage(stretch_of, kv)
+    near = [kv] + [behind(kv, "x", step) for step in range(1, NX)]
+    far = [across(piece, "core", 1) for piece in [same] + near[1:]]
+    near_probs, near_kv, *partial = forward(0, plan, qs, near)
+    own, front, back, far_a, far_b, far_probs, far_kv, delta, near_inv, far_inv = forward(
+        1, plan, qs, far, ds, out_weight, *partial)
     far_a, far_b = ahead(far_a, "y", 1), ahead(far_b, "y", NY - 1)
-    partial, give = backward(1, *saved)
+    partial, give = backward(1, plan, far_probs, far_kv, qs, ds, delta, far_inv)
     front, back = relay(front, back, far_a, far_b)
     mixed = total_of([own, ahead(front, "y", 1), ahead(back, "y", NY - 1)])
     rows = mixed.shape[0] // NH
     mixed = total_of([mixed[:rows], across(mixed[rows:], "zh", 1)])
-    q_grad, keep = backward(0, *saved, partial, front)
+    q_grad, keep = backward(0, plan, near_probs, near_kv, qs, ds, delta, near_inv, partial)
     term = total_of([keep, across(give, "core", 1)])
     part = term.shape[0] // NX
     term = total_of([term[:part]] + [

time: 89.8 us -> 87.7 us (0.977)
  starting transfers between devices: 39.9 us -> 36.7 us
  Pallas kernels: 18.8 us -> 17.1 us
  waiting for transfers between devices: 24.5 us -> 26.2 us
  local copies, waits for them, and re-layouts: 4.05 us -> 5.17 us
    ppermute x12, starting transfers between devices: 25.1 us -> 22.8 us  [across(): return lax.ppermute(block, axis, [(i, i ^ step) for i in range(count)])]
    ppermute x7, waiting for transfers between devices: 6.05 us -> 8.26 us  [ahead(): lax.ppermute(block, axis, [(i, (i + step) % count) for i in range(count)])]
    pallas_call x2 -> x3, Pallas kernels: 9.93 us -> 8.19 us  [the longest x2 6.01 us: forward(): pl.pallas_call(functools.partial(far_kernel if side else near_kernel, str...]
    unnamed x8 -> x10, local copies, waits for them, and re-layouts: 3.33 us -> 4.46 us
  transfers between devices with their start and end apart: 22 -> 22, of which waited for: 10 -> 6; matrix products, arithmetic and copies ran while one was open for 2% -> 2% of each run, Pallas kernels for 11% -> 14%
where the time goes in v5:
time: 87.7 us; the launch traced here: 87.4 us
  starting transfers between devices  36.7 us (42%)
  waiting for transfers between devices  26.2 us (30%)
  Pallas kernels  17.1 us (19%)
  local copies, waits for them, and re-layouts  5.17 us (6%)
  other arithmetic  1.45 us (2%)
    ppermute x12, starting transfers between devices, across(): return lax.ppermute(block, axis, [(i, i ^ step) for i in range(count)])  22.8 us
    ppermute x12, waiting for transfers between devices, across(): return lax.ppermute(block, axis, [(i, i ^ step) for i in range(count)])  15.9 us
    ppermute x7, starting transfers between devices, ahead(): lax.ppermute(block, axis, [(i, (i + step) % count) for i in range(count)])  9.29 us
    ppermute x7, waiting for transfers between devices, ahead(): lax.ppermute(block, axis, [(i, (i + step) % count) for i in range(count)])  8.26 us
    pallas_call x2, Pallas kernels, backward(): pl.pallas_call(functools.partial(bwd_kernel, stretch, side), out_shape=(s...  6.9 us
    pallas_call x2, Pallas kernels, forward(): pl.pallas_call(functools.partial(far_kernel if side else near_kernel, str...  6.01 us
    ppermute x3, starting transfers between devices, behind(): lax.ppermute(block, axis, [((i + step) % count, i) for i in range(count)])  4.57 us
    unnamed x10, local copies, waits for them, and re-layouts  4.46 us
  transfers between devices with their start and end apart: 22, of which 6 were waited for; matrix products, arithmetic and copies ran while one was open for 2% of the time, Pallas kernels for 14%

profile of v5, /device:TPU:1, one launch (start us, length us, event | category | flops | bytes accessed | tf_op | source)
XLA Modules:
  0.0 87.4 jit_solution(5630409921185556506)
XLA Ops:
  0.6 1.4 %pair.1.kv_ref = bf16[128,256]{1,0:T(8,128)(2,1)} custom-call(bf16[128,128]{1,0:T(8,128)(2,1)} %k_hbm.1, bf16[128,128]{1,0:T(8,128)(2,1)} %v_hbm.1), custom_call_target="tpu_custom_call" | custom-call | tf_op jit(solution)/shard_map/pair/pallas_call | solution.py:249
  2.1 5.3 %collective-permute-start.2 = (bf16[128,256]{1,0:T(8,128)(2,1)}, bf16[128,256]{1,0:T(8,128)(2,1)S(1)}, u32[]{:S(2)}, u32[]{:S(2)}) collective-permute-start(bf16[128,256]{1,0:T(8,128)(2,1)} %pair.1.kv_ref), channel_id=1, source_target_pairs={{0,48},{16,32},{32,16},{48,0},{1,49},{17,33},{33,17},{49,1},{2,50}... | collective-permute-start | bytes 196616 | tf_op jit(solution)/shard_map/ppermute | solution.py:399
  7.7 0.9 copy-done
  8.6 0.9 %copy-done.1 = bf16[128,512]{1,0:T(8,128)(2,1)S(1)} copy-done((bf16[128,512]{1,0:T(8,128)(2,1)S(1)}, bf16[128,512]{1,0:T(8,128)(2,1)}, u32[]{:S(2)}) %copy-start.1) | copy-done | bytes 131096
  9.5 0.9 %copy-done.2 = bf16[128,512]{1,0:T(8,128)(2,1)S(1)} copy-done((bf16[128,512]{1,0:T(8,128)(2,1)S(1)}, bf16[128,512]{1,0:T(8,128)(2,1)}, u32[]{:S(2)}) %copy-start.2) | copy-done | bytes 131096
  10.6 2.1 %collective-permute-done.1.refs_2_ = bf16[128,256]{1,0:T(8,128)(2,1)S(1)} collective-permute-done((bf16[128,256]{1,0:T(8,128)(2,1)}, bf16[128,256]{1,0:T(8,128)(2,1)S(1)}, u32[]{:S(2)}, u32[]{:S(2)}) %collective-permute-start.1) | collective-permute-done | bytes 65568 | tf_op jit(solution)/shard_map/ppermute | solution.py:399
  12.8 1.0 %collective-permute-start.8 = (bf16[512,256]{1,0:T(8,128)(2,1)S(1)}, bf16[512,256]{1,0:T(8,128)(2,1)S(1)}, u32[]{:S(2)}, u32[]{:S(2)}) collective-permute-start(bf16[512,256]{1,0:T(8,128)(2,1)S(1)} %stack.1.piece_ref.rest_0_), channel_id=1, source_target_pairs={{192,0},{0,64},{64,128},{128,192},{193,1},{1,65},{65,129},{129,193... | collective-permute-start | bytes 786440 | tf_op jit(solution)/shard_map/ppermute | solution.py:394
  13.7 2.5 %collective-permute-start.6 = (bf16[512,256]{1,0:T(8,128)(2,1)S(1)}, bf16[512,256]{1,0:T(8,128)(2,1)S(1)}, u32[]{:S(2)}, u32[]{:S(2)}) collective-permute-start(bf16[512,256]{1,0:T(8,128)(2,1)S(1)} %stack.1.piece_ref.rest_0_), channel_id=1, source_target_pairs={{128,0},{192,64},{0,128},{64,192},{129,1},{193,65},{1,129},{65,193... | collective-permute-start | bytes 786440 | tf_op jit(solution)/shard_map/ppermute | solution.py:394
  16.2 1.2 %collective-permute-start.4 = (bf16[512,256]{1,0:T(8,128)(2,1)S(1)}, bf16[512,256]{1,0:T(8,128)(2,1)S(1)}, u32[]{:S(2)}, u32[]{:S(2)}) collective-permute-start(bf16[512,256]{1,0:T(8,128)(2,1)S(1)} %stack.1.piece_ref.rest_0_), channel_id=1, source_target_pairs={{64,0},{128,64},{192,128},{0,192},{65,1},{129,65},{193,129},{1,193... | collective-permute-start | bytes 786440 | tf_op jit(solution)/shard_map/ppermute | solution.py:394
  18.0 2.2 %stage.1 = (s32[136]{0:T(256)S(1)}, bf16[512,256]{1,0:T(8,128)(2,1)S(1)}) custom-call(s32[64]{0:T(128)S(1)} %copy-done.3, bf16[512,256]{1,0:T(8,128)(2,1)S(1)} %stack.1.piece_ref.rest_0_), custom_call_target="tpu_custom_call" | custom-call | tf_op jit(solution)/shard_map/stage/pallas_call | solution.py:276
  20.2 2.7 %collective-permute-start.3 = (bf16[512,256]{1,0:T(8,128)(2,1)S(1)}, bf16[512,256]{1,0:T(8,128)(2,1)S(1)}, u32[]{:S(2)}, u32[]{:S(2)}) collective-permute-start(bf16[512,256]{1,0:T(8,128)(2,1)S(1)} %get-tuple-element.33), channel_id=1, source_target_pairs={{0,8},{8,0},{1,9},{9,1},{2,10},{10,2},{3,11},{11,3},{4,12},{12,4},... | collective-permute-start | bytes 786440 | tf_op jit(solution)/shard_map/ppermute | solution.py:399
  22.8 1.5 %collective-permute-start.9 = (bf16[512,256]{1,0:T(8,128)(2,1)S(1)}, bf16[512,256]{1,0:T(8,128)(2,1)S(1)}, u32[]{:S(2)}, u32[]{:S(2)}) collective-permute-start(bf16[512,256]{1,0:T(8,128)(2,1)S(1)} %collective-permute-done.8.rest_3_), channel_id=1, source_target_pairs={{0,8},{8,0},{1,9},{9,1},{2,10},{10,2},{3,11},{11,3},{4,12},{12,4},... | collective-permute-start | bytes 786440 | tf_op jit(solution)/shard_map/ppermute | solution.py:399
  24.4 2.0 %collective-permute-done.6.rest_2_ = bf16[512,256]{1,0:T(8,128)(2,1)S(1)} collective-permute-done((bf16[512,256]{1,0:T(8,128)(2,1)S(1)}, bf16[512,256]{1,0:T(8,128)(2,1)S(1)}, u32[]{:S(2)}, u32[]{:S(2)}) %collective-permute-start.6) | collective-permute-done | bytes 262176 | tf_op jit(solution)/shard_map/ppermute | solution.py:394
  26.4 2.7 %collective-permute-start.7 = (bf16[512,256]{1,0:T(8,128)(2,1)S(1)}, bf16[512,256]{1,0:T(8,128)(2,1)S(1)}, u32[]{:S(2)}, u32[]{:S(2)}) collective-permute-start(bf16[512,256]{1,0:T(8,128)(2,1)S(1)} %collective-permute-done.6.rest_2_), channel_id=1, source_target_pairs={{0,8},{8,0},{1,9},{9,1},{2,10},{10,2},{3,11},{11,3},{4,12},{12,4},... | collective-permute-start | bytes 786440 | tf_op jit(solution)/shard_map/ppermute | solution.py:399
  29.1 2.2 %attention_forward_0.1 = (bf16[9,256,256]{2,1,0:T(8,128)(2,1)S(1)}, bf16[2048,256]{1,0:T(8,128)(2,1)S(1)}, f32[2,8,256]{2,1,0:T(8,128)S(1)}, f32[2,8,256]{2,1,0:T(8,128)S(1)}, f32[2,128,256]{2,1,0:T(8,128)S(1)}) custom-call(s32[136]{0:T(256)S(1)} %get-tuple-element.32.plan_ref, bf16[2,256,128]{2,1,0:T(8,128)(2,1)S(1)} %get-tuple-element.30.token_ref.qs_ref, ...), custom_call_target="tpu_custom_call" | custom-call | flops 3000000000 | bytes 8000000 | tf_op jit(solution)/shard_map/attention_forward_0/pallas_call | solution.py:350
  31.3 1.1 %copy-done.4 = bf16[512,8192]{1,0:T(8,128)(2,1)S(1)} copy-done((bf16[512,8192]{1,0:T(8,128)(2,1)S(1)}, bf16[512,8192]{1,0:T(8,128)(2,1)}, u32[]{:S(2)}) %copy-start.4) | copy-done | bytes 8388632
  32.4 3.8 %attention_forward_1.1 = (bf16[32,8192]{1,0:T(8,128)(2,1)S(1)}, bf16[32,8192]{1,0:T(8,128)(2,1)S(1)}, bf16[32,8192]{1,0:T(8,128)(2,1)S(1)}, bf16[32,4096]{1,0:T(...) custom-call(s32[136]{0:T(256)S(1)} %get-tuple-element.32.plan_ref, ...), custom_call_target="tpu_custom_call" | custom-call | flops 3000000000 | bytes 8000000 | tf_op jit(solution)/shard_map/attention_forward_1/pallas_call | solution.py:350
  36.2 1.6 %collective-permute-start.10 = (bf16[32,4096]{1,0:T(8,128)(2,1)S(1)}, bf16[32,4096]{1,0:T(8,128)(2,1)S(1)}, u32[]{:S(2)}, u32[]{:S(2)}) collective-permute-start(bf16[32,4096]{1,0:T(8,128)(2,1)S(1)} %get-tuple-element.41), channel_id=1, source_target_pairs={{0,1},{1,2},{2,3},{3,0},{4,5},{5,6},{6,7},{7,4},{8,9},{9,10},{10,1... | collective-permute-start | bytes 786440 | tf_op jit(solution)/shard_map/ppermute | solution.py:389
  37.8 1.5 %collective-permute-start.11 = (bf16[32,4096]{1,0:T(8,128)(2,1)S(1)}, bf16[32,4096]{1,0:T(8,128)(2,1)S(1)}, u32[]{:S(2)}, u32[]{:S(2)}) collective-permute-start(bf16[32,4096]{1,0:T(8,128)(2,1)S(1)} %get-tuple-element.42), channel_id=1, source_target_pairs={{0,3},{1,0},{2,1},{3,2},{4,7},{5,4},{6,5},{7,6},{8,11},{9,8},{10,9... | collective-permute-start | bytes 786440 | tf_op jit(solution)/shard_map/ppermute | solution.py:389
  39.3 3.1 %attention_backward_1.1 = (f32[2,128,256]{2,1,0:T(8,128)S(1)}, bf16[2048,256]{1,0:T(8,128)(2,1)S(1)}) custom-call(s32[136]{0:T(256)S(1)} %get-tuple-element.32.plan_ref, bf16[9,256,256]{2,1,0:T(8,128)(2,1)S(1)} %get-tuple-element.49.p_ref, bf16[2048,256]{1,0:T(8,128)(2,1)S(1)} %get-tuple-element.50.kv_ref, ...), custom_call_target="tpu_custom_call" | custom-call | flops 20000000000 | bytes 8000000 | tf_op jit(solution)/shard_map/attention_backward_1/pallas_call | solution.py:375
  42.4 1.0 %collective-permute-start.15 = (bf16[2048,256]{1,0:T(8,128)(2,1)S(1)}, bf16[2048,256]{1,0:T(8,128)(2,1)S(1)}, u32[]{:S(2)}, u32[]{:S(2)}) collective-permute-start(bf16[2048,256]{1,0:T(8,128)(2,1)S(1)} %get-tuple-element.55), channel_id=1, source_target_pairs={{0,8},{8,0},{1,9},{9,1},{2,10},{10,2},{3,11},{11,3},{4,12},{12,4},... | collective-permute-start | bytes 3145736 | tf_op jit(solution)/shard_map/ppermute | solution.py:399
  43.4 3.8 %attention_backward_0.1 = (bf16[128,512]{1,0:T(8,128)(2,1)}, bf16[2048,256]{1,0:T(8,128)(2,1)S(1)}) custom-call(s32[136]{0:T(256)S(1)} %get-tuple-element.32.plan_ref, bf16[9,256,256]{2,1,0:T(8,128)(2,1)S(1)} %get-tuple-element.45.p_ref, bf16[2048,256]{1,0:T(8,128)(2,1)S(1)} %get-tuple-element.46.kv_ref, ...), custom_call_target="tpu_custom_call" | custom-call | flops 20000000000 | bytes 8000000 | tf_op jit(solution)/shard_map/attention_backward_0/pallas_call | solution.py:375
  47.8 2.6 %collective-permute-start.13 = (bf16[32,8192]{1,0:T(8,128)(2,1)S(1)}, bf16[32,8192]{1,0:T(8,128)(2,1)S(1)}, u32[]{:S(2)}, u32[]{:S(2)}) collective-permute-start(bf16[32,8192]{1,0:T(8,128)(2,1)S(1)} %get-tuple-element.44), channel_id=1, source_target_pairs={{0,3},{1,0},{2,1},{3,2},{4,7},{5,4},{6,5},{7,6},{8,11},{9,8},{10,9... | collective-permute-start | bytes 1572872 | tf_op jit(solution)/shard_map/ppermute | solution.py:389
  50.7 1.0 %collective-permute-start.16 = (bf16[512,256]{1,0:T(8,128)(2,1)S(1)}, bf16[512,256]{1,0:T(8,128)(2,1)S(1)}, u32[]{:S(2)}, u32[]{:S(2)}) collective-permute-start(bf16[512,256]{1,0:T(8,128)(2,1)S(1)} %get-tuple-element.56), channel_id=1, source_target_pairs={{0,64},{64,128},{128,192},{192,0},{1,65},{65,129},{129,193},{193,1... | collective-permute-start | bytes 786440 | tf_op jit(solution)/shard_map/ppermute | solution.py:389
  51.7 1.8 %collective-permute-start.18 = (bf16[512,256]{1,0:T(8,128)(2,1)S(1)}, bf16[512,256]{1,0:T(8,128)(2,1)S(1)}, u32[]{:S(2)}, u32[]{:S(2)}) collective-permute-start(bf16[512,256]{1,0:T(8,128)(2,1)S(1)} %get-tuple-element.57), channel_id=1, source_target_pairs={{0,192},{64,0},{128,64},{192,128},{1,193},{65,1},{129,65},{193,129... | collective-permute-start | bytes 786440 | tf_op jit(solution)/shard_map/ppermute | solution.py:389
  54.2 8.2 %collective-permute-done.12 = bf16[32,8192]{1,0:T(8,128)(2,1)S(1)} collective-permute-done((bf16[32,8192]{1,0:T(8,128)(2,1)S(1)}, bf16[32,8192]{1,0:T(8,128)(2,1)S(1)}, u32[]{:S(2)}, u32[]{:S(2)}) %collective-permute-start.12) | collective-permute-done | bytes 524320 | tf_op jit(solution)/shard_map/ppermute | solution.py:389
  62.6 6.6 %collective-permute-start.14 = (bf16[16,8192]{1,0:T(8,128)(2,1)S(1)}, bf16[16,8192]{1,0:T(8,128)(2,1)S(1)}, u32[]{:S(2)}, u32[]{:S(2)}) collective-permute-start(bf16[16,8192]{1,0:T(8,128)(2,1)S(1)} %slice.49), channel_id=1, source_target_pairs={{0,4},{4,0},{1,5},{5,1},{2,6},{6,2},{3,7},{7,3},{8,12},{12,8},{9,1... | collective-permute-start | bytes 786440 | tf_op jit(solution)/shard_map/ppermute | solution.py:399
  69.5 1.7 %collective-permute-start.21 = (bf16[128,256]{1,0:T(8,128)(2,1)S(1)}, bf16[128,256]{1,0:T(8,128)(2,1)S(1)}, u32[]{:S(2)}, u32[]{:S(2)}) collective-permute-start(bf16[128,256]{1,0:T(8,128)(2,1)S(1)} %get-tuple-element.60), channel_id=1, source_target_pairs={{0,48},{16,32},{32,16},{48,0},{1,49},{17,33},{33,17},{49,1},{2,50}... | collective-permute-start | bytes 196616 | tf_op jit(solution)/shard_map/ppermute | solution.py:399
  71.2 0.9 %collective-permute-start.20 = (bf16[128,256]{1,0:T(8,128)(2,1)S(1)}, bf16[128,256]{1,0:T(8,128)(2,1)S(1)}, u32[]{:S(2)}, u32[]{:S(2)}) collective-permute-start(bf16[128,256]{1,0:T(8,128)(2,1)S(1)} %get-tuple-element.61), channel_id=1, source_target_pairs={{0,32},{16,48},{32,0},{48,16},{1,33},{17,49},{33,1},{49,17},{2,34}... | collective-permute-start | bytes 196616 | tf_op jit(solution)/shard_map/ppermute | solution.py:399
  72.2 7.5 %collective-permute-done.14 = bf16[16,8192]{1,0:T(8,128)(2,1)S(1)} collective-permute-done((bf16[16,8192]{1,0:T(8,128)(2,1)S(1)}, bf16[16,8192]{1,0:T(8,128)(2,1)S(1)}, u32[]{:S(2)}, u32[]{:S(2)}) %collective-permute-start.14) | collective-permute-done | bytes 262176 | tf_op jit(solution)/shard_map/ppermute | solution.py:399
  80.4 2.0 %collective-permute-done.21 = bf16[128,256]{1,0:T(8,128)(2,1)S(1)} collective-permute-done((bf16[128,256]{1,0:T(8,128)(2,1)S(1)}, bf16[128,256]{1,0:T(8,128)(2,1)S(1)}, u32[]{:S(2)}, u32[]{:S(2)}) %collective-permute-start.21) | collective-permute-done | bytes 65568 | tf_op jit(solution)/shard_map/ppermute | solution.py:399
  82.5 4.3 %collective-permute-done.20 = bf16[128,256]{1,0:T(8,128)(2,1)S(1)} collective-permute-done((bf16[128,256]{1,0:T(8,128)(2,1)S(1)}, bf16[128,256]{1,0:T(8,128)(2,1)S(1)}, u32[]{:S(2)}, u32[]{:S(2)}) %collective-permute-start.20) | collective-permute-done | bytes 65568 | tf_op jit(solution)/shard_map/ppermute | solution.py:399
  (40 shorter events, 4.8 us)
Async XLA Ops:
  2.1 8.6 %collective-permute-start.2 = (bf16[128,256]{1,0:T(8,128)(2,1)}, bf16[128,256]{1,0:T(8,128)(2,1)S(1)}, u32[]{:S(2)}, u32[]{:S(2)}) collective-permute-start(bf16[128,256]{1,0:T(8,128)(2,1)} %pair.1.kv_ref), channel_id=1, source_target_pairs={{0,48},{16,32},{32,16},{48,0},{1,49},{17,33},{33,17},{49,1},{2,50}... | collective-permute-start | bytes 196616 | tf_op jit(solution)/shard_map/ppermute | solution.py:399
  7.3 5.4 %collective-permute-start.1 = (bf16[128,256]{1,0:T(8,128)(2,1)}, bf16[128,256]{1,0:T(8,128)(2,1)S(1)}, u32[]{:S(2)}, u32[]{:S(2)}) collective-permute-start(bf16[128,256]{1,0:T(8,128)(2,1)} %pair.1.kv_ref), channel_id=1, source_target_pairs={{0,32},{16,48},{32,0},{48,16},{1,33},{17,49},{33,1},{49,17},{2,34}... | collective-permute-start | bytes 196616 | tf_op jit(solution)/shard_map/ppermute | solution.py:399
  7.3 5.4 %collective-permute-start = (bf16[128,256]{1,0:T(8,128)(2,1)}, bf16[128,256]{1,0:T(8,128)(2,1)S(1)}, u32[]{:S(2)}, u32[]{:S(2)}) collective-permute-start(bf16[128,256]{1,0:T(8,128)(2,1)} %pair.1.kv_ref), channel_id=1, source_target_pairs={{0,16},{16,0},{32,48},{48,32},{1,17},{17,1},{33,49},{49,33},{2,18}... | collective-permute-start | bytes 196616 | tf_op jit(solution)/shard_map/ppermute | solution.py:399
  7.7 0.9 copy-start
  8.6 0.9 %copy-start.1 = (bf16[128,512]{1,0:T(8,128)(2,1)S(1)}, bf16[128,512]{1,0:T(8,128)(2,1)}, u32[]{:S(2)}) copy-start(bf16[128,512]{1,0:T(8,128)(2,1)} %q_hbm.1) | copy-start | bytes 393220
  9.5 0.9 %copy-start.2 = (bf16[128,512]{1,0:T(8,128)(2,1)S(1)}, bf16[128,512]{1,0:T(8,128)(2,1)}, u32[]{:S(2)}) copy-start(bf16[128,512]{1,0:T(8,128)(2,1)} %do_hbm.1) | copy-start | bytes 393220
  12.8 10.1 %collective-permute-start.8 = (bf16[512,256]{1,0:T(8,128)(2,1)S(1)}, bf16[512,256]{1,0:T(8,128)(2,1)S(1)}, u32[]{:S(2)}, u32[]{:S(2)}) collective-permute-start(bf16[512,256]{1,0:T(8,128)(2,1)S(1)} %stack.1.piece_ref.rest_0_), channel_id=1, source_target_pairs={{192,0},{0,64},{64,128},{128,192},{193,1},{1,65},{65,129},{129,193... | collective-permute-start | bytes 786440 | tf_op jit(solution)/shard_map/ppermute | solution.py:394
  13.7 12.7 %collective-permute-start.6 = (bf16[512,256]{1,0:T(8,128)(2,1)S(1)}, bf16[512,256]{1,0:T(8,128)(2,1)S(1)}, u32[]{:S(2)}, u32[]{:S(2)}) collective-permute-start(bf16[512,256]{1,0:T(8,128)(2,1)S(1)} %stack.1.piece_ref.rest_0_), channel_id=1, source_target_pairs={{128,0},{192,64},{0,128},{64,192},{129,1},{193,65},{1,129},{65,193... | collective-permute-start | bytes 786440 | tf_op jit(solution)/shard_map/ppermute | solution.py:394
  16.2 12.9 %collective-permute-start.4 = (bf16[512,256]{1,0:T(8,128)(2,1)S(1)}, bf16[512,256]{1,0:T(8,128)(2,1)S(1)}, u32[]{:S(2)}, u32[]{:S(2)}) collective-permute-start(bf16[512,256]{1,0:T(8,128)(2,1)S(1)} %stack.1.piece_ref.rest_0_), channel_id=1, source_target_pairs={{64,0},{128,64},{192,128},{0,192},{65,1},{129,65},{193,129},{1,193... | collective-permute-start | bytes 786440 | tf_op jit(solution)/shard_map/ppermute | solution.py:394
  17.3 0.7 copy-start.3
  20.2 11.1 %collective-permute-start.3 = (bf16[512,256]{1,0:T(8,128)(2,1)S(1)}, bf16[512,256]{1,0:T(8,128)(2,1)S(1)}, u32[]{:S(2)}, u32[]{:S(2)}) collective-permute-start(bf16[512,256]{1,0:T(8,128)(2,1)S(1)} %get-tuple-element.33), channel_id=1, source_target_pairs={{0,8},{8,0},{1,9},{9,1},{2,10},{10,2},{3,11},{11,3},{4,12},{12,4},... | collective-permute-start | bytes 786440 | tf_op jit(solution)/shard_map/ppermute | solution.py:399
  22.8 8.5 %collective-permute-start.9 = (bf16[512,256]{1,0:T(8,128)(2,1)S(1)}, bf16[512,256]{1,0:T(8,128)(2,1)S(1)}, u32[]{:S(2)}, u32[]{:S(2)}) collective-permute-start(bf16[512,256]{1,0:T(8,128)(2,1)S(1)} %collective-permute-done.8.rest_3_), channel_id=1, source_target_pairs={{0,8},{8,0},{1,9},{9,1},{2,10},{10,2},{3,11},{11,3},{4,12},{12,4},... | collective-permute-start | bytes 786440 | tf_op jit(solution)/shard_map/ppermute | solution.py:399
  26.4 4.9 %collective-permute-start.7 = (bf16[512,256]{1,0:T(8,128)(2,1)S(1)}, bf16[512,256]{1,0:T(8,128)(2,1)S(1)}, u32[]{:S(2)}, u32[]{:S(2)}) collective-permute-start(bf16[512,256]{1,0:T(8,128)(2,1)S(1)} %collective-permute-done.6.rest_2_), channel_id=1, source_target_pairs={{0,8},{8,0},{1,9},{9,1},{2,10},{10,2},{3,11},{11,3},{4,12},{12,4},... | collective-permute-start | bytes 786440 | tf_op jit(solution)/shard_map/ppermute | solution.py:399
  29.0 2.3 %collective-permute-start.5 = (bf16[512,256]{1,0:T(8,128)(2,1)S(1)}, bf16[512,256]{1,0:T(8,128)(2,1)S(1)}, u32[]{:S(2)}, u32[]{:S(2)}) collective-permute-start(bf16[512,256]{1,0:T(8,128)(2,1)S(1)} %collective-permute-done.4.rest_1_), channel_id=1, source_target_pairs={{0,8},{8,0},{1,9},{9,1},{2,10},{10,2},{3,11},{11,3},{4,12},{12,4},... | collective-permute-start | bytes 786440 | tf_op jit(solution)/shard_map/ppermute | solution.py:399
  29.1 3.4 %copy-start.4 = (bf16[512,8192]{1,0:T(8,128)(2,1)S(1)}, bf16[512,8192]{1,0:T(8,128)(2,1)}, u32[]{:S(2)}) copy-start(bf16[512,8192]{1,0:T(8,128)(2,1)} %rest_5_.1) | copy-start | bytes 25165828
  36.2 11.0 %collective-permute-start.10 = (bf16[32,4096]{1,0:T(8,128)(2,1)S(1)}, bf16[32,4096]{1,0:T(8,128)(2,1)S(1)}, u32[]{:S(2)}, u32[]{:S(2)}) collective-permute-start(bf16[32,4096]{1,0:T(8,128)(2,1)S(1)} %get-tuple-element.41), channel_id=1, source_target_pairs={{0,1},{1,2},{2,3},{3,0},{4,5},{5,6},{6,7},{7,4},{8,9},{9,10},{10,1... | collective-permute-start | bytes 786440 | tf_op jit(solution)/shard_map/ppermute | solution.py:389
  37.8 9.4 %collective-permute-start.11 = (bf16[32,4096]{1,0:T(8,128)(2,1)S(1)}, bf16[32,4096]{1,0:T(8,128)(2,1)S(1)}, u32[]{:S(2)}, u32[]{:S(2)}) collective-permute-start(bf16[32,4096]{1,0:T(8,128)(2,1)S(1)} %get-tuple-element.42), channel_id=1, source_target_pairs={{0,3},{1,0},{2,1},{3,2},{4,7},{5,4},{6,5},{7,6},{8,11},{9,8},{10,9... | collective-permute-start | bytes 786440 | tf_op jit(solution)/shard_map/ppermute | solution.py:389
  42.4 8.0 %collective-permute-start.15 = (bf16[2048,256]{1,0:T(8,128)(2,1)S(1)}, bf16[2048,256]{1,0:T(8,128)(2,1)S(1)}, u32[]{:S(2)}, u32[]{:S(2)}) collective-permute-start(bf16[2048,256]{1,0:T(8,128)(2,1)S(1)} %get-tuple-element.55), channel_id=1, source_target_pairs={{0,8},{8,0},{1,9},{9,1},{2,10},{10,2},{3,11},{11,3},{4,12},{12,4},... | collective-permute-start | bytes 3145736 | tf_op jit(solution)/shard_map/ppermute | solution.py:399
  47.6 14.8 %collective-permute-start.12 = (bf16[32,8192]{1,0:T(8,128)(2,1)S(1)}, bf16[32,8192]{1,0:T(8,128)(2,1)S(1)}, u32[]{:S(2)}, u32[]{:S(2)}) collective-permute-start(bf16[32,8192]{1,0:T(8,128)(2,1)S(1)} %get-tuple-element.43), channel_id=1, source_target_pairs={{0,1},{1,2},{2,3},{3,0},{4,5},{5,6},{6,7},{7,4},{8,9},{9,10},{10,1... | collective-permute-start | bytes 1572872 | tf_op jit(solution)/shard_map/ppermute | solution.py:389
  47.8 14.7 %collective-permute-start.13 = (bf16[32,8192]{1,0:T(8,128)(2,1)S(1)}, bf16[32,8192]{1,0:T(8,128)(2,1)S(1)}, u32[]{:S(2)}, u32[]{:S(2)}) collective-permute-start(bf16[32,8192]{1,0:T(8,128)(2,1)S(1)} %get-tuple-element.44), channel_id=1, source_target_pairs={{0,3},{1,0},{2,1},{3,2},{4,7},{5,4},{6,5},{7,6},{8,11},{9,8},{10,9... | collective-permute-start | bytes 1572872 | tf_op jit(solution)/shard_map/ppermute | solution.py:389
  50.7 18.5 %collective-permute-start.16 = (bf16[512,256]{1,0:T(8,128)(2,1)S(1)}, bf16[512,256]{1,0:T(8,128)(2,1)S(1)}, u32[]{:S(2)}, u32[]{:S(2)}) collective-permute-start(bf16[512,256]{1,0:T(8,128)(2,1)S(1)} %get-tuple-element.56), channel_id=1, source_target_pairs={{0,64},{64,128},{128,192},{192,0},{1,65},{65,129},{129,193},{193,1... | collective-permute-start | bytes 786440 | tf_op jit(solution)/shard_map/ppermute | solution.py:389
  51.7 17.6 %collective-permute-start.18 = (bf16[512,256]{1,0:T(8,128)(2,1)S(1)}, bf16[512,256]{1,0:T(8,128)(2,1)S(1)}, u32[]{:S(2)}, u32[]{:S(2)}) collective-permute-start(bf16[512,256]{1,0:T(8,128)(2,1)S(1)} %get-tuple-element.57), channel_id=1, source_target_pairs={{0,192},{64,0},{128,64},{192,128},{1,193},{65,1},{129,65},{193,129... | collective-permute-start | bytes 786440 | tf_op jit(solution)/shard_map/ppermute | solution.py:389
  53.5 15.8 %collective-permute-start.17 = (bf16[512,256]{1,0:T(8,128)(2,1)S(1)}, bf16[512,256]{1,0:T(8,128)(2,1)S(1)}, u32[]{:S(2)}, u32[]{:S(2)}) collective-permute-start(bf16[512,256]{1,0:T(8,128)(2,1)S(1)} %get-tuple-element.58), channel_id=1, source_target_pairs={{0,128},{64,192},{128,0},{192,64},{1,129},{65,193},{129,1},{193,65... | collective-permute-start | bytes 786440 | tf_op jit(solution)/shard_map/ppermute | solution.py:389
  62.6 17.0 %collective-permute-start.14 = (bf16[16,8192]{1,0:T(8,128)(2,1)S(1)}, bf16[16,8192]{1,0:T(8,128)(2,1)S(1)}, u32[]{:S(2)}, u32[]{:S(2)}) collective-permute-start(bf16[16,8192]{1,0:T(8,128)(2,1)S(1)} %slice.49), channel_id=1, source_target_pairs={{0,4},{4,0},{1,5},{5,1},{2,6},{6,2},{3,7},{7,3},{8,12},{12,8},{9,1... | collective-permute-start | bytes 786440 | tf_op jit(solution)/shard_map/ppermute | solution.py:399
  69.4 11.0 %collective-permute-start.19 = (bf16[128,256]{1,0:T(8,128)(2,1)S(1)}, bf16[128,256]{1,0:T(8,128)(2,1)S(1)}, u32[]{:S(2)}, u32[]{:S(2)}) collective-permute-start(bf16[128,256]{1,0:T(8,128)(2,1)S(1)} %get-tuple-element.59), channel_id=1, source_target_pairs={{0,16},{16,0},{32,48},{48,32},{1,17},{17,1},{33,49},{49,33},{2,18}... | collective-permute-start | bytes 196616 | tf_op jit(solution)/shard_map/ppermute | solution.py:399
  69.5 13.0 %collective-permute-start.21 = (bf16[128,256]{1,0:T(8,128)(2,1)S(1)}, bf16[128,256]{1,0:T(8,128)(2,1)S(1)}, u32[]{:S(2)}, u32[]{:S(2)}) collective-permute-start(bf16[128,256]{1,0:T(8,128)(2,1)S(1)} %get-tuple-element.60), channel_id=1, source_target_pairs={{0,48},{16,32},{32,16},{48,0},{1,49},{17,33},{33,17},{49,1},{2,50}... | collective-permute-start | bytes 196616 | tf_op jit(solution)/shard_map/ppermute | solution.py:399
  71.2 15.5 %collective-permute-start.20 = (bf16[128,256]{1,0:T(8,128)(2,1)S(1)}, bf16[128,256]{1,0:T(8,128)(2,1)S(1)}, u32[]{:S(2)}, u32[]{:S(2)}) collective-permute-start(bf16[128,256]{1,0:T(8,128)(2,1)S(1)} %get-tuple-element.61), channel_id=1, source_target_pairs={{0,32},{16,48},{32,0},{48,16},{1,33},{17,49},{33,1},{49,17},{2,34}... | collective-permute-start | bytes 196616 | tf_op jit(solution)/shard_map/ppermute | solution.py:399

commit v6 on v5

--- a/solution.py
+++ b/solution.py
@@ -161,7 +161,7 @@
 def far_kernel(stretch, plan_ref, qs_ref, *rest):
     pieces, rest = rest[:NX], rest[NX:]
     (ds_ref, w_ref, near_top, near_sum, near_acc,
-     own_ref, front_ref, back_ref, far_a, far_b, p_ref, kv_ref, delta_ref, near_inv, far_inv,
+     own_ref, front_ref, back_ref, ahead_ref, behind_ref, p_ref, kv_ref, delta_ref, near_inv, far_inv,
      top_ref, sum_ref, acc_ref, s_buf, diff_ref, attn_ref, turned_ref) = rest
     attend(stretch, 1, plan_ref, qs_ref, pieces, p_ref, kv_ref, top_ref, sum_ref, acc_ref, s_buf, diff_ref)
     cols = qs_ref.shape[1]
@@ -193,12 +193,14 @@
         at = slice(index * MIX_SPAN, (index + 1) * MIX_SPAN)
         mixed = dot(turned_ref[...], w_ref[:, at], NN).astype(jnp.bfloat16)
         own_ref[:, at] = mixed[:piece]
-        front_ref[:, at] = mixed[piece:2 * piece]
-        back_ref[:, at] = mixed[3 * piece:]
         if at.start < half:
-            far_a[:, at] = mixed[2 * piece:3 * piece]
+            ahead_ref[:, at] = mixed[2 * piece:3 * piece]
+            behind_ref[:, at] = mixed[3 * piece:]
+            front_ref[:, at] = mixed[piece:2 * piece]
         else:
-            far_b[:, at.start - half:at.stop - half] = mixed[2 * piece:3 * piece]
+            ahead_ref[:, at] = mixed[piece:2 * piece]
+            behind_ref[:, at] = mixed[2 * piece:3 * piece]
+            back_ref[:, at.start - half:at.stop - half] = mixed[3 * piece:]
 
 
 def bwd_kernel(stretch, side, plan_ref, p_ref, kv_ref, qs_ref, ds_ref, delta_ref, inv_ref, *rest):
@@ -284,28 +286,55 @@
     )(ids, piece)
 
 
-def relay_kernel(front_in, back_in, front_add, back_add, front_ref, back_ref):
-    half = front_add.shape[1]
-    for index in range(2):
-        at = slice(index * half // 2, (index + 1) * half // 2)
-        front_ref[:, at] = (front_in[:, at].astype(jnp.float32) + front_add[:, at].astype(jnp.float32)
-                            ).astype(jnp.bfloat16)
-        to = slice(half + index * half // 2, half + (index + 1) * half // 2)
-        back_ref[:, to] = (back_in[:, to].astype(jnp.float32) + back_add[:, at].astype(jnp.float32)
-                           ).astype(jnp.bfloat16)
-
-
-def relay(front, back, front_add, back_add):
+def added(*parts):
+    total = parts[0].astype(jnp.float32)
+    for part in parts[1:]:
+        total = total + part.astype(jnp.float32)
+    return total.astype(jnp.bfloat16)
+
+
+def relay_kernel(front_in, back_in, ahead_in, behind_in, token_ref, front_ref, back_ref):
+    half = front_in.shape[1]
+    for index in range(half // MIX_SPAN):
+        at = slice(index * MIX_SPAN, (index + 1) * MIX_SPAN)
+        front_ref[:, at] = added(front_in[:, at], ahead_in[:, at])
+        back_ref[:, at] = added(back_in[:, at], behind_in[:, half + at.start:half + at.stop])
+
+
+def relay(front, back, from_behind, from_ahead, token):
     shape = jax.ShapeDtypeStruct(front.shape, front.dtype)
     return pl.pallas_call(
         relay_kernel,
         out_shape=(shape, shape),
-        in_specs=[VMEM] * 4,
+        in_specs=[VMEM] * 4 + [ANY],
         out_specs=[VMEM] * 2,
-        input_output_aliases={0: 0, 1: 1},
         compiler_params=pltpu.CompilerParams(vmem_limit_bytes=8 * MIB),
         name="relay",
-    )(front, back, front_add, back_add)
+    )(front, back, from_behind, from_ahead, token)
+
+
+def settle_kernel(own, from_behind, from_ahead, front, back, keep_ref, give_ref):
+    half = front.shape[1]
+    rows = keep_ref.shape[0]
+    for index in range(half // MIX_SPAN):
+        at = slice(index * MIX_SPAN, (index + 1) * MIX_SPAN)
+        to = slice(half + at.start, half + at.stop)
+        for where, total in ((at, added(own[:, at], front[:, at], from_ahead[:, at])),
+                             (to, added(own[:, to], back[:, at], from_behind[:, to]))):
+            keep_ref[:, where] = total[:rows]
+            give_ref[:, where] = total[rows:]
+
+
+def settle(own, from_behind, from_ahead, front, back):
+    shape = jax.ShapeDtypeStruct((own.shape[0] // NH, own.shape[1]), own.dtype)
+    return pl.pallas_call(
+        settle_kernel,
+        out_shape=(shape, shape),
+        in_specs=[VMEM] * 5,
+        out_specs=[VMEM] * 2,
+        compiler_params=pltpu.CompilerParams(vmem_limit_bytes=8 * MIB),
+        name="settle",
+    )(own, from_behind, from_ahead, front, back)
 
 
 def stack_kernel(token_ref, *refs):
@@ -341,7 +370,8 @@
     scratch = [pltpu.VMEM((steps, span, cols), f32), pltpu.VMEM((stretch, cols), jnp.int32)]
     if side:
         width = more[1].shape[1]
-        outs = (shape((tokens // NY, width), b16),) * 3 + (shape((tokens // NY, width // 2), b16),) * 2 + (
+        outs = (shape((tokens // NY, width), b16),) + (shape((tokens // NY, width // 2), b16),) * 2 + (
+            shape((tokens // NY, width), b16),) * 2 + (
             weights, keys, shape(row, f32), shape(row, f32), shape(row, f32))
         scratch = [pltpu.VMEM(row, f32), pltpu.VMEM(row, f32), pltpu.VMEM(sums, f32)] + scratch + [
             pltpu.VMEM((tokens, QPG * HD), b16), pltpu.VMEM((tokens, QPG * HD), b16)]
@@ -414,16 +444,15 @@
     near = [kv] + [behind(kv, "x", step) for step in range(1, NX)]
     far = [across(piece, "core", 1) for piece in [same] + near[1:]]
     near_probs, near_kv, *partial = forward(0, plan, qs, near)
-    own, front, back, far_a, far_b, far_probs, far_kv, delta, near_inv, far_inv = forward(
+    own, front, back, to_ahead, to_behind, far_probs, far_kv, delta, near_inv, far_inv = forward(
         1, plan, qs, far, ds, out_weight, *partial)
-    far_a, far_b = ahead(far_a, "y", 1), ahead(far_b, "y", NY - 1)
+    from_behind, from_ahead = ahead(to_ahead, "y", 1), ahead(to_behind, "y", NY - 1)
     partial, give = backward(1, plan, far_probs, far_kv, qs, ds, delta, far_inv)
-    front, back = relay(front, back, far_a, far_b)
-    mixed = total_of([own, ahead(front, "y", 1), ahead(back, "y", NY - 1)])
-    rows = mixed.shape[0] // NH
-    mixed = total_of([mixed[:rows], across(mixed[rows:], "zh", 1)])
     q_grad, keep = backward(0, plan, near_probs, near_kv, qs, ds, delta, near_inv, partial)
     term = total_of([keep, across(give, "core", 1)])
+    front, back = relay(front, back, from_behind, from_ahead, term)
+    mixed, give = settle(own, from_behind, from_ahead, ahead(front, "y", 1), ahead(back, "y", NY - 1))
+    mixed = total_of([mixed, across(give, "zh", 1)])
     part = term.shape[0] // NX
     term = total_of([term[:part]] + [
         ahead(term[step * part:(step + 1) * part], "x", step) for step in range(1, NX)])

time: 87.7 us -> 86.4 us (0.985)
  the two profiles are of different devices: /device:TPU:1 before, /device:TPU:38 now
where the time goes in v6:
time: 86.4 us; the launch traced here: 86.2 us
  waiting for transfers between devices  32.7 us (38%)
  starting transfers between devices  29.2 us (34%)
  Pallas kernels  17.1 us (20%)
  local copies, waits for them, and re-layouts  5.16 us (6%)
  other arithmetic  1.26 us (1%)
    ppermute x12, starting transfers between devices, across(): return lax.ppermute(block, axis, [(i, i ^ step) for i in range(count)])  15.6 us
    ppermute x12, waiting for transfers between devices, across(): return lax.ppermute(block, axis, [(i, i ^ step) for i in range(count)])  14.8 us
    ppermute x7, starting transfers between devices, ahead(): lax.ppermute(block, axis, [(i, (i + step) % count) for i in range(count)])  10.7 us
    ppermute x7, waiting for transfers between devices, ahead(): lax.ppermute(block, axis, [(i, (i + step) % count) for i in range(count)])  9.45 us
    ppermute x3, waiting for transfers between devices, behind(): lax.ppermute(block, axis, [((i + step) % count, i) for i in range(count)])  8.39 us
    pallas_call x2, Pallas kernels, backward(): pl.pallas_call(functools.partial(bwd_kernel, stretch, side), out_shape=(s...  6.91 us
    pallas_call x2, Pallas kernels, forward(): pl.pallas_call(functools.partial(far_kernel if side else near_kernel, str...  6.01 us
    unnamed x10, local copies, waits for them, and re-layouts  4.46 us
  transfers between devices with their start and end apart: 22, of which 9 were waited for; matrix products, arithmetic and copies ran while one was open for 1% of the time, Pallas kernels for 14%

profile of v6, /device:TPU:38, one launch (start us, length us, event | category | flops | bytes accessed | tf_op | source)
XLA Modules:
  0.0 86.2 jit_solution(14228271776567134697)
XLA Ops:
  0.6 1.4 %pair.1.kv_ref = bf16[128,256]{1,0:T(8,128)(2,1)} custom-call(bf16[128,128]{1,0:T(8,128)(2,1)} %k_hbm.1, bf16[128,128]{1,0:T(8,128)(2,1)} %v_hbm.1), custom_call_target="tpu_custom_call" | custom-call | tf_op jit(solution)/shard_map/pair/pallas_call | solution.py:251
  2.1 2.0 %collective-permute-start.2 = (bf16[128,256]{1,0:T(8,128)(2,1)}, bf16[128,256]{1,0:T(8,128)(2,1)S(1)}, u32[]{:S(2)}, u32[]{:S(2)}) collective-permute-start(bf16[128,256]{1,0:T(8,128)(2,1)} %pair.1.kv_ref), channel_id=1, source_target_pairs={{0,48},{16,32},{32,16},{48,0},{1,49},{17,33},{33,17},{49,1},{2,50}... | collective-permute-start | bytes 196616 | tf_op jit(solution)/shard_map/ppermute | solution.py:429
  4.1 1.5 %collective-permute-start.1 = (bf16[128,256]{1,0:T(8,128)(2,1)}, bf16[128,256]{1,0:T(8,128)(2,1)S(1)}, u32[]{:S(2)}, u32[]{:S(2)}) collective-permute-start(bf16[128,256]{1,0:T(8,128)(2,1)} %pair.1.kv_ref), channel_id=1, source_target_pairs={{0,32},{16,48},{32,0},{48,16},{1,33},{17,49},{33,1},{49,17},{2,34}... | collective-permute-start | bytes 196616 | tf_op jit(solution)/shard_map/ppermute | solution.py:429
  5.5 1.4 %collective-permute-start = (bf16[128,256]{1,0:T(8,128)(2,1)}, bf16[128,256]{1,0:T(8,128)(2,1)S(1)}, u32[]{:S(2)}, u32[]{:S(2)}) collective-permute-start(bf16[128,256]{1,0:T(8,128)(2,1)} %pair.1.kv_ref), channel_id=1, source_target_pairs={{0,16},{16,0},{32,48},{48,32},{1,17},{17,1},{33,49},{49,33},{2,18}... | collective-permute-start | bytes 196616 | tf_op jit(solution)/shard_map/ppermute | solution.py:429
  6.9 0.9 %copy-done = bf16[128,256]{1,0:T(8,128)(2,1)S(1)} copy-done((bf16[128,256]{1,0:T(8,128)(2,1)S(1)}, bf16[128,256]{1,0:T(8,128)(2,1)}, u32[]{:S(2)}) %copy-start) | copy-done | bytes 65560
  7.8 0.9 %copy-done.1 = bf16[128,512]{1,0:T(8,128)(2,1)S(1)} copy-done((bf16[128,512]{1,0:T(8,128)(2,1)S(1)}, bf16[128,512]{1,0:T(8,128)(2,1)}, u32[]{:S(2)}) %copy-start.1) | copy-done | bytes 131096
  8.7 0.9 %copy-done.2 = bf16[128,512]{1,0:T(8,128)(2,1)S(1)} copy-done((bf16[128,512]{1,0:T(8,128)(2,1)S(1)}, bf16[128,512]{1,0:T(8,128)(2,1)}, u32[]{:S(2)}) %copy-start.2) | copy-done | bytes 131096
  10.4 1.3 %collective-permute-done.refs_1_ = bf16[128,256]{1,0:T(8,128)(2,1)S(1)} collective-permute-done((bf16[128,256]{1,0:T(8,128)(2,1)}, bf16[128,256]{1,0:T(8,128)(2,1)S(1)}, u32[]{:S(2)}, u32[]{:S(2)}) %collective-permute-start) | collective-permute-done | bytes 65568 | tf_op jit(solution)/shard_map/ppermute | solution.py:429
  12.3 2.4 %collective-permute-start.6 = (bf16[512,256]{1,0:T(8,128)(2,1)S(1)}, bf16[512,256]{1,0:T(8,128)(2,1)S(1)}, u32[]{:S(2)}, u32[]{:S(2)}) collective-permute-start(bf16[512,256]{1,0:T(8,128)(2,1)S(1)} %stack.1.piece_ref.rest_0_), channel_id=1, source_target_pairs={{128,0},{192,64},{0,128},{64,192},{129,1},{193,65},{1,129},{65,193... | collective-permute-start | bytes 786440 | tf_op jit(solution)/shard_map/ppermute | solution.py:424
  15.4 2.2 %stage.1 = (s32[136]{0:T(256)S(1)}, bf16[512,256]{1,0:T(8,128)(2,1)S(1)}) custom-call(s32[64]{0:T(128)S(1)} %copy-done.3, bf16[512,256]{1,0:T(8,128)(2,1)S(1)} %stack.1.piece_ref.rest_0_), custom_call_target="tpu_custom_call" | custom-call | tf_op jit(solution)/shard_map/stage/pallas_call | solution.py:278
  17.7 3.4 %collective-permute-done.8.rest_3_ = bf16[512,256]{1,0:T(8,128)(2,1)S(1)} collective-permute-done((bf16[512,256]{1,0:T(8,128)(2,1)S(1)}, bf16[512,256]{1,0:T(8,128)(2,1)S(1)}, u32[]{:S(2)}, u32[]{:S(2)}) %collective-permute-start.8) | collective-permute-done | bytes 262176 | tf_op jit(solution)/shard_map/ppermute | solution.py:424
  21.1 2.0 %collective-permute-done.6.rest_2_ = bf16[512,256]{1,0:T(8,128)(2,1)S(1)} collective-permute-done((bf16[512,256]{1,0:T(8,128)(2,1)S(1)}, bf16[512,256]{1,0:T(8,128)(2,1)S(1)}, u32[]{:S(2)}, u32[]{:S(2)}) %collective-permute-start.6) | collective-permute-done | bytes 262176 | tf_op jit(solution)/shard_map/ppermute | solution.py:424
  23.1 3.0 %collective-permute-done.4.rest_1_ = bf16[512,256]{1,0:T(8,128)(2,1)S(1)} collective-permute-done((bf16[512,256]{1,0:T(8,128)(2,1)S(1)}, bf16[512,256]{1,0:T(8,128)(2,1)S(1)}, u32[]{:S(2)}, u32[]{:S(2)}) %collective-permute-start.4) | collective-permute-done | bytes 262176 | tf_op jit(solution)/shard_map/ppermute | solution.py:424
  26.1 2.2 %attention_forward_0.1 = (bf16[9,256,256]{2,1,0:T(8,128)(2,1)S(1)}, bf16[2048,256]{1,0:T(8,128)(2,1)S(1)}, f32[2,8,256]{2,1,0:T(8,128)S(1)}, f32[2,8,256]{2,1,0:T(8,128)S(1)}, f32[2,128,256]{2,1,0:T(8,128)S(1)}) custom-call(s32[136]{0:T(256)S(1)} %get-tuple-element.34.plan_ref, bf16[2,256,128]{2,1,0:T(8,128)(2,1)S(1)} %get-tuple-element.32.token_ref.qs_ref, ...), custom_call_target="tpu_custom_call" | custom-call | flops 3000000000 | bytes 8000000 | tf_op jit(solution)/shard_map/attention_forward_0/pallas_call | solution.py:380
  28.4 1.1 %copy-done.4 = bf16[512,8192]{1,0:T(8,128)(2,1)S(1)} copy-done((bf16[512,8192]{1,0:T(8,128)(2,1)S(1)}, bf16[512,8192]{1,0:T(8,128)(2,1)}, u32[]{:S(2)}) %copy-start.4) | copy-done | bytes 8388632
  29.5 3.8 %attention_forward_1.1 = (bf16[32,8192]{1,0:T(8,128)(2,1)S(1)}, bf16[32,4096]{1,0:T(8,128)(2,1)S(1)}, bf16[32,4096]{1,0:T(8,128)(2,1)S(1)}, bf16[32,8192]{1,0:T(...) custom-call(s32[136]{0:T(256)S(1)} %get-tuple-element.34.plan_ref, ...), custom_call_target="tpu_custom_call" | custom-call | flops 3000000000 | bytes 8000000 | tf_op jit(solution)/shard_map/attention_forward_1/pallas_call | solution.py:380
  33.3 1.8 %collective-permute-start.10 = (bf16[32,8192]{1,0:T(8,128)(2,1)S(1)}, bf16[32,8192]{1,0:T(8,128)(2,1)S(1)}, u32[]{:S(2)}, u32[]{:S(2)}) collective-permute-start(bf16[32,8192]{1,0:T(8,128)(2,1)S(1)} %get-tuple-element.41), channel_id=1, source_target_pairs={{0,1},{1,2},{2,3},{3,0},{4,5},{5,6},{6,7},{7,4},{8,9},{9,10},{10,1... | collective-permute-start | bytes 1572872 | tf_op jit(solution)/shard_map/ppermute | solution.py:419
  35.1 1.7 %collective-permute-start.11 = (bf16[32,8192]{1,0:T(8,128)(2,1)S(1)}, bf16[32,8192]{1,0:T(8,128)(2,1)S(1)}, u32[]{:S(2)}, u32[]{:S(2)}) collective-permute-start(bf16[32,8192]{1,0:T(8,128)(2,1)S(1)} %get-tuple-element.42), channel_id=1, source_target_pairs={{0,3},{1,0},{2,1},{3,2},{4,7},{5,4},{6,5},{7,6},{8,11},{9,8},{10,9... | collective-permute-start | bytes 1572872 | tf_op jit(solution)/shard_map/ppermute | solution.py:419
  36.8 3.1 %attention_backward_1.1 = (f32[2,128,256]{2,1,0:T(8,128)S(1)}, bf16[2048,256]{1,0:T(8,128)(2,1)S(1)}) custom-call(s32[136]{0:T(256)S(1)} %get-tuple-element.34.plan_ref, bf16[9,256,256]{2,1,0:T(8,128)(2,1)S(1)} %get-tuple-element.49.p_ref, bf16[2048,256]{1,0:T(8,128)(2,1)S(1)} %get-tuple-element.50.kv_ref, ...), custom_call_target="tpu_custom_call" | custom-call | flops 20000000000 | bytes 8000000 | tf_op jit(solution)/shard_map/attention_backward_1/pallas_call | solution.py:405
  40.0 3.8 %attention_backward_0.1 = (bf16[128,512]{1,0:T(8,128)(2,1)}, bf16[2048,256]{1,0:T(8,128)(2,1)S(1)}) custom-call(s32[136]{0:T(256)S(1)} %get-tuple-element.34.plan_ref, bf16[9,256,256]{2,1,0:T(8,128)(2,1)S(1)} %get-tuple-element.45.p_ref, bf16[2048,256]{1,0:T(8,128)(2,1)S(1)} %get-tuple-element.46.kv_ref, ...), custom_call_target="tpu_custom_call" | custom-call | flops 20000000000 | bytes 8000000 | tf_op jit(solution)/shard_map/attention_backward_0/pallas_call | solution.py:405
  44.3 1.5 %collective-permute-start.16 = (bf16[512,256]{1,0:T(8,128)(2,1)S(1)}, bf16[512,256]{1,0:T(8,128)(2,1)S(1)}, u32[]{:S(2)}, u32[]{:S(2)}) collective-permute-start(bf16[512,256]{1,0:T(8,128)(2,1)S(1)} %get-tuple-element.60), channel_id=1, source_target_pairs={{0,64},{64,128},{128,192},{192,0},{1,65},{65,129},{129,193},{193,1... | collective-permute-start | bytes 786440 | tf_op jit(solution)/shard_map/ppermute | solution.py:419
  46.4 1.8 %collective-permute-start.17 = (bf16[512,256]{1,0:T(8,128)(2,1)S(1)}, bf16[512,256]{1,0:T(8,128)(2,1)S(1)}, u32[]{:S(2)}, u32[]{:S(2)}) collective-permute-start(bf16[512,256]{1,0:T(8,128)(2,1)S(1)} %get-tuple-element.62), channel_id=1, source_target_pairs={{0,128},{64,192},{128,0},{192,64},{1,129},{65,193},{129,1},{193,65... | collective-permute-start | bytes 786440 | tf_op jit(solution)/shard_map/ppermute | solution.py:419
  48.1 1.0 %collective-permute-done.10.ahead_in.from_behind = bf16[32,8192]{1,0:T(8,128)(2,1)S(1)} collective-permute-done((bf16[32,8192]{1,0:T(8,128)(2,1)S(1)}, bf16[32,8192]{1,0:T(8,128)(2,1)S(1)}, u32[]{:S(2)}, u32[]{:S(2)}) %collective-permute-start.10) | collective-permute-done | bytes 524320 | tf_op jit(solution)/shard_map/ppermute | solution.py:419
  49.3 1.6 %collective-permute-start.13 = (bf16[32,4096]{1,0:T(8,128)(2,1)S(1)}, bf16[32,4096]{1,0:T(8,128)(2,1)S(1)}, u32[]{:S(2)}, u32[]{:S(2)}) collective-permute-start(bf16[32,4096]{1,0:T(8,128)(2,1)S(1)} %get-tuple-element.55), channel_id=1, source_target_pairs={{0,1},{1,2},{2,3},{3,0},{4,5},{5,6},{6,7},{7,4},{8,9},{9,10},{10,1... | collective-permute-start | bytes 786440 | tf_op jit(solution)/shard_map/ppermute | solution.py:419
  51.0 1.7 %collective-permute-start.14 = (bf16[32,4096]{1,0:T(8,128)(2,1)S(1)}, bf16[32,4096]{1,0:T(8,128)(2,1)S(1)}, u32[]{:S(2)}, u32[]{:S(2)}) collective-permute-start(bf16[32,4096]{1,0:T(8,128)(2,1)S(1)} %get-tuple-element.56), channel_id=1, source_target_pairs={{0,3},{1,0},{2,1},{3,2},{4,7},{5,4},{6,5},{7,6},{8,11},{9,8},{10,9... | collective-permute-start | bytes 786440 | tf_op jit(solution)/shard_map/ppermute | solution.py:419
  52.6 0.8 collective-permute-done.16
  53.4 7.5 %collective-permute-done.18 = bf16[512,256]{1,0:T(8,128)(2,1)S(1)} collective-permute-done((bf16[512,256]{1,0:T(8,128)(2,1)S(1)}, bf16[512,256]{1,0:T(8,128)(2,1)S(1)}, u32[]{:S(2)}, u32[]{:S(2)}) %collective-permute-start.18) | collective-permute-done | bytes 262176 | tf_op jit(solution)/shard_map/ppermute | solution.py:419
  61.2 1.1 %collective-permute-start.19 = (bf16[128,256]{1,0:T(8,128)(2,1)S(1)}, bf16[128,256]{1,0:T(8,128)(2,1)S(1)}, u32[]{:S(2)}, u32[]{:S(2)}) collective-permute-start(bf16[128,256]{1,0:T(8,128)(2,1)S(1)} %get-tuple-element.63), channel_id=1, source_target_pairs={{0,16},{16,0},{32,48},{48,32},{1,17},{17,1},{33,49},{49,33},{2,18}... | collective-permute-start | bytes 196616 | tf_op jit(solution)/shard_map/ppermute | solution.py:429
  62.3 1.6 %collective-permute-start.21 = (bf16[128,256]{1,0:T(8,128)(2,1)S(1)}, bf16[128,256]{1,0:T(8,128)(2,1)S(1)}, u32[]{:S(2)}, u32[]{:S(2)}) collective-permute-start(bf16[128,256]{1,0:T(8,128)(2,1)S(1)} %get-tuple-element.64), channel_id=1, source_target_pairs={{0,48},{16,32},{32,16},{48,0},{1,49},{17,33},{33,17},{49,1},{2,50}... | collective-permute-start | bytes 196616 | tf_op jit(solution)/shard_map/ppermute | solution.py:429
  63.9 1.7 %collective-permute-start.20 = (bf16[128,256]{1,0:T(8,128)(2,1)S(1)}, bf16[128,256]{1,0:T(8,128)(2,1)S(1)}, u32[]{:S(2)}, u32[]{:S(2)}) collective-permute-start(bf16[128,256]{1,0:T(8,128)(2,1)S(1)} %get-tuple-element.65), channel_id=1, source_target_pairs={{0,32},{16,48},{32,0},{48,16},{1,33},{17,49},{33,1},{49,17},{2,34}... | collective-permute-start | bytes 196616 | tf_op jit(solution)/shard_map/ppermute | solution.py:429
  65.8 6.0 %collective-permute-start.15 = (bf16[16,8192]{1,0:T(8,128)(2,1)S(1)}, bf16[16,8192]{1,0:T(8,128)(2,1)S(1)}, u32[]{:S(2)}, u32[]{:S(2)}) collective-permute-start(bf16[16,8192]{1,0:T(8,128)(2,1)S(1)} %get-tuple-element.58), channel_id=1, source_target_pairs={{0,4},{4,0},{1,5},{5,1},{2,6},{6,2},{3,7},{7,3},{8,12},{12,8},{9,1... | collective-permute-start | bytes 786440 | tf_op jit(solution)/shard_map/ppermute | solution.py:429
  72.5 12.8 %collective-permute-done.15 = bf16[16,8192]{1,0:T(8,128)(2,1)S(1)} collective-permute-done((bf16[16,8192]{1,0:T(8,128)(2,1)S(1)}, bf16[16,8192]{1,0:T(8,128)(2,1)S(1)}, u32[]{:S(2)}, u32[]{:S(2)}) %collective-permute-start.15) | collective-permute-done | bytes 262176 | tf_op jit(solution)/shard_map/ppermute | solution.py:429
  (39 shorter events, 5.3 us)
Async XLA Ops:
  2.1 7.7 %collective-permute-start.2 = (bf16[128,256]{1,0:T(8,128)(2,1)}, bf16[128,256]{1,0:T(8,128)(2,1)S(1)}, u32[]{:S(2)}, u32[]{:S(2)}) collective-permute-start(bf16[128,256]{1,0:T(8,128)(2,1)} %pair.1.kv_ref), channel_id=1, source_target_pairs={{0,48},{16,32},{32,16},{48,0},{1,49},{17,33},{33,17},{49,1},{2,50}... | collective-permute-start | bytes 196616 | tf_op jit(solution)/shard_map/ppermute | solution.py:429
  4.1 6.3 %collective-permute-start.1 = (bf16[128,256]{1,0:T(8,128)(2,1)}, bf16[128,256]{1,0:T(8,128)(2,1)S(1)}, u32[]{:S(2)}, u32[]{:S(2)}) collective-permute-start(bf16[128,256]{1,0:T(8,128)(2,1)} %pair.1.kv_ref), channel_id=1, source_target_pairs={{0,32},{16,48},{32,0},{48,16},{1,33},{17,49},{33,1},{49,17},{2,34}... | collective-permute-start | bytes 196616 | tf_op jit(solution)/shard_map/ppermute | solution.py:429
  5.5 6.2 %collective-permute-start = (bf16[128,256]{1,0:T(8,128)(2,1)}, bf16[128,256]{1,0:T(8,128)(2,1)S(1)}, u32[]{:S(2)}, u32[]{:S(2)}) collective-permute-start(bf16[128,256]{1,0:T(8,128)(2,1)} %pair.1.kv_ref), channel_id=1, source_target_pairs={{0,16},{16,0},{32,48},{48,32},{1,17},{17,1},{33,49},{49,33},{2,18}... | collective-permute-start | bytes 196616 | tf_op jit(solution)/shard_map/ppermute | solution.py:429
  6.9 0.9 %copy-start = (bf16[128,256]{1,0:T(8,128)(2,1)S(1)}, bf16[128,256]{1,0:T(8,128)(2,1)}, u32[]{:S(2)}) copy-start(bf16[128,256]{1,0:T(8,128)(2,1)} %pair.1.kv_ref) | copy-start | bytes 196612
  7.8 0.9 %copy-start.1 = (bf16[128,512]{1,0:T(8,128)(2,1)S(1)}, bf16[128,512]{1,0:T(8,128)(2,1)}, u32[]{:S(2)}) copy-start(bf16[128,512]{1,0:T(8,128)(2,1)} %q_hbm.1) | copy-start | bytes 393220
  8.7 0.9 %copy-start.2 = (bf16[128,512]{1,0:T(8,128)(2,1)S(1)}, bf16[128,512]{1,0:T(8,128)(2,1)}, u32[]{:S(2)}) copy-start(bf16[128,512]{1,0:T(8,128)(2,1)} %do_hbm.1) | copy-start | bytes 393220
  11.8 9.3 %collective-permute-start.8 = (bf16[512,256]{1,0:T(8,128)(2,1)S(1)}, bf16[512,256]{1,0:T(8,128)(2,1)S(1)}, u32[]{:S(2)}, u32[]{:S(2)}) collective-permute-start(bf16[512,256]{1,0:T(8,128)(2,1)S(1)} %stack.1.piece_ref.rest_0_), channel_id=1, source_target_pairs={{192,0},{0,64},{64,128},{128,192},{193,1},{1,65},{65,129},{129,193... | collective-permute-start | bytes 786440 | tf_op jit(solution)/shard_map/ppermute | solution.py:424
  12.3 10.7 %collective-permute-start.6 = (bf16[512,256]{1,0:T(8,128)(2,1)S(1)}, bf16[512,256]{1,0:T(8,128)(2,1)S(1)}, u32[]{:S(2)}, u32[]{:S(2)}) collective-permute-start(bf16[512,256]{1,0:T(8,128)(2,1)S(1)} %stack.1.piece_ref.rest_0_), channel_id=1, source_target_pairs={{128,0},{192,64},{0,128},{64,192},{129,1},{193,65},{1,129},{65,193... | collective-permute-start | bytes 786440 | tf_op jit(solution)/shard_map/ppermute | solution.py:424
  14.7 11.3 %collective-permute-start.4 = (bf16[512,256]{1,0:T(8,128)(2,1)S(1)}, bf16[512,256]{1,0:T(8,128)(2,1)S(1)}, u32[]{:S(2)}, u32[]{:S(2)}) collective-permute-start(bf16[512,256]{1,0:T(8,128)(2,1)S(1)} %stack.1.piece_ref.rest_0_), channel_id=1, source_target_pairs={{64,0},{128,64},{192,128},{0,192},{65,1},{129,65},{193,129},{1,193... | collective-permute-start | bytes 786440 | tf_op jit(solution)/shard_map/ppermute | solution.py:424
  14.8 0.7 copy-start.3
  17.6 10.7 %collective-permute-start.3 = (bf16[512,256]{1,0:T(8,128)(2,1)S(1)}, bf16[512,256]{1,0:T(8,128)(2,1)S(1)}, u32[]{:S(2)}, u32[]{:S(2)}) collective-permute-start(bf16[512,256]{1,0:T(8,128)(2,1)S(1)} %get-tuple-element.35), channel_id=1, source_target_pairs={{0,8},{8,0},{1,9},{9,1},{2,10},{10,2},{3,11},{11,3},{4,12},{12,4},... | collective-permute-start | bytes 786440 | tf_op jit(solution)/shard_map/ppermute | solution.py:429
  21.1 7.2 %collective-permute-start.9 = (bf16[512,256]{1,0:T(8,128)(2,1)S(1)}, bf16[512,256]{1,0:T(8,128)(2,1)S(1)}, u32[]{:S(2)}, u32[]{:S(2)}) collective-permute-start(bf16[512,256]{1,0:T(8,128)(2,1)S(1)} %collective-permute-done.8.rest_3_), channel_id=1, source_target_pairs={{0,8},{8,0},{1,9},{9,1},{2,10},{10,2},{3,11},{11,3},{4,12},{12,4},... | collective-permute-start | bytes 786440 | tf_op jit(solution)/shard_map/ppermute | solution.py:429
  23.1 5.3 %collective-permute-start.7 = (bf16[512,256]{1,0:T(8,128)(2,1)S(1)}, bf16[512,256]{1,0:T(8,128)(2,1)S(1)}, u32[]{:S(2)}, u32[]{:S(2)}) collective-permute-start(bf16[512,256]{1,0:T(8,128)(2,1)S(1)} %collective-permute-done.6.rest_2_), channel_id=1, source_target_pairs={{0,8},{8,0},{1,9},{9,1},{2,10},{10,2},{3,11},{11,3},{4,12},{12,4},... | collective-permute-start | bytes 786440 | tf_op jit(solution)/shard_map/ppermute | solution.py:429
  26.1 2.2 %collective-permute-start.5 = (bf16[512,256]{1,0:T(8,128)(2,1)S(1)}, bf16[512,256]{1,0:T(8,128)(2,1)S(1)}, u32[]{:S(2)}, u32[]{:S(2)}) collective-permute-start(bf16[512,256]{1,0:T(8,128)(2,1)S(1)} %collective-permute-done.4.rest_1_), channel_id=1, source_target_pairs={{0,8},{8,0},{1,9},{9,1},{2,10},{10,2},{3,11},{11,3},{4,12},{12,4},... | collective-permute-start | bytes 786440 | tf_op jit(solution)/shard_map/ppermute | solution.py:429
  26.1 3.4 %copy-start.4 = (bf16[512,8192]{1,0:T(8,128)(2,1)S(1)}, bf16[512,8192]{1,0:T(8,128)(2,1)}, u32[]{:S(2)}) copy-start(bf16[512,8192]{1,0:T(8,128)(2,1)} %rest_5_.1) | copy-start | bytes 25165828
  33.3 15.9 %collective-permute-start.10 = (bf16[32,8192]{1,0:T(8,128)(2,1)S(1)}, bf16[32,8192]{1,0:T(8,128)(2,1)S(1)}, u32[]{:S(2)}, u32[]{:S(2)}) collective-permute-start(bf16[32,8192]{1,0:T(8,128)(2,1)S(1)} %get-tuple-element.41), channel_id=1, source_target_pairs={{0,1},{1,2},{2,3},{3,0},{4,5},{5,6},{6,7},{7,4},{8,9},{9,10},{10,1... | collective-permute-start | bytes 1572872 | tf_op jit(solution)/shard_map/ppermute | solution.py:419
  35.1 14.1 %collective-permute-start.11 = (bf16[32,8192]{1,0:T(8,128)(2,1)S(1)}, bf16[32,8192]{1,0:T(8,128)(2,1)S(1)}, u32[]{:S(2)}, u32[]{:S(2)}) collective-permute-start(bf16[32,8192]{1,0:T(8,128)(2,1)S(1)} %get-tuple-element.42), channel_id=1, source_target_pairs={{0,3},{1,0},{2,1},{3,2},{4,7},{5,4},{6,5},{7,6},{8,11},{9,8},{10,9... | collective-permute-start | bytes 1572872 | tf_op jit(solution)/shard_map/ppermute | solution.py:419
  39.9 4.0 %collective-permute-start.12 = (bf16[2048,256]{1,0:T(8,128)(2,1)S(1)}, bf16[2048,256]{1,0:T(8,128)(2,1)S(1)}, u32[]{:S(2)}, u32[]{:S(2)}) collective-permute-start(bf16[2048,256]{1,0:T(8,128)(2,1)S(1)} %get-tuple-element.54), channel_id=1, source_target_pairs={{0,8},{8,0},{1,9},{9,1},{2,10},{10,2},{3,11},{11,3},{4,12},{12,4},... | collective-permute-start | bytes 3145736 | tf_op jit(solution)/shard_map/ppermute | solution.py:429
  44.3 9.2 %collective-permute-start.16 = (bf16[512,256]{1,0:T(8,128)(2,1)S(1)}, bf16[512,256]{1,0:T(8,128)(2,1)S(1)}, u32[]{:S(2)}, u32[]{:S(2)}) collective-permute-start(bf16[512,256]{1,0:T(8,128)(2,1)S(1)} %get-tuple-element.60), channel_id=1, source_target_pairs={{0,64},{64,128},{128,192},{192,0},{1,65},{65,129},{129,193},{193,1... | collective-permute-start | bytes 786440 | tf_op jit(solution)/shard_map/ppermute | solution.py:419
  45.7 15.3 %collective-permute-start.18 = (bf16[512,256]{1,0:T(8,128)(2,1)S(1)}, bf16[512,256]{1,0:T(8,128)(2,1)S(1)}, u32[]{:S(2)}, u32[]{:S(2)}) collective-permute-start(bf16[512,256]{1,0:T(8,128)(2,1)S(1)} %get-tuple-element.61), channel_id=1, source_target_pairs={{0,192},{64,0},{128,64},{192,128},{1,193},{65,1},{129,65},{193,129... | collective-permute-start | bytes 786440 | tf_op jit(solution)/shard_map/ppermute | solution.py:419
  46.4 14.6 %collective-permute-start.17 = (bf16[512,256]{1,0:T(8,128)(2,1)S(1)}, bf16[512,256]{1,0:T(8,128)(2,1)S(1)}, u32[]{:S(2)}, u32[]{:S(2)}) collective-permute-start(bf16[512,256]{1,0:T(8,128)(2,1)S(1)} %get-tuple-element.62), channel_id=1, source_target_pairs={{0,128},{64,192},{128,0},{192,64},{1,129},{65,193},{129,1},{193,65... | collective-permute-start | bytes 786440 | tf_op jit(solution)/shard_map/ppermute | solution.py:419
  49.3 16.3 %collective-permute-start.13 = (bf16[32,4096]{1,0:T(8,128)(2,1)S(1)}, bf16[32,4096]{1,0:T(8,128)(2,1)S(1)}, u32[]{:S(2)}, u32[]{:S(2)}) collective-permute-start(bf16[32,4096]{1,0:T(8,128)(2,1)S(1)} %get-tuple-element.55), channel_id=1, source_target_pairs={{0,1},{1,2},{2,3},{3,0},{4,5},{5,6},{6,7},{7,4},{8,9},{9,10},{10,1... | collective-permute-start | bytes 786440 | tf_op jit(solution)/shard_map/ppermute | solution.py:419
  51.0 14.7 %collective-permute-start.14 = (bf16[32,4096]{1,0:T(8,128)(2,1)S(1)}, bf16[32,4096]{1,0:T(8,128)(2,1)S(1)}, u32[]{:S(2)}, u32[]{:S(2)}) collective-permute-start(bf16[32,4096]{1,0:T(8,128)(2,1)S(1)} %get-tuple-element.56), channel_id=1, source_target_pairs={{0,3},{1,0},{2,1},{3,2},{4,7},{5,4},{6,5},{7,6},{8,11},{9,8},{10,9... | collective-permute-start | bytes 786440 | tf_op jit(solution)/shard_map/ppermute | solution.py:419
  61.2 10.7 %collective-permute-start.19 = (bf16[128,256]{1,0:T(8,128)(2,1)S(1)}, bf16[128,256]{1,0:T(8,128)(2,1)S(1)}, u32[]{:S(2)}, u32[]{:S(2)}) collective-permute-start(bf16[128,256]{1,0:T(8,128)(2,1)S(1)} %get-tuple-element.63), channel_id=1, source_target_pairs={{0,16},{16,0},{32,48},{48,32},{1,17},{17,1},{33,49},{49,33},{2,18}... | collective-permute-start | bytes 196616 | tf_op jit(solution)/shard_map/ppermute | solution.py:429
  62.3 9.5 %collective-permute-start.21 = (bf16[128,256]{1,0:T(8,128)(2,1)S(1)}, bf16[128,256]{1,0:T(8,128)(2,1)S(1)}, u32[]{:S(2)}, u32[]{:S(2)}) collective-permute-start(bf16[128,256]{1,0:T(8,128)(2,1)S(1)} %get-tuple-element.64), channel_id=1, source_target_pairs={{0,48},{16,32},{32,16},{48,0},{1,49},{17,33},{33,17},{49,1},{2,50}... | collective-permute-start | bytes 196616 | tf_op jit(solution)/shard_map/ppermute | solution.py:429
  63.9 8.0 %collective-permute-start.20 = (bf16[128,256]{1,0:T(8,128)(2,1)S(1)}, bf16[128,256]{1,0:T(8,128)(2,1)S(1)}, u32[]{:S(2)}, u32[]{:S(2)}) collective-permute-start(bf16[128,256]{1,0:T(8,128)(2,1)S(1)} %get-tuple-element.65), channel_id=1, source_target_pairs={{0,32},{16,48},{32,0},{48,16},{1,33},{17,49},{33,1},{49,17},{2,34}... | collective-permute-start | bytes 196616 | tf_op jit(solution)/shard_map/ppermute | solution.py:429
  65.8 19.5 %collective-permute-start.15 = (bf16[16,8192]{1,0:T(8,128)(2,1)S(1)}, bf16[16,8192]{1,0:T(8,128)(2,1)S(1)}, u32[]{:S(2)}, u32[]{:S(2)}) collective-permute-start(bf16[16,8192]{1,0:T(8,128)(2,1)S(1)} %get-tuple-element.58), channel_id=1, source_target_pairs={{0,4},{4,0},{1,5},{5,1},{2,6},{6,2},{3,7},{7,3},{8,12},{12,8},{9,1... | collective-permute-start | bytes 786440 | tf_op jit(solution)/shard_map/ppermute | solution.py:429

commit v7 on v6

--- a/solution.py
+++ b/solution.py
@@ -313,7 +313,8 @@
     )(front, back, from_behind, from_ahead, token)
 
 
-def settle_kernel(own, from_behind, from_ahead, front, back, keep_ref, give_ref):
+def settle_kernel(own, from_behind, from_ahead, front, back, *refs):
+    keep_ref, give_ref = refs[-2:]
     half = front.shape[1]
     rows = keep_ref.shape[0]
     for index in range(half // MIX_SPAN):
@@ -325,16 +326,55 @@
             give_ref[:, where] = total[rows:]
 
 
-def settle(own, from_behind, from_ahead, front, back):
+def settle(own, from_behind, from_ahead, front, back, *tokens):
     shape = jax.ShapeDtypeStruct((own.shape[0] // NH, own.shape[1]), own.dtype)
     return pl.pallas_call(
         settle_kernel,
         out_shape=(shape, shape),
-        in_specs=[VMEM] * 5,
+        in_specs=[VMEM] * 5 + [ANY] * len(tokens),
         out_specs=[VMEM] * 2,
         compiler_params=pltpu.CompilerParams(vmem_limit_bytes=8 * MIB),
         name="settle",
-    )(own, from_behind, from_ahead, front, back)
+    )(own, from_behind, from_ahead, front, back, *tokens)
+
+
+def share_kernel(token_ref, near, *refs):
+    others, terms = refs[:NX - 1], refs[NX - 1:]
+    for index, term in enumerate(terms):
+        at = slice(index * term.shape[0], (index + 1) * term.shape[0])
+        term[...] = added(near[at, :], *[other[at, :] for other in others])
+
+
+def share(token, near, *others):
+    term = jax.ShapeDtypeStruct((near.shape[0] // NZ, near.shape[1]), near.dtype)
+    return pl.pallas_call(
+        share_kernel,
+        out_shape=(term,) * NZ,
+        in_specs=[ANY] + [VMEM] * (1 + len(others)),
+        out_specs=[VMEM] * NZ,
+        compiler_params=pltpu.CompilerParams(vmem_limit_bytes=8 * MIB),
+        cost_estimate=pl.CostEstimate(flops=BWD_FLOPS, bytes_accessed=2 * 10**6, transcendentals=0),
+        name="share",
+    )(token, near, *others)
+
+
+def finish_kernel(token_ref, *refs):
+    *parts, k_ref, v_ref = refs
+    total = added(*[part[...] for part in parts])
+    k_ref[...] = total[:, :HD]
+    v_ref[...] = total[:, HD:]
+
+
+def finish(token, *parts):
+    shape = jax.ShapeDtypeStruct((parts[0].shape[0], HD), parts[0].dtype)
+    return pl.pallas_call(
+        finish_kernel,
+        out_shape=(shape, shape),
+        in_specs=[ANY] + [VMEM] * len(parts),
+        out_specs=[VMEM] * 2,
+        compiler_params=pltpu.CompilerParams(vmem_limit_bytes=4 * MIB),
+        name="finish",
+    )(token, *parts)
 
 
 def stack_kernel(token_ref, *refs):
@@ -451,15 +491,15 @@
     q_grad, keep = backward(0, plan, near_probs, near_kv, qs, ds, delta, near_inv, partial)
     term = total_of([keep, across(give, "core", 1)])
     front, back = relay(front, back, from_behind, from_ahead, term)
-    mixed, give = settle(own, from_behind, from_ahead, ahead(front, "y", 1), ahead(back, "y", NY - 1))
+    part = term.shape[0] // NX
+    near, *others = [term[step * part:(step + 1) * part] for step in range(NX)]
+    others = [ahead(other, "x", step + 1) for step, other in enumerate(others)]
+    mixed, give = settle(
+        own, from_behind, from_ahead, ahead(front, "y", 1), ahead(back, "y", NY - 1), *others)
+    terms = share(mixed, near, *others)
     mixed = total_of([mixed, across(give, "zh", 1)])
-    part = term.shape[0] // NX
-    term = total_of([term[:part]] + [
-        ahead(term[step * part:(step + 1) * part], "x", step) for step in range(1, NX)])
-    part = term.shape[0] // NZ
-    term = total_of([term[:part]] + [
-        across(term[step * part:(step + 1) * part], "zl", step) for step in range(1, NZ)])
-    return mixed, q_grad, term[:, :HD], term[:, HD:]
+    k_grad, v_grad = finish(mixed, terms[0], *[across(terms[step], "zl", step) for step in range(1, NZ)])
+    return mixed, q_grad, k_grad, v_grad
 
 
 def solution(mesh):

time: 86.4 us -> 87.7 us (1.015)
  the two profiles are of different devices: /device:TPU:38 before, /device:TPU:1 now
where the time goes in v7:
time: 87.7 us; the launch traced here: 87.1 us
  starting transfers between devices  36.7 us (42%)
  waiting for transfers between devices  26.9 us (31%)
  Pallas kernels  17.9 us (20%)
  local copies, waits for them, and re-layouts  4.53 us (5%)
    ppermute x12, starting transfers between devices, across(): return lax.ppermute(block, axis, [(i, i ^ step) for i in range(count)])  23.4 us
    ppermute x12, waiting for transfers between devices, across(): return lax.ppermute(block, axis, [(i, i ^ step) for i in range(count)])  13.4 us
    ppermute x7, waiting for transfers between devices, ahead(): lax.ppermute(block, axis, [(i, (i + step) % count) for i in range(count)])  11.5 us
    ppermute x7, starting transfers between devices, ahead(): lax.ppermute(block, axis, [(i, (i + step) % count) for i in range(count)])  8.69 us
    pallas_call x2, Pallas kernels, backward(): pl.pallas_call(functools.partial(bwd_kernel, stretch, side), out_shape=(s...  6.91 us
    pallas_call x2, Pallas kernels, forward(): pl.pallas_call(functools.partial(far_kernel if side else near_kernel, str...  6.01 us
    ppermute x3, starting transfers between devices, behind(): lax.ppermute(block, axis, [((i + step) % count, i) for i in range(count)])  4.57 us
    unnamed x12, local copies, waits for them, and re-layouts  4.46 us
  transfers between devices with their start and end apart: 22, of which 9 were waited for; matrix products, arithmetic and copies ran while one was open for 1% of the time, Pallas kernels for 14%

profile of v7, /device:TPU:1, one launch (start us, length us, event | category | flops | bytes accessed | tf_op | source)
XLA Modules:
  0.0 87.1 jit_solution(3892090407307132923)
XLA Ops:
  0.6 1.4 %pair.1.kv_ref = bf16[128,256]{1,0:T(8,128)(2,1)} custom-call(bf16[128,128]{1,0:T(8,128)(2,1)} %k_hbm.1, bf16[128,128]{1,0:T(8,128)(2,1)} %v_hbm.1), custom_call_target="tpu_custom_call" | custom-call | tf_op jit(solution)/shard_map/pair/pallas_call | solution.py:251
  2.1 5.3 %collective-permute-start.2 = (bf16[128,256]{1,0:T(8,128)(2,1)}, bf16[128,256]{1,0:T(8,128)(2,1)S(1)}, u32[]{:S(2)}, u32[]{:S(2)}) collective-permute-start(bf16[128,256]{1,0:T(8,128)(2,1)} %pair.1.kv_ref), channel_id=1, source_target_pairs={{0,48},{16,32},{32,16},{48,0},{1,49},{17,33},{33,17},{49,1},{2,50}... | collective-permute-start | bytes 196616 | tf_op jit(solution)/shard_map/ppermute | solution.py:469
  8.6 0.9 %copy-done.2 = bf16[128,512]{1,0:T(8,128)(2,1)S(1)} copy-done((bf16[128,512]{1,0:T(8,128)(2,1)S(1)}, bf16[128,512]{1,0:T(8,128)(2,1)}, u32[]{:S(2)}) %copy-start.2) | copy-done | bytes 131096
  10.6 2.1 %collective-permute-done.1.refs_2_ = bf16[128,256]{1,0:T(8,128)(2,1)S(1)} collective-permute-done((bf16[128,256]{1,0:T(8,128)(2,1)}, bf16[128,256]{1,0:T(8,128)(2,1)S(1)}, u32[]{:S(2)}, u32[]{:S(2)}) %collective-permute-start.1) | collective-permute-done | bytes 65568 | tf_op jit(solution)/shard_map/ppermute | solution.py:469
  12.8 1.0 %collective-permute-start.8 = (bf16[512,256]{1,0:T(8,128)(2,1)S(1)}, bf16[512,256]{1,0:T(8,128)(2,1)S(1)}, u32[]{:S(2)}, u32[]{:S(2)}) collective-permute-start(bf16[512,256]{1,0:T(8,128)(2,1)S(1)} %stack.1.piece_ref.rest_0_), channel_id=1, source_target_pairs={{192,0},{0,64},{64,128},{128,192},{193,1},{1,65},{65,129},{129,193... | collective-permute-start | bytes 786440 | tf_op jit(solution)/shard_map/ppermute | solution.py:464
  13.7 2.5 %collective-permute-start.6 = (bf16[512,256]{1,0:T(8,128)(2,1)S(1)}, bf16[512,256]{1,0:T(8,128)(2,1)S(1)}, u32[]{:S(2)}, u32[]{:S(2)}) collective-permute-start(bf16[512,256]{1,0:T(8,128)(2,1)S(1)} %stack.1.piece_ref.rest_0_), channel_id=1, source_target_pairs={{128,0},{192,64},{0,128},{64,192},{129,1},{193,65},{1,129},{65,193... | collective-permute-start | bytes 786440 | tf_op jit(solution)/shard_map/ppermute | solution.py:464
  16.2 1.2 %collective-permute-start.4 = (bf16[512,256]{1,0:T(8,128)(2,1)S(1)}, bf16[512,256]{1,0:T(8,128)(2,1)S(1)}, u32[]{:S(2)}, u32[]{:S(2)}) collective-permute-start(bf16[512,256]{1,0:T(8,128)(2,1)S(1)} %stack.1.piece_ref.rest_0_), channel_id=1, source_target_pairs={{64,0},{128,64},{192,128},{0,192},{65,1},{129,65},{193,129},{1,193... | collective-permute-start | bytes 786440 | tf_op jit(solution)/shard_map/ppermute | solution.py:464
  18.0 2.2 %stage.1 = (s32[136]{0:T(256)S(1)}, bf16[512,256]{1,0:T(8,128)(2,1)S(1)}) custom-call(s32[64]{0:T(128)S(1)} %copy-done.4, bf16[512,256]{1,0:T(8,128)(2,1)S(1)} %stack.1.piece_ref.rest_0_), custom_call_target="tpu_custom_call" | custom-call | tf_op jit(solution)/shard_map/stage/pallas_call | solution.py:278
  20.2 2.7 %collective-permute-start.3 = (bf16[512,256]{1,0:T(8,128)(2,1)S(1)}, bf16[512,256]{1,0:T(8,128)(2,1)S(1)}, u32[]{:S(2)}, u32[]{:S(2)}) collective-permute-start(bf16[512,256]{1,0:T(8,128)(2,1)S(1)} %get-tuple-element.41), channel_id=1, source_target_pairs={{0,8},{8,0},{1,9},{9,1},{2,10},{10,2},{3,11},{11,3},{4,12},{12,4},... | collective-permute-start | bytes 786440 | tf_op jit(solution)/shard_map/ppermute | solution.py:469
  22.8 1.5 %collective-permute-start.9 = (bf16[512,256]{1,0:T(8,128)(2,1)S(1)}, bf16[512,256]{1,0:T(8,128)(2,1)S(1)}, u32[]{:S(2)}, u32[]{:S(2)}) collective-permute-start(bf16[512,256]{1,0:T(8,128)(2,1)S(1)} %collective-permute-done.8.rest_3_), channel_id=1, source_target_pairs={{0,8},{8,0},{1,9},{9,1},{2,10},{10,2},{3,11},{11,3},{4,12},{12,4},... | collective-permute-start | bytes 786440 | tf_op jit(solution)/shard_map/ppermute | solution.py:469
  24.4 2.0 %collective-permute-done.6.rest_2_ = bf16[512,256]{1,0:T(8,128)(2,1)S(1)} collective-permute-done((bf16[512,256]{1,0:T(8,128)(2,1)S(1)}, bf16[512,256]{1,0:T(8,128)(2,1)S(1)}, u32[]{:S(2)}, u32[]{:S(2)}) %collective-permute-start.6) | collective-permute-done | bytes 262176 | tf_op jit(solution)/shard_map/ppermute | solution.py:464
  26.4 2.7 %collective-permute-start.7 = (bf16[512,256]{1,0:T(8,128)(2,1)S(1)}, bf16[512,256]{1,0:T(8,128)(2,1)S(1)}, u32[]{:S(2)}, u32[]{:S(2)}) collective-permute-start(bf16[512,256]{1,0:T(8,128)(2,1)S(1)} %collective-permute-done.6.rest_2_), channel_id=1, source_target_pairs={{0,8},{8,0},{1,9},{9,1},{2,10},{10,2},{3,11},{11,3},{4,12},{12,4},... | collective-permute-start | bytes 786440 | tf_op jit(solution)/shard_map/ppermute | solution.py:469
  29.1 2.2 %attention_forward_0.1 = (bf16[9,256,256]{2,1,0:T(8,128)(2,1)S(1)}, bf16[2048,256]{1,0:T(8,128)(2,1)S(1)}, f32[2,8,256]{2,1,0:T(8,128)S(1)}, f32[2,8,256]{2,1,0:T(8,128)S(1)}, f32[2,128,256]{2,1,0:T(8,128)S(1)}) custom-call(s32[136]{0:T(256)S(1)} %get-tuple-element.40.plan_ref, bf16[2,256,128]{2,1,0:T(8,128)(2,1)S(1)} %get-tuple-element.38.token_ref.qs_ref, ...), custom_call_target="tpu_custom_call" | custom-call | flops 3000000000 | bytes 8000000 | tf_op jit(solution)/shard_map/attention_forward_0/pallas_call | solution.py:420
  31.3 1.1 %copy-done.5 = bf16[512,8192]{1,0:T(8,128)(2,1)S(1)} copy-done((bf16[512,8192]{1,0:T(8,128)(2,1)S(1)}, bf16[512,8192]{1,0:T(8,128)(2,1)}, u32[]{:S(2)}) %copy-start.5) | copy-done | bytes 8388632
  32.4 3.8 %attention_forward_1.1 = (bf16[32,8192]{1,0:T(8,128)(2,1)S(1)}, bf16[32,4096]{1,0:T(8,128)(2,1)S(1)}, bf16[32,4096]{1,0:T(8,128)(2,1)S(1)}, bf16[32,8192]{1,0:T(...) custom-call(s32[136]{0:T(256)S(1)} %get-tuple-element.40.plan_ref, ...), custom_call_target="tpu_custom_call" | custom-call | flops 3000000000 | bytes 8000000 | tf_op jit(solution)/shard_map/attention_forward_1/pallas_call | solution.py:420
  36.2 1.6 %collective-permute-start.10 = (bf16[32,8192]{1,0:T(8,128)(2,1)S(1)}, bf16[32,8192]{1,0:T(8,128)(2,1)S(1)}, u32[]{:S(2)}, u32[]{:S(2)}) collective-permute-start(bf16[32,8192]{1,0:T(8,128)(2,1)S(1)} %get-tuple-element.47), channel_id=1, source_target_pairs={{0,1},{1,2},{2,3},{3,0},{4,5},{5,6},{6,7},{7,4},{8,9},{9,10},{10,1... | collective-permute-start | bytes 1572872 | tf_op jit(solution)/shard_map/ppermute | solution.py:459
  37.8 1.5 %collective-permute-start.11 = (bf16[32,8192]{1,0:T(8,128)(2,1)S(1)}, bf16[32,8192]{1,0:T(8,128)(2,1)S(1)}, u32[]{:S(2)}, u32[]{:S(2)}) collective-permute-start(bf16[32,8192]{1,0:T(8,128)(2,1)S(1)} %get-tuple-element.48), channel_id=1, source_target_pairs={{0,3},{1,0},{2,1},{3,2},{4,7},{5,4},{6,5},{7,6},{8,11},{9,8},{10,9... | collective-permute-start | bytes 1572872 | tf_op jit(solution)/shard_map/ppermute | solution.py:459
  39.3 3.1 %attention_backward_1.1 = (f32[2,128,256]{2,1,0:T(8,128)S(1)}, bf16[2048,256]{1,0:T(8,128)(2,1)S(1)}) custom-call(s32[136]{0:T(256)S(1)} %get-tuple-element.40.plan_ref, bf16[9,256,256]{2,1,0:T(8,128)(2,1)S(1)} %get-tuple-element.55.p_ref, bf16[2048,256]{1,0:T(8,128)(2,1)S(1)} %get-tuple-element.56.kv_ref, ...), custom_call_target="tpu_custom_call" | custom-call | flops 20000000000 | bytes 8000000 | tf_op jit(solution)/shard_map/attention_backward_1/pallas_call | solution.py:445
  42.4 1.0 %collective-permute-start.12 = (bf16[2048,256]{1,0:T(8,128)(2,1)S(1)}, bf16[2048,256]{1,0:T(8,128)(2,1)S(1)}, u32[]{:S(2)}, u32[]{:S(2)}) collective-permute-start(bf16[2048,256]{1,0:T(8,128)(2,1)S(1)} %get-tuple-element.60), channel_id=1, source_target_pairs={{0,8},{8,0},{1,9},{9,1},{2,10},{10,2},{3,11},{11,3},{4,12},{12,4},... | collective-permute-start | bytes 3145736 | tf_op jit(solution)/shard_map/ppermute | solution.py:469
  43.4 3.8 %attention_backward_0.1 = (bf16[128,512]{1,0:T(8,128)(2,1)}, bf16[2048,256]{1,0:T(8,128)(2,1)S(1)}) custom-call(s32[136]{0:T(256)S(1)} %get-tuple-element.40.plan_ref, bf16[9,256,256]{2,1,0:T(8,128)(2,1)S(1)} %get-tuple-element.51.p_ref, bf16[2048,256]{1,0:T(8,128)(2,1)S(1)} %get-tuple-element.52.kv_ref, ...), custom_call_target="tpu_custom_call" | custom-call | flops 20000000000 | bytes 8000000 | tf_op jit(solution)/shard_map/attention_backward_0/pallas_call | solution.py:445
  47.6 1.9 %collective-permute-start.17 = (bf16[512,256]{1,0:T(8,128)(2,1)S(1)}, bf16[512,256]{1,0:T(8,128)(2,1)S(1)}, u32[]{:S(2)}, u32[]{:S(2)}) collective-permute-start(bf16[512,256]{1,0:T(8,128)(2,1)S(1)} %get-tuple-element.73), channel_id=1, source_target_pairs={{0,192},{64,0},{128,64},{192,128},{1,193},{65,1},{129,65},{193,129... | collective-permute-start | bytes 786440 | tf_op jit(solution)/shard_map/ppermute | solution.py:459
  51.0 1.0 %collective-permute-start.13 = (bf16[32,4096]{1,0:T(8,128)(2,1)S(1)}, bf16[32,4096]{1,0:T(8,128)(2,1)S(1)}, u32[]{:S(2)}, u32[]{:S(2)}) collective-permute-start(bf16[32,4096]{1,0:T(8,128)(2,1)S(1)} %get-tuple-element.61), channel_id=1, source_target_pairs={{0,1},{1,2},{2,3},{3,0},{4,5},{5,6},{6,7},{7,4},{8,9},{9,10},{10,1... | collective-permute-start | bytes 786440 | tf_op jit(solution)/shard_map/ppermute | solution.py:459
  52.0 1.8 %collective-permute-start.14 = (bf16[32,4096]{1,0:T(8,128)(2,1)S(1)}, bf16[32,4096]{1,0:T(8,128)(2,1)S(1)}, u32[]{:S(2)}, u32[]{:S(2)}) collective-permute-start(bf16[32,4096]{1,0:T(8,128)(2,1)S(1)} %get-tuple-element.62), channel_id=1, source_target_pairs={{0,3},{1,0},{2,1},{3,2},{4,7},{5,4},{6,5},{7,6},{8,11},{9,8},{10,9... | collective-permute-start | bytes 786440 | tf_op jit(solution)/shard_map/ppermute | solution.py:459
  53.7 1.9 %collective-permute-done.17.refs_2_ = bf16[512,256]{1,0:T(8,128)(2,1)S(1)} collective-permute-done((bf16[512,256]{1,0:T(8,128)(2,1)S(1)}, bf16[512,256]{1,0:T(8,128)(2,1)S(1)}, u32[]{:S(2)}, u32[]{:S(2)}) %collective-permute-start.17) | collective-permute-done | bytes 262176 | tf_op jit(solution)/shard_map/ppermute | solution.py:459
  55.6 3.0 %collective-permute-done.16.refs_1_ = bf16[512,256]{1,0:T(8,128)(2,1)S(1)} collective-permute-done((bf16[512,256]{1,0:T(8,128)(2,1)S(1)}, bf16[512,256]{1,0:T(8,128)(2,1)S(1)}, u32[]{:S(2)}, u32[]{:S(2)}) %collective-permute-start.16) | collective-permute-done | bytes 262176 | tf_op jit(solution)/shard_map/ppermute | solution.py:459
  58.7 6.2 %collective-permute-done.15.refs_0_ = bf16[512,256]{1,0:T(8,128)(2,1)S(1)} collective-permute-done((bf16[512,256]{1,0:T(8,128)(2,1)S(1)}, bf16[512,256]{1,0:T(8,128)(2,1)S(1)}, u32[]{:S(2)}, u32[]{:S(2)}) %collective-permute-start.15) | collective-permute-done | bytes 262176 | tf_op jit(solution)/shard_map/ppermute | solution.py:459
  65.1 6.3 %collective-permute-start.18 = (bf16[16,8192]{1,0:T(8,128)(2,1)S(1)}, bf16[16,8192]{1,0:T(8,128)(2,1)S(1)}, u32[]{:S(2)}, u32[]{:S(2)}) collective-permute-start(bf16[16,8192]{1,0:T(8,128)(2,1)S(1)} %get-tuple-element.64), channel_id=1, source_target_pairs={{0,4},{4,0},{1,5},{5,1},{2,6},{6,2},{3,7},{7,3},{8,12},{12,8},{9,1... | collective-permute-start | bytes 786440 | tf_op jit(solution)/shard_map/ppermute | solution.py:469
  71.6 1.9 %collective-permute-start.20 = (bf16[128,256]{1,0:T(8,128)(2,1)S(1)}, bf16[128,256]{1,0:T(8,128)(2,1)S(1)}, u32[]{:S(2)}, u32[]{:S(2)}) collective-permute-start(bf16[128,256]{1,0:T(8,128)(2,1)S(1)} %get-tuple-element.68), channel_id=1, source_target_pairs={{0,32},{16,48},{32,0},{48,16},{1,33},{17,49},{33,1},{49,17},{2,34}... | collective-permute-start | bytes 196616 | tf_op jit(solution)/shard_map/ppermute | solution.py:469
  73.5 1.6 %collective-permute-start.21 = (bf16[128,256]{1,0:T(8,128)(2,1)S(1)}, bf16[128,256]{1,0:T(8,128)(2,1)S(1)}, u32[]{:S(2)}, u32[]{:S(2)}) collective-permute-start(bf16[128,256]{1,0:T(8,128)(2,1)S(1)} %get-tuple-element.69), channel_id=1, source_target_pairs={{0,48},{16,32},{32,16},{48,0},{1,49},{17,33},{33,17},{49,1},{2,50}... | collective-permute-start | bytes 196616 | tf_op jit(solution)/shard_map/ppermute | solution.py:469
  75.2 7.4 %collective-permute-done.18 = bf16[16,8192]{1,0:T(8,128)(2,1)S(1)} collective-permute-done((bf16[16,8192]{1,0:T(8,128)(2,1)S(1)}, bf16[16,8192]{1,0:T(8,128)(2,1)S(1)}, u32[]{:S(2)}, u32[]{:S(2)}) %collective-permute-start.18) | collective-permute-done | bytes 262176 | tf_op jit(solution)/shard_map/ppermute | solution.py:469
  82.7 2.9 %collective-permute-done.20.refs_2_ = bf16[128,256]{1,0:T(8,128)(2,1)S(1)} collective-permute-done((bf16[128,256]{1,0:T(8,128)(2,1)S(1)}, bf16[128,256]{1,0:T(8,128)(2,1)S(1)}, u32[]{:S(2)}, u32[]{:S(2)}) %collective-permute-start.20) | collective-permute-done | bytes 65568 | tf_op jit(solution)/shard_map/ppermute | solution.py:469
  85.5 0.9 %collective-permute-done.21.refs_3_ = bf16[128,256]{1,0:T(8,128)(2,1)S(1)} collective-permute-done((bf16[128,256]{1,0:T(8,128)(2,1)S(1)}, bf16[128,256]{1,0:T(8,128)(2,1)S(1)}, u32[]{:S(2)}, u32[]{:S(2)}) %collective-permute-start.21) | collective-permute-done | bytes 65568 | tf_op jit(solution)/shard_map/ppermute | solution.py:469
  (39 shorter events, 6.1 us)
Async XLA Ops:
  2.1 8.6 %collective-permute-start.2 = (bf16[128,256]{1,0:T(8,128)(2,1)}, bf16[128,256]{1,0:T(8,128)(2,1)S(1)}, u32[]{:S(2)}, u32[]{:S(2)}) collective-permute-start(bf16[128,256]{1,0:T(8,128)(2,1)} %pair.1.kv_ref), channel_id=1, source_target_pairs={{0,48},{16,32},{32,16},{48,0},{1,49},{17,33},{33,17},{49,1},{2,50}... | collective-permute-start | bytes 196616 | tf_op jit(solution)/shard_map/ppermute | solution.py:469
  7.3 5.4 %collective-permute-start.1 = (bf16[128,256]{1,0:T(8,128)(2,1)}, bf16[128,256]{1,0:T(8,128)(2,1)S(1)}, u32[]{:S(2)}, u32[]{:S(2)}) collective-permute-start(bf16[128,256]{1,0:T(8,128)(2,1)} %pair.1.kv_ref), channel_id=1, source_target_pairs={{0,32},{16,48},{32,0},{48,16},{1,33},{17,49},{33,1},{49,17},{2,34}... | collective-permute-start | bytes 196616 | tf_op jit(solution)/shard_map/ppermute | solution.py:469
  7.3 5.4 %collective-permute-start = (bf16[128,256]{1,0:T(8,128)(2,1)}, bf16[128,256]{1,0:T(8,128)(2,1)S(1)}, u32[]{:S(2)}, u32[]{:S(2)}) collective-permute-start(bf16[128,256]{1,0:T(8,128)(2,1)} %pair.1.kv_ref), channel_id=1, source_target_pairs={{0,16},{16,0},{32,48},{48,32},{1,17},{17,1},{33,49},{49,33},{2,18}... | collective-permute-start | bytes 196616 | tf_op jit(solution)/shard_map/ppermute | solution.py:469
  7.7 0.9 %copy-start.1 = (bf16[128,256]{1,0:T(8,128)(2,1)S(1)}, bf16[128,256]{1,0:T(8,128)(2,1)}, u32[]{:S(2)}) copy-start(bf16[128,256]{1,0:T(8,128)(2,1)} %pair.1.kv_ref) | copy-start | bytes 196612
  8.6 0.9 %copy-start.2 = (bf16[128,512]{1,0:T(8,128)(2,1)S(1)}, bf16[128,512]{1,0:T(8,128)(2,1)}, u32[]{:S(2)}) copy-start(bf16[128,512]{1,0:T(8,128)(2,1)} %q_hbm.1) | copy-start | bytes 393220
  9.5 0.9 %copy-start.3 = (bf16[128,512]{1,0:T(8,128)(2,1)S(1)}, bf16[128,512]{1,0:T(8,128)(2,1)}, u32[]{:S(2)}) copy-start(bf16[128,512]{1,0:T(8,128)(2,1)} %do_hbm.1) | copy-start | bytes 393220
  12.8 10.1 %collective-permute-start.8 = (bf16[512,256]{1,0:T(8,128)(2,1)S(1)}, bf16[512,256]{1,0:T(8,128)(2,1)S(1)}, u32[]{:S(2)}, u32[]{:S(2)}) collective-permute-start(bf16[512,256]{1,0:T(8,128)(2,1)S(1)} %stack.1.piece_ref.rest_0_), channel_id=1, source_target_pairs={{192,0},{0,64},{64,128},{128,192},{193,1},{1,65},{65,129},{129,193... | collective-permute-start | bytes 786440 | tf_op jit(solution)/shard_map/ppermute | solution.py:464
  13.7 12.7 %collective-permute-start.6 = (bf16[512,256]{1,0:T(8,128)(2,1)S(1)}, bf16[512,256]{1,0:T(8,128)(2,1)S(1)}, u32[]{:S(2)}, u32[]{:S(2)}) collective-permute-start(bf16[512,256]{1,0:T(8,128)(2,1)S(1)} %stack.1.piece_ref.rest_0_), channel_id=1, source_target_pairs={{128,0},{192,64},{0,128},{64,192},{129,1},{193,65},{1,129},{65,193... | collective-permute-start | bytes 786440 | tf_op jit(solution)/shard_map/ppermute | solution.py:464
  16.2 12.9 %collective-permute-start.4 = (bf16[512,256]{1,0:T(8,128)(2,1)S(1)}, bf16[512,256]{1,0:T(8,128)(2,1)S(1)}, u32[]{:S(2)}, u32[]{:S(2)}) collective-permute-start(bf16[512,256]{1,0:T(8,128)(2,1)S(1)} %stack.1.piece_ref.rest_0_), channel_id=1, source_target_pairs={{64,0},{128,64},{192,128},{0,192},{65,1},{129,65},{193,129},{1,193... | collective-permute-start | bytes 786440 | tf_op jit(solution)/shard_map/ppermute | solution.py:464
  17.3 0.7 copy-start.4
  20.2 11.1 %collective-permute-start.3 = (bf16[512,256]{1,0:T(8,128)(2,1)S(1)}, bf16[512,256]{1,0:T(8,128)(2,1)S(1)}, u32[]{:S(2)}, u32[]{:S(2)}) collective-permute-start(bf16[512,256]{1,0:T(8,128)(2,1)S(1)} %get-tuple-element.41), channel_id=1, source_target_pairs={{0,8},{8,0},{1,9},{9,1},{2,10},{10,2},{3,11},{11,3},{4,12},{12,4},... | collective-permute-start | bytes 786440 | tf_op jit(solution)/shard_map/ppermute | solution.py:469
  22.8 8.4 %collective-permute-start.9 = (bf16[512,256]{1,0:T(8,128)(2,1)S(1)}, bf16[512,256]{1,0:T(8,128)(2,1)S(1)}, u32[]{:S(2)}, u32[]{:S(2)}) collective-permute-start(bf16[512,256]{1,0:T(8,128)(2,1)S(1)} %collective-permute-done.8.rest_3_), channel_id=1, source_target_pairs={{0,8},{8,0},{1,9},{9,1},{2,10},{10,2},{3,11},{11,3},{4,12},{12,4},... | collective-permute-start | bytes 786440 | tf_op jit(solution)/shard_map/ppermute | solution.py:469
  26.4 4.9 %collective-permute-start.7 = (bf16[512,256]{1,0:T(8,128)(2,1)S(1)}, bf16[512,256]{1,0:T(8,128)(2,1)S(1)}, u32[]{:S(2)}, u32[]{:S(2)}) collective-permute-start(bf16[512,256]{1,0:T(8,128)(2,1)S(1)} %collective-permute-done.6.rest_2_), channel_id=1, source_target_pairs={{0,8},{8,0},{1,9},{9,1},{2,10},{10,2},{3,11},{11,3},{4,12},{12,4},... | collective-permute-start | bytes 786440 | tf_op jit(solution)/shard_map/ppermute | solution.py:469
  29.0 2.3 %collective-permute-start.5 = (bf16[512,256]{1,0:T(8,128)(2,1)S(1)}, bf16[512,256]{1,0:T(8,128)(2,1)S(1)}, u32[]{:S(2)}, u32[]{:S(2)}) collective-permute-start(bf16[512,256]{1,0:T(8,128)(2,1)S(1)} %collective-permute-done.4.rest_1_), channel_id=1, source_target_pairs={{0,8},{8,0},{1,9},{9,1},{2,10},{10,2},{3,11},{11,3},{4,12},{12,4},... | collective-permute-start | bytes 786440 | tf_op jit(solution)/shard_map/ppermute | solution.py:469
  29.1 3.4 %copy-start.5 = (bf16[512,8192]{1,0:T(8,128)(2,1)S(1)}, bf16[512,8192]{1,0:T(8,128)(2,1)}, u32[]{:S(2)}) copy-start(bf16[512,8192]{1,0:T(8,128)(2,1)} %rest_5_.1) | copy-start | bytes 25165828
  36.2 14.6 %collective-permute-start.10 = (bf16[32,8192]{1,0:T(8,128)(2,1)S(1)}, bf16[32,8192]{1,0:T(8,128)(2,1)S(1)}, u32[]{:S(2)}, u32[]{:S(2)}) collective-permute-start(bf16[32,8192]{1,0:T(8,128)(2,1)S(1)} %get-tuple-element.47), channel_id=1, source_target_pairs={{0,1},{1,2},{2,3},{3,0},{4,5},{5,6},{6,7},{7,4},{8,9},{9,10},{10,1... | collective-permute-start | bytes 1572872 | tf_op jit(solution)/shard_map/ppermute | solution.py:459
  37.8 13.0 %collective-permute-start.11 = (bf16[32,8192]{1,0:T(8,128)(2,1)S(1)}, bf16[32,8192]{1,0:T(8,128)(2,1)S(1)}, u32[]{:S(2)}, u32[]{:S(2)}) collective-permute-start(bf16[32,8192]{1,0:T(8,128)(2,1)S(1)} %get-tuple-element.48), channel_id=1, source_target_pairs={{0,3},{1,0},{2,1},{3,2},{4,7},{5,4},{6,5},{7,6},{8,11},{9,8},{10,9... | collective-permute-start | bytes 1572872 | tf_op jit(solution)/shard_map/ppermute | solution.py:459
  42.4 4.8 %collective-permute-start.12 = (bf16[2048,256]{1,0:T(8,128)(2,1)S(1)}, bf16[2048,256]{1,0:T(8,128)(2,1)S(1)}, u32[]{:S(2)}, u32[]{:S(2)}) collective-permute-start(bf16[2048,256]{1,0:T(8,128)(2,1)S(1)} %get-tuple-element.60), channel_id=1, source_target_pairs={{0,8},{8,0},{1,9},{9,1},{2,10},{10,2},{3,11},{11,3},{4,12},{12,4},... | collective-permute-start | bytes 3145736 | tf_op jit(solution)/shard_map/ppermute | solution.py:469
  47.6 8.0 %collective-permute-start.17 = (bf16[512,256]{1,0:T(8,128)(2,1)S(1)}, bf16[512,256]{1,0:T(8,128)(2,1)S(1)}, u32[]{:S(2)}, u32[]{:S(2)}) collective-permute-start(bf16[512,256]{1,0:T(8,128)(2,1)S(1)} %get-tuple-element.73), channel_id=1, source_target_pairs={{0,192},{64,0},{128,64},{192,128},{1,193},{65,1},{129,65},{193,129... | collective-permute-start | bytes 786440 | tf_op jit(solution)/shard_map/ppermute | solution.py:459
  49.5 9.1 %collective-permute-start.16 = (bf16[512,256]{1,0:T(8,128)(2,1)S(1)}, bf16[512,256]{1,0:T(8,128)(2,1)S(1)}, u32[]{:S(2)}, u32[]{:S(2)}) collective-permute-start(bf16[512,256]{1,0:T(8,128)(2,1)S(1)} %get-tuple-element.74), channel_id=1, source_target_pairs={{0,128},{64,192},{128,0},{192,64},{1,129},{65,193},{129,1},{193,65... | collective-permute-start | bytes 786440 | tf_op jit(solution)/shard_map/ppermute | solution.py:459
  50.4 14.5 %collective-permute-start.15 = (bf16[512,256]{1,0:T(8,128)(2,1)S(1)}, bf16[512,256]{1,0:T(8,128)(2,1)S(1)}, u32[]{:S(2)}, u32[]{:S(2)}) collective-permute-start(bf16[512,256]{1,0:T(8,128)(2,1)S(1)} %get-tuple-element.75), channel_id=1, source_target_pairs={{0,64},{64,128},{128,192},{192,0},{1,65},{65,129},{129,193},{193,1... | collective-permute-start | bytes 786440 | tf_op jit(solution)/shard_map/ppermute | solution.py:459
  51.0 13.9 %collective-permute-start.13 = (bf16[32,4096]{1,0:T(8,128)(2,1)S(1)}, bf16[32,4096]{1,0:T(8,128)(2,1)S(1)}, u32[]{:S(2)}, u32[]{:S(2)}) collective-permute-start(bf16[32,4096]{1,0:T(8,128)(2,1)S(1)} %get-tuple-element.61), channel_id=1, source_target_pairs={{0,1},{1,2},{2,3},{3,0},{4,5},{5,6},{6,7},{7,4},{8,9},{9,10},{10,1... | collective-permute-start | bytes 786440 | tf_op jit(solution)/shard_map/ppermute | solution.py:459
  52.0 12.9 %collective-permute-start.14 = (bf16[32,4096]{1,0:T(8,128)(2,1)S(1)}, bf16[32,4096]{1,0:T(8,128)(2,1)S(1)}, u32[]{:S(2)}, u32[]{:S(2)}) collective-permute-start(bf16[32,4096]{1,0:T(8,128)(2,1)S(1)} %get-tuple-element.62), channel_id=1, source_target_pairs={{0,3},{1,0},{2,1},{3,2},{4,7},{5,4},{6,5},{7,6},{8,11},{9,8},{10,9... | collective-permute-start | bytes 786440 | tf_op jit(solution)/shard_map/ppermute | solution.py:459
  65.1 17.5 %collective-permute-start.18 = (bf16[16,8192]{1,0:T(8,128)(2,1)S(1)}, bf16[16,8192]{1,0:T(8,128)(2,1)S(1)}, u32[]{:S(2)}, u32[]{:S(2)}) collective-permute-start(bf16[16,8192]{1,0:T(8,128)(2,1)S(1)} %get-tuple-element.64), channel_id=1, source_target_pairs={{0,4},{4,0},{1,5},{5,1},{2,6},{6,2},{3,7},{7,3},{8,12},{12,8},{9,1... | collective-permute-start | bytes 786440 | tf_op jit(solution)/shard_map/ppermute | solution.py:469
  71.5 11.2 %collective-permute-start.19 = (bf16[128,256]{1,0:T(8,128)(2,1)S(1)}, bf16[128,256]{1,0:T(8,128)(2,1)S(1)}, u32[]{:S(2)}, u32[]{:S(2)}) collective-permute-start(bf16[128,256]{1,0:T(8,128)(2,1)S(1)} %get-tuple-element.67), channel_id=1, source_target_pairs={{0,16},{16,0},{32,48},{48,32},{1,17},{17,1},{33,49},{49,33},{2,18}... | collective-permute-start | bytes 196616 | tf_op jit(solution)/shard_map/ppermute | solution.py:469
  71.6 13.9 %collective-permute-start.20 = (bf16[128,256]{1,0:T(8,128)(2,1)S(1)}, bf16[128,256]{1,0:T(8,128)(2,1)S(1)}, u32[]{:S(2)}, u32[]{:S(2)}) collective-permute-start(bf16[128,256]{1,0:T(8,128)(2,1)S(1)} %get-tuple-element.68), channel_id=1, source_target_pairs={{0,32},{16,48},{32,0},{48,16},{1,33},{17,49},{33,1},{49,17},{2,34}... | collective-permute-start | bytes 196616 | tf_op jit(solution)/shard_map/ppermute | solution.py:469
  73.5 12.9 %collective-permute-start.21 = (bf16[128,256]{1,0:T(8,128)(2,1)S(1)}, bf16[128,256]{1,0:T(8,128)(2,1)S(1)}, u32[]{:S(2)}, u32[]{:S(2)}) collective-permute-start(bf16[128,256]{1,0:T(8,128)(2,1)S(1)} %get-tuple-element.69), channel_id=1, source_target_pairs={{0,48},{16,32},{32,16},{48,0},{1,49},{17,33},{33,17},{49,1},{2,50}... | collective-permute-start | bytes 196616 | tf_op jit(solution)/shard_map/ppermute | solution.py:469
  82.7 4.5 %copy-start = (bf16[16,8192]{1,0:T(8,128)(2,1)}, bf16[16,8192]{1,0:T(8,128)(2,1)S(1)}, u32[]{:S(2)}) copy-start(bf16[16,8192]{1,0:T(8,128)(2,1)S(1)} %add_convert_fusion.1.token_ref) | copy-start | bytes 786436

commit v8 on v7

--- a/solution.py
+++ b/solution.py
@@ -495,7 +495,7 @@
     near, *others = [term[step * part:(step + 1) * part] for step in range(NX)]
     others = [ahead(other, "x", step + 1) for step, other in enumerate(others)]
     mixed, give = settle(
-        own, from_behind, from_ahead, ahead(front, "y", 1), ahead(back, "y", NY - 1), *others)
+        own, from_behind, from_ahead, ahead(front, "y", 1), ahead(back, "y", NY - 1))
     terms = share(mixed, near, *others)
     mixed = total_of([mixed, across(give, "zh", 1)])
     k_grad, v_grad = finish(mixed, terms[0], *[across(terms[step], "zl", step) for step in range(1, NZ)])

time: 87.7 us -> 82.9 us (0.945)
  the two profiles are of different devices: /device:TPU:1 before, /device:TPU:35 now
where the time goes in v8:
time: 82.9 us; the launch traced here: 82.6 us
  starting transfers between devices  34.2 us (41%)
  waiting for transfers between devices  24.9 us (30%)
  Pallas kernels  17.9 us (22%)
  local copies, waits for them, and re-layouts  4.54 us (5%)
    ppermute x12, starting transfers between devices, across(): return lax.ppermute(block, axis, [(i, i ^ step) for i in range(count)])  20.7 us
    ppermute x12, waiting for transfers between devices, across(): return lax.ppermute(block, axis, [(i, i ^ step) for i in range(count)])  13.3 us
    ppermute x7, waiting for transfers between devices, ahead(): lax.ppermute(block, axis, [(i, (i + step) % count) for i in range(count)])  10.5 us
    ppermute x7, starting transfers between devices, ahead(): lax.ppermute(block, axis, [(i, (i + step) % count) for i in range(count)])  9.48 us
    pallas_call x2, Pallas kernels, backward(): pl.pallas_call(functools.partial(bwd_kernel, stretch, side), out_shape=(s...  6.91 us
    pallas_call x2, Pallas kernels, forward(): pl.pallas_call(functools.partial(far_kernel if side else near_kernel, str...  6 us
    unnamed x12, local copies, waits for them, and re-layouts  4.47 us
    ppermute x3, starting transfers between devices, behind(): lax.ppermute(block, axis, [((i + step) % count, i) for i in range(count)])  3.99 us
  transfers between devices with their start and end apart: 22, of which 10 were waited for; matrix products, arithmetic and copies ran while one was open for 1% of the time, Pallas kernels for 14%

profile of v8, /device:TPU:35, one launch (start us, length us, event | category | flops | bytes accessed | tf_op | source)
XLA Modules:
  0.0 82.6 jit_solution(16611819111079924591)
XLA Ops:
  0.6 1.4 %pair.1.kv_ref = bf16[128,256]{1,0:T(8,128)(2,1)} custom-call(bf16[128,128]{1,0:T(8,128)(2,1)} %k_hbm.1, bf16[128,128]{1,0:T(8,128)(2,1)} %v_hbm.1), custom_call_target="tpu_custom_call" | custom-call | tf_op jit(solution)/shard_map/pair/pallas_call | solution.py:251
  2.1 1.7 %collective-permute-start.2 = (bf16[128,256]{1,0:T(8,128)(2,1)}, bf16[128,256]{1,0:T(8,128)(2,1)S(1)}, u32[]{:S(2)}, u32[]{:S(2)}) collective-permute-start(bf16[128,256]{1,0:T(8,128)(2,1)} %pair.1.kv_ref), channel_id=1, source_target_pairs={{0,48},{16,32},{32,16},{48,0},{1,49},{17,33},{33,17},{49,1},{2,50}... | collective-permute-start | bytes 196616 | tf_op jit(solution)/shard_map/ppermute | solution.py:469
  3.8 1.5 %collective-permute-start.1 = (bf16[128,256]{1,0:T(8,128)(2,1)}, bf16[128,256]{1,0:T(8,128)(2,1)S(1)}, u32[]{:S(2)}, u32[]{:S(2)}) collective-permute-start(bf16[128,256]{1,0:T(8,128)(2,1)} %pair.1.kv_ref), channel_id=1, source_target_pairs={{0,32},{16,48},{32,0},{48,16},{1,33},{17,49},{33,1},{49,17},{2,34}... | collective-permute-start | bytes 196616 | tf_op jit(solution)/shard_map/ppermute | solution.py:469
  5.2 1.1 %collective-permute-start = (bf16[128,256]{1,0:T(8,128)(2,1)}, bf16[128,256]{1,0:T(8,128)(2,1)S(1)}, u32[]{:S(2)}, u32[]{:S(2)}) collective-permute-start(bf16[128,256]{1,0:T(8,128)(2,1)} %pair.1.kv_ref), channel_id=1, source_target_pairs={{0,16},{16,0},{32,48},{48,32},{1,17},{17,1},{33,49},{49,33},{2,18}... | collective-permute-start | bytes 196616 | tf_op jit(solution)/shard_map/ppermute | solution.py:469
  9.3 1.4 %collective-permute-done.refs_1_ = bf16[128,256]{1,0:T(8,128)(2,1)S(1)} collective-permute-done((bf16[128,256]{1,0:T(8,128)(2,1)}, bf16[128,256]{1,0:T(8,128)(2,1)S(1)}, u32[]{:S(2)}, u32[]{:S(2)}) %collective-permute-start) | collective-permute-done | bytes 65568 | tf_op jit(solution)/shard_map/ppermute | solution.py:469
  10.6 1.3 %collective-permute-start.8 = (bf16[512,256]{1,0:T(8,128)(2,1)S(1)}, bf16[512,256]{1,0:T(8,128)(2,1)S(1)}, u32[]{:S(2)}, u32[]{:S(2)}) collective-permute-start(bf16[512,256]{1,0:T(8,128)(2,1)S(1)} %stack.1.piece_ref.rest_0_), channel_id=1, source_target_pairs={{192,0},{0,64},{64,128},{128,192},{193,1},{1,65},{65,129},{129,193... | collective-permute-start | bytes 786440 | tf_op jit(solution)/shard_map/ppermute | solution.py:464
  12.8 1.9 %collective-permute-start.4 = (bf16[512,256]{1,0:T(8,128)(2,1)S(1)}, bf16[512,256]{1,0:T(8,128)(2,1)S(1)}, u32[]{:S(2)}, u32[]{:S(2)}) collective-permute-start(bf16[512,256]{1,0:T(8,128)(2,1)S(1)} %stack.1.piece_ref.rest_0_), channel_id=1, source_target_pairs={{64,0},{128,64},{192,128},{0,192},{65,1},{129,65},{193,129},{1,193... | collective-permute-start | bytes 786440 | tf_op jit(solution)/shard_map/ppermute | solution.py:464
  15.3 2.2 %stage.1 = (s32[136]{0:T(256)S(1)}, bf16[512,256]{1,0:T(8,128)(2,1)S(1)}) custom-call(s32[64]{0:T(128)S(1)} %copy-done.4, bf16[512,256]{1,0:T(8,128)(2,1)S(1)} %stack.1.piece_ref.rest_0_), custom_call_target="tpu_custom_call" | custom-call | tf_op jit(solution)/shard_map/stage/pallas_call | solution.py:278
  17.5 2.7 %collective-permute-start.3 = (bf16[512,256]{1,0:T(8,128)(2,1)S(1)}, bf16[512,256]{1,0:T(8,128)(2,1)S(1)}, u32[]{:S(2)}, u32[]{:S(2)}) collective-permute-start(bf16[512,256]{1,0:T(8,128)(2,1)S(1)} %get-tuple-element.41), channel_id=1, source_target_pairs={{0,8},{8,0},{1,9},{9,1},{2,10},{10,2},{3,11},{11,3},{4,12},{12,4},... | collective-permute-start | bytes 786440 | tf_op jit(solution)/shard_map/ppermute | solution.py:469
  20.2 1.6 %collective-permute-start.9 = (bf16[512,256]{1,0:T(8,128)(2,1)S(1)}, bf16[512,256]{1,0:T(8,128)(2,1)S(1)}, u32[]{:S(2)}, u32[]{:S(2)}) collective-permute-start(bf16[512,256]{1,0:T(8,128)(2,1)S(1)} %collective-permute-done.8.rest_3_), channel_id=1, source_target_pairs={{0,8},{8,0},{1,9},{9,1},{2,10},{10,2},{3,11},{11,3},{4,12},{12,4},... | collective-permute-start | bytes 786440 | tf_op jit(solution)/shard_map/ppermute | solution.py:469
  21.8 3.0 %collective-permute-start.7 = (bf16[512,256]{1,0:T(8,128)(2,1)S(1)}, bf16[512,256]{1,0:T(8,128)(2,1)S(1)}, u32[]{:S(2)}, u32[]{:S(2)}) collective-permute-start(bf16[512,256]{1,0:T(8,128)(2,1)S(1)} %collective-permute-done.6.rest_2_), channel_id=1, source_target_pairs={{0,8},{8,0},{1,9},{9,1},{2,10},{10,2},{3,11},{11,3},{4,12},{12,4},... | collective-permute-start | bytes 786440 | tf_op jit(solution)/shard_map/ppermute | solution.py:469
  24.8 1.1 %collective-permute-done.4.rest_1_ = bf16[512,256]{1,0:T(8,128)(2,1)S(1)} collective-permute-done((bf16[512,256]{1,0:T(8,128)(2,1)S(1)}, bf16[512,256]{1,0:T(8,128)(2,1)S(1)}, u32[]{:S(2)}, u32[]{:S(2)}) %collective-permute-start.4) | collective-permute-done | bytes 262176 | tf_op jit(solution)/shard_map/ppermute | solution.py:464
  25.9 1.2 %collective-permute-start.5 = (bf16[512,256]{1,0:T(8,128)(2,1)S(1)}, bf16[512,256]{1,0:T(8,128)(2,1)S(1)}, u32[]{:S(2)}, u32[]{:S(2)}) collective-permute-start(bf16[512,256]{1,0:T(8,128)(2,1)S(1)} %collective-permute-done.4.rest_1_), channel_id=1, source_target_pairs={{0,8},{8,0},{1,9},{9,1},{2,10},{10,2},{3,11},{11,3},{4,12},{12,4},... | collective-permute-start | bytes 786440 | tf_op jit(solution)/shard_map/ppermute | solution.py:469
  27.1 2.2 %attention_forward_0.1 = (bf16[9,256,256]{2,1,0:T(8,128)(2,1)S(1)}, bf16[2048,256]{1,0:T(8,128)(2,1)S(1)}, f32[2,8,256]{2,1,0:T(8,128)S(1)}, f32[2,8,256]{2,1,0:T(8,128)S(1)}, f32[2,128,256]{2,1,0:T(8,128)S(1)}) custom-call(s32[136]{0:T(256)S(1)} %get-tuple-element.40.plan_ref, bf16[2,256,128]{2,1,0:T(8,128)(2,1)S(1)} %get-tuple-element.38.token_ref.qs_ref, ...), custom_call_target="tpu_custom_call" | custom-call | flops 3000000000 | bytes 8000000 | tf_op jit(solution)/shard_map/attention_forward_0/pallas_call | solution.py:420
  29.4 1.1 %copy-done.5 = bf16[512,8192]{1,0:T(8,128)(2,1)S(1)} copy-done((bf16[512,8192]{1,0:T(8,128)(2,1)S(1)}, bf16[512,8192]{1,0:T(8,128)(2,1)}, u32[]{:S(2)}) %copy-start.5) | copy-done | bytes 8388632
  30.5 3.8 %attention_forward_1.1 = (bf16[32,8192]{1,0:T(8,128)(2,1)S(1)}, bf16[32,4096]{1,0:T(8,128)(2,1)S(1)}, bf16[32,4096]{1,0:T(8,128)(2,1)S(1)}, bf16[32,8192]{1,0:T(...) custom-call(s32[136]{0:T(256)S(1)} %get-tuple-element.40.plan_ref, ...), custom_call_target="tpu_custom_call" | custom-call | flops 3000000000 | bytes 8000000 | tf_op jit(solution)/shard_map/attention_forward_1/pallas_call | solution.py:420
  34.3 1.6 %collective-permute-start.10 = (bf16[32,8192]{1,0:T(8,128)(2,1)S(1)}, bf16[32,8192]{1,0:T(8,128)(2,1)S(1)}, u32[]{:S(2)}, u32[]{:S(2)}) collective-permute-start(bf16[32,8192]{1,0:T(8,128)(2,1)S(1)} %get-tuple-element.47), channel_id=1, source_target_pairs={{0,1},{1,2},{2,3},{3,0},{4,5},{5,6},{6,7},{7,4},{8,9},{9,10},{10,1... | collective-permute-start | bytes 1572872 | tf_op jit(solution)/shard_map/ppermute | solution.py:459
  35.9 1.5 %collective-permute-start.11 = (bf16[32,8192]{1,0:T(8,128)(2,1)S(1)}, bf16[32,8192]{1,0:T(8,128)(2,1)S(1)}, u32[]{:S(2)}, u32[]{:S(2)}) collective-permute-start(bf16[32,8192]{1,0:T(8,128)(2,1)S(1)} %get-tuple-element.48), channel_id=1, source_target_pairs={{0,3},{1,0},{2,1},{3,2},{4,7},{5,4},{6,5},{7,6},{8,11},{9,8},{10,9... | collective-permute-start | bytes 1572872 | tf_op jit(solution)/shard_map/ppermute | solution.py:459
  37.4 3.1 %attention_backward_1.1 = (f32[2,128,256]{2,1,0:T(8,128)S(1)}, bf16[2048,256]{1,0:T(8,128)(2,1)S(1)}) custom-call(s32[136]{0:T(256)S(1)} %get-tuple-element.40.plan_ref, bf16[9,256,256]{2,1,0:T(8,128)(2,1)S(1)} %get-tuple-element.55.p_ref, bf16[2048,256]{1,0:T(8,128)(2,1)S(1)} %get-tuple-element.56.kv_ref, ...), custom_call_target="tpu_custom_call" | custom-call | flops 20000000000 | bytes 8000000 | tf_op jit(solution)/shard_map/attention_backward_1/pallas_call | solution.py:445
  41.0 3.9 %attention_backward_0.1 = (bf16[128,512]{1,0:T(8,128)(2,1)}, bf16[2048,256]{1,0:T(8,128)(2,1)S(1)}) custom-call(s32[136]{0:T(256)S(1)} %get-tuple-element.40.plan_ref, bf16[9,256,256]{2,1,0:T(8,128)(2,1)S(1)} %get-tuple-element.51.p_ref, bf16[2048,256]{1,0:T(8,128)(2,1)S(1)} %get-tuple-element.52.kv_ref, ...), custom_call_target="tpu_custom_call" | custom-call | flops 20000000000 | bytes 8000000 | tf_op jit(solution)/shard_map/attention_backward_0/pallas_call | solution.py:445
  45.1 4.3 %collective-permute-done.10.ahead_in.from_behind = bf16[32,8192]{1,0:T(8,128)(2,1)S(1)} collective-permute-done((bf16[32,8192]{1,0:T(8,128)(2,1)S(1)}, bf16[32,8192]{1,0:T(8,128)(2,1)S(1)}, u32[]{:S(2)}, u32[]{:S(2)}) %collective-permute-start.10) | collective-permute-done | bytes 524320 | tf_op jit(solution)/shard_map/ppermute | solution.py:459
  50.6 1.8 %collective-permute-start.14 = (bf16[32,4096]{1,0:T(8,128)(2,1)S(1)}, bf16[32,4096]{1,0:T(8,128)(2,1)S(1)}, u32[]{:S(2)}, u32[]{:S(2)}) collective-permute-start(bf16[32,4096]{1,0:T(8,128)(2,1)S(1)} %get-tuple-element.62), channel_id=1, source_target_pairs={{0,3},{1,0},{2,1},{3,2},{4,7},{5,4},{6,5},{7,6},{8,11},{9,8},{10,9... | collective-permute-start | bytes 786440 | tf_op jit(solution)/shard_map/ppermute | solution.py:459
  52.5 2.2 %collective-permute-start.17 = (bf16[512,256]{1,0:T(8,128)(2,1)S(1)}, bf16[512,256]{1,0:T(8,128)(2,1)S(1)}, u32[]{:S(2)}, u32[]{:S(2)}) collective-permute-start(bf16[512,256]{1,0:T(8,128)(2,1)S(1)} %get-tuple-element.73), channel_id=1, source_target_pairs={{0,128},{64,192},{128,0},{192,64},{1,129},{65,193},{129,1},{193,65... | collective-permute-start | bytes 786440 | tf_op jit(solution)/shard_map/ppermute | solution.py:459
  54.7 1.4 %collective-permute-start.16 = (bf16[512,256]{1,0:T(8,128)(2,1)S(1)}, bf16[512,256]{1,0:T(8,128)(2,1)S(1)}, u32[]{:S(2)}, u32[]{:S(2)}) collective-permute-start(bf16[512,256]{1,0:T(8,128)(2,1)S(1)} %get-tuple-element.74), channel_id=1, source_target_pairs={{0,64},{64,128},{128,192},{192,0},{1,65},{65,129},{129,193},{193,1... | collective-permute-start | bytes 786440 | tf_op jit(solution)/shard_map/ppermute | solution.py:459
  56.1 1.9 %collective-permute-done.13.front = bf16[32,4096]{1,0:T(8,128)(2,1)S(1)} collective-permute-done((bf16[32,4096]{1,0:T(8,128)(2,1)S(1)}, bf16[32,4096]{1,0:T(8,128)(2,1)S(1)}, u32[]{:S(2)}, u32[]{:S(2)}) %collective-permute-start.13) | collective-permute-done | bytes 262176 | tf_op jit(solution)/shard_map/ppermute | solution.py:459
  58.2 4.7 %collective-permute-start.15 = (bf16[16,8192]{1,0:T(8,128)(2,1)S(1)}, bf16[16,8192]{1,0:T(8,128)(2,1)S(1)}, u32[]{:S(2)}, u32[]{:S(2)}) collective-permute-start(bf16[16,8192]{1,0:T(8,128)(2,1)S(1)} %get-tuple-element.64), channel_id=1, source_target_pairs={{0,4},{4,0},{1,5},{5,1},{2,6},{6,2},{3,7},{7,3},{8,12},{12,8},{9,1... | collective-permute-start | bytes 786440 | tf_op jit(solution)/shard_map/ppermute | solution.py:469
  62.9 2.4 %collective-permute-done.17.refs_1_ = bf16[512,256]{1,0:T(8,128)(2,1)S(1)} collective-permute-done((bf16[512,256]{1,0:T(8,128)(2,1)S(1)}, bf16[512,256]{1,0:T(8,128)(2,1)S(1)}, u32[]{:S(2)}, u32[]{:S(2)}) %collective-permute-start.17) | collective-permute-done | bytes 262176 | tf_op jit(solution)/shard_map/ppermute | solution.py:459
  65.3 1.8 %collective-permute-done.16.refs_0_ = bf16[512,256]{1,0:T(8,128)(2,1)S(1)} collective-permute-done((bf16[512,256]{1,0:T(8,128)(2,1)S(1)}, bf16[512,256]{1,0:T(8,128)(2,1)S(1)}, u32[]{:S(2)}, u32[]{:S(2)}) %collective-permute-start.16) | collective-permute-done | bytes 262176 | tf_op jit(solution)/shard_map/ppermute | solution.py:459
  67.3 1.0 %collective-permute-start.19 = (bf16[128,256]{1,0:T(8,128)(2,1)S(1)}, bf16[128,256]{1,0:T(8,128)(2,1)S(1)}, u32[]{:S(2)}, u32[]{:S(2)}) collective-permute-start(bf16[128,256]{1,0:T(8,128)(2,1)S(1)} %get-tuple-element.67), channel_id=1, source_target_pairs={{0,16},{16,0},{32,48},{48,32},{1,17},{17,1},{33,49},{49,33},{2,18}... | collective-permute-start | bytes 196616 | tf_op jit(solution)/shard_map/ppermute | solution.py:469
  70.8 3.9 %collective-permute-done.19.refs_1_ = bf16[128,256]{1,0:T(8,128)(2,1)S(1)} collective-permute-done((bf16[128,256]{1,0:T(8,128)(2,1)S(1)}, bf16[128,256]{1,0:T(8,128)(2,1)S(1)}, u32[]{:S(2)}, u32[]{:S(2)}) %collective-permute-start.19) | collective-permute-done | bytes 65568 | tf_op jit(solution)/shard_map/ppermute | solution.py:469
  74.7 2.3 %collective-permute-done.20.refs_2_ = bf16[128,256]{1,0:T(8,128)(2,1)S(1)} collective-permute-done((bf16[128,256]{1,0:T(8,128)(2,1)S(1)}, bf16[128,256]{1,0:T(8,128)(2,1)S(1)}, u32[]{:S(2)}, u32[]{:S(2)}) %collective-permute-start.20) | collective-permute-done | bytes 65568 | tf_op jit(solution)/shard_map/ppermute | solution.py:469
  77.0 5.0 %collective-permute-done.21.refs_3_ = bf16[128,256]{1,0:T(8,128)(2,1)S(1)} collective-permute-done((bf16[128,256]{1,0:T(8,128)(2,1)S(1)}, bf16[128,256]{1,0:T(8,128)(2,1)S(1)}, u32[]{:S(2)}, u32[]{:S(2)}) %collective-permute-start.21) | collective-permute-done | bytes 65568 | tf_op jit(solution)/shard_map/ppermute | solution.py:469
  (39 shorter events, 10.0 us)
Async XLA Ops:
  2.1 7.2 %collective-permute-start.2 = (bf16[128,256]{1,0:T(8,128)(2,1)}, bf16[128,256]{1,0:T(8,128)(2,1)S(1)}, u32[]{:S(2)}, u32[]{:S(2)}) collective-permute-start(bf16[128,256]{1,0:T(8,128)(2,1)} %pair.1.kv_ref), channel_id=1, source_target_pairs={{0,48},{16,32},{32,16},{48,0},{1,49},{17,33},{33,17},{49,1},{2,50}... | collective-permute-start | bytes 196616 | tf_op jit(solution)/shard_map/ppermute | solution.py:469
  3.8 5.5 %collective-permute-start.1 = (bf16[128,256]{1,0:T(8,128)(2,1)}, bf16[128,256]{1,0:T(8,128)(2,1)S(1)}, u32[]{:S(2)}, u32[]{:S(2)}) collective-permute-start(bf16[128,256]{1,0:T(8,128)(2,1)} %pair.1.kv_ref), channel_id=1, source_target_pairs={{0,32},{16,48},{32,0},{48,16},{1,33},{17,49},{33,1},{49,17},{2,34}... | collective-permute-start | bytes 196616 | tf_op jit(solution)/shard_map/ppermute | solution.py:469
  5.2 5.4 %collective-permute-start = (bf16[128,256]{1,0:T(8,128)(2,1)}, bf16[128,256]{1,0:T(8,128)(2,1)S(1)}, u32[]{:S(2)}, u32[]{:S(2)}) collective-permute-start(bf16[128,256]{1,0:T(8,128)(2,1)} %pair.1.kv_ref), channel_id=1, source_target_pairs={{0,16},{16,0},{32,48},{48,32},{1,17},{17,1},{33,49},{49,33},{2,18}... | collective-permute-start | bytes 196616 | tf_op jit(solution)/shard_map/ppermute | solution.py:469
  6.3 0.9 %copy-start.1 = (bf16[128,256]{1,0:T(8,128)(2,1)S(1)}, bf16[128,256]{1,0:T(8,128)(2,1)}, u32[]{:S(2)}) copy-start(bf16[128,256]{1,0:T(8,128)(2,1)} %pair.1.kv_ref) | copy-start | bytes 196612
  7.2 0.9 %copy-start.2 = (bf16[128,512]{1,0:T(8,128)(2,1)S(1)}, bf16[128,512]{1,0:T(8,128)(2,1)}, u32[]{:S(2)}) copy-start(bf16[128,512]{1,0:T(8,128)(2,1)} %q_hbm.1) | copy-start | bytes 393220
  8.1 0.9 %copy-start.3 = (bf16[128,512]{1,0:T(8,128)(2,1)S(1)}, bf16[128,512]{1,0:T(8,128)(2,1)}, u32[]{:S(2)}) copy-start(bf16[128,512]{1,0:T(8,128)(2,1)} %do_hbm.1) | copy-start | bytes 393220
  10.6 9.6 %collective-permute-start.8 = (bf16[512,256]{1,0:T(8,128)(2,1)S(1)}, bf16[512,256]{1,0:T(8,128)(2,1)S(1)}, u32[]{:S(2)}, u32[]{:S(2)}) collective-permute-start(bf16[512,256]{1,0:T(8,128)(2,1)S(1)} %stack.1.piece_ref.rest_0_), channel_id=1, source_target_pairs={{192,0},{0,64},{64,128},{128,192},{193,1},{1,65},{65,129},{129,193... | collective-permute-start | bytes 786440 | tf_op jit(solution)/shard_map/ppermute | solution.py:464
  11.9 9.8 %collective-permute-start.6 = (bf16[512,256]{1,0:T(8,128)(2,1)S(1)}, bf16[512,256]{1,0:T(8,128)(2,1)S(1)}, u32[]{:S(2)}, u32[]{:S(2)}) collective-permute-start(bf16[512,256]{1,0:T(8,128)(2,1)S(1)} %stack.1.piece_ref.rest_0_), channel_id=1, source_target_pairs={{128,0},{192,64},{0,128},{64,192},{129,1},{193,65},{1,129},{65,193... | collective-permute-start | bytes 786440 | tf_op jit(solution)/shard_map/ppermute | solution.py:464
  12.8 13.1 %collective-permute-start.4 = (bf16[512,256]{1,0:T(8,128)(2,1)S(1)}, bf16[512,256]{1,0:T(8,128)(2,1)S(1)}, u32[]{:S(2)}, u32[]{:S(2)}) collective-permute-start(bf16[512,256]{1,0:T(8,128)(2,1)S(1)} %stack.1.piece_ref.rest_0_), channel_id=1, source_target_pairs={{64,0},{128,64},{192,128},{0,192},{65,1},{129,65},{193,129},{1,193... | collective-permute-start | bytes 786440 | tf_op jit(solution)/shard_map/ppermute | solution.py:464
  14.6 0.7 copy-start.4
  17.5 11.8 %collective-permute-start.3 = (bf16[512,256]{1,0:T(8,128)(2,1)S(1)}, bf16[512,256]{1,0:T(8,128)(2,1)S(1)}, u32[]{:S(2)}, u32[]{:S(2)}) collective-permute-start(bf16[512,256]{1,0:T(8,128)(2,1)S(1)} %get-tuple-element.41), channel_id=1, source_target_pairs={{0,8},{8,0},{1,9},{9,1},{2,10},{10,2},{3,11},{11,3},{4,12},{12,4},... | collective-permute-start | bytes 786440 | tf_op jit(solution)/shard_map/ppermute | solution.py:469
  20.2 9.1 %collective-permute-start.9 = (bf16[512,256]{1,0:T(8,128)(2,1)S(1)}, bf16[512,256]{1,0:T(8,128)(2,1)S(1)}, u32[]{:S(2)}, u32[]{:S(2)}) collective-permute-start(bf16[512,256]{1,0:T(8,128)(2,1)S(1)} %collective-permute-done.8.rest_3_), channel_id=1, source_target_pairs={{0,8},{8,0},{1,9},{9,1},{2,10},{10,2},{3,11},{11,3},{4,12},{12,4},... | collective-permute-start | bytes 786440 | tf_op jit(solution)/shard_map/ppermute | solution.py:469
  21.8 7.6 %collective-permute-start.7 = (bf16[512,256]{1,0:T(8,128)(2,1)S(1)}, bf16[512,256]{1,0:T(8,128)(2,1)S(1)}, u32[]{:S(2)}, u32[]{:S(2)}) collective-permute-start(bf16[512,256]{1,0:T(8,128)(2,1)S(1)} %collective-permute-done.6.rest_2_), channel_id=1, source_target_pairs={{0,8},{8,0},{1,9},{9,1},{2,10},{10,2},{3,11},{11,3},{4,12},{12,4},... | collective-permute-start | bytes 786440 | tf_op jit(solution)/shard_map/ppermute | solution.py:469
  25.9 3.5 %collective-permute-start.5 = (bf16[512,256]{1,0:T(8,128)(2,1)S(1)}, bf16[512,256]{1,0:T(8,128)(2,1)S(1)}, u32[]{:S(2)}, u32[]{:S(2)}) collective-permute-start(bf16[512,256]{1,0:T(8,128)(2,1)S(1)} %collective-permute-done.4.rest_1_), channel_id=1, source_target_pairs={{0,8},{8,0},{1,9},{9,1},{2,10},{10,2},{3,11},{11,3},{4,12},{12,4},... | collective-permute-start | bytes 786440 | tf_op jit(solution)/shard_map/ppermute | solution.py:469
  27.1 3.4 %copy-start.5 = (bf16[512,8192]{1,0:T(8,128)(2,1)S(1)}, bf16[512,8192]{1,0:T(8,128)(2,1)}, u32[]{:S(2)}) copy-start(bf16[512,8192]{1,0:T(8,128)(2,1)} %rest_5_.1) | copy-start | bytes 25165828
  34.3 15.2 %collective-permute-start.10 = (bf16[32,8192]{1,0:T(8,128)(2,1)S(1)}, bf16[32,8192]{1,0:T(8,128)(2,1)S(1)}, u32[]{:S(2)}, u32[]{:S(2)}) collective-permute-start(bf16[32,8192]{1,0:T(8,128)(2,1)S(1)} %get-tuple-element.47), channel_id=1, source_target_pairs={{0,1},{1,2},{2,3},{3,0},{4,5},{5,6},{6,7},{7,4},{8,9},{9,10},{10,1... | collective-permute-start | bytes 1572872 | tf_op jit(solution)/shard_map/ppermute | solution.py:459
  35.9 13.6 %collective-permute-start.11 = (bf16[32,8192]{1,0:T(8,128)(2,1)S(1)}, bf16[32,8192]{1,0:T(8,128)(2,1)S(1)}, u32[]{:S(2)}, u32[]{:S(2)}) collective-permute-start(bf16[32,8192]{1,0:T(8,128)(2,1)S(1)} %get-tuple-element.48), channel_id=1, source_target_pairs={{0,3},{1,0},{2,1},{3,2},{4,7},{5,4},{6,5},{7,6},{8,11},{9,8},{10,9... | collective-permute-start | bytes 1572872 | tf_op jit(solution)/shard_map/ppermute | solution.py:459
  40.5 4.4 %collective-permute-start.12 = (bf16[2048,256]{1,0:T(8,128)(2,1)S(1)}, bf16[2048,256]{1,0:T(8,128)(2,1)S(1)}, u32[]{:S(2)}, u32[]{:S(2)}) collective-permute-start(bf16[2048,256]{1,0:T(8,128)(2,1)S(1)} %get-tuple-element.60), channel_id=1, source_target_pairs={{0,8},{8,0},{1,9},{9,1},{2,10},{10,2},{3,11},{11,3},{4,12},{12,4},... | collective-permute-start | bytes 3145736 | tf_op jit(solution)/shard_map/ppermute | solution.py:469
  49.6 8.4 %collective-permute-start.13 = (bf16[32,4096]{1,0:T(8,128)(2,1)S(1)}, bf16[32,4096]{1,0:T(8,128)(2,1)S(1)}, u32[]{:S(2)}, u32[]{:S(2)}) collective-permute-start(bf16[32,4096]{1,0:T(8,128)(2,1)S(1)} %get-tuple-element.61), channel_id=1, source_target_pairs={{0,1},{1,2},{2,3},{3,0},{4,5},{5,6},{6,7},{7,4},{8,9},{9,10},{10,1... | collective-permute-start | bytes 786440 | tf_op jit(solution)/shard_map/ppermute | solution.py:459
  50.6 7.4 %collective-permute-start.14 = (bf16[32,4096]{1,0:T(8,128)(2,1)S(1)}, bf16[32,4096]{1,0:T(8,128)(2,1)S(1)}, u32[]{:S(2)}, u32[]{:S(2)}) collective-permute-start(bf16[32,4096]{1,0:T(8,128)(2,1)S(1)} %get-tuple-element.62), channel_id=1, source_target_pairs={{0,3},{1,0},{2,1},{3,2},{4,7},{5,4},{6,5},{7,6},{8,11},{9,8},{10,9... | collective-permute-start | bytes 786440 | tf_op jit(solution)/shard_map/ppermute | solution.py:459
  52.4 10.5 %collective-permute-start.18 = (bf16[512,256]{1,0:T(8,128)(2,1)S(1)}, bf16[512,256]{1,0:T(8,128)(2,1)S(1)}, u32[]{:S(2)}, u32[]{:S(2)}) collective-permute-start(bf16[512,256]{1,0:T(8,128)(2,1)S(1)} %get-tuple-element.72), channel_id=1, source_target_pairs={{0,192},{64,0},{128,64},{192,128},{1,193},{65,1},{129,65},{193,129... | collective-permute-start | bytes 786440 | tf_op jit(solution)/shard_map/ppermute | solution.py:459
  52.5 12.8 %collective-permute-start.17 = (bf16[512,256]{1,0:T(8,128)(2,1)S(1)}, bf16[512,256]{1,0:T(8,128)(2,1)S(1)}, u32[]{:S(2)}, u32[]{:S(2)}) collective-permute-start(bf16[512,256]{1,0:T(8,128)(2,1)S(1)} %get-tuple-element.73), channel_id=1, source_target_pairs={{0,128},{64,192},{128,0},{192,64},{1,129},{65,193},{129,1},{193,65... | collective-permute-start | bytes 786440 | tf_op jit(solution)/shard_map/ppermute | solution.py:459
  54.7 12.4 %collective-permute-start.16 = (bf16[512,256]{1,0:T(8,128)(2,1)S(1)}, bf16[512,256]{1,0:T(8,128)(2,1)S(1)}, u32[]{:S(2)}, u32[]{:S(2)}) collective-permute-start(bf16[512,256]{1,0:T(8,128)(2,1)S(1)} %get-tuple-element.74), channel_id=1, source_target_pairs={{0,64},{64,128},{128,192},{192,0},{1,65},{65,129},{129,193},{193,1... | collective-permute-start | bytes 786440 | tf_op jit(solution)/shard_map/ppermute | solution.py:459
  58.2 12.5 %collective-permute-start.15 = (bf16[16,8192]{1,0:T(8,128)(2,1)S(1)}, bf16[16,8192]{1,0:T(8,128)(2,1)S(1)}, u32[]{:S(2)}, u32[]{:S(2)}) collective-permute-start(bf16[16,8192]{1,0:T(8,128)(2,1)S(1)} %get-tuple-element.64), channel_id=1, source_target_pairs={{0,4},{4,0},{1,5},{5,1},{2,6},{6,2},{3,7},{7,3},{8,12},{12,8},{9,1... | collective-permute-start | bytes 786440 | tf_op jit(solution)/shard_map/ppermute | solution.py:469
  67.3 7.4 %collective-permute-start.19 = (bf16[128,256]{1,0:T(8,128)(2,1)S(1)}, bf16[128,256]{1,0:T(8,128)(2,1)S(1)}, u32[]{:S(2)}, u32[]{:S(2)}) collective-permute-start(bf16[128,256]{1,0:T(8,128)(2,1)S(1)} %get-tuple-element.67), channel_id=1, source_target_pairs={{0,16},{16,0},{32,48},{48,32},{1,17},{17,1},{33,49},{49,33},{2,18}... | collective-permute-start | bytes 196616 | tf_op jit(solution)/shard_map/ppermute | solution.py:469
  68.3 8.7 %collective-permute-start.20 = (bf16[128,256]{1,0:T(8,128)(2,1)S(1)}, bf16[128,256]{1,0:T(8,128)(2,1)S(1)}, u32[]{:S(2)}, u32[]{:S(2)}) collective-permute-start(bf16[128,256]{1,0:T(8,128)(2,1)S(1)} %get-tuple-element.68), channel_id=1, source_target_pairs={{0,32},{16,48},{32,0},{48,16},{1,33},{17,49},{33,1},{49,17},{2,34}... | collective-permute-start | bytes 196616 | tf_op jit(solution)/shard_map/ppermute | solution.py:469
  69.3 12.7 %collective-permute-start.21 = (bf16[128,256]{1,0:T(8,128)(2,1)S(1)}, bf16[128,256]{1,0:T(8,128)(2,1)S(1)}, u32[]{:S(2)}, u32[]{:S(2)}) collective-permute-start(bf16[128,256]{1,0:T(8,128)(2,1)S(1)} %get-tuple-element.69), channel_id=1, source_target_pairs={{0,48},{16,32},{32,16},{48,0},{1,49},{17,33},{33,17},{49,1},{2,50}... | collective-permute-start | bytes 196616 | tf_op jit(solution)/shard_map/ppermute | solution.py:469
  70.8 11.8 %copy-start = (bf16[16,8192]{1,0:T(8,128)(2,1)}, bf16[16,8192]{1,0:T(8,128)(2,1)S(1)}, u32[]{:S(2)}) copy-start(bf16[16,8192]{1,0:T(8,128)(2,1)S(1)} %add_convert_fusion.1.token_ref) | copy-start | bytes 786436

commit v9 on v8

--- a/solution.py
+++ b/solution.py
@@ -18,7 +18,7 @@
 CTX = ("x", "zl", "core")
 TP = ("zh", "y")
 MIX_SPAN = 1024
-CHUNK = 4
+CHUNK = 8
 FWD_MIB = 32
 BWD_FLOPS = 2 * 10**10
 SMEM = pl.BlockSpec(memory_space=pltpu.SMEM)
@@ -193,14 +193,21 @@
         at = slice(index * MIX_SPAN, (index + 1) * MIX_SPAN)
         mixed = dot(turned_ref[...], w_ref[:, at], NN).astype(jnp.bfloat16)
         own_ref[:, at] = mixed[:piece]
+        far, near, last = mixed[2 * piece:3 * piece], mixed[piece:2 * piece], mixed[3 * piece:]
+        quarter = half // 2
         if at.start < half:
-            ahead_ref[:, at] = mixed[2 * piece:3 * piece]
-            behind_ref[:, at] = mixed[3 * piece:]
-            front_ref[:, at] = mixed[piece:2 * piece]
+            ahead_ref[:, at] = far
+            front_ref[:, at] = near
         else:
-            ahead_ref[:, at] = mixed[piece:2 * piece]
-            behind_ref[:, at] = mixed[2 * piece:3 * piece]
-            back_ref[:, at.start - half:at.stop - half] = mixed[3 * piece:]
+            behind_ref[:, at.start - quarter:at.stop - quarter] = far
+            if at.start < half + quarter:
+                ahead_ref[:, at] = near
+            else:
+                front_ref[:, at.start - quarter:at.stop - quarter] = near
+        if at.start < quarter:
+            behind_ref[:, at] = last
+        else:
+            back_ref[:, at.start - quarter:at.stop - quarter] = last
 
 
 def bwd_kernel(stretch, side, plan_ref, p_ref, kv_ref, qs_ref, ds_ref, delta_ref, inv_ref, *rest):
@@ -252,7 +259,7 @@
         pair_kernel,
         out_shape=jax.ShapeDtypeStruct((keys.shape[0], 2 * HD), jnp.bfloat16),
         in_specs=[HBM] * 2,
-        out_specs=VMEM,
+        out_specs=HBM,
         scratch_shapes=[pltpu.SemaphoreType.DMA((2,))],
         compiler_params=pltpu.CompilerParams(vmem_limit_bytes=60 * MIB),
         name="pair",
@@ -294,11 +301,12 @@
 
 
 def relay_kernel(front_in, back_in, ahead_in, behind_in, token_ref, front_ref, back_ref):
-    half = front_in.shape[1]
-    for index in range(half // MIX_SPAN):
+    quarter = front_in.shape[1] // 3
+    for index in range(2 * quarter // MIX_SPAN):
         at = slice(index * MIX_SPAN, (index + 1) * MIX_SPAN)
         front_ref[:, at] = added(front_in[:, at], ahead_in[:, at])
-        back_ref[:, at] = added(back_in[:, at], behind_in[:, half + at.start:half + at.stop])
+        to = slice(quarter + at.start, quarter + at.stop)
+        back_ref[:, to] = added(back_in[:, to], behind_in[:, to])
 
 
 def relay(front, back, from_behind, from_ahead, token):
@@ -308,34 +316,36 @@
         out_shape=(shape, shape),
         in_specs=[VMEM] * 4 + [ANY],
         out_specs=[VMEM] * 2,
+        input_output_aliases={0: 0, 1: 1},
         compiler_params=pltpu.CompilerParams(vmem_limit_bytes=8 * MIB),
         name="relay",
     )(front, back, from_behind, from_ahead, token)
 
 
-def settle_kernel(own, from_behind, from_ahead, front, back, *refs):
-    keep_ref, give_ref = refs[-2:]
-    half = front.shape[1]
+def settle_kernel(own, from_behind, from_ahead, front, back, keep_ref, give_ref):
+    quarter = front.shape[1] // 3
     rows = keep_ref.shape[0]
-    for index in range(half // MIX_SPAN):
+    for index in range(own.shape[1] // MIX_SPAN):
         at = slice(index * MIX_SPAN, (index + 1) * MIX_SPAN)
-        to = slice(half + at.start, half + at.stop)
-        for where, total in ((at, added(own[:, at], front[:, at], from_ahead[:, at])),
-                             (to, added(own[:, to], back[:, at], from_behind[:, to]))):
-            keep_ref[:, where] = total[:rows]
-            give_ref[:, where] = total[rows:]
-
-
-def settle(own, from_behind, from_ahead, front, back, *tokens):
+        less = slice(at.start - quarter, at.stop - quarter)
+        which = at.start // quarter
+        behind = from_behind[:, at] if which == 2 else front[:, at if which < 2 else less]
+        before = from_ahead[:, at] if which == 0 else back[:, less]
+        total = added(own[:, at], behind, before)
+        keep_ref[:, at] = total[:rows]
+        give_ref[:, at] = total[rows:]
+
+
+def settle(own, from_behind, from_ahead, front, back):
     shape = jax.ShapeDtypeStruct((own.shape[0] // NH, own.shape[1]), own.dtype)
     return pl.pallas_call(
         settle_kernel,
         out_shape=(shape, shape),
-        in_specs=[VMEM] * 5 + [ANY] * len(tokens),
+        in_specs=[VMEM] * 5,
         out_specs=[VMEM] * 2,
         compiler_params=pltpu.CompilerParams(vmem_limit_bytes=8 * MIB),
         name="settle",
-    )(own, from_behind, from_ahead, front, back, *tokens)
+    )(own, from_behind, from_ahead, front, back)
 
 
 def share_kernel(token_ref, near, *refs):
@@ -410,8 +420,7 @@
     scratch = [pltpu.VMEM((steps, span, cols), f32), pltpu.VMEM((stretch, cols), jnp.int32)]
     if side:
         width = more[1].shape[1]
-        outs = (shape((tokens // NY, width), b16),) + (shape((tokens // NY, width // 2), b16),) * 2 + (
-            shape((tokens // NY, width), b16),) * 2 + (
+        outs = (shape((tokens // NY, width), b16),) + (shape((tokens // NY, 3 * width // 4), b16),) * 4 + (
             weights, keys, shape(row, f32), shape(row, f32), shape(row, f32))
         scratch = [pltpu.VMEM(row, f32), pltpu.VMEM(row, f32), pltpu.VMEM(sums, f32)] + scratch + [
             pltpu.VMEM((tokens, QPG * HD), b16), pltpu.VMEM((tokens, QPG * HD), b16)]
@@ -498,7 +507,7 @@
         own, from_behind, from_ahead, ahead(front, "y", 1), ahead(back, "y", NY - 1))
     terms = share(mixed, near, *others)
     mixed = total_of([mixed, across(give, "zh", 1)])
-    k_grad, v_grad = finish(mixed, terms[0], *[across(terms[step], "zl", step) for step in range(1, NZ)])
+    k_grad, v_grad = finish(mixed, terms[0], *[across(terms[step], "zl", step) for step in (2, 3, 1)])
     return mixed, q_grad, k_grad, v_grad
 
 

time: 82.9 us -> 84.7 us (1.022)
  the two profiles are of different devices: /device:TPU:35 before, /device:TPU:1 now
where the time goes in v9:
time: 84.7 us; the launch traced here: 84.2 us
  starting transfers between devices  37.2 us (44%)
  waiting for transfers between devices  22.5 us (27%)
  Pallas kernels  18.9 us (22%)
  local copies, waits for them, and re-layouts  4.44 us (5%)
    ppermute x12, starting transfers between devices, across(): return lax.ppermute(block, axis, [(i, i ^ step) for i in range(count)])  22.8 us
    ppermute x12, waiting for transfers between devices, across(): return lax.ppermute(block, axis, [(i, i ^ step) for i in range(count)])  11.6 us
    ppermute x7, starting transfers between devices, ahead(): lax.ppermute(block, axis, [(i, (i + step) % count) for i in range(count)])  9.78 us
    ppermute x7, waiting for transfers between devices, ahead(): lax.ppermute(block, axis, [(i, (i + step) % count) for i in range(count)])  8.9 us
    pallas_call x2, Pallas kernels, forward(): pl.pallas_call(functools.partial(far_kernel if side else near_kernel, str...  6.16 us
    pallas_call x2, Pallas kernels, backward(): pl.pallas_call(functools.partial(bwd_kernel, stretch, side), out_shape=(s...  5.95 us
    ppermute x3, starting transfers between devices, behind(): lax.ppermute(block, axis, [((i + step) % count, i) for i in range(count)])  4.57 us
    unnamed x12, local copies, waits for them, and re-layouts  4.37 us
  transfers between devices with their start and end apart: 22, of which 7 were waited for; matrix products, arithmetic and copies ran while one was open for 1% of the time, Pallas kernels for 13%

profile of v9, /device:TPU:1, one launch (start us, length us, event | category | flops | bytes accessed | tf_op | source)
XLA Modules:
  0.0 84.2 jit_solution(8457733327656710334)
XLA Ops:
  0.6 3.1 %pair.1.kv_ref = bf16[128,256]{1,0:T(8,128)(2,1)} custom-call(bf16[128,128]{1,0:T(8,128)(2,1)} %k_hbm.1, bf16[128,128]{1,0:T(8,128)(2,1)} %v_hbm.1), custom_call_target="tpu_custom_call" | custom-call | tf_op jit(solution)/shard_map/pair/pallas_call | solution.py:258
  3.7 5.3 %collective-permute-start.2 = (bf16[128,256]{1,0:T(8,128)(2,1)}, bf16[128,256]{1,0:T(8,128)(2,1)S(1)}, u32[]{:S(2)}, u32[]{:S(2)}) collective-permute-start(bf16[128,256]{1,0:T(8,128)(2,1)} %pair.1.kv_ref), channel_id=1, source_target_pairs={{0,48},{16,32},{32,16},{48,0},{1,49},{17,33},{33,17},{49,1},{2,50}... | collective-permute-start | bytes 196616 | tf_op jit(solution)/shard_map/ppermute | solution.py:478
  9.4 0.9 %copy-done.1 = bf16[128,256]{1,0:T(8,128)(2,1)S(1)} copy-done((bf16[128,256]{1,0:T(8,128)(2,1)S(1)}, bf16[128,256]{1,0:T(8,128)(2,1)}, u32[]{:S(2)}) %copy-start.1) | copy-done | bytes 65560
  10.3 0.9 %copy-done.2 = bf16[128,512]{1,0:T(8,128)(2,1)S(1)} copy-done((bf16[128,512]{1,0:T(8,128)(2,1)S(1)}, bf16[128,512]{1,0:T(8,128)(2,1)}, u32[]{:S(2)}) %copy-start.2) | copy-done | bytes 131096
  11.2 0.9 %copy-done.3 = bf16[128,512]{1,0:T(8,128)(2,1)S(1)} copy-done((bf16[128,512]{1,0:T(8,128)(2,1)S(1)}, bf16[128,512]{1,0:T(8,128)(2,1)}, u32[]{:S(2)}) %copy-start.3) | copy-done | bytes 131096
  12.3 2.1 %collective-permute-done.1.refs_2_ = bf16[128,256]{1,0:T(8,128)(2,1)S(1)} collective-permute-done((bf16[128,256]{1,0:T(8,128)(2,1)}, bf16[128,256]{1,0:T(8,128)(2,1)S(1)}, u32[]{:S(2)}, u32[]{:S(2)}) %collective-permute-start.1) | collective-permute-done | bytes 65568 | tf_op jit(solution)/shard_map/ppermute | solution.py:478
  14.4 1.0 %collective-permute-start.8 = (bf16[512,256]{1,0:T(8,128)(2,1)S(1)}, bf16[512,256]{1,0:T(8,128)(2,1)S(1)}, u32[]{:S(2)}, u32[]{:S(2)}) collective-permute-start(bf16[512,256]{1,0:T(8,128)(2,1)S(1)} %stack.1.piece_ref.rest_0_), channel_id=1, source_target_pairs={{192,0},{0,64},{64,128},{128,192},{193,1},{1,65},{65,129},{129,193... | collective-permute-start | bytes 786440 | tf_op jit(solution)/shard_map/ppermute | solution.py:473
  15.4 2.5 %collective-permute-start.6 = (bf16[512,256]{1,0:T(8,128)(2,1)S(1)}, bf16[512,256]{1,0:T(8,128)(2,1)S(1)}, u32[]{:S(2)}, u32[]{:S(2)}) collective-permute-start(bf16[512,256]{1,0:T(8,128)(2,1)S(1)} %stack.1.piece_ref.rest_0_), channel_id=1, source_target_pairs={{128,0},{192,64},{0,128},{64,192},{129,1},{193,65},{1,129},{65,193... | collective-permute-start | bytes 786440 | tf_op jit(solution)/shard_map/ppermute | solution.py:473
  17.9 1.2 %collective-permute-start.4 = (bf16[512,256]{1,0:T(8,128)(2,1)S(1)}, bf16[512,256]{1,0:T(8,128)(2,1)S(1)}, u32[]{:S(2)}, u32[]{:S(2)}) collective-permute-start(bf16[512,256]{1,0:T(8,128)(2,1)S(1)} %stack.1.piece_ref.rest_0_), channel_id=1, source_target_pairs={{64,0},{128,64},{192,128},{0,192},{65,1},{129,65},{193,129},{1,193... | collective-permute-start | bytes 786440 | tf_op jit(solution)/shard_map/ppermute | solution.py:473
  19.7 2.2 %stage.1 = (s32[136]{0:T(256)S(1)}, bf16[512,256]{1,0:T(8,128)(2,1)S(1)}) custom-call(s32[64]{0:T(128)S(1)} %copy-done.4, bf16[512,256]{1,0:T(8,128)(2,1)S(1)} %stack.1.piece_ref.rest_0_), custom_call_target="tpu_custom_call" | custom-call | tf_op jit(solution)/shard_map/stage/pallas_call | solution.py:285
  21.9 2.7 %collective-permute-start.3 = (bf16[512,256]{1,0:T(8,128)(2,1)S(1)}, bf16[512,256]{1,0:T(8,128)(2,1)S(1)}, u32[]{:S(2)}, u32[]{:S(2)}) collective-permute-start(bf16[512,256]{1,0:T(8,128)(2,1)S(1)} %get-tuple-element.41), channel_id=1, source_target_pairs={{0,8},{8,0},{1,9},{9,1},{2,10},{10,2},{3,11},{11,3},{4,12},{12,4},... | collective-permute-start | bytes 786440 | tf_op jit(solution)/shard_map/ppermute | solution.py:478
  24.5 1.5 %collective-permute-start.9 = (bf16[512,256]{1,0:T(8,128)(2,1)S(1)}, bf16[512,256]{1,0:T(8,128)(2,1)S(1)}, u32[]{:S(2)}, u32[]{:S(2)}) collective-permute-start(bf16[512,256]{1,0:T(8,128)(2,1)S(1)} %collective-permute-done.8.rest_3_), channel_id=1, source_target_pairs={{0,8},{8,0},{1,9},{9,1},{2,10},{10,2},{3,11},{11,3},{4,12},{12,4},... | collective-permute-start | bytes 786440 | tf_op jit(solution)/shard_map/ppermute | solution.py:478
  26.0 2.0 %collective-permute-done.6.rest_2_ = bf16[512,256]{1,0:T(8,128)(2,1)S(1)} collective-permute-done((bf16[512,256]{1,0:T(8,128)(2,1)S(1)}, bf16[512,256]{1,0:T(8,128)(2,1)S(1)}, u32[]{:S(2)}, u32[]{:S(2)}) %collective-permute-start.6) | collective-permute-done | bytes 262176 | tf_op jit(solution)/shard_map/ppermute | solution.py:473
  28.1 2.7 %collective-permute-start.7 = (bf16[512,256]{1,0:T(8,128)(2,1)S(1)}, bf16[512,256]{1,0:T(8,128)(2,1)S(1)}, u32[]{:S(2)}, u32[]{:S(2)}) collective-permute-start(bf16[512,256]{1,0:T(8,128)(2,1)S(1)} %collective-permute-done.6.rest_2_), channel_id=1, source_target_pairs={{0,8},{8,0},{1,9},{9,1},{2,10},{10,2},{3,11},{11,3},{4,12},{12,4},... | collective-permute-start | bytes 786440 | tf_op jit(solution)/shard_map/ppermute | solution.py:478
  30.7 2.3 %attention_forward_0.1 = (bf16[5,512,256]{2,1,0:T(8,128)(2,1)S(1)}, bf16[2048,256]{1,0:T(8,128)(2,1)S(1)}, f32[2,8,256]{2,1,0:T(8,128)S(1)}, f32[2,8,256]{2,1,0:T(8,128)S(1)}, f32[2,128,256]{2,1,0:T(8,128)S(1)}) custom-call(s32[136]{0:T(256)S(1)} %get-tuple-element.40.plan_ref, bf16[2,256,128]{2,1,0:T(8,128)(2,1)S(1)} %get-tuple-element.38.token_ref.qs_ref, ...), custom_call_target="tpu_custom_call" | custom-call | flops 3000000000 | bytes 8000000 | tf_op jit(solution)/shard_map/attention_forward_0/pallas_call | solution.py:429
  33.1 1.0 %copy-done.5 = bf16[512,8192]{1,0:T(8,128)(2,1)S(1)} copy-done((bf16[512,8192]{1,0:T(8,128)(2,1)S(1)}, bf16[512,8192]{1,0:T(8,128)(2,1)}, u32[]{:S(2)}) %copy-start.5) | copy-done | bytes 8388632
  34.1 3.9 %attention_forward_1.1 = (bf16[32,8192]{1,0:T(8,128)(2,1)S(1)}, bf16[32,6144]{1,0:T(8,128)(2,1)S(1)}, bf16[32,6144]{1,0:T(8,128)(2,1)S(1)}, bf16[32,6144]{1,0:T(...) custom-call(s32[136]{0:T(256)S(1)} %get-tuple-element.40.plan_ref, ...), custom_call_target="tpu_custom_call" | custom-call | flops 3000000000 | bytes 8000000 | tf_op jit(solution)/shard_map/attention_forward_1/pallas_call | solution.py:429
  38.0 1.4 %collective-permute-start.10 = (bf16[32,6144]{1,0:T(8,128)(2,1)S(1)}, bf16[32,6144]{1,0:T(8,128)(2,1)S(1)}, u32[]{:S(2)}, u32[]{:S(2)}) collective-permute-start(bf16[32,6144]{1,0:T(8,128)(2,1)S(1)} %get-tuple-element.47), channel_id=1, source_target_pairs={{0,1},{1,2},{2,3},{3,0},{4,5},{5,6},{6,7},{7,4},{8,9},{9,10},{10,1... | collective-permute-start | bytes 1179656 | tf_op jit(solution)/shard_map/ppermute | solution.py:468
  39.4 1.5 %collective-permute-start.11 = (bf16[32,6144]{1,0:T(8,128)(2,1)S(1)}, bf16[32,6144]{1,0:T(8,128)(2,1)S(1)}, u32[]{:S(2)}, u32[]{:S(2)}) collective-permute-start(bf16[32,6144]{1,0:T(8,128)(2,1)S(1)} %get-tuple-element.48), channel_id=1, source_target_pairs={{0,3},{1,0},{2,1},{3,2},{4,7},{5,4},{6,5},{7,6},{8,11},{9,8},{10,9... | collective-permute-start | bytes 1179656 | tf_op jit(solution)/shard_map/ppermute | solution.py:468
  40.9 2.6 %attention_backward_1.1 = (f32[2,128,256]{2,1,0:T(8,128)S(1)}, bf16[2048,256]{1,0:T(8,128)(2,1)S(1)}) custom-call(s32[136]{0:T(256)S(1)} %get-tuple-element.40.plan_ref, bf16[5,512,256]{2,1,0:T(8,128)(2,1)S(1)} %get-tuple-element.55.p_ref, bf16[2048,256]{1,0:T(8,128)(2,1)S(1)} %get-tuple-element.56.kv_ref, ...), custom_call_target="tpu_custom_call" | custom-call | flops 20000000000 | bytes 8000000 | tf_op jit(solution)/shard_map/attention_backward_1/pallas_call | solution.py:454
  43.5 1.0 %collective-permute-start.12 = (bf16[2048,256]{1,0:T(8,128)(2,1)S(1)}, bf16[2048,256]{1,0:T(8,128)(2,1)S(1)}, u32[]{:S(2)}, u32[]{:S(2)}) collective-permute-start(bf16[2048,256]{1,0:T(8,128)(2,1)S(1)} %get-tuple-element.60), channel_id=1, source_target_pairs={{0,8},{8,0},{1,9},{9,1},{2,10},{10,2},{3,11},{11,3},{4,12},{12,4},... | collective-permute-start | bytes 3145736 | tf_op jit(solution)/shard_map/ppermute | solution.py:478
  44.5 3.4 %attention_backward_0.1 = (bf16[128,512]{1,0:T(8,128)(2,1)}, bf16[2048,256]{1,0:T(8,128)(2,1)S(1)}) custom-call(s32[136]{0:T(256)S(1)} %get-tuple-element.40.plan_ref, bf16[5,512,256]{2,1,0:T(8,128)(2,1)S(1)} %get-tuple-element.51.p_ref, bf16[2048,256]{1,0:T(8,128)(2,1)S(1)} %get-tuple-element.52.kv_ref, ...), custom_call_target="tpu_custom_call" | custom-call | flops 20000000000 | bytes 8000000 | tf_op jit(solution)/shard_map/attention_backward_0/pallas_call | solution.py:454
  48.2 1.4 %collective-permute-done.10.ahead_in.from_behind = bf16[32,6144]{1,0:T(8,128)(2,1)S(1)} collective-permute-done((bf16[32,6144]{1,0:T(8,128)(2,1)S(1)}, bf16[32,6144]{1,0:T(8,128)(2,1)S(1)}, u32[]{:S(2)}, u32[]{:S(2)}) %collective-permute-start.10) | collective-permute-done | bytes 393248 | tf_op jit(solution)/shard_map/ppermute | solution.py:468
  49.9 1.2 %collective-permute-start.13 = (bf16[32,6144]{1,0:T(8,128)(2,1)S(1)}, bf16[32,6144]{1,0:T(8,128)(2,1)S(1)}, u32[]{:S(2)}, u32[]{:S(2)}) collective-permute-start(bf16[32,6144]{1,0:T(8,128)(2,1)S(1)} %get-tuple-element.61), channel_id=1, source_target_pairs={{0,1},{1,2},{2,3},{3,0},{4,5},{5,6},{6,7},{7,4},{8,9},{9,10},{10,1... | collective-permute-start | bytes 1179656 | tf_op jit(solution)/shard_map/ppermute | solution.py:468
  51.1 1.8 %collective-permute-start.14 = (bf16[32,6144]{1,0:T(8,128)(2,1)S(1)}, bf16[32,6144]{1,0:T(8,128)(2,1)S(1)}, u32[]{:S(2)}, u32[]{:S(2)}) collective-permute-start(bf16[32,6144]{1,0:T(8,128)(2,1)S(1)} %get-tuple-element.62), channel_id=1, source_target_pairs={{0,3},{1,0},{2,1},{3,2},{4,7},{5,4},{6,5},{7,6},{8,11},{9,8},{10,9... | collective-permute-start | bytes 1179656 | tf_op jit(solution)/shard_map/ppermute | solution.py:468
  52.9 2.8 %collective-permute-start.18 = (bf16[512,256]{1,0:T(8,128)(2,1)S(1)}, bf16[512,256]{1,0:T(8,128)(2,1)S(1)}, u32[]{:S(2)}, u32[]{:S(2)}) collective-permute-start(bf16[512,256]{1,0:T(8,128)(2,1)S(1)} %get-tuple-element.72), channel_id=1, source_target_pairs={{0,192},{64,0},{128,64},{192,128},{1,193},{65,1},{129,65},{193,129... | collective-permute-start | bytes 786440 | tf_op jit(solution)/shard_map/ppermute | solution.py:468
  55.7 0.9 %collective-permute-start.17 = (bf16[512,256]{1,0:T(8,128)(2,1)S(1)}, bf16[512,256]{1,0:T(8,128)(2,1)S(1)}, u32[]{:S(2)}, u32[]{:S(2)}) collective-permute-start(bf16[512,256]{1,0:T(8,128)(2,1)S(1)} %get-tuple-element.73), channel_id=1, source_target_pairs={{0,128},{64,192},{128,0},{192,64},{1,129},{65,193},{129,1},{193,65... | collective-permute-start | bytes 786440 | tf_op jit(solution)/shard_map/ppermute | solution.py:468
  56.8 3.9 %collective-permute-done.13.front = bf16[32,6144]{1,0:T(8,128)(2,1)S(1)} collective-permute-done((bf16[32,6144]{1,0:T(8,128)(2,1)S(1)}, bf16[32,6144]{1,0:T(8,128)(2,1)S(1)}, u32[]{:S(2)}, u32[]{:S(2)}) %collective-permute-start.13) | collective-permute-done | bytes 393248 | tf_op jit(solution)/shard_map/ppermute | solution.py:468
  60.9 6.6 %collective-permute-start.15 = (bf16[16,8192]{1,0:T(8,128)(2,1)S(1)}, bf16[16,8192]{1,0:T(8,128)(2,1)S(1)}, u32[]{:S(2)}, u32[]{:S(2)}) collective-permute-start(bf16[16,8192]{1,0:T(8,128)(2,1)S(1)} %get-tuple-element.64), channel_id=1, source_target_pairs={{0,4},{4,0},{1,5},{5,1},{2,6},{6,2},{3,7},{7,3},{8,12},{12,8},{9,1... | collective-permute-start | bytes 786440 | tf_op jit(solution)/shard_map/ppermute | solution.py:478
  67.4 3.6 %collective-permute-done.16.refs_0_ = bf16[512,256]{1,0:T(8,128)(2,1)S(1)} collective-permute-done((bf16[512,256]{1,0:T(8,128)(2,1)S(1)}, bf16[512,256]{1,0:T(8,128)(2,1)S(1)}, u32[]{:S(2)}, u32[]{:S(2)}) %collective-permute-start.16) | collective-permute-done | bytes 262176 | tf_op jit(solution)/shard_map/ppermute | solution.py:468
  71.7 2.2 %collective-permute-start.20 = (bf16[128,256]{1,0:T(8,128)(2,1)S(1)}, bf16[128,256]{1,0:T(8,128)(2,1)S(1)}, u32[]{:S(2)}, u32[]{:S(2)}) collective-permute-start(bf16[128,256]{1,0:T(8,128)(2,1)S(1)} %get-tuple-element.68), channel_id=1, source_target_pairs={{0,48},{16,32},{32,16},{48,0},{1,49},{17,33},{33,17},{49,1},{2,50}... | collective-permute-start | bytes 196616 | tf_op jit(solution)/shard_map/ppermute | solution.py:478
  74.8 8.7 %collective-permute-done.19.refs_1_ = bf16[128,256]{1,0:T(8,128)(2,1)S(1)} collective-permute-done((bf16[128,256]{1,0:T(8,128)(2,1)S(1)}, bf16[128,256]{1,0:T(8,128)(2,1)S(1)}, u32[]{:S(2)}, u32[]{:S(2)}) %collective-permute-start.19) | collective-permute-done | bytes 65568 | tf_op jit(solution)/shard_map/ppermute | solution.py:478
  (39 shorter events, 4.6 us)
Async XLA Ops:
  3.7 8.6 %collective-permute-start.2 = (bf16[128,256]{1,0:T(8,128)(2,1)}, bf16[128,256]{1,0:T(8,128)(2,1)S(1)}, u32[]{:S(2)}, u32[]{:S(2)}) collective-permute-start(bf16[128,256]{1,0:T(8,128)(2,1)} %pair.1.kv_ref), channel_id=1, source_target_pairs={{0,48},{16,32},{32,16},{48,0},{1,49},{17,33},{33,17},{49,1},{2,50}... | collective-permute-start | bytes 196616 | tf_op jit(solution)/shard_map/ppermute | solution.py:478
  9.0 5.4 %collective-permute-start.1 = (bf16[128,256]{1,0:T(8,128)(2,1)}, bf16[128,256]{1,0:T(8,128)(2,1)S(1)}, u32[]{:S(2)}, u32[]{:S(2)}) collective-permute-start(bf16[128,256]{1,0:T(8,128)(2,1)} %pair.1.kv_ref), channel_id=1, source_target_pairs={{0,32},{16,48},{32,0},{48,16},{1,33},{17,49},{33,1},{49,17},{2,34}... | collective-permute-start | bytes 196616 | tf_op jit(solution)/shard_map/ppermute | solution.py:478
  9.0 5.4 %collective-permute-start = (bf16[128,256]{1,0:T(8,128)(2,1)}, bf16[128,256]{1,0:T(8,128)(2,1)S(1)}, u32[]{:S(2)}, u32[]{:S(2)}) collective-permute-start(bf16[128,256]{1,0:T(8,128)(2,1)} %pair.1.kv_ref), channel_id=1, source_target_pairs={{0,16},{16,0},{32,48},{48,32},{1,17},{17,1},{33,49},{49,33},{2,18}... | collective-permute-start | bytes 196616 | tf_op jit(solution)/shard_map/ppermute | solution.py:478
  9.4 0.9 %copy-start.1 = (bf16[128,256]{1,0:T(8,128)(2,1)S(1)}, bf16[128,256]{1,0:T(8,128)(2,1)}, u32[]{:S(2)}) copy-start(bf16[128,256]{1,0:T(8,128)(2,1)} %pair.1.kv_ref) | copy-start | bytes 196612
  10.3 0.9 %copy-start.2 = (bf16[128,512]{1,0:T(8,128)(2,1)S(1)}, bf16[128,512]{1,0:T(8,128)(2,1)}, u32[]{:S(2)}) copy-start(bf16[128,512]{1,0:T(8,128)(2,1)} %q_hbm.1) | copy-start | bytes 393220
  11.2 0.9 %copy-start.3 = (bf16[128,512]{1,0:T(8,128)(2,1)S(1)}, bf16[128,512]{1,0:T(8,128)(2,1)}, u32[]{:S(2)}) copy-start(bf16[128,512]{1,0:T(8,128)(2,1)} %do_hbm.1) | copy-start | bytes 393220
  14.4 10.1 %collective-permute-start.8 = (bf16[512,256]{1,0:T(8,128)(2,1)S(1)}, bf16[512,256]{1,0:T(8,128)(2,1)S(1)}, u32[]{:S(2)}, u32[]{:S(2)}) collective-permute-start(bf16[512,256]{1,0:T(8,128)(2,1)S(1)} %stack.1.piece_ref.rest_0_), channel_id=1, source_target_pairs={{192,0},{0,64},{64,128},{128,192},{193,1},{1,65},{65,129},{129,193... | collective-permute-start | bytes 786440 | tf_op jit(solution)/shard_map/ppermute | solution.py:473
  15.4 12.7 %collective-permute-start.6 = (bf16[512,256]{1,0:T(8,128)(2,1)S(1)}, bf16[512,256]{1,0:T(8,128)(2,1)S(1)}, u32[]{:S(2)}, u32[]{:S(2)}) collective-permute-start(bf16[512,256]{1,0:T(8,128)(2,1)S(1)} %stack.1.piece_ref.rest_0_), channel_id=1, source_target_pairs={{128,0},{192,64},{0,128},{64,192},{129,1},{193,65},{1,129},{65,193... | collective-permute-start | bytes 786440 | tf_op jit(solution)/shard_map/ppermute | solution.py:473
  17.9 12.9 %collective-permute-start.4 = (bf16[512,256]{1,0:T(8,128)(2,1)S(1)}, bf16[512,256]{1,0:T(8,128)(2,1)S(1)}, u32[]{:S(2)}, u32[]{:S(2)}) collective-permute-start(bf16[512,256]{1,0:T(8,128)(2,1)S(1)} %stack.1.piece_ref.rest_0_), channel_id=1, source_target_pairs={{64,0},{128,64},{192,128},{0,192},{65,1},{129,65},{193,129},{1,193... | collective-permute-start | bytes 786440 | tf_op jit(solution)/shard_map/ppermute | solution.py:473
  19.0 0.7 copy-start.4
  21.9 11.2 %collective-permute-start.3 = (bf16[512,256]{1,0:T(8,128)(2,1)S(1)}, bf16[512,256]{1,0:T(8,128)(2,1)S(1)}, u32[]{:S(2)}, u32[]{:S(2)}) collective-permute-start(bf16[512,256]{1,0:T(8,128)(2,1)S(1)} %get-tuple-element.41), channel_id=1, source_target_pairs={{0,8},{8,0},{1,9},{9,1},{2,10},{10,2},{3,11},{11,3},{4,12},{12,4},... | collective-permute-start | bytes 786440 | tf_op jit(solution)/shard_map/ppermute | solution.py:478
  24.5 8.5 %collective-permute-start.9 = (bf16[512,256]{1,0:T(8,128)(2,1)S(1)}, bf16[512,256]{1,0:T(8,128)(2,1)S(1)}, u32[]{:S(2)}, u32[]{:S(2)}) collective-permute-start(bf16[512,256]{1,0:T(8,128)(2,1)S(1)} %collective-permute-done.8.rest_3_), channel_id=1, source_target_pairs={{0,8},{8,0},{1,9},{9,1},{2,10},{10,2},{3,11},{11,3},{4,12},{12,4},... | collective-permute-start | bytes 786440 | tf_op jit(solution)/shard_map/ppermute | solution.py:478
  28.1 5.0 %collective-permute-start.7 = (bf16[512,256]{1,0:T(8,128)(2,1)S(1)}, bf16[512,256]{1,0:T(8,128)(2,1)S(1)}, u32[]{:S(2)}, u32[]{:S(2)}) collective-permute-start(bf16[512,256]{1,0:T(8,128)(2,1)S(1)} %collective-permute-done.6.rest_2_), channel_id=1, source_target_pairs={{0,8},{8,0},{1,9},{9,1},{2,10},{10,2},{3,11},{11,3},{4,12},{12,4},... | collective-permute-start | bytes 786440 | tf_op jit(solution)/shard_map/ppermute | solution.py:478
  30.7 2.3 %collective-permute-start.5 = (bf16[512,256]{1,0:T(8,128)(2,1)S(1)}, bf16[512,256]{1,0:T(8,128)(2,1)S(1)}, u32[]{:S(2)}, u32[]{:S(2)}) collective-permute-start(bf16[512,256]{1,0:T(8,128)(2,1)S(1)} %collective-permute-done.4.rest_1_), channel_id=1, source_target_pairs={{0,8},{8,0},{1,9},{9,1},{2,10},{10,2},{3,11},{11,3},{4,12},{12,4},... | collective-permute-start | bytes 786440 | tf_op jit(solution)/shard_map/ppermute | solution.py:478
  30.7 3.4 %copy-start.5 = (bf16[512,8192]{1,0:T(8,128)(2,1)S(1)}, bf16[512,8192]{1,0:T(8,128)(2,1)}, u32[]{:S(2)}) copy-start(bf16[512,8192]{1,0:T(8,128)(2,1)} %rest_5_.1) | copy-start | bytes 25165828
  38.0 11.6 %collective-permute-start.10 = (bf16[32,6144]{1,0:T(8,128)(2,1)S(1)}, bf16[32,6144]{1,0:T(8,128)(2,1)S(1)}, u32[]{:S(2)}, u32[]{:S(2)}) collective-permute-start(bf16[32,6144]{1,0:T(8,128)(2,1)S(1)} %get-tuple-element.47), channel_id=1, source_target_pairs={{0,1},{1,2},{2,3},{3,0},{4,5},{5,6},{6,7},{7,4},{8,9},{9,10},{10,1... | collective-permute-start | bytes 1179656 | tf_op jit(solution)/shard_map/ppermute | solution.py:468
  39.4 10.2 %collective-permute-start.11 = (bf16[32,6144]{1,0:T(8,128)(2,1)S(1)}, bf16[32,6144]{1,0:T(8,128)(2,1)S(1)}, u32[]{:S(2)}, u32[]{:S(2)}) collective-permute-start(bf16[32,6144]{1,0:T(8,128)(2,1)S(1)} %get-tuple-element.48), channel_id=1, source_target_pairs={{0,3},{1,0},{2,1},{3,2},{4,7},{5,4},{6,5},{7,6},{8,11},{9,8},{10,9... | collective-permute-start | bytes 1179656 | tf_op jit(solution)/shard_map/ppermute | solution.py:468
  43.5 4.4 %collective-permute-start.12 = (bf16[2048,256]{1,0:T(8,128)(2,1)S(1)}, bf16[2048,256]{1,0:T(8,128)(2,1)S(1)}, u32[]{:S(2)}, u32[]{:S(2)}) collective-permute-start(bf16[2048,256]{1,0:T(8,128)(2,1)S(1)} %get-tuple-element.60), channel_id=1, source_target_pairs={{0,8},{8,0},{1,9},{9,1},{2,10},{10,2},{3,11},{11,3},{4,12},{12,4},... | collective-permute-start | bytes 3145736 | tf_op jit(solution)/shard_map/ppermute | solution.py:478
  49.9 10.8 %collective-permute-start.13 = (bf16[32,6144]{1,0:T(8,128)(2,1)S(1)}, bf16[32,6144]{1,0:T(8,128)(2,1)S(1)}, u32[]{:S(2)}, u32[]{:S(2)}) collective-permute-start(bf16[32,6144]{1,0:T(8,128)(2,1)S(1)} %get-tuple-element.61), channel_id=1, source_target_pairs={{0,1},{1,2},{2,3},{3,0},{4,5},{5,6},{6,7},{7,4},{8,9},{9,10},{10,1... | collective-permute-start | bytes 1179656 | tf_op jit(solution)/shard_map/ppermute | solution.py:468
  51.1 9.6 %collective-permute-start.14 = (bf16[32,6144]{1,0:T(8,128)(2,1)S(1)}, bf16[32,6144]{1,0:T(8,128)(2,1)S(1)}, u32[]{:S(2)}, u32[]{:S(2)}) collective-permute-start(bf16[32,6144]{1,0:T(8,128)(2,1)S(1)} %get-tuple-element.62), channel_id=1, source_target_pairs={{0,3},{1,0},{2,1},{3,2},{4,7},{5,4},{6,5},{7,6},{8,11},{9,8},{10,9... | collective-permute-start | bytes 1179656 | tf_op jit(solution)/shard_map/ppermute | solution.py:468
  52.9 14.5 %collective-permute-start.18 = (bf16[512,256]{1,0:T(8,128)(2,1)S(1)}, bf16[512,256]{1,0:T(8,128)(2,1)S(1)}, u32[]{:S(2)}, u32[]{:S(2)}) collective-permute-start(bf16[512,256]{1,0:T(8,128)(2,1)S(1)} %get-tuple-element.72), channel_id=1, source_target_pairs={{0,192},{64,0},{128,64},{192,128},{1,193},{65,1},{129,65},{193,129... | collective-permute-start | bytes 786440 | tf_op jit(solution)/shard_map/ppermute | solution.py:468
  55.7 11.7 %collective-permute-start.17 = (bf16[512,256]{1,0:T(8,128)(2,1)S(1)}, bf16[512,256]{1,0:T(8,128)(2,1)S(1)}, u32[]{:S(2)}, u32[]{:S(2)}) collective-permute-start(bf16[512,256]{1,0:T(8,128)(2,1)S(1)} %get-tuple-element.73), channel_id=1, source_target_pairs={{0,128},{64,192},{128,0},{192,64},{1,129},{65,193},{129,1},{193,65... | collective-permute-start | bytes 786440 | tf_op jit(solution)/shard_map/ppermute | solution.py:468
  56.6 14.5 %collective-permute-start.16 = (bf16[512,256]{1,0:T(8,128)(2,1)S(1)}, bf16[512,256]{1,0:T(8,128)(2,1)S(1)}, u32[]{:S(2)}, u32[]{:S(2)}) collective-permute-start(bf16[512,256]{1,0:T(8,128)(2,1)S(1)} %get-tuple-element.74), channel_id=1, source_target_pairs={{0,64},{64,128},{128,192},{192,0},{1,65},{65,129},{129,193},{193,1... | collective-permute-start | bytes 786440 | tf_op jit(solution)/shard_map/ppermute | solution.py:468
  60.9 13.9 %collective-permute-start.15 = (bf16[16,8192]{1,0:T(8,128)(2,1)S(1)}, bf16[16,8192]{1,0:T(8,128)(2,1)S(1)}, u32[]{:S(2)}, u32[]{:S(2)}) collective-permute-start(bf16[16,8192]{1,0:T(8,128)(2,1)S(1)} %get-tuple-element.64), channel_id=1, source_target_pairs={{0,4},{4,0},{1,5},{5,1},{2,6},{6,2},{3,7},{7,3},{8,12},{12,8},{9,1... | collective-permute-start | bytes 786440 | tf_op jit(solution)/shard_map/ppermute | solution.py:478
  71.2 12.3 %collective-permute-start.19 = (bf16[128,256]{1,0:T(8,128)(2,1)S(1)}, bf16[128,256]{1,0:T(8,128)(2,1)S(1)}, u32[]{:S(2)}, u32[]{:S(2)}) collective-permute-start(bf16[128,256]{1,0:T(8,128)(2,1)S(1)} %get-tuple-element.67), channel_id=1, source_target_pairs={{0,32},{16,48},{32,0},{48,16},{1,33},{17,49},{33,1},{49,17},{2,34}... | collective-permute-start | bytes 196616 | tf_op jit(solution)/shard_map/ppermute | solution.py:478
  71.7 11.8 %collective-permute-start.20 = (bf16[128,256]{1,0:T(8,128)(2,1)S(1)}, bf16[128,256]{1,0:T(8,128)(2,1)S(1)}, u32[]{:S(2)}, u32[]{:S(2)}) collective-permute-start(bf16[128,256]{1,0:T(8,128)(2,1)S(1)} %get-tuple-element.68), channel_id=1, source_target_pairs={{0,48},{16,32},{32,16},{48,0},{1,49},{17,33},{33,17},{49,1},{2,50}... | collective-permute-start | bytes 196616 | tf_op jit(solution)/shard_map/ppermute | solution.py:478
  73.9 9.7 %collective-permute-start.21 = (bf16[128,256]{1,0:T(8,128)(2,1)S(1)}, bf16[128,256]{1,0:T(8,128)(2,1)S(1)}, u32[]{:S(2)}, u32[]{:S(2)}) collective-permute-start(bf16[128,256]{1,0:T(8,128)(2,1)S(1)} %get-tuple-element.69), channel_id=1, source_target_pairs={{0,16},{16,0},{32,48},{48,32},{1,17},{17,1},{33,49},{49,33},{2,18}... | collective-permute-start | bytes 196616 | tf_op jit(solution)/shard_map/ppermute | solution.py:478
  74.8 9.4 %copy-start = (bf16[16,8192]{1,0:T(8,128)(2,1)}, bf16[16,8192]{1,0:T(8,128)(2,1)S(1)}, u32[]{:S(2)}) copy-start(bf16[16,8192]{1,0:T(8,128)(2,1)S(1)} %add_convert_fusion.1.token_ref) | copy-start | bytes 786436

commit v10 on v9

--- a/solution.py
+++ b/solution.py
@@ -259,7 +259,7 @@
         pair_kernel,
         out_shape=jax.ShapeDtypeStruct((keys.shape[0], 2 * HD), jnp.bfloat16),
         in_specs=[HBM] * 2,
-        out_specs=HBM,
+        out_specs=VMEM,
         scratch_shapes=[pltpu.SemaphoreType.DMA((2,))],
         compiler_params=pltpu.CompilerParams(vmem_limit_bytes=60 * MIB),
         name="pair",
@@ -507,7 +507,7 @@
         own, from_behind, from_ahead, ahead(front, "y", 1), ahead(back, "y", NY - 1))
     terms = share(mixed, near, *others)
     mixed = total_of([mixed, across(give, "zh", 1)])
-    k_grad, v_grad = finish(mixed, terms[0], *[across(terms[step], "zl", step) for step in (2, 3, 1)])
+    k_grad, v_grad = finish(mixed, terms[0], *[across(terms[step], "zl", step) for step in range(1, NZ)])
     return mixed, q_grad, k_grad, v_grad
 
 

time: 84.7 us -> 83.1 us (0.981)
  the two profiles are of different devices: /device:TPU:1 before, /device:TPU:35 now
where the time goes in v10:
time: 83.1 us; the launch traced here: 82.8 us
  starting transfers between devices  34.2 us (41%)
  waiting for transfers between devices  25.8 us (31%)
  Pallas kernels  17.2 us (21%)
  local copies, waits for them, and re-layouts  4.45 us (5%)
    ppermute x12, starting transfers between devices, across(): return lax.ppermute(block, axis, [(i, i ^ step) for i in range(count)])  20.7 us
    ppermute x12, waiting for transfers between devices, across(): return lax.ppermute(block, axis, [(i, i ^ step) for i in range(count)])  16.1 us
    ppermute x7, starting transfers between devices, ahead(): lax.ppermute(block, axis, [(i, (i + step) % count) for i in range(count)])  9.52 us
    ppermute x7, waiting for transfers between devices, ahead(): lax.ppermute(block, axis, [(i, (i + step) % count) for i in range(count)])  8.63 us
    pallas_call x2, Pallas kernels, forward(): pl.pallas_call(functools.partial(far_kernel if side else near_kernel, str...  6.16 us
    pallas_call x2, Pallas kernels, backward(): pl.pallas_call(functools.partial(bwd_kernel, stretch, side), out_shape=(s...  5.95 us
    unnamed x12, local copies, waits for them, and re-layouts  4.38 us
    ppermute x3, starting transfers between devices, behind(): lax.ppermute(block, axis, [((i + step) % count, i) for i in range(count)])  3.99 us
  transfers between devices with their start and end apart: 22, of which 9 were waited for; matrix products, arithmetic and copies ran while one was open for 1% of the time, Pallas kernels for 13%

profile of v10, /device:TPU:35, one launch (start us, length us, event | category | flops | bytes accessed | tf_op | source)
XLA Modules:
  0.0 82.8 jit_solution(13247919841843273187)
XLA Ops:
  0.6 1.4 %pair.1.kv_ref = bf16[128,256]{1,0:T(8,128)(2,1)} custom-call(bf16[128,128]{1,0:T(8,128)(2,1)} %k_hbm.1, bf16[128,128]{1,0:T(8,128)(2,1)} %v_hbm.1), custom_call_target="tpu_custom_call" | custom-call | tf_op jit(solution)/shard_map/pair/pallas_call | solution.py:258
  2.1 1.7 %collective-permute-start.2 = (bf16[128,256]{1,0:T(8,128)(2,1)}, bf16[128,256]{1,0:T(8,128)(2,1)S(1)}, u32[]{:S(2)}, u32[]{:S(2)}) collective-permute-start(bf16[128,256]{1,0:T(8,128)(2,1)} %pair.1.kv_ref), channel_id=1, source_target_pairs={{0,48},{16,32},{32,16},{48,0},{1,49},{17,33},{33,17},{49,1},{2,50}... | collective-permute-start | bytes 196616 | tf_op jit(solution)/shard_map/ppermute | solution.py:478
  3.8 1.5 %collective-permute-start.1 = (bf16[128,256]{1,0:T(8,128)(2,1)}, bf16[128,256]{1,0:T(8,128)(2,1)S(1)}, u32[]{:S(2)}, u32[]{:S(2)}) collective-permute-start(bf16[128,256]{1,0:T(8,128)(2,1)} %pair.1.kv_ref), channel_id=1, source_target_pairs={{0,32},{16,48},{32,0},{48,16},{1,33},{17,49},{33,1},{49,17},{2,34}... | collective-permute-start | bytes 196616 | tf_op jit(solution)/shard_map/ppermute | solution.py:478
  5.2 1.1 %collective-permute-start = (bf16[128,256]{1,0:T(8,128)(2,1)}, bf16[128,256]{1,0:T(8,128)(2,1)S(1)}, u32[]{:S(2)}, u32[]{:S(2)}) collective-permute-start(bf16[128,256]{1,0:T(8,128)(2,1)} %pair.1.kv_ref), channel_id=1, source_target_pairs={{0,16},{16,0},{32,48},{48,32},{1,17},{17,1},{33,49},{49,33},{2,18}... | collective-permute-start | bytes 196616 | tf_op jit(solution)/shard_map/ppermute | solution.py:478
  9.3 1.4 %collective-permute-done.refs_1_ = bf16[128,256]{1,0:T(8,128)(2,1)S(1)} collective-permute-done((bf16[128,256]{1,0:T(8,128)(2,1)}, bf16[128,256]{1,0:T(8,128)(2,1)S(1)}, u32[]{:S(2)}, u32[]{:S(2)}) %collective-permute-start) | collective-permute-done | bytes 65568 | tf_op jit(solution)/shard_map/ppermute | solution.py:478
  10.6 1.3 %collective-permute-start.8 = (bf16[512,256]{1,0:T(8,128)(2,1)S(1)}, bf16[512,256]{1,0:T(8,128)(2,1)S(1)}, u32[]{:S(2)}, u32[]{:S(2)}) collective-permute-start(bf16[512,256]{1,0:T(8,128)(2,1)S(1)} %stack.1.piece_ref.rest_0_), channel_id=1, source_target_pairs={{192,0},{0,64},{64,128},{128,192},{193,1},{1,65},{65,129},{129,193... | collective-permute-start | bytes 786440 | tf_op jit(solution)/shard_map/ppermute | solution.py:473
  12.8 1.9 %collective-permute-start.4 = (bf16[512,256]{1,0:T(8,128)(2,1)S(1)}, bf16[512,256]{1,0:T(8,128)(2,1)S(1)}, u32[]{:S(2)}, u32[]{:S(2)}) collective-permute-start(bf16[512,256]{1,0:T(8,128)(2,1)S(1)} %stack.1.piece_ref.rest_0_), channel_id=1, source_target_pairs={{64,0},{128,64},{192,128},{0,192},{65,1},{129,65},{193,129},{1,193... | collective-permute-start | bytes 786440 | tf_op jit(solution)/shard_map/ppermute | solution.py:473
  15.3 2.2 %stage.1 = (s32[136]{0:T(256)S(1)}, bf16[512,256]{1,0:T(8,128)(2,1)S(1)}) custom-call(s32[64]{0:T(128)S(1)} %copy-done.4, bf16[512,256]{1,0:T(8,128)(2,1)S(1)} %stack.1.piece_ref.rest_0_), custom_call_target="tpu_custom_call" | custom-call | tf_op jit(solution)/shard_map/stage/pallas_call | solution.py:285
  17.5 2.7 %collective-permute-start.3 = (bf16[512,256]{1,0:T(8,128)(2,1)S(1)}, bf16[512,256]{1,0:T(8,128)(2,1)S(1)}, u32[]{:S(2)}, u32[]{:S(2)}) collective-permute-start(bf16[512,256]{1,0:T(8,128)(2,1)S(1)} %get-tuple-element.41), channel_id=1, source_target_pairs={{0,8},{8,0},{1,9},{9,1},{2,10},{10,2},{3,11},{11,3},{4,12},{12,4},... | collective-permute-start | bytes 786440 | tf_op jit(solution)/shard_map/ppermute | solution.py:478
  20.2 1.6 %collective-permute-start.9 = (bf16[512,256]{1,0:T(8,128)(2,1)S(1)}, bf16[512,256]{1,0:T(8,128)(2,1)S(1)}, u32[]{:S(2)}, u32[]{:S(2)}) collective-permute-start(bf16[512,256]{1,0:T(8,128)(2,1)S(1)} %collective-permute-done.8.rest_3_), channel_id=1, source_target_pairs={{0,8},{8,0},{1,9},{9,1},{2,10},{10,2},{3,11},{11,3},{4,12},{12,4},... | collective-permute-start | bytes 786440 | tf_op jit(solution)/shard_map/ppermute | solution.py:478
  21.8 3.0 %collective-permute-start.7 = (bf16[512,256]{1,0:T(8,128)(2,1)S(1)}, bf16[512,256]{1,0:T(8,128)(2,1)S(1)}, u32[]{:S(2)}, u32[]{:S(2)}) collective-permute-start(bf16[512,256]{1,0:T(8,128)(2,1)S(1)} %collective-permute-done.6.rest_2_), channel_id=1, source_target_pairs={{0,8},{8,0},{1,9},{9,1},{2,10},{10,2},{3,11},{11,3},{4,12},{12,4},... | collective-permute-start | bytes 786440 | tf_op jit(solution)/shard_map/ppermute | solution.py:478
  24.8 1.1 %collective-permute-done.4.rest_1_ = bf16[512,256]{1,0:T(8,128)(2,1)S(1)} collective-permute-done((bf16[512,256]{1,0:T(8,128)(2,1)S(1)}, bf16[512,256]{1,0:T(8,128)(2,1)S(1)}, u32[]{:S(2)}, u32[]{:S(2)}) %collective-permute-start.4) | collective-permute-done | bytes 262176 | tf_op jit(solution)/shard_map/ppermute | solution.py:473
  25.9 1.2 %collective-permute-start.5 = (bf16[512,256]{1,0:T(8,128)(2,1)S(1)}, bf16[512,256]{1,0:T(8,128)(2,1)S(1)}, u32[]{:S(2)}, u32[]{:S(2)}) collective-permute-start(bf16[512,256]{1,0:T(8,128)(2,1)S(1)} %collective-permute-done.4.rest_1_), channel_id=1, source_target_pairs={{0,8},{8,0},{1,9},{9,1},{2,10},{10,2},{3,11},{11,3},{4,12},{12,4},... | collective-permute-start | bytes 786440 | tf_op jit(solution)/shard_map/ppermute | solution.py:478
  27.1 2.3 %attention_forward_0.1 = (bf16[5,512,256]{2,1,0:T(8,128)(2,1)S(1)}, bf16[2048,256]{1,0:T(8,128)(2,1)S(1)}, f32[2,8,256]{2,1,0:T(8,128)S(1)}, f32[2,8,256]{2,1,0:T(8,128)S(1)}, f32[2,128,256]{2,1,0:T(8,128)S(1)}) custom-call(s32[136]{0:T(256)S(1)} %get-tuple-element.40.plan_ref, bf16[2,256,128]{2,1,0:T(8,128)(2,1)S(1)} %get-tuple-element.38.token_ref.qs_ref, ...), custom_call_target="tpu_custom_call" | custom-call | flops 3000000000 | bytes 8000000 | tf_op jit(solution)/shard_map/attention_forward_0/pallas_call | solution.py:429
  30.5 3.9 %attention_forward_1.1 = (bf16[32,8192]{1,0:T(8,128)(2,1)S(1)}, bf16[32,6144]{1,0:T(8,128)(2,1)S(1)}, bf16[32,6144]{1,0:T(8,128)(2,1)S(1)}, bf16[32,6144]{1,0:T(...) custom-call(s32[136]{0:T(256)S(1)} %get-tuple-element.40.plan_ref, ...), custom_call_target="tpu_custom_call" | custom-call | flops 3000000000 | bytes 8000000 | tf_op jit(solution)/shard_map/attention_forward_1/pallas_call | solution.py:429
  34.4 1.4 %collective-permute-start.10 = (bf16[32,6144]{1,0:T(8,128)(2,1)S(1)}, bf16[32,6144]{1,0:T(8,128)(2,1)S(1)}, u32[]{:S(2)}, u32[]{:S(2)}) collective-permute-start(bf16[32,6144]{1,0:T(8,128)(2,1)S(1)} %get-tuple-element.47), channel_id=1, source_target_pairs={{0,1},{1,2},{2,3},{3,0},{4,5},{5,6},{6,7},{7,4},{8,9},{9,10},{10,1... | collective-permute-start | bytes 1179656 | tf_op jit(solution)/shard_map/ppermute | solution.py:468
  35.7 1.5 %collective-permute-start.11 = (bf16[32,6144]{1,0:T(8,128)(2,1)S(1)}, bf16[32,6144]{1,0:T(8,128)(2,1)S(1)}, u32[]{:S(2)}, u32[]{:S(2)}) collective-permute-start(bf16[32,6144]{1,0:T(8,128)(2,1)S(1)} %get-tuple-element.48), channel_id=1, source_target_pairs={{0,3},{1,0},{2,1},{3,2},{4,7},{5,4},{6,5},{7,6},{8,11},{9,8},{10,9... | collective-permute-start | bytes 1179656 | tf_op jit(solution)/shard_map/ppermute | solution.py:468
  37.3 2.6 %attention_backward_1.1 = (f32[2,128,256]{2,1,0:T(8,128)S(1)}, bf16[2048,256]{1,0:T(8,128)(2,1)S(1)}) custom-call(s32[136]{0:T(256)S(1)} %get-tuple-element.40.plan_ref, bf16[5,512,256]{2,1,0:T(8,128)(2,1)S(1)} %get-tuple-element.55.p_ref, bf16[2048,256]{1,0:T(8,128)(2,1)S(1)} %get-tuple-element.56.kv_ref, ...), custom_call_target="tpu_custom_call" | custom-call | flops 20000000000 | bytes 8000000 | tf_op jit(solution)/shard_map/attention_backward_1/pallas_call | solution.py:454
  40.4 3.4 %attention_backward_0.1 = (bf16[128,512]{1,0:T(8,128)(2,1)}, bf16[2048,256]{1,0:T(8,128)(2,1)S(1)}) custom-call(s32[136]{0:T(256)S(1)} %get-tuple-element.40.plan_ref, bf16[5,512,256]{2,1,0:T(8,128)(2,1)S(1)} %get-tuple-element.51.p_ref, bf16[2048,256]{1,0:T(8,128)(2,1)S(1)} %get-tuple-element.52.kv_ref, ...), custom_call_target="tpu_custom_call" | custom-call | flops 20000000000 | bytes 8000000 | tf_op jit(solution)/shard_map/attention_backward_0/pallas_call | solution.py:454
  44.1 2.5 %collective-permute-done.10.ahead_in.from_behind = bf16[32,6144]{1,0:T(8,128)(2,1)S(1)} collective-permute-done((bf16[32,6144]{1,0:T(8,128)(2,1)S(1)}, bf16[32,6144]{1,0:T(8,128)(2,1)S(1)}, u32[]{:S(2)}, u32[]{:S(2)}) %collective-permute-start.10) | collective-permute-done | bytes 393248 | tf_op jit(solution)/shard_map/ppermute | solution.py:468
  46.8 1.2 %collective-permute-start.13 = (bf16[32,6144]{1,0:T(8,128)(2,1)S(1)}, bf16[32,6144]{1,0:T(8,128)(2,1)S(1)}, u32[]{:S(2)}, u32[]{:S(2)}) collective-permute-start(bf16[32,6144]{1,0:T(8,128)(2,1)S(1)} %get-tuple-element.61), channel_id=1, source_target_pairs={{0,1},{1,2},{2,3},{3,0},{4,5},{5,6},{6,7},{7,4},{8,9},{9,10},{10,1... | collective-permute-start | bytes 1179656 | tf_op jit(solution)/shard_map/ppermute | solution.py:468
  48.0 1.8 %collective-permute-start.14 = (bf16[32,6144]{1,0:T(8,128)(2,1)S(1)}, bf16[32,6144]{1,0:T(8,128)(2,1)S(1)}, u32[]{:S(2)}, u32[]{:S(2)}) collective-permute-start(bf16[32,6144]{1,0:T(8,128)(2,1)S(1)} %get-tuple-element.62), channel_id=1, source_target_pairs={{0,3},{1,0},{2,1},{3,2},{4,7},{5,4},{6,5},{7,6},{8,11},{9,8},{10,9... | collective-permute-start | bytes 1179656 | tf_op jit(solution)/shard_map/ppermute | solution.py:468
  50.0 2.2 %collective-permute-start.17 = (bf16[512,256]{1,0:T(8,128)(2,1)S(1)}, bf16[512,256]{1,0:T(8,128)(2,1)S(1)}, u32[]{:S(2)}, u32[]{:S(2)}) collective-permute-start(bf16[512,256]{1,0:T(8,128)(2,1)S(1)} %get-tuple-element.73), channel_id=1, source_target_pairs={{0,128},{64,192},{128,0},{192,64},{1,129},{65,193},{129,1},{193,65... | collective-permute-start | bytes 786440 | tf_op jit(solution)/shard_map/ppermute | solution.py:468
  52.1 1.4 %collective-permute-start.16 = (bf16[512,256]{1,0:T(8,128)(2,1)S(1)}, bf16[512,256]{1,0:T(8,128)(2,1)S(1)}, u32[]{:S(2)}, u32[]{:S(2)}) collective-permute-start(bf16[512,256]{1,0:T(8,128)(2,1)S(1)} %get-tuple-element.74), channel_id=1, source_target_pairs={{0,64},{64,128},{128,192},{192,0},{1,65},{65,129},{129,193},{193,1... | collective-permute-start | bytes 786440 | tf_op jit(solution)/shard_map/ppermute | solution.py:468
  53.5 4.7 %collective-permute-done.13.front = bf16[32,6144]{1,0:T(8,128)(2,1)S(1)} collective-permute-done((bf16[32,6144]{1,0:T(8,128)(2,1)S(1)}, bf16[32,6144]{1,0:T(8,128)(2,1)S(1)}, u32[]{:S(2)}, u32[]{:S(2)}) %collective-permute-start.13) | collective-permute-done | bytes 393248 | tf_op jit(solution)/shard_map/ppermute | solution.py:468
  58.5 4.7 %collective-permute-start.15 = (bf16[16,8192]{1,0:T(8,128)(2,1)S(1)}, bf16[16,8192]{1,0:T(8,128)(2,1)S(1)}, u32[]{:S(2)}, u32[]{:S(2)}) collective-permute-start(bf16[16,8192]{1,0:T(8,128)(2,1)S(1)} %get-tuple-element.64), channel_id=1, source_target_pairs={{0,4},{4,0},{1,5},{5,1},{2,6},{6,2},{3,7},{7,3},{8,12},{12,8},{9,1... | collective-permute-start | bytes 786440 | tf_op jit(solution)/shard_map/ppermute | solution.py:478
  63.2 1.4 %collective-permute-done.16.refs_0_ = bf16[512,256]{1,0:T(8,128)(2,1)S(1)} collective-permute-done((bf16[512,256]{1,0:T(8,128)(2,1)S(1)}, bf16[512,256]{1,0:T(8,128)(2,1)S(1)}, u32[]{:S(2)}, u32[]{:S(2)}) %collective-permute-start.16) | collective-permute-done | bytes 262176 | tf_op jit(solution)/shard_map/ppermute | solution.py:468
  64.7 1.4 %collective-permute-start.19 = (bf16[128,256]{1,0:T(8,128)(2,1)S(1)}, bf16[128,256]{1,0:T(8,128)(2,1)S(1)}, u32[]{:S(2)}, u32[]{:S(2)}) collective-permute-start(bf16[128,256]{1,0:T(8,128)(2,1)S(1)} %get-tuple-element.67), channel_id=1, source_target_pairs={{0,16},{16,0},{32,48},{48,32},{1,17},{17,1},{33,49},{49,33},{2,18}... | collective-permute-start | bytes 196616 | tf_op jit(solution)/shard_map/ppermute | solution.py:478
  67.4 3.6 %collective-permute-done.15 = bf16[16,8192]{1,0:T(8,128)(2,1)S(1)} collective-permute-done((bf16[16,8192]{1,0:T(8,128)(2,1)S(1)}, bf16[16,8192]{1,0:T(8,128)(2,1)S(1)}, u32[]{:S(2)}, u32[]{:S(2)}) %collective-permute-start.15) | collective-permute-done | bytes 262176 | tf_op jit(solution)/shard_map/ppermute | solution.py:478
  71.2 3.7 %collective-permute-done.19.refs_1_ = bf16[128,256]{1,0:T(8,128)(2,1)S(1)} collective-permute-done((bf16[128,256]{1,0:T(8,128)(2,1)S(1)}, bf16[128,256]{1,0:T(8,128)(2,1)S(1)}, u32[]{:S(2)}, u32[]{:S(2)}) %collective-permute-start.19) | collective-permute-done | bytes 65568 | tf_op jit(solution)/shard_map/ppermute | solution.py:478
  74.9 2.3 %collective-permute-done.20.refs_2_ = bf16[128,256]{1,0:T(8,128)(2,1)S(1)} collective-permute-done((bf16[128,256]{1,0:T(8,128)(2,1)S(1)}, bf16[128,256]{1,0:T(8,128)(2,1)S(1)}, u32[]{:S(2)}, u32[]{:S(2)}) %collective-permute-start.20) | collective-permute-done | bytes 65568 | tf_op jit(solution)/shard_map/ppermute | solution.py:478
  77.2 5.0 %collective-permute-done.21.refs_3_ = bf16[128,256]{1,0:T(8,128)(2,1)S(1)} collective-permute-done((bf16[128,256]{1,0:T(8,128)(2,1)S(1)}, bf16[128,256]{1,0:T(8,128)(2,1)S(1)}, u32[]{:S(2)}, u32[]{:S(2)}) %collective-permute-start.21) | collective-permute-done | bytes 65568 | tf_op jit(solution)/shard_map/ppermute | solution.py:478
  (39 shorter events, 9.2 us)
Async XLA Ops:
  2.1 7.2 %collective-permute-start.2 = (bf16[128,256]{1,0:T(8,128)(2,1)}, bf16[128,256]{1,0:T(8,128)(2,1)S(1)}, u32[]{:S(2)}, u32[]{:S(2)}) collective-permute-start(bf16[128,256]{1,0:T(8,128)(2,1)} %pair.1.kv_ref), channel_id=1, source_target_pairs={{0,48},{16,32},{32,16},{48,0},{1,49},{17,33},{33,17},{49,1},{2,50}... | collective-permute-start | bytes 196616 | tf_op jit(solution)/shard_map/ppermute | solution.py:478
  3.8 5.5 %collective-permute-start.1 = (bf16[128,256]{1,0:T(8,128)(2,1)}, bf16[128,256]{1,0:T(8,128)(2,1)S(1)}, u32[]{:S(2)}, u32[]{:S(2)}) collective-permute-start(bf16[128,256]{1,0:T(8,128)(2,1)} %pair.1.kv_ref), channel_id=1, source_target_pairs={{0,32},{16,48},{32,0},{48,16},{1,33},{17,49},{33,1},{49,17},{2,34}... | collective-permute-start | bytes 196616 | tf_op jit(solution)/shard_map/ppermute | solution.py:478
  5.2 5.4 %collective-permute-start = (bf16[128,256]{1,0:T(8,128)(2,1)}, bf16[128,256]{1,0:T(8,128)(2,1)S(1)}, u32[]{:S(2)}, u32[]{:S(2)}) collective-permute-start(bf16[128,256]{1,0:T(8,128)(2,1)} %pair.1.kv_ref), channel_id=1, source_target_pairs={{0,16},{16,0},{32,48},{48,32},{1,17},{17,1},{33,49},{49,33},{2,18}... | collective-permute-start | bytes 196616 | tf_op jit(solution)/shard_map/ppermute | solution.py:478
  6.3 0.9 %copy-start.1 = (bf16[128,256]{1,0:T(8,128)(2,1)S(1)}, bf16[128,256]{1,0:T(8,128)(2,1)}, u32[]{:S(2)}) copy-start(bf16[128,256]{1,0:T(8,128)(2,1)} %pair.1.kv_ref) | copy-start | bytes 196612
  7.2 0.9 %copy-start.2 = (bf16[128,512]{1,0:T(8,128)(2,1)S(1)}, bf16[128,512]{1,0:T(8,128)(2,1)}, u32[]{:S(2)}) copy-start(bf16[128,512]{1,0:T(8,128)(2,1)} %q_hbm.1) | copy-start | bytes 393220
  8.1 0.9 %copy-start.3 = (bf16[128,512]{1,0:T(8,128)(2,1)S(1)}, bf16[128,512]{1,0:T(8,128)(2,1)}, u32[]{:S(2)}) copy-start(bf16[128,512]{1,0:T(8,128)(2,1)} %do_hbm.1) | copy-start | bytes 393220
  10.6 9.6 %collective-permute-start.8 = (bf16[512,256]{1,0:T(8,128)(2,1)S(1)}, bf16[512,256]{1,0:T(8,128)(2,1)S(1)}, u32[]{:S(2)}, u32[]{:S(2)}) collective-permute-start(bf16[512,256]{1,0:T(8,128)(2,1)S(1)} %stack.1.piece_ref.rest_0_), channel_id=1, source_target_pairs={{192,0},{0,64},{64,128},{128,192},{193,1},{1,65},{65,129},{129,193... | collective-permute-start | bytes 786440 | tf_op jit(solution)/shard_map/ppermute | solution.py:473
  11.9 9.8 %collective-permute-start.6 = (bf16[512,256]{1,0:T(8,128)(2,1)S(1)}, bf16[512,256]{1,0:T(8,128)(2,1)S(1)}, u32[]{:S(2)}, u32[]{:S(2)}) collective-permute-start(bf16[512,256]{1,0:T(8,128)(2,1)S(1)} %stack.1.piece_ref.rest_0_), channel_id=1, source_target_pairs={{128,0},{192,64},{0,128},{64,192},{129,1},{193,65},{1,129},{65,193... | collective-permute-start | bytes 786440 | tf_op jit(solution)/shard_map/ppermute | solution.py:473
  12.8 13.1 %collective-permute-start.4 = (bf16[512,256]{1,0:T(8,128)(2,1)S(1)}, bf16[512,256]{1,0:T(8,128)(2,1)S(1)}, u32[]{:S(2)}, u32[]{:S(2)}) collective-permute-start(bf16[512,256]{1,0:T(8,128)(2,1)S(1)} %stack.1.piece_ref.rest_0_), channel_id=1, source_target_pairs={{64,0},{128,64},{192,128},{0,192},{65,1},{129,65},{193,129},{1,193... | collective-permute-start | bytes 786440 | tf_op jit(solution)/shard_map/ppermute | solution.py:473
  14.6 0.7 copy-start.4
  17.5 11.9 %collective-permute-start.3 = (bf16[512,256]{1,0:T(8,128)(2,1)S(1)}, bf16[512,256]{1,0:T(8,128)(2,1)S(1)}, u32[]{:S(2)}, u32[]{:S(2)}) collective-permute-start(bf16[512,256]{1,0:T(8,128)(2,1)S(1)} %get-tuple-element.41), channel_id=1, source_target_pairs={{0,8},{8,0},{1,9},{9,1},{2,10},{10,2},{3,11},{11,3},{4,12},{12,4},... | collective-permute-start | bytes 786440 | tf_op jit(solution)/shard_map/ppermute | solution.py:478
  20.2 9.2 %collective-permute-start.9 = (bf16[512,256]{1,0:T(8,128)(2,1)S(1)}, bf16[512,256]{1,0:T(8,128)(2,1)S(1)}, u32[]{:S(2)}, u32[]{:S(2)}) collective-permute-start(bf16[512,256]{1,0:T(8,128)(2,1)S(1)} %collective-permute-done.8.rest_3_), channel_id=1, source_target_pairs={{0,8},{8,0},{1,9},{9,1},{2,10},{10,2},{3,11},{11,3},{4,12},{12,4},... | collective-permute-start | bytes 786440 | tf_op jit(solution)/shard_map/ppermute | solution.py:478
  21.8 7.7 %collective-permute-start.7 = (bf16[512,256]{1,0:T(8,128)(2,1)S(1)}, bf16[512,256]{1,0:T(8,128)(2,1)S(1)}, u32[]{:S(2)}, u32[]{:S(2)}) collective-permute-start(bf16[512,256]{1,0:T(8,128)(2,1)S(1)} %collective-permute-done.6.rest_2_), channel_id=1, source_target_pairs={{0,8},{8,0},{1,9},{9,1},{2,10},{10,2},{3,11},{11,3},{4,12},{12,4},... | collective-permute-start | bytes 786440 | tf_op jit(solution)/shard_map/ppermute | solution.py:478
  25.9 3.6 %collective-permute-start.5 = (bf16[512,256]{1,0:T(8,128)(2,1)S(1)}, bf16[512,256]{1,0:T(8,128)(2,1)S(1)}, u32[]{:S(2)}, u32[]{:S(2)}) collective-permute-start(bf16[512,256]{1,0:T(8,128)(2,1)S(1)} %collective-permute-done.4.rest_1_), channel_id=1, source_target_pairs={{0,8},{8,0},{1,9},{9,1},{2,10},{10,2},{3,11},{11,3},{4,12},{12,4},... | collective-permute-start | bytes 786440 | tf_op jit(solution)/shard_map/ppermute | solution.py:478
  27.1 3.4 %copy-start.5 = (bf16[512,8192]{1,0:T(8,128)(2,1)S(1)}, bf16[512,8192]{1,0:T(8,128)(2,1)}, u32[]{:S(2)}) copy-start(bf16[512,8192]{1,0:T(8,128)(2,1)} %rest_5_.1) | copy-start | bytes 25165828
  34.4 12.2 %collective-permute-start.10 = (bf16[32,6144]{1,0:T(8,128)(2,1)S(1)}, bf16[32,6144]{1,0:T(8,128)(2,1)S(1)}, u32[]{:S(2)}, u32[]{:S(2)}) collective-permute-start(bf16[32,6144]{1,0:T(8,128)(2,1)S(1)} %get-tuple-element.47), channel_id=1, source_target_pairs={{0,1},{1,2},{2,3},{3,0},{4,5},{5,6},{6,7},{7,4},{8,9},{9,10},{10,1... | collective-permute-start | bytes 1179656 | tf_op jit(solution)/shard_map/ppermute | solution.py:468
  35.7 10.8 %collective-permute-start.11 = (bf16[32,6144]{1,0:T(8,128)(2,1)S(1)}, bf16[32,6144]{1,0:T(8,128)(2,1)S(1)}, u32[]{:S(2)}, u32[]{:S(2)}) collective-permute-start(bf16[32,6144]{1,0:T(8,128)(2,1)S(1)} %get-tuple-element.48), channel_id=1, source_target_pairs={{0,3},{1,0},{2,1},{3,2},{4,7},{5,4},{6,5},{7,6},{8,11},{9,8},{10,9... | collective-permute-start | bytes 1179656 | tf_op jit(solution)/shard_map/ppermute | solution.py:468
  39.9 3.9 %collective-permute-start.12 = (bf16[2048,256]{1,0:T(8,128)(2,1)S(1)}, bf16[2048,256]{1,0:T(8,128)(2,1)S(1)}, u32[]{:S(2)}, u32[]{:S(2)}) collective-permute-start(bf16[2048,256]{1,0:T(8,128)(2,1)S(1)} %get-tuple-element.60), channel_id=1, source_target_pairs={{0,8},{8,0},{1,9},{9,1},{2,10},{10,2},{3,11},{11,3},{4,12},{12,4},... | collective-permute-start | bytes 3145736 | tf_op jit(solution)/shard_map/ppermute | solution.py:478
  46.8 11.4 %collective-permute-start.13 = (bf16[32,6144]{1,0:T(8,128)(2,1)S(1)}, bf16[32,6144]{1,0:T(8,128)(2,1)S(1)}, u32[]{:S(2)}, u32[]{:S(2)}) collective-permute-start(bf16[32,6144]{1,0:T(8,128)(2,1)S(1)} %get-tuple-element.61), channel_id=1, source_target_pairs={{0,1},{1,2},{2,3},{3,0},{4,5},{5,6},{6,7},{7,4},{8,9},{9,10},{10,1... | collective-permute-start | bytes 1179656 | tf_op jit(solution)/shard_map/ppermute | solution.py:468
  48.0 10.2 %collective-permute-start.14 = (bf16[32,6144]{1,0:T(8,128)(2,1)S(1)}, bf16[32,6144]{1,0:T(8,128)(2,1)S(1)}, u32[]{:S(2)}, u32[]{:S(2)}) collective-permute-start(bf16[32,6144]{1,0:T(8,128)(2,1)S(1)} %get-tuple-element.62), channel_id=1, source_target_pairs={{0,3},{1,0},{2,1},{3,2},{4,7},{5,4},{6,5},{7,6},{8,11},{9,8},{10,9... | collective-permute-start | bytes 1179656 | tf_op jit(solution)/shard_map/ppermute | solution.py:468
  49.9 13.3 %collective-permute-start.18 = (bf16[512,256]{1,0:T(8,128)(2,1)S(1)}, bf16[512,256]{1,0:T(8,128)(2,1)S(1)}, u32[]{:S(2)}, u32[]{:S(2)}) collective-permute-start(bf16[512,256]{1,0:T(8,128)(2,1)S(1)} %get-tuple-element.72), channel_id=1, source_target_pairs={{0,192},{64,0},{128,64},{192,128},{1,193},{65,1},{129,65},{193,129... | collective-permute-start | bytes 786440 | tf_op jit(solution)/shard_map/ppermute | solution.py:468
  50.0 13.2 %collective-permute-start.17 = (bf16[512,256]{1,0:T(8,128)(2,1)S(1)}, bf16[512,256]{1,0:T(8,128)(2,1)S(1)}, u32[]{:S(2)}, u32[]{:S(2)}) collective-permute-start(bf16[512,256]{1,0:T(8,128)(2,1)S(1)} %get-tuple-element.73), channel_id=1, source_target_pairs={{0,128},{64,192},{128,0},{192,64},{1,129},{65,193},{129,1},{193,65... | collective-permute-start | bytes 786440 | tf_op jit(solution)/shard_map/ppermute | solution.py:468
  52.1 12.4 %collective-permute-start.16 = (bf16[512,256]{1,0:T(8,128)(2,1)S(1)}, bf16[512,256]{1,0:T(8,128)(2,1)S(1)}, u32[]{:S(2)}, u32[]{:S(2)}) collective-permute-start(bf16[512,256]{1,0:T(8,128)(2,1)S(1)} %get-tuple-element.74), channel_id=1, source_target_pairs={{0,64},{64,128},{128,192},{192,0},{1,65},{65,129},{129,193},{193,1... | collective-permute-start | bytes 786440 | tf_op jit(solution)/shard_map/ppermute | solution.py:468
  58.5 12.6 %collective-permute-start.15 = (bf16[16,8192]{1,0:T(8,128)(2,1)S(1)}, bf16[16,8192]{1,0:T(8,128)(2,1)S(1)}, u32[]{:S(2)}, u32[]{:S(2)}) collective-permute-start(bf16[16,8192]{1,0:T(8,128)(2,1)S(1)} %get-tuple-element.64), channel_id=1, source_target_pairs={{0,4},{4,0},{1,5},{5,1},{2,6},{6,2},{3,7},{7,3},{8,12},{12,8},{9,1... | collective-permute-start | bytes 786440 | tf_op jit(solution)/shard_map/ppermute | solution.py:478
  64.7 10.2 %collective-permute-start.19 = (bf16[128,256]{1,0:T(8,128)(2,1)S(1)}, bf16[128,256]{1,0:T(8,128)(2,1)S(1)}, u32[]{:S(2)}, u32[]{:S(2)}) collective-permute-start(bf16[128,256]{1,0:T(8,128)(2,1)S(1)} %get-tuple-element.67), channel_id=1, source_target_pairs={{0,16},{16,0},{32,48},{48,32},{1,17},{17,1},{33,49},{49,33},{2,18}... | collective-permute-start | bytes 196616 | tf_op jit(solution)/shard_map/ppermute | solution.py:478
  66.1 11.1 %collective-permute-start.20 = (bf16[128,256]{1,0:T(8,128)(2,1)S(1)}, bf16[128,256]{1,0:T(8,128)(2,1)S(1)}, u32[]{:S(2)}, u32[]{:S(2)}) collective-permute-start(bf16[128,256]{1,0:T(8,128)(2,1)S(1)} %get-tuple-element.68), channel_id=1, source_target_pairs={{0,32},{16,48},{32,0},{48,16},{1,33},{17,49},{33,1},{49,17},{2,34}... | collective-permute-start | bytes 196616 | tf_op jit(solution)/shard_map/ppermute | solution.py:478
  66.7 15.5 %collective-permute-start.21 = (bf16[128,256]{1,0:T(8,128)(2,1)S(1)}, bf16[128,256]{1,0:T(8,128)(2,1)S(1)}, u32[]{:S(2)}, u32[]{:S(2)}) collective-permute-start(bf16[128,256]{1,0:T(8,128)(2,1)S(1)} %get-tuple-element.69), channel_id=1, source_target_pairs={{0,48},{16,32},{32,16},{48,0},{1,49},{17,33},{33,17},{49,1},{2,50}... | collective-permute-start | bytes 196616 | tf_op jit(solution)/shard_map/ppermute | solution.py:478
  71.1 11.7 %copy-start = (bf16[16,8192]{1,0:T(8,128)(2,1)}, bf16[16,8192]{1,0:T(8,128)(2,1)S(1)}, u32[]{:S(2)}) copy-start(bf16[16,8192]{1,0:T(8,128)(2,1)S(1)} %add_convert_fusion.1.token_ref) | copy-start | bytes 786436
